TPU v7x, 32 devices: a whole 2x2x4 slice. The times are simulated.
32 devices in a mesh: dp: 8 (over z, x), seq: 4 (over y, core).
Axes of the slice: x: 2, y: 2, z: 4, core: 2. Of those that a mesh axis runs over, the one named last changes fastest.
Arguments:
- tokens: bfloat16 [24, 324, 512], P('dp', 'seq'), may hold values from -6 to 6
- res_class: int32 [24], P('dp'), may hold values from 0 to 2, as said below
- skip_mask: int32 [24], P('dp'), may hold values 0 or 1
- w_in: bfloat16 [512, 3072], replicated, may hold values from -0.25 to 0.25
- w_out: bfloat16 [1536, 512], replicated, may hold values from -0.15625 to 0.15625
- spatial: bfloat16 [324, 324], P('seq'), may hold values from -0.3125 to 0.3125
- spatial_bias: float32 [324], P('seq'), may hold values from 0.1 to 1.9
- gain_one: float32 [512], replicated, may hold values from 0.5 to 1.5
- shift_one: float32 [512], replicated, may hold values from -1.75 to 1.75
- gain_two: float32 [1536], replicated, may hold values from 0.5 to 1.5
- shift_two: float32 [1536], replicated, may hold values from -1.75 to 1.75
- cotangent: bfloat16 [24, 324, 512], P('dp', 'seq'), may hold values from -6 to 6
Outputs:
- output: bfloat16 [24, 324, 512], P('dp', 'seq')
- grad_tokens: bfloat16 [24, 324, 512], P('dp', 'seq')
- grad_w_in: float32 [512, 3072], replicated
- grad_w_out: float32 [1536, 512], replicated
- grad_spatial: float32 [324, 324], P('seq')
- grad_bias: float32 [324], P('seq')
- grad_gain_one: float32 [512], replicated
- grad_shift_one: float32 [512], replicated
- grad_gain_two: float32 [1536], replicated
- grad_shift_two: float32 [1536], replicated
Inputs may be any that keep to these rules, and one draw needn't show every extreme that they name: `res_class`: 0, 1, 2 stand for 100, 196 and 324 patches; the images of every index of dp include at least one of class 2.
All inputs are finite; a program needn't handle non-finite values. No bound on the sum of `skip_mask` on one device may be relied on, other than what follows from the above.
Results may differ from a plain program's by a relative error of at most 0.011.
Values may be sent and summed in bfloat16 or wider, within the bound.
No kernel may reach another device: no remote copies, remote signals or barrier semaphores. Data moves between devices by JAX's collectives and lax.ppermute only.
A program may use at most 128 MiB of HBM per device.

v0:
```python
import jax
import jax.numpy as jnp
from jax import lax
from jax.sharding import PartitionSpec as P

PATCHES = 324
SMALL_P = 100
MID_P = 196


EPSILON = 1e-05
SURVIVAL = 0.9


def norm_parts(values):
    center = values - jnp.mean(values, axis=-1, keepdims=True)
    inverse = lax.rsqrt(jnp.mean(center * center, axis=-1, keepdims=True) + EPSILON)
    return (center * inverse, inverse)


def norm_back(grad_out, standard, inverse, gain_vector):
    grad_std = grad_out * gain_vector
    mean_grad = jnp.mean(grad_std, axis=-1, keepdims=True)
    mean_proj = jnp.mean(grad_std * standard, axis=-1, keepdims=True)
    grad_in = inverse * (grad_std - mean_grad - standard * mean_proj)
    return (grad_in, jnp.sum(grad_out * standard, axis=(0, 1)), jnp.sum(grad_out, axis=(0, 1)))


def shards(
    tokens,
    res_class,
    skip_mask,
    w_in,
    w_out,
    spatial,
    spatial_bias,
    gain_one,
    shift_one,
    gain_two,
    shift_two,
    cotangent,
):
    samples, patch_rows, model_width = tokens.shape
    half_width = w_out.shape[0]
    row_anchor = lax.axis_index("seq") * patch_rows
    patch_counts = jnp.where(res_class == 0, SMALL_P, jnp.where(res_class == 1, MID_P, PATCHES))
    positions = row_anchor + jnp.arange(patch_rows)
    valid_rows = (positions[None, :] < patch_counts[:, None]).astype(jnp.float32)
    branch_scale = valid_rows * skip_mask[:, None].astype(jnp.float32) / SURVIVAL
    inputs = tokens.astype(jnp.float32)
    standard_one, inverse_one = norm_parts(inputs)
    normed_low = (standard_one * gain_one + shift_one).astype(jnp.bfloat16)
    hidden = jnp.einsum("spd,dh->sph", normed_low, w_in, preferred_element_type=jnp.float32)
    active, gelu_back = jax.vjp(jax.nn.gelu, hidden)
    gate_u = active[..., :half_width]
    standard_two, inverse_two = norm_parts(active[..., half_width:])
    mixed_low = ((standard_two * gain_two + shift_two) * valid_rows[..., None]).astype(jnp.bfloat16)
    gathered = lax.all_gather(mixed_low, "seq", axis=1, tiled=True)
    spatial_sum = jnp.einsum("pq,sqc->spc", spatial, gathered, preferred_element_type=jnp.float32)
    spatial_out = spatial_sum + spatial_bias[None, :, None]
    product_low = (gate_u * spatial_out).astype(jnp.bfloat16)
    branch = jnp.einsum("spc,cd->spd", product_low, w_out, preferred_element_type=jnp.float32)
    output = (inputs + branch_scale[..., None] * branch).astype(jnp.bfloat16)
    grad_out = cotangent.astype(jnp.float32)
    grad_branch = (grad_out * branch_scale[..., None]).astype(jnp.bfloat16)
    grad_w_out = jnp.einsum(
        "spc,spd->cd", product_low, grad_branch, preferred_element_type=jnp.float32
    )
    grad_product = jnp.einsum("spd,cd->spc", grad_branch, w_out, preferred_element_type=jnp.float32)
    grad_u = grad_product * spatial_out
    grad_spatial_low = (grad_product * gate_u).astype(jnp.bfloat16)
    grad_bias = jnp.sum(grad_spatial_low, axis=(0, 2), dtype=jnp.float32)
    grad_mixed = lax.psum_scatter(
        jnp.einsum(
            "pq,spc->qsc", spatial, grad_spatial_low, preferred_element_type=jnp.float32
        ).astype(jnp.bfloat16),
        "seq",
        scatter_dimension=0,
        tiled=True,
    ).astype(jnp.float32)
    grad_mixed = jnp.transpose(grad_mixed, (1, 0, 2)) * valid_rows[..., None]
    grad_spatial = jnp.einsum(
        "spc,sqc->pq", grad_spatial_low, gathered, preferred_element_type=jnp.float32
    )
    grad_v, grad_gain_two, grad_shift_two = norm_back(
        grad_mixed, standard_two, inverse_two, gain_two
    )
    (grad_hidden,) = gelu_back(jnp.concatenate([grad_u, grad_v], axis=-1))
    grad_hidden_low = grad_hidden.astype(jnp.bfloat16)
    grad_w_in = jnp.einsum(
        "spd,sph->dh", normed_low, grad_hidden_low, preferred_element_type=jnp.float32
    )
    grad_normed = jnp.einsum(
        "sph,dh->spd", grad_hidden_low, w_in, preferred_element_type=jnp.float32
    )
    grad_inner, grad_gain_one, grad_shift_one = norm_back(
        grad_normed, standard_one, inverse_one, gain_one
    )
    grad_tokens = (grad_out + grad_inner).astype(jnp.bfloat16)
    small_grads = jnp.concatenate([grad_gain_one, grad_shift_one, grad_gain_two, grad_shift_two])
    grad_w_in, grad_w_out, small_grads = lax.psum(
        (grad_w_in, grad_w_out, small_grads), ("dp", "seq")
    )
    grad_spatial, grad_bias = lax.psum((grad_spatial, grad_bias), "dp")
    grad_gain_one = small_grads[:model_width]
    grad_shift_one = small_grads[model_width : 2 * model_width]
    grad_gain_two = small_grads[2 * model_width : 2 * model_width + half_width]
    grad_shift_two = small_grads[2 * model_width + half_width :]
    return (
        output,
        grad_tokens,
        grad_w_in,
        grad_w_out,
        grad_spatial,
        grad_bias,
        grad_gain_one,
        grad_shift_one,
        grad_gain_two,
        grad_shift_two,
    )


def solution(mesh):
    placed = (
        P("dp", "seq", None),
        P("dp"),
        P("dp"),
        P(),
        P(),
        P("seq", None),
        P("seq"),
        P(),
        P(),
        P(),
        P(),
        P("dp", "seq", None),
    )
    return jax.shard_map(
        shards,
        mesh=mesh,
        in_specs=placed,
        out_specs=(
            P("dp", "seq", None),
            P("dp", "seq", None),
            P(),
            P(),
            P("seq", None),
            P("seq"),
            P(),
            P(),
            P(),
            P(),
        ),
        check_vma=False,
    )
```

profile of v0, /device:TPU:0, one launch (start us, length us, event | category | flops | bytes accessed | tf_op | source)
XLA Modules:
  0.0 418.5 jit_solution(6637738261397913409)
XLA Ops:
  7.3 0.8 compare_select_fusion.2
  8.1 0.7 convert_element_type.52
  8.8 1.1 convert_reduce_fusion.1
  9.9 1.2 fusion.55
  11.1 4.3 %multiply_multiply_fusion.2 = (f32[3,81,3072]{2,1,0:T(8,128)S(1)}, f32[3,81,3072]{2,1,0:T(8,128)}) fusion(bf16[512,3072]{1,0:T(8,128)(2,1)S(1)} %copy-done, bf16[3,81,512]{2,1,0:T(8,128)(2,1)} %param.12, f32[512]{0:T(512)} %param.20, f32[512]{0:T(512)} %param.19, f32[3,81]{1,0:T(4,128)S(1)} %add_rsqrt_fusion.1, f32[3,81]{1,0:T(4,128)S(1)} %broadcast_multiply_fusion.5), kind=kOutput, calls=%fused_computation.18 | convolution fusion | flops 771130368 | bytes 9372568 | tf_op jit(solution)/shard_map/spd,dh->sph/dot_general | solution.py:53
  15.7 2.1 convert_reduce_fusion
  17.8 0.9 copy-done.6
  18.6 2.6 fusion.7
  21.4 0.6 dynamic-slice
  22.7 68.2 %all-reduce.8.cloned.1.call-done = bf16[324,3,1536]{2,0,1:T(8,128)(2,1)} async-done(((bf16[324,3,1536]{2,0,1:T(8,128)(2,1)}), bf16[324,3,1536]{2,0,1:T(8,128)(2,1)}) %all-reduce.8.cloned.1.call-update) | async-done | bytes 2986000
  90.9 2.7 fusion.25
  93.6 3.8 fusion.23
  97.4 1.5 copy.22
  99.0 33.4 %all-gather.2.cloned.1.call-done = bf16[3,324,1536]{2,0,1:T(4,128)(2,1)} async-done(((bf16[3,81,1536]{2,0,1:T(4,128)(2,1)}), bf16[3,324,1536]{2,0,1:T(4,128)(2,1)}) %all-gather.2.cloned.1.call-update) | async-done | bytes 2986000 | tf_op jit(solution)/shard_map/all_gather | solution.py:58
  132.4 4.1 fusion.40
  136.5 0.2 all-reduce.10.cloned.1.call-start
  136.8 4.2 %fusion.65 = (f32[3,81,1536]{2,1,0:T(8,128)S(1)}, bf16[3,81,1536]{2,1,0:T(8,128)(2,1)S(1)}) fusion(f32[3,81,1536]{2,1,0:T(8,128)} %get-tuple-element.33, f32[3,81,3072]{2,1,0:T(8,128)} %copy-done.1, f32[81]{0:T(128)S(1)} %copy-done.18, bf16[81,324]{1,0:T(8,128)(2,1)S(1)} %copy-done.12, bf16[3,324,1536]{2,0,1:T(4,128)(2,1)} %all-gather.2.cloned.1.call-done), kind=kOutput, calls=%fused_computation.88 | convolution fusion | flops 243357696 | bytes 8264268 | tf_op jit(solution)/shard_map/pq,sqc->spc/dot_general | solution.py:59
  141.1 0.2 copy-done.7
  141.3 2.5 fusion.6
  143.9 4.7 %convolution_bitcast_fusion = f32[512,3072]{1,0:T(8,128)} fusion(bf16[3,81,3072]{2,1,0:T(8,128)(2,1)S(1)} %fusion.6, bf16[3,81,512]{2,1,0:T(8,128)(2,1)S(1)} %copy-done.5, f32[512]{0:T(512)S(1)} %copy-done.16, f32[512]{0:T(512)S(1)} %copy-done.14, f32[3,81]{1,0:T(4,128)S(1)} %add_rsqrt_fusion.1, f32[3,81]{1,0:T(4,128)S(1)} %broadcast_multiply_fusion.5), kind=kOutput, calls=%fused_computation | convolution fusion | flops 765158400 | bytes 8039320 | tf_op jit(solution)/shard_map/spd,sph->dh/dot_general | solution.py:90
  148.6 2.8 convolution_bitcast_fusion.1
  151.4 21.9 %psum.38 = f32[81]{0:T(128)} all-reduce(f32[81]{0:T(128)S(1)} %get-tuple-element.20), channel_id=1, replica_groups=mesh['dp'=8,'seq'=4] {'dp'}, use_global_device_ids=true, to_apply=%region_13.14 | all-reduce | flops 81 | bytes 648 | tf_op jit(solution)/shard_map/psum | solution.py:104
  173.3 3.3 fusion.54
  176.6 37.1 %psum.39 = f32[4096]{0:T(1024)S(1)} all-reduce(f32[4096]{0:T(1024)S(1)} %pad_maximum_fusion.1), channel_id=1, replica_groups=mesh['dp'=8,'seq'=4] {'dp','seq'}, use_global_device_ids=true, to_apply=%region_18.19 | all-reduce | flops 4096 | bytes 32768 | tf_op jit(solution)/shard_map/psum | solution.py:101
  213.7 0.6 fusion.67
  214.3 0.6 fusion.66
  214.9 2.1 fusion.57
  217.0 3.7 fusion.37
  220.7 182.6 %all-reduce.10.cloned.1.call-done = (f32[512,3072]{1,0:T(8,128)}, f32[1536,512]{1,0:T(8,128)}) async-done(((f32[512,3072]{1,0:T(8,128)}, f32[1536,512]{1,0:T(8,128)}), (f32[512,3072]{1,0:T(8,128)}, f32[1536,512]{1,0:T(8,128)})) %all-reduce.10.cloned.1.call-update) | async-done | bytes 9437200 | tf_op jit(solution)/shard_map/psum | solution.py:101
  403.2 6.4 %copy.39 = f32[512,3072]{1,0:T(8,128)} copy(f32[512,3072]{1,0:T(8,128)} %get-tuple-element.39) | data formatting | bytes 12582912
  409.6 1.7 copy.40
  411.3 0.7 copy.41
  (58 shorter events, 0.6 us)
Async XLA Ops:
  7.2 3.9 copy-start
  7.2 83.7 %all-reduce.8.cloned.1.call-start = ((), (), s32[]{:S(2)}) async-start(), calls=%async_computation.2 | async-start | bytes 6045696
  11.1 4.6 %copy-start.9 = (bf16[3,81,512]{2,1,0:T(8,128)(2,1)S(1)}, bf16[3,81,512]{2,1,0:T(8,128)(2,1)}, u32[]{:S(2)}) copy-start(bf16[3,81,512]{2,1,0:T(8,128)(2,1)} %param.23) | copy-start | bytes 746500
  11.1 4.5 %copy-start.11 = (bf16[1536,512]{1,0:T(8,128)(2,1)S(1)}, bf16[1536,512]{1,0:T(8,128)(2,1)}, u32[]{:S(2)}) copy-start(bf16[1536,512]{1,0:T(8,128)(2,1)} %param.16) | copy-start | bytes 4718596
  15.4 2.3 copy-start.1
  15.6 3.0 copy-start.12
  17.8 0.9 copy-start.6
  18.6 2.7 copy-start.19
  18.6 72.2 %copy-start.15 = (f32[1536]{0:T(1024)S(1)}, f32[1536]{0:T(1024)}, u32[]{:S(2)}) copy-start(f32[1536]{0:T(1024)} %param.21) | copy-start | bytes 18436
  21.3 72.3 %copy-start.17 = (f32[1536]{0:T(1024)S(1)}, f32[1536]{0:T(1024)}, u32[]{:S(2)}) copy-start(f32[1536]{0:T(1024)} %param.22) | copy-start | bytes 18436
  21.3 111.1 %all-gather.2.cloned.1.call-start = ((), (), s32[]{:S(2)}) async-start(), calls=%async_computation | async-start | bytes 4976640 | tf_op jit(solution)/shard_map/all_gather | solution.py:58
  98.9 37.8 %copy-start.18 = (f32[81]{0:T(128)S(1)}, f32[81]{0:T(128)}, u32[]{:S(2)}) copy-start(f32[81]{0:T(128)} %param.18) | copy-start | bytes 976
  98.9 121.7 %all-reduce.6.cloned.1.call-start = ((), (), s32[]{:S(2)}) async-start(), calls=%async_computation.1 | async-start | bytes 270336 | tf_op jit(solution)/shard_map/psum | solution.py:104
  136.5 266.7 %all-reduce.10.cloned.1.call-start = ((), (), s32[]{:S(2)}) async-start(), calls=%async_computation.3 | async-start | bytes 18874368 | tf_op jit(solution)/shard_map/psum | solution.py:101
  136.8 4.3 %copy-start.2 = (f32[3,81,1536]{2,1,0:T(8,128)S(1)}, f32[3,81,1536]{2,1,0:T(8,128)}, u32[]{:S(2)}) copy-start(f32[3,81,1536]{2,1,0:T(8,128)} %get-tuple-element.22) | copy-start | bytes 4478980
  136.8 4.5 %copy-start.7 = (f32[3,81,3072]{2,1,0:T(8,128)S(1)}, f32[3,81,3072]{2,1,0:T(8,128)}, u32[]{:S(2)}) copy-start(f32[3,81,3072]{2,1,0:T(8,128)} %get-tuple-element.32) | copy-start | bytes 8957956
  141.0 7.6 %copy-start.4 = (bf16[3,81,1536]{2,1,0:T(8,128)(2,1)}, bf16[3,81,1536]{2,1,0:T(8,128)(2,1)S(1)}, u32[]{:S(2)}) copy-start(bf16[3,81,1536]{2,1,0:T(8,128)(2,1)S(1)} %get-tuple-element.26) | copy-start | bytes 2239492
  141.3 2.5 copy-start.5
  141.3 2.5 copy-start.14
  141.3 2.6 copy-start.16
  143.9 4.7 %copy-start.3 = (bf16[3,81,3072]{2,1,0:T(8,128)(2,1)}, bf16[3,81,3072]{2,1,0:T(8,128)(2,1)S(1)}, u32[]{:S(2)}) copy-start(bf16[3,81,3072]{2,1,0:T(8,128)(2,1)S(1)} %fusion.6) | copy-start | bytes 4478980
  143.9 4.7 %copy-start.10 = (bf16[3,81,512]{2,1,0:T(8,128)(2,1)S(1)}, bf16[3,81,512]{2,1,0:T(8,128)(2,1)}, u32[]{:S(2)}) copy-start(bf16[3,81,512]{2,1,0:T(8,128)(2,1)} %param.23) | copy-start | bytes 746500
  403.2 6.4 %copy-start.8 = (f32[1536,512]{1,0:T(8,128)S(1)}, f32[1536,512]{1,0:T(8,128)}, u32[]{:S(2)}) copy-start(f32[1536,512]{1,0:T(8,128)} %get-tuple-element.40) | copy-start | bytes 9437188
  409.6 1.7 copy-start.13
Sparse Core Ops, SparseCore 0:
  21.4 69.3 all-reduce.7
  99.1 33.2 all-gather.1
  136.7 69.7 all-reduce.5
  212.7 190.4 all-reduce.9
where the time goes:
time: 419 us; the launch traced here: 418 us
  waiting for transfers between devices  284 us (68%)
  blocking collectives  58.9 us (14%)
  matrix products  31.8 us (8%)
  other arithmetic  15.3 us (4%)
  between operations  14.7 us (4%)
  local copies, waits for them, and re-layouts  13.2 us (3%)
    psum x1, waiting for transfers between devices, shards(): lax.psum((grad_w_in, grad_w_out, small_grads), ('dp', 'seq'))  183 us
    unnamed x5, waiting for transfers between devices  68.2 us
    psum x1, blocking collectives, shards(): lax.psum((grad_w_in, grad_w_out, small_grads), ('dp', 'seq'))  37.1 us
    all_gather x1, waiting for transfers between devices, shards(): gathered = lax.all_gather(mixed_low, 'seq', axis=1, tiled=True)  33.4 us
    psum x1, blocking collectives, shards(): grad_spatial, grad_bias = lax.psum((grad_spatial, grad_bias), 'dp')  21.9 us
    unnamed x44, local copies, waits for them, and re-layouts  10.5 us
  transfers between devices with their start and end apart: 4, of which 3 were waited for; matrix products, arithmetic and copies ran while one was open for 6% of the time, Pallas kernels for 0%

commit v1 on v0

v1 whole, which is shorter than its diff:
```python
import functools

import jax
import jax.numpy as jnp
from jax import lax
from jax.experimental import pallas as pl
from jax.experimental.pallas import tpu as pltpu
from jax.sharding import PartitionSpec as P

PATCHES = 324
SMALL_P = 100
MID_P = 196

EPSILON = 1e-05
SURVIVAL = 0.9

BF = jnp.bfloat16
F32 = jnp.float32
CHUNK = 16
VM = pl.BlockSpec(memory_space=pltpu.VMEM)
SM = pl.BlockSpec(memory_space=pltpu.SMEM)
HB = pl.BlockSpec(memory_space=pl.ANY)


def round_up(size, multiple):
    return -(-size // multiple) * multiple


def dot(a, b, ca, cb):
    return lax.dot_general(a, b, (((ca,), (cb,)), ((), ())), preferred_element_type=F32)


def iota(shape, axis):
    return lax.broadcasted_iota(jnp.int32, shape, axis)


def rows_at(start, size, multiple):
    return pl.ds(pl.multiple_of(start, multiple), size)


def call(body, outs, ins, scratch=(), specs=None, out_specs=None, flops=0, nbytes=0, **more):
    return pl.pallas_call(
        body,
        out_shape=outs,
        in_specs=specs if specs is not None else [VM] * len(ins),
        out_specs=out_specs if out_specs is not None else [VM] * len(outs),
        scratch_shapes=list(scratch),
        compiler_params=pltpu.CompilerParams(vmem_limit_bytes=48 * 2**20),
        cost_estimate=pl.CostEstimate(flops=flops, bytes_accessed=nbytes, transcendentals=0),
        **more,
    )(*ins)


def shape_of(shape, dtype):
    return jax.ShapeDtypeStruct(shape, dtype)


def project_body(first, pad, *refs):
    if first:
        tok_a, tok_b, g1, s1, wu, wv, normed, gu, dgu, v, dgv, st, xs, hid, tile = refs
    else:
        tok_a, tok_b, g1, s1, wu, wv, n_in, st_in, normed, gu, dgu, v, dgv, st, xs, hid, tile = refs
    samples, rows, width = tok_a.shape
    half = wu.shape[1]
    base = 0 if first else 2 * pad
    tile[...] = jnp.zeros_like(tile)
    xs[rows // 8 * 8 :, :] = jnp.zeros((pad - rows // 8 * 8, width), F32)
    gain, shift = g1[...], s1[...]
    for i in range(samples):
        for b, tok in enumerate((tok_a, tok_b)):
            xs[0:rows, :] = tok[i].astype(F32)

            def norm_chunk(c, carry, i=i, b=b):
                x = xs[rows_at(c * CHUNK, CHUNK, CHUNK), :]
                center = x - jnp.mean(x, axis=-1, keepdims=True)
                inverse = lax.rsqrt(jnp.mean(center * center, axis=-1, keepdims=True) + EPSILON)
                out = center * inverse * gain + shift
                normed[i, rows_at(base + b * pad + c * CHUNK, CHUNK, CHUNK), :] = out.astype(BF)
                return carry

            lax.fori_loop(0, pad // CHUNK, norm_chunk, 0, unroll=3)
        both = normed[i, base : base + 2 * pad, :]
        hid[i, :, 0:half] = dot(both, wu[...], 1, 0)
        hid[i, :, half:] = dot(both, wv[...], 1, 0)
        if not first:
            normed[i, 0:base, :] = n_in[i]
    c0 = 0.7978845608028654
    c1 = 0.7978845608028654 * 0.044715

    def gelu_pair(h):
        a = (c1 * h) * h
        s = 0.5 + 0.5 * jnp.tanh(h * (c0 + a))
        g = h * s
        return g, s + (2.0 * g) * (1.0 - s) * (c0 + 3.0 * a)

    lane = iota((CHUNK, 128), 1)
    for i in range(samples):
        for b in range(2):
            blk = i * 4 + b + (0 if first else 2)

            def gelu_chunk(c, carry, i=i, b=b, blk=blk):
                at = rows_at(b * pad + c * CHUNK, CHUNK, CHUNK)
                g, d = gelu_pair(hid[i, at, 0:half])
                gu[i, at, :] = g.astype(BF)
                dgu[i, at, :] = d.astype(BF)
                g, d = gelu_pair(hid[i, at, half:])
                v[i, at, :] = g
                dgv[i, at, :] = d.astype(BF)
                mean = jnp.mean(g, axis=-1, keepdims=True)
                center = g - mean
                square = jnp.sum(center * center, axis=-1, keepdims=True)
                here = rows_at(c * CHUNK, CHUNK, CHUNK)
                old = tile[here, :]
                tile[here, :] = jnp.where(
                    lane == 2 * blk, mean, jnp.where(lane == 2 * blk + 1, square, old)
                )
                return carry

            lax.fori_loop(0, pad // CHUNK, gelu_chunk, 0, unroll=2)
    flipped = jnp.transpose(tile[...])[0 : st.shape[0], :]
    st[...] = flipped if first else flipped + st_in[...]


def project(first, pad, tok_a, tok_b, g1, s1, wu, wv, extra):
    samples, rows, width = tok_a.shape
    half = wu.shape[1]
    n_rows = 2 * pad if first else 4 * pad
    st_rows = round_up(samples * 8, 8)
    outs = [
        shape_of((samples, n_rows, width), BF),
        shape_of((samples, 2 * pad, half), BF),
        shape_of((samples, 2 * pad, half), BF),
        shape_of((samples, 2 * pad, half), F32),
        shape_of((samples, 2 * pad, half), BF),
        shape_of((st_rows, 128), F32),
    ]
    scratch = [
        pltpu.VMEM((pad, width), F32),
        pltpu.VMEM((samples, 2 * pad, 2 * half), F32),
        pltpu.VMEM((128, 128), F32),
    ]
    flops = 2 * samples * 2 * pad * width * 2 * half
    return call(
        functools.partial(project_body, first, pad),
        outs,
        [tok_a, tok_b, g1, s1, wu, wv, *extra],
        scratch,
        flops=flops,
        nbytes=6_000_000,
        name="project",
    )


def position_map(seq, rows, pad, n, columns):
    a = iota((columns, n * pad), 0)
    j = iota((columns, n * pad), 1)
    r = jnp.zeros_like(j)
    for k in range(1, n):
        r = r + (j >= k * pad).astype(jnp.int32)
    q = j - r * pad
    hit = (a == (r ^ seq) * rows + q) & (q < rows)
    hit = hit | ((a == n * rows) & (j == pad - 1)) | ((a == n * rows + 1) & (j == pad - 2))
    return jnp.where(hit, 1.0, 0.0).astype(BF)


def spatial_body(
    n, pad, meta, va, vb, gua, gub, dgua, dgub, normed, c0, c1, c2, c3, wo, g2, s2, t0, t1, t2, t3,
    mixed, prod, gs, ghu, gmix, cols, st, o_keep, o_send, u_keep, u_send,
    pm, sp, spt, gb, so, gp, tile, ow, uw,
):
    samples, rows, half = c0.shape[0] - 1, c0.shape[1], wo.shape[0]
    seq, dp = meta[0], meta[1]
    cots = (c0, c1, c2, c3)
    columns = pm.shape[0]
    pm[...] = position_map(seq, rows, pad, n, columns)
    low = rows // 16 * 16
    for r in range(n):
        sp[r * pad + low : (r + 1) * pad, :] = jnp.zeros((pad - low, n * pad), BF)
        sp[r * pad : r * pad + rows, :] = dot(cots[r][samples, :, 0:columns], pm[...], 1, 0).astype(BF)
    spt[...] = jnp.transpose(sp[...].astype(F32)).astype(BF)
    whole = half * n
    stats = (t0, t1, t2, t3)
    tile[...] = jnp.zeros_like(tile)
    for i in range(samples):
        for r in range(n):
            means = [stats[k][pl.ds(2 * (i * n + (r ^ k)), 1), :] for k in range(n)]
            squares = [stats[k][pl.ds(2 * (i * n + (r ^ k)) + 1, 1), :] for k in range(n)]
            mean = ((means[0] + means[1]) + (means[2] + means[3])) / n
            spread = (squares[0] + squares[1]) + (squares[2] + squares[3])
            for k in range(n):
                spread = spread + half * (means[k] - mean) * (means[k] - mean)
            blk = 2 * (i * n + r)
            tile[blk : blk + 1, :] = mean
            tile[blk + 1 : blk + 2, :] = lax.rsqrt(spread / whole + EPSILON)
    cols[...] = jnp.transpose(tile[...])
    row = iota((CHUNK, 1), 0)
    gain, shift = g2[...], s2[...]

    def position(c, r):
        p = c * CHUNK + row
        return p, (seq ^ r) * rows + p

    for i in range(samples):
        count = meta[2 + i]
        for r in range(n):
            v = (va, vb)[r // 2]
            blk = 2 * (i * n + r)

            def mix_chunk(c, carry, i=i, r=r, v=v, blk=blk, count=count):
                p, where = position(c, r)
                valid = jnp.where((p < rows) & (where < count), 1.0, 0.0)
                here = rows_at(c * CHUNK, CHUNK, CHUNK)
                mean, inverse = cols[here, blk : blk + 1], cols[here, blk + 1 : blk + 2]
                x = v[i, rows_at((r % 2) * pad + c * CHUNK, CHUNK, CHUNK), :]
                out = ((x - mean) * inverse * gain + shift) * valid
                if r == 0:
                    out = jnp.where(p >= pad - 2, 1.0, out)
                mixed[i, rows_at(r * pad + c * CHUNK, CHUNK, CHUNK), :] = out.astype(BF)
                return carry

            lax.fori_loop(0, pad // CHUNK, mix_chunk, 0, unroll=3)
            p = iota((rows, 1), 0)
            keep = jnp.where((seq ^ r) * rows + p < count, meta[2 + samples + i], 0).astype(F32)
            scale = keep / SURVIVAL
            gb[i, r * pad + low : (r + 1) * pad, :] = jnp.zeros((pad - low, gb.shape[2]), BF)
            gb[i, r * pad : r * pad + rows, :] = (cots[r][i].astype(F32) * scale).astype(BF)
        so[i] = dot(sp[...], mixed[i], 1, 0)
        gp[i] = dot(gb[i], wo[...], 1, 1)
    for i in range(samples):
        for r in range(n):
            gu, dgu = (gua, gub)[r // 2], (dgua, dgub)[r // 2]

            def gate_chunk(c, carry, i=i, r=r, gu=gu, dgu=dgu):
                src = rows_at((r % 2) * pad + c * CHUNK, CHUNK, CHUNK)
                at = rows_at(r * pad + c * CHUNK, CHUNK, CHUNK)
                g = gu[i, src, :].astype(F32)
                s, q = so[i, at, :], gp[i, at, :]
                prod[i, at, :] = (g * s).astype(BF)
                gs[i, at, :] = (q * g).astype(BF)
                ghu[i, at, :] = (q * s * dgu[i, src, :].astype(F32)).astype(BF)
                return carry

            lax.fori_loop(0, pad // CHUNK, gate_chunk, 0, unroll=3)
        so[i] = dot(spt[...], gs[i], 1, 0)
    total_o = dot(prod[0], gb[0], 0, 0)
    total_u = dot(normed[0], ghu[0], 0, 0)
    for i in range(1, samples):
        total_o = total_o + dot(prod[i], gb[i], 0, 0)
        total_u = total_u + dot(normed[i], ghu[i], 0, 0)
    ow[...] = total_o
    uw[...] = total_u
    store_shards(dp, ow, o_keep, o_send)
    store_shards(dp, uw, u_keep, u_send)
    lane = iota((CHUNK, 128), 1)
    tile[...] = jnp.zeros_like(tile)
    for i in range(samples):
        count = meta[2 + i]
        for r in range(n):
            v = (va, vb)[r // 2]
            blk = 2 * (i * n + r)

            def back_chunk(c, carry, i=i, r=r, v=v, blk=blk, count=count):
                p, where = position(c, r)
                valid = jnp.where((p < rows) & (where < count), 1.0, 0.0)
                here = rows_at(c * CHUNK, CHUNK, CHUNK)
                at = rows_at(r * pad + c * CHUNK, CHUNK, CHUNK)
                mean, inverse = cols[here, blk : blk + 1], cols[here, blk + 1 : blk + 2]
                x = v[i, rows_at((r % 2) * pad + c * CHUNK, CHUNK, CHUNK), :]
                g = so[i, at, :] * valid
                gmix[i, at, :] = g
                t = g * gain
                first = jnp.sum(t, axis=-1, keepdims=True)
                second = jnp.sum(t * ((x - mean) * inverse), axis=-1, keepdims=True)
                tile[here, :] = jnp.where(
                    lane == blk, first, jnp.where(lane == blk + 1, second, tile[here, :])
                )
                return carry

            lax.fori_loop(0, pad // CHUNK, back_chunk, 0, unroll=3)
    st[...] = jnp.transpose(tile[...])[0 : st.shape[0], :]


def store_shards(dp, whole, keep, send):
    size = keep.shape[1]
    for e in range(2):
        here = whole[rows_at(((dp ^ (2 * e)) & 3) * size, size, 16), :]
        keep[e] = here.astype(BF)
        here = whole[rows_at(((dp ^ (2 * e + 1)) & 3) * size, size, 16), :]
        send[e] = here.astype(BF)


def branch_body(n, pad, meta, prod, wo, gs, mixed, keep, send, pm):
    samples = prod.shape[0]
    rows = keep.shape[2]
    pm[...] = position_map(meta[0], rows, pad, n, pm.shape[0])
    total = dot(gs[0], mixed[0], 1, 1)
    for i in range(1, samples):
        total = total + dot(gs[i], mixed[i], 1, 1)
    placed = dot(total.astype(BF), pm[...], 1, 1)
    for r in range(n):
        out = (keep, send)[r % 2]
        out[r // 2, samples, :, 0 : pm.shape[0]] = placed[r * pad : r * pad + rows, :].astype(BF)
        out[r // 2, samples, :, pm.shape[0] :] = jnp.zeros((rows, out.shape[3] - pm.shape[0]), BF)
    for i in range(samples):
        full = dot(prod[i], wo[...], 1, 0)
        for r in range(n):
            out = (keep, send)[r % 2]
            out[r // 2, i] = full[r * pad : r * pad + rows, :].astype(BF)


def back_body(
    n, pad, meta, gmix, va, vb, dgva, dgvb, cols, t0, t1, t2, t3, g2, normed, ghu, wu, wv,
    v_keep, v_send, keep, send, small,
    tile, col, ghv, vw, acc,
):
    samples, rows, half = gmix.shape[0], keep.shape[2], gmix.shape[2]
    dp = meta[1]
    stats = (t0, t1, t2, t3)
    tile[...] = jnp.zeros_like(tile)
    for i in range(samples):
        for r in range(n):
            blk = 2 * (i * n + r)
            for j in range(2):
                part = [stats[k][pl.ds(2 * (i * n + (r ^ k)) + j, 1), :] for k in range(n)]
                tile[blk + j : blk + j + 1, :] = ((part[0] + part[1]) + (part[2] + part[3])) / (
                    half * n
                )
    col[...] = jnp.transpose(tile[...])
    gain = g2[...]
    acc[...] = jnp.zeros_like(acc)
    for i in range(samples):
        for r in range(n):
            v, dgv = (va, vb)[r // 2], (dgva, dgvb)[r // 2]
            blk = 2 * (i * n + r)

            def back_chunk(c, carry, i=i, r=r, v=v, dgv=dgv, blk=blk):
                here = rows_at(c * CHUNK, CHUNK, CHUNK)
                at = rows_at(r * pad + c * CHUNK, CHUNK, CHUNK)
                src = rows_at((r % 2) * pad + c * CHUNK, CHUNK, CHUNK)
                mean, inverse = cols[here, blk : blk + 1], cols[here, blk + 1 : blk + 2]
                first, second = col[here, blk : blk + 1], col[here, blk + 1 : blk + 2]
                standard = (v[i, src, :] - mean) * inverse
                g = gmix[i, at, :]
                grad = inverse * (g * gain - first - standard * second)
                ghv[i, at, :] = (grad * dgv[i, src, :].astype(F32)).astype(BF)
                acc[0] += g * standard
                acc[1] += g
                return carry

            lax.fori_loop(0, pad // CHUNK, back_chunk, 0, unroll=3)
    small[...] = jnp.zeros_like(small)
    small[0:1, :] = jnp.sum(acc[0], axis=0, keepdims=True)
    small[1:2, :] = jnp.sum(acc[1], axis=0, keepdims=True)
    total = dot(normed[0], ghv[0], 0, 0)
    for i in range(1, samples):
        total = total + dot(normed[i], ghv[i], 0, 0)
    vw[...] = total
    store_shards(dp, vw, v_keep, v_send)
    for i in range(samples):
        full = dot(ghu[i], wu[...], 1, 1) + dot(ghv[i], wv[...], 1, 1)
        for r in range(n):
            out = (keep, send)[r % 2]
            out[r // 2, i] = full[r * pad : r * pad + rows, :].astype(BF)


def tokens_body(tok, cot, a, b, ea, eb, g1, small, grad_tokens, extra):
    samples, rows, width = tok.shape
    half = small.shape[1]
    gain = g1[...]
    extra[...] = jnp.zeros_like(extra)
    extra[0:rows, :] = (ea[...].astype(F32) + eb[...].astype(F32)).astype(BF)
    sums = jnp.zeros((1, width), F32)
    shifts = jnp.zeros((1, width), F32)
    for i in range(samples):
        x = tok[i].astype(F32)
        center = x - jnp.mean(x, axis=-1, keepdims=True)
        inverse = lax.rsqrt(jnp.mean(center * center, axis=-1, keepdims=True) + EPSILON)
        standard = center * inverse
        g = a[i].astype(F32) + b[i].astype(F32)
        t = g * gain
        first = jnp.mean(t, axis=-1, keepdims=True)
        second = jnp.mean(t * standard, axis=-1, keepdims=True)
        grad = cot[i].astype(F32) + inverse * (t - first - standard * second)
        grad_tokens[i] = grad.astype(BF)
        sums = sums + jnp.sum(g * standard, axis=0, keepdims=True)
        shifts = shifts + jnp.sum(g, axis=0, keepdims=True)
    row = iota((16, width), 0)
    low = rows // 16 * 16
    tail = jnp.where(row == 8, sums, jnp.where(row == 9, shifts, 0.0))
    two = jnp.concatenate(
        [small[0:2, :], jnp.zeros((2, width - half), F32)], axis=1
    )
    tail = jnp.where(row == 10, two[0:1, :], jnp.where(row == 11, two[1:2, :], tail))
    extra[low : low + 16, :] = (extra[low : low + 16, :].astype(F32) + tail).astype(BF)


def sources(meta):
    seq, shard = meta[0], meta[1] & 3
    out = []
    for flip in (0, 1):
        s = seq ^ flip
        core = s & 1
        out += [
            (shard, s),
            (shard ^ (1 - core), s ^ (2 * core)),
            (shard ^ core, s ^ (2 * (1 - core))),
            (shard ^ 1, s ^ 2),
        ]
    return out


def place_body(by_column, offset, has_base, meta, *refs):
    pieces = refs[:8]
    out, wide, sems = refs[8 + has_base :]
    size, width = pieces[0].shape[1:]
    copies = []
    for k, (shard, seq) in enumerate(sources(meta)):
        for e in range(2):
            slot = 2 * k + e
            wide[slot] = pieces[k][e].astype(F32)
            at = shard ^ (2 * e)
            if by_column:
                dst = out.at[
                    rows_at(at * size, size, 16),
                    rows_at(offset + seq * width, width, 128),
                ]
            else:
                dst = out.at[rows_at((seq * 4 + at) * size, size, 16), :]
            copy = pltpu.make_async_copy(wide.at[slot], dst, sems.at[slot])
            copy.start()
            copies.append(copy)
    for copy in copies:
        copy.wait()


def place(meta, pieces, out_shape, by_column, offset=0, base=None):
    size, width = pieces[0].shape[1:]
    ins = [meta, *pieces] + ([base] if base is not None else [])
    return call(
        functools.partial(place_body, by_column, offset, int(base is not None)),
        [shape_of(out_shape, F32)],
        ins,
        [pltpu.VMEM((16, size, width), F32), pltpu.SemaphoreType.DMA((16,))],
        specs=[SM] + [VM] * 8 + ([HB] if base is not None else []),
        out_specs=[HB],
        input_output_aliases={9: 0} if base is not None else {},
        nbytes=10_000_000,
        name="place",
    )[0]


def solution(mesh):
    n, m = mesh.shape["seq"], mesh.shape["dp"]

    def over_seq(x, flip):
        return lax.ppermute(x, "seq", [(i, i ^ flip) for i in range(n)])

    def over_dp(x, flip):
        return lax.ppermute(x, "dp", [(i, i ^ flip) for i in range(m)])

    def mixed_axes(x, core_of_x):
        pairs = []
        for d in range(m):
            for s in range(n):
                other = (d ^ 1, s) if s & 1 == core_of_x else (d, s ^ 2)
                pairs.append((d * n + s, other[0] * n + other[1]))
        return lax.ppermute(x, ("dp", "seq"), pairs)

    def add(a, b):
        return (a.astype(F32) + b.astype(F32)).astype(BF)

    def reduce_gather(keep, send):
        got = over_dp(send, 1)
        mine = add(keep[0], got[0])
        other = add(keep[1], got[1])
        mine = add(mine, over_dp(other, 2))
        flip = 4
        while flip < m:
            mine = add(mine, over_dp(mine, flip))
            flip *= 2
        pair = jnp.stack([mine, over_dp(mine, 2)])
        first = mixed_axes(pair, 0)
        second = mixed_axes(pair, 1)
        third = mixed_axes(first, 1)
        own = [pair, first, second, third]
        return own + [over_seq(x, 1) for x in own]

    def shards(
        tokens,
        res_class,
        skip_mask,
        w_in,
        w_out,
        spatial,
        spatial_bias,
        gain_one,
        shift_one,
        gain_two,
        shift_two,
        cotangent,
    ):
        samples, rows, width = tokens.shape
        gate = w_out.shape[0]
        half = gate // n
        pad = round_up(rows + 2, 16)
        full = n * pad
        columns = round_up(n * rows + 2, 128)
        seq, dp = lax.axis_index("seq"), lax.axis_index("dp")
        counts = jnp.where(res_class == 0, SMALL_P, jnp.where(res_class == 1, MID_P, PATCHES))
        meta = jnp.concatenate([seq[None], dp[None], counts, skip_mask]).astype(jnp.int32)

        t0 = tokens
        t1 = over_seq(t0, 1)
        t2 = over_seq(t0, 2)
        t3 = over_seq(t2, 1)
        high = lax.reduce_precision(spatial_bias, 8, 7)
        side = jnp.stack([high, spatial_bias - high], axis=1).astype(BF)
        packed = jnp.concatenate([spatial, side], axis=1)
        packed = jnp.pad(packed, ((0, 0), (0, width - packed.shape[1])))
        c0 = jnp.concatenate([cotangent, packed[None]])
        c1 = over_seq(c0, 1)
        c2 = over_seq(c0, 2)
        c3 = over_seq(c2, 1)

        wu = lax.dynamic_slice(w_in, (0, seq * half), (width, half))
        wv = lax.dynamic_slice(w_in, (0, gate + seq * half), (width, half))
        wo = lax.dynamic_slice(w_out, (seq * half, 0), (half, width))
        g2 = lax.dynamic_slice(gain_two, (seq * half,), (half,))[None]
        s2 = lax.dynamic_slice(shift_two, (seq * half,), (half,))[None]
        g1, s1 = gain_one[None], shift_one[None]

        na, gua, dgua, va, dgva, sa = project(True, pad, t0, t1, g1, s1, wu, wv, ())
        normed, gub, dgub, vb, dgvb, st = project(False, pad, t2, t3, g1, s1, wu, wv, (na, sa))
        stats = [st] + [over_seq(st, k) for k in range(1, n)]

        big = shape_of((samples, full, half), BF)
        square = round_up(samples * 2 * n, 8)
        o_shape = shape_of((2, half // 4, width), BF)
        u_shape = shape_of((2, width // 4, half), BF)
        outs = [
            big, big, big, big,
            shape_of((samples, full, half), F32),
            shape_of((128, 128), F32),
            shape_of((square, 128), F32),
            o_shape, o_shape, u_shape, u_shape,
        ]
        scratch = [
            pltpu.VMEM((columns, full), BF),
            pltpu.VMEM((full, full), BF),
            pltpu.VMEM((full, full), BF),
            pltpu.VMEM((samples, full, width), BF),
            pltpu.VMEM((samples, full, half), F32),
            pltpu.VMEM((samples, full, half), F32),
            pltpu.VMEM((128, 128), F32),
            pltpu.VMEM((half, width), F32),
            pltpu.VMEM((width, half), F32),
        ]
        ins = [meta, va, vb, gua, gub, dgua, dgub, normed, c0, c1, c2, c3, wo, g2, s2, *stats]
        mixed, prod, gs, ghu, gmix, cols, st2, o_keep, o_send, u_keep, u_send = call(
            functools.partial(spatial_body, n, pad),
            outs,
            ins,
            scratch,
            specs=[SM] + [VM] * (len(ins) - 1),
            flops=3_000_000_000,
            nbytes=12_000_000,
            name="spatial",
        )
        o_pieces = reduce_gather(o_keep, o_send)
        u_pieces = reduce_gather(u_keep, u_send)
        stats = [st2] + [over_seq(st2, k) for k in range(1, n)]

        branch = shape_of((n // 2, samples + 1, rows, width), BF)
        b_keep, b_send = call(
            functools.partial(branch_body, n, pad),
            [branch, branch],
            [meta, prod, wo, gs, mixed],
            [pltpu.VMEM((columns, full), BF)],
            specs=[SM] + [VM] * 4,
            flops=1_000_000_000,
            nbytes=5_000_000,
            name="branch",
        )
        rest = shape_of((n // 2, samples, rows, width), BF)
        ins = [meta, gmix, va, vb, dgva, dgvb, cols, *stats, g2, normed, ghu, wu, wv]
        v_keep, v_send, n_keep, n_send, small = call(
            functools.partial(back_body, n, pad),
            [u_shape, u_shape, rest, rest, shape_of((8, half), F32)],
            ins,
            [
                pltpu.VMEM((128, 128), F32),
                pltpu.VMEM((128, 128), F32),
                pltpu.VMEM((samples, full, half), BF),
                pltpu.VMEM((width, half), F32),
                pltpu.VMEM((2, CHUNK, half), F32),
            ],
            specs=[SM] + [VM] * (len(ins) - 1),
            flops=2_000_000_000,
            nbytes=10_000_000,
            name="back",
        )
        v_pieces = reduce_gather(v_keep, v_send)

        got = over_seq(b_send, 1)
        b_mine = add(b_keep[0], got[0])
        b_got = over_seq(add(b_keep[1], got[1]), 2)
        got = over_seq(n_send, 1)
        n_mine = add(n_keep[0], got[0])
        n_got = over_seq(add(n_keep[1], got[1]), 2)

        valid = seq * rows + jnp.arange(rows)[None, :] < counts[:, None]
        scale = valid.astype(F32) * skip_mask[:, None].astype(F32) / SURVIVAL
        total = b_mine[:samples].astype(F32) + b_got[:samples].astype(F32)
        output = (tokens.astype(F32) + scale[..., None] * total).astype(BF)

        extra_rows = round_up(rows, 16)
        grad_tokens, extra = call(
            tokens_body,
            [shape_of(tokens.shape, BF), shape_of((extra_rows, width), BF)],
            [tokens, cotangent, n_mine, n_got, b_mine[samples], b_got[samples], g1, small],
            flops=10_000_000,
            nbytes=2_000_000,
            name="tokens_back",
        )
        flip = 1
        while flip < m:
            extra = add(extra, over_dp(extra, flip))
            flip *= 2
        grad_spatial = extra[:rows, : n * rows].astype(F32)
        grad_bias = extra[:rows, n * rows].astype(F32)
        tail = extra[rows // 16 * 16 + 8 :, :]
        tails = [tail] + [over_seq(tail, k) for k in range(1, n)]
        tails = [t.astype(F32) for t in tails]
        norm_one = (tails[0] + tails[1]) + (tails[2] + tails[3])
        order = []
        for j in range(n):
            part = tails[0]
            for k in range(1, n):
                part = jnp.where(seq ^ k == j, tails[k], part)
            order.append(part[2:4, :half])
        norm_two = jnp.concatenate(order, axis=1)

        grad_w_out = place(meta, o_pieces, (gate, width), False)
        grad_w_in = place(meta, u_pieces, (width, 2 * gate), True)
        grad_w_in = place(meta, v_pieces, (width, 2 * gate), True, gate, grad_w_in)
        return (
            output,
            grad_tokens,
            grad_w_in,
            grad_w_out,
            grad_spatial,
            grad_bias,
            norm_one[0],
            norm_one[1],
            norm_two[0],
            norm_two[1],
        )

    placed = (
        P("dp", "seq", None),
        P("dp"),
        P("dp"),
        P(),
        P(),
        P("seq", None),
        P("seq"),
        P(),
        P(),
        P(),
        P(),
        P("dp", "seq", None),
    )
    return jax.shard_map(
        shards,
        mesh=mesh,
        in_specs=placed,
        out_specs=(
            P("dp", "seq", None),
            P("dp", "seq", None),
            P(),
            P(),
            P("seq", None),
            P("seq"),
            P(),
            P(),
            P(),
            P(),
        ),
        check_vma=False,
    )
```

time: 419 us -> 165 us (0.39)
  waiting for transfers between devices: 284 us -> 50.7 us
  blocking collectives: 58.9 us -> 0 us
  Pallas kernels: 0 us -> 48.9 us
  starting transfers between devices: 0.34 us -> 42.7 us
  matrix products: 31.8 us -> 0 us
  between operations: 14.7 us -> 1.14 us
  other arithmetic: 15.3 us -> 8.46 us
    psum x2 -> x0, waiting for transfers between devices: 183 us -> none  [the longest x1 183 us: shards(): lax.psum((grad_w_in, grad_w_out, small_grads), ('dp', 'seq'))]
    unnamed x5 -> x0, waiting for transfers between devices: 68.2 us -> none
    psum x2 -> x0, blocking collectives: 58.9 us -> none  [the longest x1 37.1 us: shards(): lax.psum((grad_w_in, grad_w_out, small_grads), ('dp', 'seq'))]
    ppermute x0 -> x55, waiting for transfers between devices: none -> 50.7 us  [the longest x31 28.6 us: over_seq(): return lax.ppermute(x, 'seq', [(i, i ^ flip) for i in range(n)])]
    pallas_call x0 -> x9, Pallas kernels: none -> 48.9 us  [call(): pl.pallas_call(body, out_shape=outs, in_specs=specs if specs is not None...]
    ppermute x0 -> x55, starting transfers between devices: none -> 42.7 us  [the longest x15 18.2 us: over_dp(): return lax.ppermute(x, 'dp', [(i, i ^ flip) for i in range(m)])]
    all_gather x1 -> x0, waiting for transfers between devices: 33.4 us -> none  [shards(): gathered = lax.all_gather(mixed_low, 'seq', axis=1, tiled=True)]
    dot_general x9 -> x0, matrix products: 31.8 us -> none  [the longest x1 4.72 us: shards(): jnp.einsum('spd,sph->dh', normed_low, grad_hidden_low, preferred_element_...]
  transfers between devices with their start and end apart: 4 -> 55, of which waited for: 3 -> 21; matrix products, arithmetic and copies ran while one was open for 6% -> 8% of each run, Pallas kernels for 0% -> 20%
where the time goes in v1:
time: 165 us; the launch traced here: 164 us
  waiting for transfers between devices  50.7 us (31%)
  Pallas kernels  48.9 us (30%)
  starting transfers between devices  42.7 us (26%)
  local copies, waits for them, and re-layouts  12.4 us (8%)
  other arithmetic  8.46 us (5%)
    pallas_call x9, Pallas kernels, call(): pl.pallas_call(body, out_shape=outs, in_specs=specs if specs is not None...  48.9 us
    ppermute x31, waiting for transfers between devices, over_seq(): return lax.ppermute(x, 'seq', [(i, i ^ flip) for i in range(n)])  28.6 us
    ppermute x15, starting transfers between devices, over_dp(): return lax.ppermute(x, 'dp', [(i, i ^ flip) for i in range(m)])  18.2 us
    ppermute x15, waiting for transfers between devices, over_dp(): return lax.ppermute(x, 'dp', [(i, i ^ flip) for i in range(m)])  17.9 us
    ppermute x31, starting transfers between devices, over_seq(): return lax.ppermute(x, 'seq', [(i, i ^ flip) for i in range(n)])  14.4 us
    ppermute x9, starting transfers between devices, mixed_axes(): return lax.ppermute(x, ('dp', 'seq'), pairs)  10.1 us
    unnamed x44, local copies, waits for them, and re-layouts  6.46 us
    ppermute x9, waiting for transfers between devices, mixed_axes(): return lax.ppermute(x, ('dp', 'seq'), pairs)  4.18 us
  transfers between devices with their start and end apart: 55, of which 21 were waited for; matrix products, arithmetic and copies ran while one was open for 8% of the time, Pallas kernels for 20%

profile of v1, /device:TPU:0, one launch (start us, length us, event | category | flops | bytes accessed | tf_op | source)
XLA Modules:
  0.0 164.3 jit_solution(8090698888764656943)
XLA Ops:
  1.2 2.6 %collective-permute-start.1 = (bf16[3,81,512]{2,1,0:T(8,128)(2,1)}, bf16[3,81,512]{2,1,0:T(8,128)(2,1)S(1)}, u32[]{:S(2)}, u32[]{:S(2)}) collective-permute-start(bf16[3,81,512]{2,1,0:T(8,128)(2,1)} %tok.1), channel_id=1, source_target_pairs={{0,2},{1,3},{2,0},{3,1},{4,6},{5,7},{6,4},{7,5},{8,10},{9,11},{10,... | collective-permute-start | bytes 746504 | tf_op jit(solution)/shard_map/ppermute | solution.py:456
  7.9 3.4 %collective-permute-done.1.refs_0_ = bf16[3,81,512]{2,1,0:T(8,128)(2,1)S(1)} collective-permute-done((bf16[3,81,512]{2,1,0:T(8,128)(2,1)}, bf16[3,81,512]{2,1,0:T(8,128)(2,1)S(1)}, u32[]{:S(2)}, u32[]{:S(2)}) %collective-permute-start.1) | collective-permute-done | bytes 248864 | tf_op jit(solution)/shard_map/ppermute | solution.py:456
  11.3 7.6 %collective-permute-done.4.c2 = bf16[4,81,512]{2,1,0:T(8,128)(2,1)} collective-permute-done((bf16[4,81,512]{2,1,0:T(8,128)(2,1)S(1)}, bf16[4,81,512]{2,1,0:T(8,128)(2,1)}, u32[]{:S(2)}, u32[]{:S(2)}) %collective-permute-start.4) | collective-permute-done | bytes 331808 | tf_op jit(solution)/shard_map/ppermute | solution.py:456
  20.2 7.2 %project.2 = (bf16[3,192,512]{2,1,0:T(8,128)(2,1)S(1)}, bf16[3,192,384]{2,1,0:T(8,128)(2,1)S(1)}, bf16[3,192,384]{2,1,0:T(8,128)(2,1)S(1)}, f32[3,192,384]{2,1,0...) custom-call(bf16[3,81,512]{2,1,0:T(8,128)(2,1)S(1)} %copy-done.2, ...), custom_call_target="tpu_custom_call" | custom-call | flops 452984832 | bytes 6000000 | tf_op jit(solution)/shard_map/project/pallas_call | solution.py:42
  28.3 7.2 %project.3 = (bf16[3,384,512]{2,1,0:T(8,128)(2,1)S(1)}, bf16[3,192,384]{2,1,0:T(8,128)(2,1)S(1)}, bf16[3,192,384]{2,1,0:T(8,128)(2,1)S(1)}, f32[3,192,384]{2,1,0...) custom-call(bf16[3,81,512]{2,1,0:T(8,128)(2,1)S(1)} %collective-permute-done.1.refs_0_, ...), custom_call_target="tpu_custom_call" | custom-call | flops 452984832 | bytes 6000000 | tf_op jit(solution)/shard_map/project/pallas_call | solution.py:42
  38.0 1.8 %collective-permute-start.7 = (f32[24,128]{1,0:T(8,128)S(1)}, f32[24,128]{1,0:T(8,128)S(1)}, u32[]{:S(2)}, u32[]{:S(2)}) collective-permute-start(f32[24,128]{1,0:T(8,128)S(1)} %get-tuple-element.51.t0), channel_id=1, source_target_pairs={{0,2},{1,3},{2,0},{3,1},{4,6},{5,7},{6,4},{7,5},{8,10},{9,11},{10,... | collective-permute-start | bytes 36872 | tf_op jit(solution)/shard_map/ppermute | solution.py:456
  42.9 16.5 %spatial.1 = (bf16[3,384,384]{2,1,0:T(8,128)(2,1)S(1)}, bf16[3,384,384]{2,1,0:T(8,128)(2,1)}, bf16[3,384,384]{2,1,0:T(8,128)(2,1)}, bf16[3,384,384]{2,1,0:T(8,12...) custom-call(s32[8]{0:T(128)S(1)} %pad_add_fusion.meta, ...), custom_call_target="tpu_custom_call" | custom-call | flops 3000000000 | bytes 12000000 | tf_op jit(solution)/shard_map/spatial/pallas_call | solution.py:42
  61.3 1.5 collective-permute-start.27
  65.1 2.3 %branch.1 = (bf16[2,4,81,512]{3,2,1,0:T(8,128)(2,1)S(1)}, bf16[2,4,81,512]{3,2,1,0:T(8,128)(2,1)S(1)}) custom-call(s32[8]{0:T(128)S(1)} %pad_add_fusion.meta, bf16[3,384,384]{2,1,0:T(8,128)(2,1)S(1)} %copy-done.17, bf16[384,512]{1,0:T(8,128)(2,1)S(1)} %constant_dynamic-slice_fusion.wo, bf16[3,384,384]{2,1,0:T(8,128)(2,1)S(1)} %copy-done.18, ...), custom_call_target="tpu_custom_call" | custom-call | flops 1000000000 | bytes 5000000 | tf_op jit(solution)/shard_map/branch/pallas_call | solution.py:42
  68.5 6.8 %back.1 = (bf16[2,128,384]{2,1,0:T(8,128)(2,1)S(1)}, bf16[2,128,384]{2,1,0:T(8,128)(2,1)S(1)}, bf16[2,3,81,512]{3,2,1,0:T(8,128)(2,1)S(1)}, bf16[2,3,81,512]{3,2,1,0:T(8,128)(2,1)S(1)}, f32[8,384]{1,0:T(8,128)S(1)}) custom-call(s32[8]{0:T(128)S(1)} %pad_add_fusion.meta, f32[3,384,384]{2,1,0:T(8,128)} %get-tuple-element.57.gmix, ...), custom_call_target="tpu_custom_call" | custom-call | flops 2000000000 | bytes 10000000 | tf_op jit(solution)/shard_map/back/pallas_call | solution.py:42
  76.0 1.5 collective-permute-start.16
  77.5 1.7 %collective-permute-start.28 = (bf16[128,384]{1,0:T(8,128)(2,1)S(1)}, bf16[128,384]{1,0:T(8,128)(2,1)S(1)}, u32[]{:S(2)}, u32[]{:S(2)}) collective-permute-start(bf16[128,384]{1,0:T(8,128)(2,1)S(1)} %fusion.15), channel_id=1, source_target_pairs={{0,8},{4,12},{8,0},{12,4},{16,24},{20,28},{24,16},{28,20},{1,9},{5... | collective-permute-start | bytes 294920 | tf_op jit(solution)/shard_map/ppermute | solution.py:459
  79.7 3.5 %collective-permute-done.16 = bf16[2,128,384]{2,1,0:T(8,128)(2,1)S(1)} collective-permute-done((bf16[2,128,384]{2,1,0:T(8,128)(2,1)S(1)}, bf16[2,128,384]{2,1,0:T(8,128)(2,1)S(1)}, u32[]{:S(2)}, u32[]{:S(2)}) %collective-permute-start.16) | collective-permute-done | bytes 196640 | tf_op jit(solution)/shard_map/ppermute | solution.py:459
  83.2 1.6 collective-permute-start.17
  84.8 2.7 %collective-permute-start.29 = (bf16[128,384]{1,0:T(8,128)(2,1)S(1)}, bf16[128,384]{1,0:T(8,128)(2,1)S(1)}, u32[]{:S(2)}, u32[]{:S(2)}) collective-permute-start(bf16[128,384]{1,0:T(8,128)(2,1)S(1)} %fusion.7), channel_id=1, source_target_pairs={{0,16},{4,20},{8,24},{12,28},{16,0},{20,4},{24,8},{28,12},{1,17},{... | collective-permute-start | bytes 294920 | tf_op jit(solution)/shard_map/ppermute | solution.py:459
  88.8 2.9 %collective-permute-start.18 = (bf16[128,384]{1,0:T(8,128)(2,1)S(1)}, bf16[128,384]{1,0:T(8,128)(2,1)S(1)}, u32[]{:S(2)}, u32[]{:S(2)}) collective-permute-start(bf16[128,384]{1,0:T(8,128)(2,1)S(1)} %fusion.8), channel_id=1, source_target_pairs={{0,16},{4,20},{8,24},{12,28},{16,0},{20,4},{24,8},{28,12},{1,17},{... | collective-permute-start | bytes 294920 | tf_op jit(solution)/shard_map/ppermute | solution.py:459
  91.6 4.7 %collective-permute-done.29 = bf16[128,384]{1,0:T(8,128)(2,1)S(1)} collective-permute-done((bf16[128,384]{1,0:T(8,128)(2,1)S(1)}, bf16[128,384]{1,0:T(8,128)(2,1)S(1)}, u32[]{:S(2)}, u32[]{:S(2)}) %collective-permute-start.29) | collective-permute-done | bytes 98336 | tf_op jit(solution)/shard_map/ppermute | solution.py:459
  97.1 1.8 %collective-permute-done.40 = bf16[96,512]{1,0:T(8,128)(2,1)S(1)} collective-permute-done((bf16[96,512]{1,0:T(8,128)(2,1)S(1)}, bf16[96,512]{1,0:T(8,128)(2,1)S(1)}, u32[]{:S(2)}, u32[]{:S(2)}) %collective-permute-start.40) | collective-permute-done | bytes 98336 | tf_op jit(solution)/shard_map/ppermute | solution.py:459
  102.4 1.6 collective-permute-start.31
  106.4 1.5 collective-permute-start.10
  108.7 11.2 %collective-permute-done.10 = bf16[4,81,512]{2,1,0:T(8,128)(2,1)S(1)} collective-permute-done((bf16[4,81,512]{2,1,0:T(8,128)(2,1)S(1)}, bf16[4,81,512]{2,1,0:T(8,128)(2,1)S(1)}, u32[]{:S(2)}, u32[]{:S(2)}) %collective-permute-start.10) | collective-permute-done | bytes 331808 | tf_op jit(solution)/shard_map/ppermute | solution.py:456
  120.0 3.2 %collective-permute-done.15.b = bf16[3,81,512]{2,1,0:T(8,128)(2,1)S(1)} collective-permute-done((bf16[3,81,512]{2,1,0:T(8,128)(2,1)S(1)}, bf16[3,81,512]{2,1,0:T(8,128)(2,1)S(1)}, u32[]{:S(2)}, u32[]{:S(2)}) %collective-permute-start.15) | collective-permute-done | bytes 248864 | tf_op jit(solution)/shard_map/ppermute | solution.py:456
  125.0 1.5 collective-permute-start.49
  127.8 3.5 %collective-permute-done.49 = bf16[96,512]{1,0:T(8,128)(2,1)S(1)} collective-permute-done((bf16[96,512]{1,0:T(8,128)(2,1)S(1)}, bf16[96,512]{1,0:T(8,128)(2,1)S(1)}, u32[]{:S(2)}, u32[]{:S(2)}) %collective-permute-start.49) | collective-permute-done | bytes 98336 | tf_op jit(solution)/shard_map/ppermute | solution.py:459
  131.3 1.9 %collective-permute-start.21 = (bf16[2,128,384]{2,1,0:T(8,128)(2,1)S(1)}, bf16[2,128,384]{2,1,0:T(8,128)(2,1)S(1)}, u32[]{:S(2)}, u32[]{:S(2)}) collective-permute-start(bf16[2,128,384]{2,1,0:T(8,128)(2,1)S(1)} %pad_maximum_fusion.1.refs_0_), channel_id=1, source_target_pairs={{0,2},{1,5},{2,0},{3,7},{4,6},{5,1},{6,4},{7,3},{8,10},{9,13},{10,... | collective-permute-start | bytes 589832 | tf_op jit(solution)/shard_map/ppermute | solution.py:467
  135.3 2.1 %collective-permute-start.44 = (bf16[2,96,512]{2,1,0:T(8,128)(2,1)S(1)}, bf16[2,96,512]{2,1,0:T(8,128)(2,1)S(1)}, u32[]{:S(2)}, u32[]{:S(2)}) collective-permute-start(bf16[2,96,512]{2,1,0:T(8,128)(2,1)S(1)} %collective-permute-done.42.refs_1_), channel_id=1, source_target_pairs={{0,2},{1,5},{2,0},{3,7},{4,6},{5,1},{6,4},{7,3},{8,10},{9,13},{10,... | collective-permute-start | bytes 589832 | tf_op jit(solution)/shard_map/ppermute | solution.py:467
  139.7 1.9 %collective-permute-start.22 = (bf16[2,128,384]{2,1,0:T(8,128)(2,1)}, bf16[2,128,384]{2,1,0:T(8,128)(2,1)S(1)}, u32[]{:S(2)}, u32[]{:S(2)}) collective-permute-start(bf16[2,128,384]{2,1,0:T(8,128)(2,1)} %copy-done.5), channel_id=1, source_target_pairs={{0,2},{1,5},{2,0},{3,7},{4,6},{5,1},{6,4},{7,3},{8,10},{9,13},{10,... | collective-permute-start | bytes 589832 | tf_op jit(solution)/shard_map/ppermute | solution.py:467
  143.8 1.8 %collective-permute-done.22.refs_3_ = bf16[2,128,384]{2,1,0:T(8,128)(2,1)S(1)} collective-permute-done((bf16[2,128,384]{2,1,0:T(8,128)(2,1)}, bf16[2,128,384]{2,1,0:T(8,128)(2,1)S(1)}, u32[]{:S(2)}, u32[]{:S(2)}) %collective-permute-start.22) | collective-permute-done | bytes 196640 | tf_op jit(solution)/shard_map/ppermute | solution.py:467
  147.6 1.9 %fusion.2 = bf16[3,81,512]{2,1,0:T(8,128)(2,1)} fusion(bf16[3,81,512]{2,1,0:T(8,128)(2,1)S(1)} %copy-done.2, bf16[4,81,512]{2,1,0:T(8,128)(2,1)} %copy-done.20, bf16[1,4,81,512]{3,2,1,0:T(8,128)(2,1)} %copy-done.19, f32[3,81]{1,0:T(4,128)S(1)} %select_multiply_fusion), kind=kLoop, calls=%fused_computation.5 | loop fusion | flops 870912 | bytes 996300 | tf_op jit(solution)/shard_map/convert_element_type | solution.py:614
  150.4 3.0 %place.3.refs_8_ = f32[512,3072]{1,0:T(8,128)} custom-call(s32[8]{0:T(128)S(1)} %pad_add_fusion.meta, bf16[2,128,384]{2,1,0:T(8,128)(2,1)S(1)} %pad_maximum_fusion.2.refs_0_, bf16[2,128,384]{2,1,0:T(8,128)(2,1)S(1)} %collective-permute-done.31.refs_1_, bf16[2,128,384]{2,1,0:T(8,128)(2,1)} %collective-permute-done.32.refs_2_, ...), custom_call_target="tpu_custom_call" | custom-call | bytes 10000000 | tf_op jit(solution)/shard_map/place/pallas_call | solution.py:42
  153.4 2.3 %place.5 = f32[1536,512]{1,0:T(8,128)} custom-call(s32[8]{0:T(128)S(1)} %pad_add_fusion.meta, bf16[2,96,512]{2,1,0:T(8,128)(2,1)S(1)} %pad_maximum_fusion.3.refs_0_, bf16[2,96,512]{2,1,0:T(8,128)(2,1)S(1)} %collective-permute-done.42.refs_1_, bf16[2,96,512]{2,1,0:T(8,128)(2,1)S(1)} %collective-permute-done.43.refs_2_, ...), custom_call_target="tpu_custom_call" | custom-call | bytes 10000000 | tf_op jit(solution)/shard_map/place/pallas_call | solution.py:42
  155.8 2.3 %place.4 = f32[512,3072]{1,0:T(8,128)} custom-call(s32[8]{0:T(128)S(1)} %pad_add_fusion.meta, bf16[2,128,384]{2,1,0:T(8,128)(2,1)S(1)} %pad_maximum_fusion.1.refs_0_, bf16[2,128,384]{2,1,0:T(8,128)(2,1)S(1)} %copy-done.6, bf16[2,128,384]{2,1,0:T(8,128)(2,1)S(1)} %copy-done.8, ...), custom_call_target="tpu_custom_call", output_to_operand_aliasing={{}: (9, {})} | custom-call | bytes 10000000 | tf_op jit(solution)/shard_map/place/pallas_call | solution.py:42
  (183 shorter events, 46.3 us)
Async XLA Ops:
  0.7 19.4 %collective-permute-start = (bf16[3,81,512]{2,1,0:T(8,128)(2,1)}, bf16[3,81,512]{2,1,0:T(8,128)(2,1)S(1)}, u32[]{:S(2)}, u32[]{:S(2)}) collective-permute-start(bf16[3,81,512]{2,1,0:T(8,128)(2,1)} %tok.1), channel_id=1, source_target_pairs={{0,1},{1,0},{2,3},{3,2},{4,5},{5,4},{6,7},{7,6},{8,9},{9,8},{10,11... | collective-permute-start | bytes 746504 | tf_op jit(solution)/shard_map/ppermute | solution.py:456
  1.2 10.1 %collective-permute-start.1 = (bf16[3,81,512]{2,1,0:T(8,128)(2,1)}, bf16[3,81,512]{2,1,0:T(8,128)(2,1)S(1)}, u32[]{:S(2)}, u32[]{:S(2)}) collective-permute-start(bf16[3,81,512]{2,1,0:T(8,128)(2,1)} %tok.1), channel_id=1, source_target_pairs={{0,2},{1,3},{2,0},{3,1},{4,6},{5,7},{6,4},{7,5},{8,10},{9,11},{10,... | collective-permute-start | bytes 746504 | tf_op jit(solution)/shard_map/ppermute | solution.py:456
  6.7 34.6 %collective-permute-start.3 = (bf16[4,81,512]{2,1,0:T(8,128)(2,1)S(1)}, bf16[4,81,512]{2,1,0:T(8,128)(2,1)}, u32[]{:S(2)}, u32[]{:S(2)}) collective-permute-start(bf16[4,81,512]{2,1,0:T(8,128)(2,1)S(1)} %pad_maximum_fusion.c0), channel_id=1, source_target_pairs={{0,1},{1,0},{2,3},{3,2},{4,5},{5,4},{6,7},{7,6},{8,9},{9,8},{10,11... | collective-permute-start | bytes 995336 | tf_op jit(solution)/shard_map/ppermute | solution.py:456
  6.9 12.0 %collective-permute-start.4 = (bf16[4,81,512]{2,1,0:T(8,128)(2,1)S(1)}, bf16[4,81,512]{2,1,0:T(8,128)(2,1)}, u32[]{:S(2)}, u32[]{:S(2)}) collective-permute-start(bf16[4,81,512]{2,1,0:T(8,128)(2,1)S(1)} %pad_maximum_fusion.c0), channel_id=1, source_target_pairs={{0,2},{1,3},{2,0},{3,1},{4,6},{5,7},{6,4},{7,5},{8,10},{9,11},{10,... | collective-permute-start | bytes 995336 | tf_op jit(solution)/shard_map/ppermute | solution.py:456
  11.3 17.0 %collective-permute-start.2 = (bf16[3,81,512]{2,1,0:T(8,128)(2,1)S(1)}, bf16[3,81,512]{2,1,0:T(8,128)(2,1)S(1)}, u32[]{:S(2)}, u32[]{:S(2)}) collective-permute-start(bf16[3,81,512]{2,1,0:T(8,128)(2,1)S(1)} %collective-permute-done.1.refs_0_), channel_id=1, source_target_pairs={{0,1},{1,0},{2,3},{3,2},{4,5},{5,4},{6,7},{7,6},{8,9},{9,8},{10,11... | collective-permute-start | bytes 746504 | tf_op jit(solution)/shard_map/ppermute | solution.py:456
  18.9 24.0 %collective-permute-start.5 = (bf16[4,81,512]{2,1,0:T(8,128)(2,1)}, bf16[4,81,512]{2,1,0:T(8,128)(2,1)}, u32[]{:S(2)}, u32[]{:S(2)}) collective-permute-start(bf16[4,81,512]{2,1,0:T(8,128)(2,1)} %collective-permute-done.4.c2), channel_id=1, source_target_pairs={{0,1},{1,0},{2,3},{3,2},{4,5},{5,4},{6,7},{7,6},{8,9},{9,8},{10,11... | collective-permute-start | bytes 995336 | tf_op jit(solution)/shard_map/ppermute | solution.py:456
  59.4 8.5 %collective-permute-start.11 = (f32[24,128]{1,0:T(8,128)S(1)}, f32[24,128]{1,0:T(8,128)S(1)}, u32[]{:S(2)}, u32[]{:S(2)}) collective-permute-start(f32[24,128]{1,0:T(8,128)S(1)} %get-tuple-element.61.t0), channel_id=1, source_target_pairs={{0,1},{1,0},{2,3},{3,2},{4,5},{5,4},{6,7},{7,6},{8,9},{9,8},{10,11... | collective-permute-start | bytes 36872 | tf_op jit(solution)/shard_map/ppermute | solution.py:456
  59.5 9.0 %collective-permute-start.12 = (f32[24,128]{1,0:T(8,128)S(1)}, f32[24,128]{1,0:T(8,128)S(1)}, u32[]{:S(2)}, u32[]{:S(2)}) collective-permute-start(f32[24,128]{1,0:T(8,128)S(1)} %get-tuple-element.61.t0), channel_id=1, source_target_pairs={{0,2},{1,3},{2,0},{3,1},{4,6},{5,7},{6,4},{7,5},{8,10},{9,11},{10,... | collective-permute-start | bytes 36872 | tf_op jit(solution)/shard_map/ppermute | solution.py:456
  60.1 8.3 %collective-permute-start.13 = (f32[24,128]{1,0:T(8,128)S(1)}, f32[24,128]{1,0:T(8,128)S(1)}, u32[]{:S(2)}, u32[]{:S(2)}) collective-permute-start(f32[24,128]{1,0:T(8,128)S(1)} %get-tuple-element.61.t0), channel_id=1, source_target_pairs={{0,3},{1,2},{2,1},{3,0},{4,7},{5,6},{6,5},{7,4},{8,11},{9,10},{10,... | collective-permute-start | bytes 36872 | tf_op jit(solution)/shard_map/ppermute | solution.py:456
  61.3 16.1 %collective-permute-start.27 = (bf16[2,128,384]{2,1,0:T(8,128)(2,1)S(1)}, bf16[2,128,384]{2,1,0:T(8,128)(2,1)S(1)}, u32[]{:S(2)}, u32[]{:S(2)}) collective-permute-start(bf16[2,128,384]{2,1,0:T(8,128)(2,1)S(1)} %get-tuple-element.70), channel_id=1, source_target_pairs={{0,4},{4,0},{8,12},{12,8},{16,20},{20,16},{24,28},{28,24},{1,5},{5... | collective-permute-start | bytes 589832 | tf_op jit(solution)/shard_map/ppermute | solution.py:459
  67.8 38.1 %collective-permute-start.9 = (bf16[2,4,81,512]{3,1,2,0:T(4,128)(2,1)S(1)}, bf16[2,4,81,512]{3,1,2,0:T(4,128)(2,1)S(1)}, u32[]{:S(2)}, u32[]{:S(2)}) collective-permute-start(bf16[2,4,81,512]{3,1,2,0:T(4,128)(2,1)S(1)} %copy.29), channel_id=1, source_target_pairs={{0,1},{1,0},{2,3},{3,2},{4,5},{5,4},{6,7},{7,6},{8,9},{9,8},{10,11... | collective-permute-start | bytes 1990664 | tf_op jit(solution)/shard_map/ppermute | solution.py:456
  67.9 11.3 %collective-permute-start.38 = (bf16[2,96,512]{2,1,0:T(8,128)(2,1)S(1)}, bf16[2,96,512]{2,1,0:T(8,128)(2,1)S(1)}, u32[]{:S(2)}, u32[]{:S(2)}) collective-permute-start(bf16[2,96,512]{2,1,0:T(8,128)(2,1)S(1)} %get-tuple-element.72), channel_id=1, source_target_pairs={{0,4},{4,0},{8,12},{12,8},{16,20},{20,16},{24,28},{28,24},{1,5},{5... | collective-permute-start | bytes 589832 | tf_op jit(solution)/shard_map/ppermute | solution.py:459
  75.7 29.4 %collective-permute-start.14 = (bf16[2,3,81,512]{3,0,2,1:T(2,128)(2,1)S(1)}, bf16[2,3,81,512]{3,0,2,1:T(2,128)(2,1)S(1)}, u32[]{:S(2)}, u32[]{:S(2)}) collective-permute-start(bf16[2,3,81,512]{3,0,2,1:T(2,128)(2,1)S(1)} %copy.32), channel_id=1, source_target_pairs={{0,1},{1,0},{2,3},{3,2},{4,5},{5,4},{6,7},{7,6},{8,9},{9,8},{10,11... | collective-permute-start | bytes 1493000 | tf_op jit(solution)/shard_map/ppermute | solution.py:456
  77.5 7.3 %collective-permute-start.28 = (bf16[128,384]{1,0:T(8,128)(2,1)S(1)}, bf16[128,384]{1,0:T(8,128)(2,1)S(1)}, u32[]{:S(2)}, u32[]{:S(2)}) collective-permute-start(bf16[128,384]{1,0:T(8,128)(2,1)S(1)} %fusion.15), channel_id=1, source_target_pairs={{0,8},{4,12},{8,0},{12,4},{16,24},{20,28},{24,16},{28,20},{1,9},{5... | collective-permute-start | bytes 294920 | tf_op jit(solution)/shard_map/ppermute | solution.py:459
  79.2 8.3 %collective-permute-start.39 = (bf16[96,512]{1,0:T(8,128)(2,1)S(1)}, bf16[96,512]{1,0:T(8,128)(2,1)S(1)}, u32[]{:S(2)}, u32[]{:S(2)}) collective-permute-start(bf16[96,512]{1,0:T(8,128)(2,1)S(1)} %fusion.17), channel_id=1, source_target_pairs={{0,8},{4,12},{8,0},{12,4},{16,24},{20,28},{24,16},{28,20},{1,9},{5... | collective-permute-start | bytes 294920 | tf_op jit(solution)/shard_map/ppermute | solution.py:459
  84.8 11.5 %collective-permute-start.29 = (bf16[128,384]{1,0:T(8,128)(2,1)S(1)}, bf16[128,384]{1,0:T(8,128)(2,1)S(1)}, u32[]{:S(2)}, u32[]{:S(2)}) collective-permute-start(bf16[128,384]{1,0:T(8,128)(2,1)S(1)} %fusion.7), channel_id=1, source_target_pairs={{0,16},{4,20},{8,24},{12,28},{16,0},{20,4},{24,8},{28,12},{1,17},{... | collective-permute-start | bytes 294920 | tf_op jit(solution)/shard_map/ppermute | solution.py:459
  87.5 11.4 %collective-permute-start.40 = (bf16[96,512]{1,0:T(8,128)(2,1)S(1)}, bf16[96,512]{1,0:T(8,128)(2,1)S(1)}, u32[]{:S(2)}, u32[]{:S(2)}) collective-permute-start(bf16[96,512]{1,0:T(8,128)(2,1)S(1)} %fusion.6), channel_id=1, source_target_pairs={{0,16},{4,20},{8,24},{12,28},{16,0},{20,4},{24,8},{28,12},{1,17},{... | collective-permute-start | bytes 294920 | tf_op jit(solution)/shard_map/ppermute | solution.py:459
  88.8 11.6 %collective-permute-start.18 = (bf16[128,384]{1,0:T(8,128)(2,1)S(1)}, bf16[128,384]{1,0:T(8,128)(2,1)S(1)}, u32[]{:S(2)}, u32[]{:S(2)}) collective-permute-start(bf16[128,384]{1,0:T(8,128)(2,1)S(1)} %fusion.8), channel_id=1, source_target_pairs={{0,16},{4,20},{8,24},{12,28},{16,0},{20,4},{24,8},{28,12},{1,17},{... | collective-permute-start | bytes 294920 | tf_op jit(solution)/shard_map/ppermute | solution.py:459
  100.4 24.6 %collective-permute-start.19 = (bf16[128,384]{1,0:T(8,128)(2,1)S(1)}, bf16[128,384]{1,0:T(8,128)(2,1)S(1)}, u32[]{:S(2)}, u32[]{:S(2)}) collective-permute-start(bf16[128,384]{1,0:T(8,128)(2,1)S(1)} %add_convert_fusion.13), channel_id=1, source_target_pairs={{0,8},{4,12},{8,0},{12,4},{16,24},{20,28},{24,16},{28,20},{1,9},{5... | collective-permute-start | bytes 294920 | tf_op jit(solution)/shard_map/ppermute | solution.py:459
  102.4 24.1 %collective-permute-start.31 = (bf16[2,128,384]{2,1,0:T(8,128)(2,1)S(1)}, bf16[2,128,384]{2,1,0:T(8,128)(2,1)S(1)}, u32[]{:S(2)}, u32[]{:S(2)}) collective-permute-start(bf16[2,128,384]{2,1,0:T(8,128)(2,1)S(1)} %pad_maximum_fusion.2.refs_0_), channel_id=1, source_target_pairs={{0,4},{1,3},{2,6},{3,1},{4,0},{5,7},{6,2},{7,5},{8,12},{9,11},{10,... | collective-permute-start | bytes 589832 | tf_op jit(solution)/shard_map/ppermute | solution.py:467
  104.5 22.7 %collective-permute-start.32 = (bf16[2,128,384]{2,1,0:T(8,128)(2,1)S(1)}, bf16[2,128,384]{2,1,0:T(8,128)(2,1)}, u32[]{:S(2)}, u32[]{:S(2)}) collective-permute-start(bf16[2,128,384]{2,1,0:T(8,128)(2,1)S(1)} %pad_maximum_fusion.2.refs_0_), channel_id=1, source_target_pairs={{0,2},{1,5},{2,0},{3,7},{4,6},{5,1},{6,4},{7,3},{8,10},{9,13},{10,... | collective-permute-start | bytes 589832 | tf_op jit(solution)/shard_map/ppermute | solution.py:467
  106.4 13.6 %collective-permute-start.10 = (bf16[4,81,512]{2,1,0:T(8,128)(2,1)S(1)}, bf16[4,81,512]{2,1,0:T(8,128)(2,1)S(1)}, u32[]{:S(2)}, u32[]{:S(2)}) collective-permute-start(bf16[4,81,512]{2,1,0:T(8,128)(2,1)S(1)} %get-tuple-element.79), channel_id=1, source_target_pairs={{0,2},{1,3},{2,0},{3,1},{4,6},{5,7},{6,4},{7,5},{8,10},{9,11},{10,... | collective-permute-start | bytes 995336 | tf_op jit(solution)/shard_map/ppermute | solution.py:456
  108.0 15.2 %collective-permute-start.15 = (bf16[3,81,512]{2,1,0:T(8,128)(2,1)S(1)}, bf16[3,81,512]{2,1,0:T(8,128)(2,1)S(1)}, u32[]{:S(2)}, u32[]{:S(2)}) collective-permute-start(bf16[3,81,512]{2,1,0:T(8,128)(2,1)S(1)} %get-tuple-element.82), channel_id=1, source_target_pairs={{0,2},{1,3},{2,0},{3,1},{4,6},{5,7},{6,4},{7,5},{8,10},{9,11},{10,... | collective-permute-start | bytes 746504 | tf_op jit(solution)/shard_map/ppermute | solution.py:456
  120.0 7.3 %collective-permute-start.34 = (bf16[2,128,384]{2,1,0:T(8,128)(2,1)S(1)}, bf16[2,128,384]{2,1,0:T(8,128)(2,1)S(1)}, u32[]{:S(2)}, u32[]{:S(2)}) collective-permute-start(bf16[2,128,384]{2,1,0:T(8,128)(2,1)S(1)} %pad_maximum_fusion.2.refs_0_), channel_id=1, source_target_pairs={{0,1},{1,0},{2,3},{3,2},{4,5},{5,4},{6,7},{7,6},{8,9},{9,8},{10,11... | collective-permute-start | bytes 589832 | tf_op jit(solution)/shard_map/ppermute | solution.py:456
  123.2 10.0 %collective-permute-start.42 = (bf16[2,96,512]{2,1,0:T(8,128)(2,1)S(1)}, bf16[2,96,512]{2,1,0:T(8,128)(2,1)S(1)}, u32[]{:S(2)}, u32[]{:S(2)}) collective-permute-start(bf16[2,96,512]{2,1,0:T(8,128)(2,1)S(1)} %pad_maximum_fusion.3.refs_0_), channel_id=1, source_target_pairs={{0,4},{1,3},{2,6},{3,1},{4,0},{5,7},{6,2},{7,5},{8,12},{9,11},{10,... | collective-permute-start | bytes 589832 | tf_op jit(solution)/shard_map/ppermute | solution.py:467
  126.5 7.6 %collective-permute-start.43 = (bf16[2,96,512]{2,1,0:T(8,128)(2,1)S(1)}, bf16[2,96,512]{2,1,0:T(8,128)(2,1)S(1)}, u32[]{:S(2)}, u32[]{:S(2)}) collective-permute-start(bf16[2,96,512]{2,1,0:T(8,128)(2,1)S(1)} %pad_maximum_fusion.3.refs_0_), channel_id=1, source_target_pairs={{0,2},{1,5},{2,0},{3,7},{4,6},{5,1},{6,4},{7,3},{8,10},{9,13},{10,... | collective-permute-start | bytes 589832 | tf_op jit(solution)/shard_map/ppermute | solution.py:467
  127.3 8.1 %collective-permute-start.20 = (bf16[2,128,384]{2,1,0:T(8,128)(2,1)S(1)}, bf16[2,128,384]{2,1,0:T(8,128)(2,1)S(1)}, u32[]{:S(2)}, u32[]{:S(2)}) collective-permute-start(bf16[2,128,384]{2,1,0:T(8,128)(2,1)S(1)} %pad_maximum_fusion.1.refs_0_), channel_id=1, source_target_pairs={{0,4},{1,3},{2,6},{3,1},{4,0},{5,7},{6,2},{7,5},{8,12},{9,11},{10,... | collective-permute-start | bytes 589832 | tf_op jit(solution)/shard_map/ppermute | solution.py:467
  143.1 12.6 %collective-permute-start.23 = (bf16[2,128,384]{2,1,0:T(8,128)(2,1)S(1)}, bf16[2,128,384]{2,1,0:T(8,128)(2,1)S(1)}, u32[]{:S(2)}, u32[]{:S(2)}) collective-permute-start(bf16[2,128,384]{2,1,0:T(8,128)(2,1)S(1)} %pad_maximum_fusion.1.refs_0_), channel_id=1, source_target_pairs={{0,1},{1,0},{2,3},{3,2},{4,5},{5,4},{6,7},{7,6},{8,9},{9,8},{10,11... | collective-permute-start | bytes 589832 | tf_op jit(solution)/shard_map/ppermute | solution.py:456
  143.7 12.1 %collective-permute-start.24 = (bf16[2,128,384]{2,1,0:T(8,128)(2,1)}, bf16[2,128,384]{2,1,0:T(8,128)(2,1)S(1)}, u32[]{:S(2)}, u32[]{:S(2)}) collective-permute-start(bf16[2,128,384]{2,1,0:T(8,128)(2,1)} %copy-done.5), channel_id=1, source_target_pairs={{0,1},{1,0},{2,3},{3,2},{4,5},{5,4},{6,7},{7,6},{8,9},{9,8},{10,11... | collective-permute-start | bytes 589832 | tf_op jit(solution)/shard_map/ppermute | solution.py:456
  145.6 10.2 %collective-permute-start.25 = (bf16[2,128,384]{2,1,0:T(8,128)(2,1)}, bf16[2,128,384]{2,1,0:T(8,128)(2,1)S(1)}, u32[]{:S(2)}, u32[]{:S(2)}) collective-permute-start(bf16[2,128,384]{2,1,0:T(8,128)(2,1)} %copy-done.7), channel_id=1, source_target_pairs={{0,1},{1,0},{2,3},{3,2},{4,5},{5,4},{6,7},{7,6},{8,9},{9,8},{10,11... | collective-permute-start | bytes 589832 | tf_op jit(solution)/shard_map/ppermute | solution.py:456
  145.6 10.2 %collective-permute-start.26 = (bf16[2,128,384]{2,1,0:T(8,128)(2,1)S(1)}, bf16[2,128,384]{2,1,0:T(8,128)(2,1)S(1)}, u32[]{:S(2)}, u32[]{:S(2)}) collective-permute-start(bf16[2,128,384]{2,1,0:T(8,128)(2,1)S(1)} %collective-permute-done.22.refs_3_), channel_id=1, source_target_pairs={{0,1},{1,0},{2,3},{3,2},{4,5},{5,4},{6,7},{7,6},{8,9},{9,8},{10,11... | collective-permute-start | bytes 589832 | tf_op jit(solution)/shard_map/ppermute | solution.py:456
  146.1 12.1 %collective-permute-start.51 = (bf16[96,512]{1,0:T(8,128)(2,1)S(1)}, bf16[96,512]{1,0:T(8,128)(2,1)S(1)}, u32[]{:S(2)}, u32[]{:S(2)}) collective-permute-start(bf16[96,512]{1,0:T(8,128)(2,1)S(1)} %add_convert_fusion.5), channel_id=1, source_target_pairs={{0,16},{4,20},{8,24},{12,28},{16,0},{20,4},{24,8},{28,12},{1,17},{... | collective-permute-start | bytes 294920 | tf_op jit(solution)/shard_map/ppermute | solution.py:459
  (45 other events, 328.3 us)

commit v2 on v0

v2 whole, which is shorter than its diff:
```python
import functools

import jax
import jax.numpy as jnp
from jax import lax
from jax.experimental import pallas as pl
from jax.experimental.pallas import tpu as pltpu
from jax.sharding import PartitionSpec as P

PATCHES = 324
SMALL_P = 100
MID_P = 196

EPSILON = 1e-05
SURVIVAL = 0.9

BF = jnp.bfloat16
F32 = jnp.float32
CHUNK = 16
VM = pl.BlockSpec(memory_space=pltpu.VMEM)
SM = pl.BlockSpec(memory_space=pltpu.SMEM)
HB = pl.BlockSpec(memory_space=pltpu.HBM)


def round_up(size, multiple):
    return -(-size // multiple) * multiple


def dot(a, b, ca, cb):
    return lax.dot_general(a, b, (((ca,), (cb,)), ((), ())), preferred_element_type=F32)


def iota(shape, axis):
    return lax.broadcasted_iota(jnp.int32, shape, axis)


def rows_at(start, size, multiple):
    return pl.ds(pl.multiple_of(start, multiple), size)


def call(body, outs, ins, scratch=(), specs=None, out_specs=None, **more):
    return pl.pallas_call(
        body,
        out_shape=outs,
        in_specs=specs if specs is not None else [VM] * len(ins),
        out_specs=out_specs if out_specs is not None else [VM] * len(outs),
        scratch_shapes=list(scratch),
        compiler_params=pltpu.CompilerParams(vmem_limit_bytes=20 * 2**20),
        cost_estimate=pl.CostEstimate(flops=1, bytes_accessed=1, transcendentals=0),
        **more,
    )(*ins)


def shape_of(shape, dtype):
    return jax.ShapeDtypeStruct(shape, dtype)


def project_body(pad, first_block, *refs):
    refs = list(refs)
    n_tok = len(refs) - 13 - (1 if first_block else 0)
    toks, refs = refs[:n_tok], refs[n_tok:]
    g1, s1, wu, wv = refs[:4]
    refs = refs[4:]
    if first_block:
        st_in, refs = refs[0], refs[1:]
    normed, gu, dgu, v, dgv, st, xs, hid, tile = refs
    samples, rows, width = toks[0].shape
    half = wu.shape[1]
    found = [jnp.zeros((CHUNK, 128), F32)] * (128 // CHUNK)
    low = rows // 8 * 8
    gain, shift = g1[...], s1[...]
    for i in range(samples):
        for b, tok in enumerate(toks):
            xs[i, b, low:, :] = jnp.zeros((pad - low, width), F32)
            xs[i, b, 0:rows, :] = tok[i].astype(F32)
            for c in range(pad // CHUNK):
                x = xs[i, b, c * CHUNK : (c + 1) * CHUNK, :]
                center = x - jnp.mean(x, axis=-1, keepdims=True)
                inverse = lax.rsqrt(jnp.mean(center * center, axis=-1, keepdims=True) + EPSILON)
                out = center * inverse * gain + shift
                normed[i, b * pad + c * CHUNK : b * pad + (c + 1) * CHUNK, :] = out.astype(BF)
        hid[i, :, 0:half] = dot(normed[i], wu[...], 1, 0)
        hid[i, :, half:] = dot(normed[i], wv[...], 1, 0)
    c0 = 0.7978845608028654
    c1 = 0.7978845608028654 * 0.044715

    def gelu_pair(h):
        a = (c1 * h) * h
        s = 0.5 + 0.5 * jnp.tanh(h * (c0 + a))
        g = h * s
        return g, s + (2.0 * g) * (1.0 - s) * (c0 + 3.0 * a)

    lane = iota((CHUNK, 128), 1)
    for i in range(samples):
        for b in range(len(toks)):
            blk = 2 * (i * 4 + first_block + b)
            for c in range(pad // CHUNK):
                at = slice(b * pad + c * CHUNK, b * pad + (c + 1) * CHUNK)
                g, d = gelu_pair(hid[i, at, 0:half])
                gu[i, at, :] = g.astype(BF)
                dgu[i, at, :] = d.astype(BF)
                g, d = gelu_pair(hid[i, at, half:])
                v[i, at, :] = g
                dgv[i, at, :] = d.astype(BF)
                mean = jnp.mean(g, axis=-1, keepdims=True)
                center = g - mean
                square = jnp.sum(center * center, axis=-1, keepdims=True)
                found[c] = jnp.where(
                    lane == blk, mean, jnp.where(lane == blk + 1, square, found[c])
                )
    for c, part_found in enumerate(found):
        tile[c * CHUNK : (c + 1) * CHUNK, :] = part_found
    flipped = jnp.transpose(tile[...])[0 : st.shape[0], :]
    st[...] = flipped + st_in[...] if first_block else flipped


def project(pad, first_block, toks, g1, s1, wu, wv, st_in=None):
    samples, rows, width = toks[0].shape
    half = wu.shape[1]
    n_rows = len(toks) * pad
    outs = [
        shape_of((samples, n_rows, width), BF),
        shape_of((samples, n_rows, half), BF),
        shape_of((samples, n_rows, half), BF),
        shape_of((samples, n_rows, half), F32),
        shape_of((samples, n_rows, half), BF),
        shape_of((round_up(samples * 8, 8), 128), F32),
    ]
    scratch = [
        pltpu.VMEM((samples, len(toks), pad, width), F32),
        pltpu.VMEM((samples, n_rows, 2 * half), F32),
        pltpu.VMEM((128, 128), F32),
    ]
    ins = [*toks, g1, s1, wu, wv] + ([st_in] if first_block else [])
    return call(
        functools.partial(project_body, pad, first_block),
        outs,
        ins,
        scratch,
        name="project",
    )


GROUPS = ((0, 1), (2,), (3,))


def part(r, pad):
    for k, blocks in enumerate(GROUPS):
        if r in blocks:
            return k, (r - blocks[0]) * pad


def position_map(seq, rows, pad, n, columns):
    a = iota((columns, n * pad), 0)
    j = iota((columns, n * pad), 1)
    r = jnp.zeros_like(j)
    for k in range(1, n):
        r = r + (j >= k * pad).astype(jnp.int32)
    q = j - r * pad
    hit = (a == (r ^ seq) * rows + q) & (q < rows)
    hit = hit | ((a == n * rows) & (j == pad - 1)) | ((a == n * rows + 1) & (j == pad - 2))
    return jnp.where(hit, 1.0, 0.0).astype(BF)


def patch_count(meta, i):
    kind = meta[2 + i]
    return jnp.where(kind == 0, SMALL_P, jnp.where(kind == 1, MID_P, PATCHES))


def branch_scale(meta, i, samples, where):
    keep = jnp.where(where < patch_count(meta, i), meta[2 + samples + i], 0)
    return keep.astype(F32) / SURVIVAL


def valid_rows(meta, i, r, c, rows):
    p = c * CHUNK + iota((CHUNK, 1), 0)
    return (p < rows) & ((meta[0] ^ r) * rows + p < patch_count(meta, i))


def prepare_body(
    n, pad, meta, c0, c1, c2, c3, wo, gu0, gu1, gu2,
    sp, gb, gp, gs, gmix, pm,
    spt,
):
    samples, rows = c0.shape[0] - 1, c0.shape[1]
    seq = meta[0]
    cots, gus = (c0, c1, c2, c3), (gu0, gu1, gu2)
    columns = pm.shape[0]
    low = rows // 16 * 16
    pm[...] = position_map(seq, rows, pad, n, columns)
    for r in range(n):
        sp[r * pad + low : (r + 1) * pad, :] = jnp.zeros((pad - low, n * pad), BF)
        sp[r * pad : r * pad + rows, :] = dot(cots[r][samples, :, 0:columns], pm[...], 1, 0).astype(BF)
    spt[...] = jnp.transpose(sp[...].astype(F32)).astype(BF)
    for i in range(samples):
        for r in range(n):
            p = iota((rows, 1), 0)
            scale = branch_scale(meta, i, samples, (seq ^ r) * rows + p)
            gb[i, r * pad + low : (r + 1) * pad, :] = jnp.zeros((pad - low, gb.shape[2]), BF)
            gb[i, r * pad : r * pad + rows, :] = (cots[r][i].astype(F32) * scale).astype(BF)
        gp[i] = dot(gb[i], wo[...], 1, 1)
        for r in range(n):
            k, base = part(r, pad)
            for c in range(pad // CHUNK):
                at = slice(r * pad + c * CHUNK, r * pad + (c + 1) * CHUNK)
                src = slice(base + c * CHUNK, base + (c + 1) * CHUNK)
                gs[i, at, :] = (gp[i, at, :] * gus[k][i, src, :].astype(F32)).astype(BF)
        full = dot(spt[...], gs[i], 1, 0)
        for r in range(n):
            for c in range(pad // CHUNK):
                at = slice(r * pad + c * CHUNK, r * pad + (c + 1) * CHUNK)
                gmix[i, at, :] = jnp.where(valid_rows(meta, i, r, c, rows), full[at], 0.0)


def own_lanes(rows, seq, half):
    count = half // 128
    return jnp.concatenate([rows[pl.ds(seq * count + k, 1), :] for k in range(count)], axis=1)


def lane_sum(x):
    total = x[:, 0:128]
    for k in range(1, x.shape[1] // 128):
        total = total + x[:, k * 128 : (k + 1) * 128]
    return total


def row_sums(parts, st, pad):
    ones = jnp.ones((8, 128), BF)
    blocks = parts.shape[0] // 2
    for b in range(blocks):
        for j in range(2):
            x = parts[j * blocks + b]
            high = x.astype(BF)
            low = (x - high.astype(F32)).astype(BF)
            sums = dot(ones, high, 1, 1) + dot(ones, low, 1, 1)
            st[2 * b + j : 2 * b + j + 1, 0:pad] = sums[0:1, :]


def spatial_body(
    n, pad, meta, v0, v1, v2, gu0, gu1, gu2, dgu0, dgu1, dgu2, sp, gp, gs, pm, gmix, g2, s2, t0, t1, t2, t3,
    prod, ghu, cols, st, keep, send,
    mixed, so, tile, parts,
):
    samples, half, rows = gp.shape[0], gp.shape[2], PATCHES // n
    whole = half * n
    stats, vs, gus, dgus = (t0, t1, t2, t3), (v0, v1, v2), (gu0, gu1, gu2), (dgu0, dgu1, dgu2)
    tile[...] = jnp.zeros_like(tile)
    for i in range(samples):
        for r in range(n):
            at = [2 * (i * n + (r ^ k)) for k in range(n)]
            means = [stats[k][at[k] : at[k] + 1, :] for k in range(n)]
            squares = [stats[k][at[k] + 1 : at[k] + 2, :] for k in range(n)]
            mean = ((means[0] + means[1]) + (means[2] + means[3])) / n
            spread = (squares[0] + squares[1]) + (squares[2] + squares[3])
            for k in range(n):
                spread = spread + half * (means[k] - mean) * (means[k] - mean)
            blk = 2 * (i * n + r)
            tile[blk : blk + 1, :] = mean
            tile[blk + 1 : blk + 2, :] = lax.rsqrt(spread / whole + EPSILON)
    cols[...] = jnp.transpose(tile[...])
    gain, shift = own_lanes(g2, meta[0], half), own_lanes(s2, meta[0], half)
    for i in range(samples):
        for r in range(n):
            k, base = part(r, pad)
            blk = 2 * (i * n + r)
            for c in range(pad // CHUNK):
                here = slice(c * CHUNK, (c + 1) * CHUNK)
                at = slice(r * pad + c * CHUNK, r * pad + (c + 1) * CHUNK)
                mean, inverse = cols[here, blk : blk + 1], cols[here, blk + 1 : blk + 2]
                standard = (vs[k][i, base + c * CHUNK : base + (c + 1) * CHUNK, :] - mean) * inverse
                out = jnp.where(valid_rows(meta, i, r, c, rows), standard * gain + shift, 0.0)
                if r == 0 and (c + 1) * CHUNK == pad:
                    p = c * CHUNK + iota((CHUNK, 1), 0)
                    out = jnp.where(p >= pad - 2, 1.0, out)
                mixed[i, at, :] = out.astype(BF)
                t = gmix[i, at, :] * gain
                parts[i * n + r, here, :] = lane_sum(t)
                parts[samples * n + i * n + r, here, :] = lane_sum(t * standard)
        so[i] = dot(sp[...], mixed[i], 1, 0)
    row_sums(parts, st, pad)
    total = dot(gs[0], mixed[0], 1, 1)
    for i in range(1, samples):
        total = total + dot(gs[i], mixed[i], 1, 1)
    placed = dot(total.astype(BF), pm[...], 1, 1).astype(BF)
    for r in range(n):
        (keep, send)[r % 2][r // 2] = placed[r * pad : (r + 1) * pad, :]
    for i in range(samples):
        for r in range(n):
            k, base = part(r, pad)
            for c in range(pad // CHUNK):
                src = slice(base + c * CHUNK, base + (c + 1) * CHUNK)
                at = slice(r * pad + c * CHUNK, r * pad + (c + 1) * CHUNK)
                s = so[i, at, :]
                prod[i, at, :] = (gus[k][i, src, :].astype(F32) * s).astype(BF)
                ghu[i, at, :] = (gp[i, at, :] * s * dgus[k][i, src, :].astype(F32)).astype(BF)


def weight_sum(normed, grads, pad):
    total = None
    for i in range(grads.shape[0]):
        for k, blocks in enumerate(GROUPS):
            rows = slice(blocks[0] * pad, (blocks[-1] + 1) * pad)
            term = dot(normed[k][i], grads[i, rows, :], 0, 0)
            total = term if total is None else total + term
    return total


def store_shards(dp, whole, outs, base):
    shard = whole.shape[0] // 4
    for rho, out in enumerate(outs):
        here = whole[rows_at(((dp ^ rho) & 3) * shard, shard, 16), :]
        out[base : base + shard, :] = here.astype(BF)


def weights_body(n, pad, meta, prod, gb, ghu, n0, n1, n2, keep_a, keep_b, send, ow, uw):
    total = dot(gb[0], prod[0], 0, 0)
    for i in range(1, prod.shape[0]):
        total = total + dot(gb[i], prod[i], 0, 0)
    ow[...] = total
    uw[...] = weight_sum((n0, n1, n2), ghu, pad)
    shard = ow.shape[0] // 4
    outs = (keep_a, send.at[0], keep_b, send.at[1])
    store_shards(meta[1], ow, outs, 0)
    store_shards(meta[1], uw, outs, shard)


EXTRA = 32


def back_body(
    n, pad, meta, gmix, v0, v1, v2, dgv0, dgv1, dgv2, cols, t0, t1, t2, t3, g1, s1, g2, n0, n1, n2,
    ghu, wu, wv, e0, e1, e2,
    grad, keep_a, keep_b, send,
    tile, col, ghv, vw, acc, sums, extra,
):
    samples, half = gmix.shape[0], gmix.shape[2]
    width = grad.shape[2]
    stats, vs, dgvs = (t0, t1, t2, t3), (v0, v1, v2), (dgv0, dgv1, dgv2)
    tile[...] = jnp.zeros_like(tile)
    for i in range(samples):
        for r in range(n):
            blk = 2 * (i * n + r)
            terms = [
                stats[k][2 * (i * n + (r ^ k)) : 2 * (i * n + (r ^ k)) + 2, :] for k in range(n)
            ]
            tile[blk : blk + 2, :] = ((terms[0] + terms[1]) + (terms[2] + terms[3])) / (half * n)
    col[...] = jnp.transpose(tile[...])
    gain = own_lanes(g2, meta[0], half)
    acc[...] = jnp.zeros_like(acc)
    for i in range(samples):
        for r in range(n):
            k, base = part(r, pad)
            blk = 2 * (i * n + r)
            for c in range(pad // CHUNK):
                here = slice(c * CHUNK, (c + 1) * CHUNK)
                at = slice(r * pad + c * CHUNK, r * pad + (c + 1) * CHUNK)
                src = slice(base + c * CHUNK, base + (c + 1) * CHUNK)
                mean, inverse = cols[here, blk : blk + 1], cols[here, blk + 1 : blk + 2]
                first, second = col[here, blk : blk + 1], col[here, blk + 1 : blk + 2]
                standard = (vs[k][i, src, :] - mean) * inverse
                g = gmix[i, at, :]
                out = inverse * (g * gain - first - standard * second)
                ghv[i, at, :] = (out * dgvs[k][i, src, :].astype(F32)).astype(BF)
                acc[0] += g * standard
                acc[1] += g
    normed = (n0, n1, n2)
    vw[...] = weight_sum(normed, ghv, pad)
    sums[...] = jnp.zeros_like(sums)
    for i in range(samples):
        grad[i] = dot(ghu[i], wu[...], 1, 1) + dot(ghv[i], wv[...], 1, 1)
        for r in range(n):
            k, base = part(r, pad)
            for c in range(pad // CHUNK):
                at = slice(r * pad + c * CHUNK, r * pad + (c + 1) * CHUNK)
                src = slice(base + c * CHUNK, base + (c + 1) * CHUNK)
                g = grad[i, at, :]
                sums[0] += g * normed[k][i, src, :].astype(F32)
                sums[1] += g
    shift_one = jnp.sum(sums[1], axis=0, keepdims=True)
    gain_one = (jnp.sum(sums[0], axis=0, keepdims=True) - s1[...] * shift_one) / g1[...]
    edge = e0[0].astype(F32) + e1[0].astype(F32) + e2[...].astype(F32)
    size = pad // 4
    extra[...] = jnp.zeros_like(extra)
    for k in range(4):
        extra[k, 0:size, :] = edge[k * size : (k + 1) * size, :]
    extra[0, size : size + 1, :] = jnp.sum(acc[0], axis=0, keepdims=True)
    extra[1, size : size + 1, :] = jnp.sum(acc[1], axis=0, keepdims=True)
    for k, row in ((2, gain_one), (3, shift_one)):
        extra[k, size : size + 1, :] = row[:, 0:half]
        extra[k, size + 1 : size + 2, 0 : width - half] = row[:, half:]
    outs = (keep_a, send.at[0], keep_b, send.at[1])
    store_shards(meta[1], vw, outs, 0)
    shard = vw.shape[0] // 4
    for rho, out in enumerate(outs):
        out[shard:, :] = extra[(meta[1] ^ rho) & 3].astype(BF)


def rows_body(n, pad, prod, wo, grad, keep_a, send_a, keep_b, send_b):
    samples, rows = prod.shape[0], keep_a.shape[1]
    outs = (keep_a, send_a, keep_b, send_b)
    for i in range(samples):
        full = dot(prod[i], wo[...], 1, 0)
        for r in range(n):
            outs[r][i] = full[r * pad : r * pad + rows, :].astype(BF)
            outs[r][samples + i] = grad[i, r * pad : r * pad + rows, :].astype(BF)


def finish_rows_body(meta, tok, cot, keep, got_a, got_b, g1, output, grad_tokens):
    samples, rows = tok.shape[0], tok.shape[1]
    gain = g1[...]
    p = meta[0] * rows + iota((rows, 1), 0)
    for i in range(samples):
        x = tok[i].astype(F32)
        total = keep[i].astype(F32) + got_a[i].astype(F32) + got_b[i].astype(F32)
        output[i] = (x + branch_scale(meta, i, samples, p) * total).astype(BF)
        center = x - jnp.mean(x, axis=-1, keepdims=True)
        inverse = lax.rsqrt(jnp.mean(center * center, axis=-1, keepdims=True) + EPSILON)
        standard = center * inverse
        k = samples + i
        t = (keep[k].astype(F32) + got_a[k].astype(F32) + got_b[k].astype(F32)) * gain
        first = jnp.mean(t, axis=-1, keepdims=True)
        second = jnp.mean(t * standard, axis=-1, keepdims=True)
        grad = cot[i].astype(F32) + inverse * (t - first - standard * second)
        grad_tokens[i] = grad.astype(BF)


def sources(meta):
    seq, shard = meta[0], meta[1] & 3
    out = []
    for flip in (0, 1):
        s = seq ^ flip
        core = s & 1
        out += [
            (shard, s),
            (shard ^ (1 - core), s ^ (2 * core)),
            (shard ^ core, s ^ (2 * (1 - core))),
            (shard ^ 1, s ^ 2),
        ]
    return out


def place_first_body(half, meta, *refs):
    pieces = refs[:8]
    w_in, w_out, wide, tall, sems = refs[8:]
    shard = wide.shape[1]
    copies = []
    for k, (group, seq) in enumerate(sources(meta)):
        for e in range(2):
            slot = 2 * k + e
            row = (group ^ (2 * e)) * shard
            columns = rows_at(seq * half, half, 128)
            tall[slot] = jnp.transpose(pieces[k][e, 0:shard, :].astype(F32))
            target = w_out.at[columns, rows_at(row, shard, 128)]
            copies.append(pltpu.make_async_copy(tall.at[slot], target, sems.at[2 * slot]))
            copies[-1].start()
            wide[slot] = pieces[k][e, shard:, :].astype(F32)
            target = w_in.at[rows_at(row, shard, 16), columns]
            copies.append(pltpu.make_async_copy(wide.at[slot], target, sems.at[2 * slot + 1]))
            copies[-1].start()
    for copy in copies:
        copy.wait()


def place_last_body(half, gate, meta, *refs):
    pieces = refs[:8]
    w_in, spatial, bias, gain_one, shift_one, gain_two, shift_two, wide, edge, norms, sems = refs[9:]
    shard = wide.shape[1]
    rows, patches = spatial.shape
    size = edge.shape[0] // 4
    me, core = meta[0], meta[0] & 1
    origins = sources(meta)
    copies = []
    small = []
    for k, (group, seq) in enumerate(origins):
        for e in range(2):
            slot = 2 * k + e
            at = group ^ (2 * e)
            wide[slot] = pieces[k][e, 0:shard, :].astype(F32)
            columns = rows_at(gate + seq * half, half, 128)
            target = w_in.at[rows_at(at * shard, shard, 16), columns]
            copies.append(pltpu.make_async_copy(wide.at[slot], target, sems.at[slot]))
            copies[-1].start()
            rest = pieces[k][e, shard:, :].astype(F32)
            small.append((at, rest[0:size]))
            norms[at, seq] = rest[size:]
    for e in range(2):
        at, own = small[e]
        edge[rows_at(at * size, size, 8), :] = own
        at = (meta[1] & 3) ^ 1 ^ (2 * e)
        edge[rows_at(at * size, size, 8), :] = jnp.where(core == 0, small[2 + e][1], small[4 + e][1])
    spatial[...] = edge[0:rows, 0:patches]
    first = patches // 128 * 128
    tail = edge[0:rows, first:]
    column = jnp.sum(
        jnp.where(iota(tail.shape, 1) == patches - first, tail, 0.0), axis=1, keepdims=True
    )
    diagonal = iota((rows, rows), 0) == iota((rows, rows), 1)
    bias[...] = jnp.sum(jnp.where(diagonal, column, 0.0), axis=0, keepdims=True)
    for at, out in ((2, gain_one), (3, shift_one)):
        total = (norms[at, 0] + norms[at, 1]) + (norms[at, 2] + norms[at, 3])
        out[:, 0:half] = total[0:1, :]
        out[:, half:] = total[1:2, 0 : out.shape[1] - half]
    for at, out in ((0, gain_two), (1, shift_two)):
        for j in range(4):
            out[:, j * half : (j + 1) * half] = norms[at, j, 0:1, :]
    for copy in copies:
        copy.wait()


def solution(mesh):
    n, m = mesh.shape["seq"], mesh.shape["dp"]

    def over_seq(x, flip):
        return lax.ppermute(x, "seq", [(i, i ^ flip) for i in range(n)])

    def over_dp(x, flip):
        return lax.ppermute(x, "dp", [(i, i ^ flip) for i in range(m)])

    def mixed_axes(x, core_of_x):
        pairs = []
        for d in range(m):
            for s in range(n):
                other = (d ^ 1, s) if s & 1 == core_of_x else (d, s ^ 2)
                pairs.append((d * n + s, other[0] * n + other[1]))
        return lax.ppermute(x, ("dp", "seq"), pairs)

    def add(*terms):
        total = terms[0].astype(F32)
        for t in terms[1:]:
            total = total + t.astype(F32)
        return total.astype(BF)

    def ordered():
        last = []

        def step(body, *ins):
            if last:
                ins, _ = lax.optimization_barrier((ins, last[0]))
            out = body(*ins) if body else ins[0]
            last[:] = [jax.tree.leaves(out)[0]]
            return out

        return step

    def shards(
        tokens,
        res_class,
        skip_mask,
        w_in,
        w_out,
        spatial,
        spatial_bias,
        gain_one,
        shift_one,
        gain_two,
        shift_two,
        cotangent,
    ):
        samples, rows, width = tokens.shape
        gate = w_out.shape[0]
        half = gate // n
        pad = round_up(rows + 2, 16)
        full = n * pad
        columns = round_up(n * rows + 2, 128)
        seq, dp = lax.axis_index("seq"), lax.axis_index("dp")
        meta = jnp.concatenate([seq[None], dp[None], res_class, skip_mask]).astype(jnp.int32)
        step = ordered()
        big_bf, big_f32 = (shape_of((samples, full, half), d) for d in (BF, F32))
        shard = width // 4
        square = shape_of((round_up(samples * 2 * n, 8), 128), F32)

        t0 = tokens
        t2 = over_seq(t0, 2)
        t1 = over_seq(t0, 1)
        high = lax.reduce_precision(spatial_bias, 8, 7)
        side = jnp.stack([high, spatial_bias - high], axis=1).astype(BF)
        packed = jnp.concatenate([spatial, side], axis=1)
        packed = jnp.pad(packed, ((0, 0), (0, width - packed.shape[1])))
        c0 = jnp.concatenate([cotangent, packed[None]])
        c2 = over_seq(c0, 2)
        wu = lax.dynamic_slice(w_in, (0, seq * half), (width, half))
        wv = lax.dynamic_slice(w_in, (0, gate + seq * half), (width, half))
        wo = lax.dynamic_slice(w_out, (seq * half, 0), (half, width))
        g1, s1 = gain_one[None], shift_one[None]
        g2, s2 = gain_two.reshape(-1, 128), shift_two.reshape(-1, 128)
        meta, wu, wv, wo, c0, t1 = lax.optimization_barrier((meta, wu, wv, wo, c0, t1))
        c1 = over_seq(c0, 1)

        n0, gu0, dgu0, v0, dgv0, st = step(
            lambda *a: project(pad, 0, a[:2], *a[2:]), t0, t1, g1, s1, wu, wv
        )
        t2 = step(None, t2)
        t3 = over_seq(t2, 1)
        n1, gu1, dgu1, v1, dgv1, st = step(
            lambda *a: project(pad, 2, a[:1], *a[1:]), t2, g1, s1, wu, wv, st
        )
        n2, gu2, dgu2, v2, dgv2, st = step(
            lambda *a: project(pad, 3, a[:1], *a[1:]), t3, g1, s1, wu, wv, st
        )
        normed = [n0, n1, n2]
        stats = step(None, [st] + [over_seq(st, k) for k in range(1, n)])
        c2 = step(None, c2)
        c3 = over_seq(c2, 1)

        def prepare(*ins):
            return call(
                functools.partial(prepare_body, n, pad),
                [
                    shape_of((full, full), BF), shape_of((samples, full, width), BF),
                    big_f32, big_bf, big_f32, shape_of((columns, full), BF),
                ],
                ins,
                [pltpu.VMEM((full, full), BF)],
                specs=[SM] + [VM] * (len(ins) - 1),
                name="prepare",
            )

        sp, gb, gp, gs, gmix, pm = step(
            prepare, meta, c0, c1, c2, c3, wo, gu0, gu1, gu2
        )

        def spatial_unit(*ins):
            edge = shape_of((n // 2, pad, columns), BF)
            return call(
                functools.partial(spatial_body, n, pad),
                [big_bf, big_bf, shape_of((128, 128), F32), square, edge, edge],
                ins,
                [
                    pltpu.VMEM((samples, full, half), BF),
                    pltpu.VMEM((samples, full, half), F32),
                    pltpu.VMEM((128, 128), F32),
                    pltpu.VMEM((2 * samples * n, pad, 128), F32),
                ],
                specs=[SM] + [VM] * (len(ins) - 1),
                name="spatial",
            )

        prod, ghu, cols, st2, e_keep, e_send = step(
            spatial_unit, meta, v0, v1, v2, gu0, gu1, gu2, dgu0, dgu1, dgu2, sp, gp, gs, pm, gmix,
            g2, s2, *stats,
        )
        stats = [st2] + [over_seq(st2, k) for k in range(1, n)]
        e_got = over_seq(e_send, 1)

        def weights(*ins):
            shape = shape_of((2 * shard, half), BF)
            return call(
                functools.partial(weights_body, n, pad),
                [shape, shape, shape_of((2, 2 * shard, half), BF)],
                ins,
                [pltpu.VMEM((width, half), F32), pltpu.VMEM((width, half), F32)],
                specs=[SM] + [VM] * (len(ins) - 1),
                name="weights",
            )

        def add_second(a, b):
            return add(a, b[1])

        def add_first(a, b, c):
            return add(a, b[0], c)

        def pair_up(*a):
            return jnp.stack(a)

        def twin(x):
            return over_seq(x, 1)

        w_a, w_b, w_send = step(weights, meta, prod, gb, ghu, *normed)
        w_got = over_dp(w_send, 1)
        e_last = over_seq(step(lambda a, b: add(a[1], b[1]), e_keep, e_got), 2)

        def back(*ins):
            shape = shape_of((shard + EXTRA, half), BF)
            return call(
                functools.partial(back_body, n, pad),
                [
                    shape_of((samples, full, width), F32), shape, shape,
                    shape_of((2, shard + EXTRA, half), BF),
                ],
                ins,
                [
                    pltpu.VMEM((128, 128), F32),
                    pltpu.VMEM((128, 128), F32),
                    pltpu.VMEM((samples, full, half), BF),
                    pltpu.VMEM((width, half), F32),
                    pltpu.VMEM((2, CHUNK, half), F32),
                    pltpu.VMEM((2, CHUNK, width), F32),
                    pltpu.VMEM((4, EXTRA, half), F32),
                ],
                specs=[SM] + [VM] * (len(ins) - 1),
                name="back",
            )

        grad, v_a, v_b, v_send = step(
            back, meta, gmix, v0, v1, v2, dgv0, dgv1, dgv2, cols, *stats, g1, s1, g2, *normed, ghu,
            wu, wv, e_keep, e_got, e_last,
        )
        v_got = over_dp(v_send, 1)

        def rows_out(*ins):
            shape = shape_of((2 * samples, rows, width), BF)
            return call(functools.partial(rows_body, n, pad), [shape] * 4, ins, name="rows_out")

        r_a, send_a, r_b, send_b = step(rows_out, prod, wo, grad)
        r_got, r_got_b = twin(send_a), twin(send_b)

        w_z = over_dp(step(add_second, w_b, w_got), 2)
        r_got, r_got_b = step(None, (r_got, r_got_b))
        r_last = over_seq(step(add, r_b, r_got_b), 2)
        v_z = over_dp(step(add_second, v_b, v_got), 2)
        w_mine = step(add_first, w_a, w_got, w_z)
        w_z = over_dp(w_mine, 4) if m > 4 else None
        v_mine = step(add_first, v_a, v_got, v_z)
        v_z = over_dp(v_mine, 4) if m > 4 else None
        flip = 8
        while flip < m:
            w_mine, v_mine = step(add, w_mine, w_z), step(add, v_mine, v_z)
            w_z, v_z = over_dp(w_mine, flip), over_dp(v_mine, flip)
            flip *= 2
        if m > 4:
            w_mine = step(add, w_mine, w_z)
        w_z = over_dp(w_mine, 2)

        def finish_rows(*ins):
            shape = shape_of(tokens.shape, BF)
            return call(
                finish_rows_body, [shape, shape], ins, specs=[SM] + [VM] * 6, name="finish_rows"
            )

        output, grad_tokens = step(finish_rows, meta, t0, c0, r_a, r_got, r_last, g1)
        if m > 4:
            v_mine = step(add, v_mine, v_z)
        v_z = over_dp(v_mine, 2)
        w_pair = step(pair_up, w_mine, w_z)
        w_first, w_second, w_pair_b = mixed_axes(w_pair, 0), mixed_axes(w_pair, 1), twin(w_pair)
        v_z, w_pair_b = step(None, (v_z, w_pair_b))
        v_pair = step(pair_up, v_mine, v_z)
        v_first, v_second = mixed_axes(v_pair, 0), mixed_axes(v_pair, 1)
        w_first, w_second = step(None, (w_first, w_second))
        w_third, w_first_b, w_second_b = mixed_axes(w_first, 1), twin(w_first), twin(w_second)
        v_first, v_second, w_first_b, w_second_b = step(
            None, (v_first, v_second, w_first_b, w_second_b)
        )
        v_third, v_pair_b, v_first_b = mixed_axes(v_first, 1), twin(v_pair), twin(v_first)
        w_third, v_pair_b, v_first_b = step(None, (w_third, v_pair_b, v_first_b))
        w_third_b, v_second_b = twin(w_third), twin(v_second)

        def place_first(*ins):
            return call(
                functools.partial(place_first_body, half),
                [shape_of((width, 2 * gate), F32), shape_of((gate, width), F32)],
                ins,
                [
                    pltpu.VMEM((16, shard, half), F32),
                    pltpu.VMEM((16, half, shard), F32),
                    pltpu.SemaphoreType.DMA((32,)),
                ],
                specs=[SM] + [VM] * 8,
                out_specs=[HB] * 2,
                name="place_first",
            )

        def place_last(*ins):
            one, two = shape_of((1, width), F32), shape_of((1, gate), F32)
            small = [shape_of((rows, n * rows), F32), shape_of((1, rows), F32), one, one, two, two]
            return call(
                functools.partial(place_last_body, half, gate),
                [shape_of((width, 2 * gate), F32)] + small,
                ins,
                [
                    pltpu.VMEM((16, shard, half), F32),
                    pltpu.VMEM((pad, columns), F32),
                    pltpu.VMEM((4, n, EXTRA - pad // 4, half), F32),
                    pltpu.SemaphoreType.DMA((16,)),
                ],
                specs=[SM] + [VM] * 8 + [HB],
                out_specs=[HB] + [VM] * 6,
                input_output_aliases={9: 0},
                name="place_last",
            )

        grad_w_in, grad_w_out = step(
            place_first, meta, w_pair, w_first, w_second, w_third, w_pair_b, w_first_b, w_second_b,
            w_third_b,
        )
        v_third = step(None, v_third)
        v_third_b = twin(v_third)
        grad_w_in, grad_spatial, *sums = step(
            place_last, meta, v_pair, v_first, v_second, v_third, v_pair_b, v_first_b, v_second_b,
            v_third_b, grad_w_in,
        )
        sums = [v.reshape(-1) for v in sums]
        return (output, grad_tokens, grad_w_in, grad_w_out, grad_spatial, *sums)

    placed = (
        P("dp", "seq", None),
        P("dp"),
        P("dp"),
        P(),
        P(),
        P("seq", None),
        P("seq"),
        P(),
        P(),
        P(),
        P(),
        P("dp", "seq", None),
    )
    return jax.shard_map(
        shards,
        mesh=mesh,
        in_specs=placed,
        out_specs=(
            P("dp", "seq", None),
            P("dp", "seq", None),
            P(),
            P(),
            P("seq", None),
            P("seq"),
            P(),
            P(),
            P(),
            P(),
        ),
        check_vma=False,
    )
```

time: 419 us -> 110 us (0.26)
  waiting for transfers between devices: 284 us -> 47.7 us
  blocking collectives: 58.9 us -> 0 us
  matrix products: 31.8 us -> 0 us
  starting transfers between devices: 0.34 us -> 29 us
  Pallas kernels: 0 us -> 26.5 us
  between operations: 14.7 us -> 0.94 us
  local copies, waits for them, and re-layouts: 13.2 us -> 1.54 us
  other arithmetic: 15.3 us -> 4.48 us
    psum x2 -> x0, waiting for transfers between devices: 183 us -> none  [the longest x1 183 us: shards(): lax.psum((grad_w_in, grad_w_out, small_grads), ('dp', 'seq'))]
    unnamed x5 -> x0, waiting for transfers between devices: 68.2 us -> none
    psum x2 -> x0, blocking collectives: 58.9 us -> none  [the longest x1 37.1 us: shards(): lax.psum((grad_w_in, grad_w_out, small_grads), ('dp', 'seq'))]
    ppermute x0 -> x39, waiting for transfers between devices: none -> 47.7 us  [the longest x8 22.3 us: over_dp(): return lax.ppermute(x, 'dp', [(i, i ^ flip) for i in range(m)])]
    all_gather x1 -> x0, waiting for transfers between devices: 33.4 us -> none  [shards(): gathered = lax.all_gather(mixed_low, 'seq', axis=1, tiled=True)]
    dot_general x9 -> x0, matrix products: 31.8 us -> none  [the longest x1 4.72 us: shards(): jnp.einsum('spd,sph->dh', normed_low, grad_hidden_low, preferred_element_...]
    ppermute x0 -> x39, starting transfers between devices: none -> 29 us  [the longest x25 12.2 us: over_seq(): return lax.ppermute(x, 'seq', [(i, i ^ flip) for i in range(n)])]
    pallas_call x0 -> x11, Pallas kernels: none -> 26.5 us  [call(): pl.pallas_call(body, out_shape=outs, in_specs=specs if specs is not None...]
  transfers between devices with their start and end apart: 4 -> 39, of which waited for: 3 -> 19; matrix products, arithmetic and copies ran while one was open for 6% -> 4% of each run, Pallas kernels for 0% -> 16%
where the time goes in v2:
time: 110 us
  waiting for transfers between devices  47.7 us (43%)
  starting transfers between devices  29 us (26%)
  Pallas kernels  26.5 us (24%)
  other arithmetic  4.48 us (4%)
  local copies, waits for them, and re-layouts  1.54 us (1%)
    pallas_call x11, Pallas kernels, call(): pl.pallas_call(body, out_shape=outs, in_specs=specs if specs is not None...  26.5 us
    ppermute x8, waiting for transfers between devices, over_dp(): return lax.ppermute(x, 'dp', [(i, i ^ flip) for i in range(m)])  22.3 us
    ppermute x6, waiting for transfers between devices, mixed_axes(): return lax.ppermute(x, ('dp', 'seq'), pairs)  15.6 us
    ppermute x25, starting transfers between devices, over_seq(): return lax.ppermute(x, 'seq', [(i, i ^ flip) for i in range(n)])  12.2 us
    ppermute x8, starting transfers between devices, over_dp(): return lax.ppermute(x, 'dp', [(i, i ^ flip) for i in range(m)])  11.1 us
    ppermute x25, waiting for transfers between devices, over_seq(): return lax.ppermute(x, 'seq', [(i, i ^ flip) for i in range(n)])  9.75 us
    ppermute x6, starting transfers between devices, mixed_axes(): return lax.ppermute(x, ('dp', 'seq'), pairs)  5.71 us
  transfers between devices with their start and end apart: 39, of which 19 were waited for; matrix products, arithmetic and copies ran while one was open for 4% of the time, Pallas kernels for 16%

profile of v2, /device:TPU:0, one launch (start us, length us, event | category | flops | bytes accessed | tf_op | source)
XLA Modules:
  0.0 110.1 jit_solution(10856879532887105680)
XLA Ops:
  1.2 2.6 %collective-permute-start.1 = (bf16[3,81,512]{2,1,0:T(8,128)(2,1)}, bf16[3,81,512]{2,1,0:T(8,128)(2,1)S(1)}, u32[]{:S(2)}, u32[]{:S(2)}) collective-permute-start(bf16[3,81,512]{2,1,0:T(8,128)(2,1)} %tok), channel_id=1, source_target_pairs={{0,2},{1,3},{2,0},{3,1},{4,6},{5,7},{6,4},{7,5},{8,10},{9,11},{10,... | collective-permute-start | bytes 746504 | tf_op jit(solution)/shard_map/ppermute | solution.py:514
  8.3 2.0 %project.3 = (bf16[3,192,512]{2,1,0:T(8,128)(2,1)S(1)}, bf16[3,192,384]{2,1,0:T(8,128)(2,1)S(1)}, bf16[3,192,384]{2,1,0:T(8,128)(2,1)S(1)}, f32[3,192,384]{2,1,0...) custom-call(bf16[3,81,512]{2,1,0:T(8,128)(2,1)S(1)} %copy-done.1, ...), custom_call_target="tpu_custom_call" | custom-call | flops 1 | bytes 1 | tf_op jit(solution)/shard_map/project/pallas_call | solution.py:42
  14.1 1.7 %collective-permute-start.7 = (f32[24,128]{1,0:T(8,128)S(1)}, f32[24,128]{1,0:T(8,128)S(1)}, u32[]{:S(2)}, u32[]{:S(2)}) collective-permute-start(f32[24,128]{1,0:T(8,128)S(1)} %get-tuple-element.283.t0), channel_id=1, source_target_pairs={{0,3},{1,2},{2,1},{3,0},{4,7},{5,6},{6,5},{7,4},{8,11},{9,10},{10,... | collective-permute-start | bytes 36872 | tf_op jit(solution)/shard_map/ppermute | solution.py:514
  16.6 2.2 %collective-permute-done.7.t3 = f32[24,128]{1,0:T(8,128)S(1)} collective-permute-done((f32[24,128]{1,0:T(8,128)S(1)}, f32[24,128]{1,0:T(8,128)S(1)}, u32[]{:S(2)}, u32[]{:S(2)}) %collective-permute-start.7) | collective-permute-done | bytes 12320 | tf_op jit(solution)/shard_map/ppermute | solution.py:514
  19.5 1.7 %collective-permute-done.8.c3 = bf16[4,81,512]{2,1,0:T(8,128)(2,1)S(1)} collective-permute-done((bf16[4,81,512]{2,1,0:T(8,128)(2,1)S(1)}, bf16[4,81,512]{2,1,0:T(8,128)(2,1)S(1)}, u32[]{:S(2)}, u32[]{:S(2)}) %collective-permute-start.8) | collective-permute-done | bytes 331808 | tf_op jit(solution)/shard_map/ppermute | solution.py:514
  21.2 2.6 %prepare.1 = (bf16[384,384]{1,0:T(8,128)(2,1)S(1)}, bf16[3,384,512]{2,1,0:T(8,128)(2,1)S(1)}, f32[3,384,384]{2,1,0:T(8,128)S(1)}, bf16[3,384,384]{2,1,0:T(8,128)...) custom-call(s32[8]{0:T(128)S(1)} %pad_add_fusion.meta, ...), custom_call_target="tpu_custom_call" | custom-call | flops 1 | bytes 1 | tf_op jit(solution)/shard_map/prepare/pallas_call | solution.py:42
  23.8 3.5 %spatial.1 = (bf16[3,384,384]{2,1,0:T(8,128)(2,1)S(1)}, bf16[3,384,384]{2,1,0:T(8,128)(2,1)S(1)}, f32[128,128]{1,0:T(8,128)S(1)}, f32[24,128]{1,0:T(8,128)S(1)},...) custom-call(s32[8]{0:T(128)S(1)} %pad_add_fusion.meta, f32[3,192,384]{2,1,0:T(8,128)S(1)} %get-tuple-element.309.v0, ...), custom_call_target="tpu_custom_call" | custom-call | flops 1 | bytes 1 | tf_op jit(solution)/shard_map/spatial/pallas_call | solution.py:42
  27.5 2.7 %weights.1 = (bf16[256,384]{1,0:T(8,128)(2,1)S(1)}, bf16[256,384]{1,0:T(8,128)(2,1)S(1)}, bf16[2,256,384]{2,1,0:T(8,128)(2,1)S(1)}) custom-call(s32[8]{0:T(128)S(1)} %pad_add_fusion.meta, bf16[3,384,384]{2,1,0:T(8,128)(2,1)S(1)} %get-tuple-element.333.prod, bf16[3,384,512]{2,1,0:T(8,128)(2,1)S(1)} %get-tuple-element.299.gb, ...), custom_call_target="tpu_custom_call" | custom-call | flops 1 | bytes 1 | tf_op jit(solution)/shard_map/weights/pallas_call | solution.py:42
  30.1 1.7 %collective-permute-start.16 = (bf16[2,256,384]{2,1,0:T(8,128)(2,1)S(1)}, bf16[2,256,384]{2,1,0:T(8,128)(2,1)S(1)}, u32[]{:S(2)}, u32[]{:S(2)}) collective-permute-start(bf16[2,256,384]{2,1,0:T(8,128)(2,1)S(1)} %get-tuple-element.340), channel_id=1, source_target_pairs={{0,4},{4,0},{8,12},{12,8},{16,20},{20,16},{24,28},{28,24},{1,5},{5... | collective-permute-start | bytes 1179656 | tf_op jit(solution)/shard_map/ppermute | solution.py:517
  31.9 1.6 %collective-permute-start.13 = (bf16[96,384]{1,0:T(8,128)(2,1)S(1)}, bf16[96,384]{1,0:T(8,128)(2,1)S(1)}, u32[]{:S(2)}, u32[]{:S(2)}) collective-permute-start(bf16[96,384]{1,0:T(8,128)(2,1)S(1)} %fusion.12), channel_id=1, source_target_pairs={{0,2},{1,3},{2,0},{3,1},{4,6},{5,7},{6,4},{7,5},{8,10},{9,11},{10,... | collective-permute-start | bytes 221192 | tf_op jit(solution)/shard_map/ppermute | solution.py:514
  33.5 1.4 %collective-permute-start.10 = (f32[24,128]{1,0:T(8,128)S(1)}, f32[24,128]{1,0:T(8,128)S(1)}, u32[]{:S(2)}, u32[]{:S(2)}) collective-permute-start(f32[24,128]{1,0:T(8,128)S(1)} %get-tuple-element.316.t0), channel_id=1, source_target_pairs={{0,2},{1,3},{2,0},{3,1},{4,6},{5,7},{6,4},{7,5},{8,10},{9,11},{10,... | collective-permute-start | bytes 36872 | tf_op jit(solution)/shard_map/ppermute | solution.py:514
  37.2 4.3 %back.1 = (f32[3,384,512]{2,1,0:T(8,128)S(1)}, bf16[160,384]{1,0:T(8,128)(2,1)S(1)}, bf16[160,384]{1,0:T(8,128)(2,1)S(1)}, bf16[2,160,384]{2,1,0:T(8,128)(2,1)S(1)}) custom-call(s32[8]{0:T(128)S(1)} %pad_add_fusion.meta, f32[3,384,384]{2,1,0:T(8,128)S(1)} %get-tuple-element.308.gmix, f32[3,192,384]{2,1,0:T(8,128)S(1)} %get-tuple-element.309.v0, ...), custom_call_target="tpu_custom_call" | custom-call | flops 1 | bytes 1 | tf_op jit(solution)/shard_map/back/pallas_call | solution.py:42
  43.5 1.6 %collective-permute-start.18 = (bf16[256,384]{1,0:T(8,128)(2,1)S(1)}, bf16[256,384]{1,0:T(8,128)(2,1)S(1)}, u32[]{:S(2)}, u32[]{:S(2)}) collective-permute-start(bf16[256,384]{1,0:T(8,128)(2,1)S(1)} %fusion.2), channel_id=1, source_target_pairs={{0,8},{4,12},{8,0},{12,4},{16,24},{20,28},{24,16},{28,20},{1,9},{5... | collective-permute-start | bytes 589832 | tf_op jit(solution)/shard_map/ppermute | solution.py:517
  45.3 1.5 %collective-permute-start.17 = (bf16[6,81,512]{2,1,0:T(8,128)(2,1)S(1)}, bf16[6,81,512]{2,1,0:T(8,128)(2,1)S(1)}, u32[]{:S(2)}, u32[]{:S(2)}) collective-permute-start(bf16[6,81,512]{2,1,0:T(8,128)(2,1)S(1)} %add_convert_fusion), channel_id=1, source_target_pairs={{0,2},{1,3},{2,0},{3,1},{4,6},{5,7},{6,4},{7,5},{8,10},{9,11},{10,... | collective-permute-start | bytes 1493000 | tf_op jit(solution)/shard_map/ppermute | solution.py:514
  46.7 4.1 %collective-permute-done.19 = bf16[2,160,384]{2,1,0:T(8,128)(2,1)S(1)} collective-permute-done((bf16[2,160,384]{2,1,0:T(8,128)(2,1)S(1)}, bf16[2,160,384]{2,1,0:T(8,128)(2,1)S(1)}, u32[]{:S(2)}, u32[]{:S(2)}) %collective-permute-start.19) | collective-permute-done | bytes 245792 | tf_op jit(solution)/shard_map/ppermute | solution.py:517
  50.9 1.6 %collective-permute-start.21 = (bf16[160,384]{1,0:T(8,128)(2,1)S(1)}, bf16[160,384]{1,0:T(8,128)(2,1)S(1)}, u32[]{:S(2)}, u32[]{:S(2)}) collective-permute-start(bf16[160,384]{1,0:T(8,128)(2,1)S(1)} %fusion.5), channel_id=1, source_target_pairs={{0,8},{4,12},{8,0},{12,4},{16,24},{20,28},{24,16},{28,20},{1,9},{5... | collective-permute-start | bytes 368648 | tf_op jit(solution)/shard_map/ppermute | solution.py:517
  52.6 2.7 %collective-permute-start.20 = (bf16[256,384]{1,0:T(8,128)(2,1)S(1)}, bf16[256,384]{1,0:T(8,128)(2,1)S(1)}, u32[]{:S(2)}, u32[]{:S(2)}) collective-permute-start(bf16[256,384]{1,0:T(8,128)(2,1)S(1)} %fusion.1), channel_id=1, source_target_pairs={{0,16},{4,20},{8,24},{12,28},{16,0},{20,4},{24,8},{28,12},{1,17},{... | collective-permute-start | bytes 589832 | tf_op jit(solution)/shard_map/ppermute | solution.py:517
  55.2 1.7 %collective-permute-done.21 = bf16[160,384]{1,0:T(8,128)(2,1)S(1)} collective-permute-done((bf16[160,384]{1,0:T(8,128)(2,1)S(1)}, bf16[160,384]{1,0:T(8,128)(2,1)S(1)}, u32[]{:S(2)}, u32[]{:S(2)}) %collective-permute-start.21) | collective-permute-done | bytes 122912 | tf_op jit(solution)/shard_map/ppermute | solution.py:517
  57.0 2.9 %collective-permute-start.22 = (bf16[160,384]{1,0:T(8,128)(2,1)S(1)}, bf16[160,384]{1,0:T(8,128)(2,1)S(1)}, u32[]{:S(2)}, u32[]{:S(2)}) collective-permute-start(bf16[160,384]{1,0:T(8,128)(2,1)S(1)} %fusion.4), channel_id=1, source_target_pairs={{0,16},{4,20},{8,24},{12,28},{16,0},{20,4},{24,8},{28,12},{1,17},{... | collective-permute-start | bytes 368648 | tf_op jit(solution)/shard_map/ppermute | solution.py:517
  59.9 7.6 %collective-permute-done.20 = bf16[256,384]{1,0:T(8,128)(2,1)S(1)} collective-permute-done((bf16[256,384]{1,0:T(8,128)(2,1)S(1)}, bf16[256,384]{1,0:T(8,128)(2,1)S(1)}, u32[]{:S(2)}, u32[]{:S(2)}) %collective-permute-start.20) | collective-permute-done | bytes 196640 | tf_op jit(solution)/shard_map/ppermute | solution.py:517
  67.6 1.8 %finish_rows.1 = (bf16[3,81,512]{2,1,0:T(8,128)(2,1)}, bf16[3,81,512]{2,1,0:T(8,128)(2,1)}) custom-call(s32[8]{0:T(128)S(1)} %pad_add_fusion.meta, bf16[3,81,512]{2,1,0:T(8,128)(2,1)S(1)} %copy-done.1, bf16[4,81,512]{2,1,0:T(8,128)(2,1)S(1)} %pad_maximum_fusion.1.c0.cot, bf16[6,81,512]{2,1,0:T(8,128)(2,1)S(1)} %get-tuple-element.364.keep, ...), custom_call_target="tpu_custom_call" | custom-call | flops 1 | bytes 1 | tf_op jit(solution)/shard_map/finish_rows/pallas_call | solution.py:42
  69.5 3.8 %collective-permute-done.24 = bf16[256,384]{1,0:T(8,128)(2,1)S(1)} collective-permute-done((bf16[256,384]{1,0:T(8,128)(2,1)S(1)}, bf16[256,384]{1,0:T(8,128)(2,1)S(1)}, u32[]{:S(2)}, u32[]{:S(2)}) %collective-permute-start.24) | collective-permute-done | bytes 196640 | tf_op jit(solution)/shard_map/ppermute | solution.py:517
  73.4 1.5 %collective-permute-start.29 = (bf16[2,256,384]{2,1,0:T(8,128)(2,1)S(1)}, bf16[2,256,384]{2,1,0:T(8,128)(2,1)S(1)}, u32[]{:S(2)}, u32[]{:S(2)}) collective-permute-start(bf16[2,256,384]{2,1,0:T(8,128)(2,1)S(1)} %pad_maximum_fusion.refs_0_), channel_id=1, source_target_pairs={{0,2},{1,5},{2,0},{3,7},{4,6},{5,1},{6,4},{7,3},{8,10},{9,13},{10,... | collective-permute-start | bytes 1179656 | tf_op jit(solution)/shard_map/ppermute | solution.py:525
  75.4 5.1 %collective-permute-done.23 = bf16[160,384]{1,0:T(8,128)(2,1)S(1)} collective-permute-done((bf16[160,384]{1,0:T(8,128)(2,1)S(1)}, bf16[160,384]{1,0:T(8,128)(2,1)S(1)}, u32[]{:S(2)}, u32[]{:S(2)}) %collective-permute-start.23) | collective-permute-done | bytes 122912 | tf_op jit(solution)/shard_map/ppermute | solution.py:517
  80.5 4.6 %collective-permute-done.29.refs_2_ = bf16[2,256,384]{2,1,0:T(8,128)(2,1)S(1)} collective-permute-done((bf16[2,256,384]{2,1,0:T(8,128)(2,1)S(1)}, bf16[2,256,384]{2,1,0:T(8,128)(2,1)S(1)}, u32[]{:S(2)}, u32[]{:S(2)}) %collective-permute-start.29) | collective-permute-done | bytes 393248 | tf_op jit(solution)/shard_map/ppermute | solution.py:525
  88.0 5.9 %collective-permute-done.27.refs_2_ = bf16[2,160,384]{2,1,0:T(8,128)(2,1)S(1)} collective-permute-done((bf16[2,160,384]{2,1,0:T(8,128)(2,1)S(1)}, bf16[2,160,384]{2,1,0:T(8,128)(2,1)S(1)}, u32[]{:S(2)}, u32[]{:S(2)}) %collective-permute-start.27) | collective-permute-done | bytes 245792 | tf_op jit(solution)/shard_map/ppermute | solution.py:525
  93.9 2.1 %collective-permute-done.26.refs_1_ = bf16[2,160,384]{2,1,0:T(8,128)(2,1)S(1)} collective-permute-done((bf16[2,160,384]{2,1,0:T(8,128)(2,1)S(1)}, bf16[2,160,384]{2,1,0:T(8,128)(2,1)S(1)}, u32[]{:S(2)}, u32[]{:S(2)}) %collective-permute-start.26) | collective-permute-done | bytes 245792 | tf_op jit(solution)/shard_map/ppermute | solution.py:525
  96.0 2.1 %collective-permute-done.33.refs_3_ = bf16[2,256,384]{2,1,0:T(8,128)(2,1)S(1)} collective-permute-done((bf16[2,256,384]{2,1,0:T(8,128)(2,1)S(1)}, bf16[2,256,384]{2,1,0:T(8,128)(2,1)S(1)}, u32[]{:S(2)}, u32[]{:S(2)}) %collective-permute-start.33) | collective-permute-done | bytes 393248 | tf_op jit(solution)/shard_map/ppermute | solution.py:525
  98.1 1.4 %collective-permute-start.32 = (bf16[2,160,384]{2,1,0:T(8,128)(2,1)S(1)}, bf16[2,160,384]{2,1,0:T(8,128)(2,1)S(1)}, u32[]{:S(2)}, u32[]{:S(2)}) collective-permute-start(bf16[2,160,384]{2,1,0:T(8,128)(2,1)S(1)} %collective-permute-done.26.refs_1_), channel_id=1, source_target_pairs={{0,2},{1,5},{2,0},{3,7},{4,6},{5,1},{6,4},{7,3},{8,10},{9,13},{10,... | collective-permute-start | bytes 737288 | tf_op jit(solution)/shard_map/ppermute | solution.py:525
  99.9 3.6 %place_first.1 = (f32[512,3072]{1,0:T(8,128)}, f32[1536,512]{1,0:T(8,128)}) custom-call(s32[8]{0:T(128)S(1)} %pad_add_fusion.meta, bf16[2,256,384]{2,1,0:T(8,128)(2,1)S(1)} %pad_maximum_fusion.refs_0_, bf16[2,256,384]{2,1,0:T(8,128)(2,1)S(1)} %collective-permute-done.28.refs_1_, bf16[2,256,384]{2,1,0:T(8,128)(2,1)S(1)} %collective-permute-done.29.refs_2_, ...), custom_call_target="tpu_custom_call" | custom-call | flops 1 | bytes 1 | tf_op jit(solution)/shard_map/place_first/pallas_call | solution.py:42
  104.3 1.5 %collective-permute-done.38.refs_7_ = bf16[2,160,384]{2,1,0:T(8,128)(2,1)S(1)} collective-permute-done((bf16[2,160,384]{2,1,0:T(8,128)(2,1)S(1)}, bf16[2,160,384]{2,1,0:T(8,128)(2,1)S(1)}, u32[]{:S(2)}, u32[]{:S(2)}) %collective-permute-start.38) | collective-permute-done | bytes 245792 | tf_op jit(solution)/shard_map/ppermute | solution.py:514
  105.8 3.0 %place_last.1 = (f32[512,3072]{1,0:T(8,128)}, f32[81,324]{1,0:T(8,128)}, f32[1,81]{1,0:T(1,128)}, f32[1,512]{1,0:T(1,128)}, f32[1,512]{1,0:T(1,128)}, /*index=5*/f32[1,1536]{1,0:T(1,128)S(1)}, f32[1,1536]{1,0:T(1,128)S(1)}) custom-call(s32[8]{0:T(128)S(1)} %pad_add_fusion.meta, ...), custom_call_target="tpu_custom_call", output_to_operand_aliasing={{0}: (9, {})} | custom-call | flops 1 | bytes 1 | tf_op jit(solution)/shard_map/place_last/pallas_call | solution.py:42
  (93 shorter events, 21.2 us)
Async XLA Ops:
  0.7 7.6 %collective-permute-start = (bf16[3,81,512]{2,1,0:T(8,128)(2,1)}, bf16[3,81,512]{2,1,0:T(8,128)(2,1)S(1)}, u32[]{:S(2)}, u32[]{:S(2)}) collective-permute-start(bf16[3,81,512]{2,1,0:T(8,128)(2,1)} %tok), channel_id=1, source_target_pairs={{0,1},{1,0},{2,3},{3,2},{4,5},{5,4},{6,7},{7,6},{8,9},{9,8},{10,11... | collective-permute-start | bytes 746504 | tf_op jit(solution)/shard_map/ppermute | solution.py:514
  1.2 10.1 %collective-permute-start.1 = (bf16[3,81,512]{2,1,0:T(8,128)(2,1)}, bf16[3,81,512]{2,1,0:T(8,128)(2,1)S(1)}, u32[]{:S(2)}, u32[]{:S(2)}) collective-permute-start(bf16[3,81,512]{2,1,0:T(8,128)(2,1)} %tok), channel_id=1, source_target_pairs={{0,2},{1,3},{2,0},{3,1},{4,6},{5,7},{6,4},{7,5},{8,10},{9,11},{10,... | collective-permute-start | bytes 746504 | tf_op jit(solution)/shard_map/ppermute | solution.py:514
  6.7 12.8 %collective-permute-start.4 = (bf16[4,81,512]{2,1,0:T(8,128)(2,1)S(1)}, bf16[4,81,512]{2,1,0:T(8,128)(2,1)S(1)}, u32[]{:S(2)}, u32[]{:S(2)}) collective-permute-start(bf16[4,81,512]{2,1,0:T(8,128)(2,1)S(1)} %pad_maximum_fusion.1.c0.cot), channel_id=1, source_target_pairs={{0,2},{1,3},{2,0},{3,1},{4,6},{5,7},{6,4},{7,5},{8,10},{9,11},{10,... | collective-permute-start | bytes 995336 | tf_op jit(solution)/shard_map/ppermute | solution.py:514
  14.1 4.8 %collective-permute-start.7 = (f32[24,128]{1,0:T(8,128)S(1)}, f32[24,128]{1,0:T(8,128)S(1)}, u32[]{:S(2)}, u32[]{:S(2)}) collective-permute-start(f32[24,128]{1,0:T(8,128)S(1)} %get-tuple-element.283.t0), channel_id=1, source_target_pairs={{0,3},{1,2},{2,1},{3,0},{4,7},{5,6},{6,5},{7,4},{8,11},{9,10},{10,... | collective-permute-start | bytes 36872 | tf_op jit(solution)/shard_map/ppermute | solution.py:514
  15.8 3.7 %collective-permute-start.6 = (f32[24,128]{1,0:T(8,128)S(1)}, f32[24,128]{1,0:T(8,128)S(1)}, u32[]{:S(2)}, u32[]{:S(2)}) collective-permute-start(f32[24,128]{1,0:T(8,128)S(1)} %get-tuple-element.283.t0), channel_id=1, source_target_pairs={{0,2},{1,3},{2,0},{3,1},{4,6},{5,7},{6,4},{7,5},{8,10},{9,11},{10,... | collective-permute-start | bytes 36872 | tf_op jit(solution)/shard_map/ppermute | solution.py:514
  16.1 3.4 %collective-permute-start.5 = (f32[24,128]{1,0:T(8,128)S(1)}, f32[24,128]{1,0:T(8,128)S(1)}, u32[]{:S(2)}, u32[]{:S(2)}) collective-permute-start(f32[24,128]{1,0:T(8,128)S(1)} %get-tuple-element.283.t0), channel_id=1, source_target_pairs={{0,1},{1,0},{2,3},{3,2},{4,5},{5,4},{6,7},{7,6},{8,9},{9,8},{10,11... | collective-permute-start | bytes 36872 | tf_op jit(solution)/shard_map/ppermute | solution.py:514
  16.1 3.4 %collective-permute-start.3 = (bf16[4,81,512]{2,1,0:T(8,128)(2,1)S(1)}, bf16[4,81,512]{2,1,0:T(8,128)(2,1)S(1)}, u32[]{:S(2)}, u32[]{:S(2)}) collective-permute-start(bf16[4,81,512]{2,1,0:T(8,128)(2,1)S(1)} %pad_maximum_fusion.1.c0.cot), channel_id=1, source_target_pairs={{0,1},{1,0},{2,3},{3,2},{4,5},{5,4},{6,7},{7,6},{8,9},{9,8},{10,11... | collective-permute-start | bytes 995336 | tf_op jit(solution)/shard_map/ppermute | solution.py:514
  27.3 4.6 %collective-permute-start.12 = (bf16[2,96,384]{2,1,0:T(8,128)(2,1)S(1)}, bf16[2,96,384]{2,1,0:T(8,128)(2,1)S(1)}, u32[]{:S(2)}, u32[]{:S(2)}) collective-permute-start(bf16[2,96,384]{2,1,0:T(8,128)(2,1)S(1)} %get-tuple-element.295), channel_id=1, source_target_pairs={{0,1},{1,0},{2,3},{3,2},{4,5},{5,4},{6,7},{7,6},{8,9},{9,8},{10,11... | collective-permute-start | bytes 442376 | tf_op jit(solution)/shard_map/ppermute | solution.py:514
  30.1 13.3 %collective-permute-start.16 = (bf16[2,256,384]{2,1,0:T(8,128)(2,1)S(1)}, bf16[2,256,384]{2,1,0:T(8,128)(2,1)S(1)}, u32[]{:S(2)}, u32[]{:S(2)}) collective-permute-start(bf16[2,256,384]{2,1,0:T(8,128)(2,1)S(1)} %get-tuple-element.340), channel_id=1, source_target_pairs={{0,4},{4,0},{8,12},{12,8},{16,20},{20,16},{24,28},{28,24},{1,5},{5... | collective-permute-start | bytes 1179656 | tf_op jit(solution)/shard_map/ppermute | solution.py:517
  31.9 5.3 %collective-permute-start.13 = (bf16[96,384]{1,0:T(8,128)(2,1)S(1)}, bf16[96,384]{1,0:T(8,128)(2,1)S(1)}, u32[]{:S(2)}, u32[]{:S(2)}) collective-permute-start(bf16[96,384]{1,0:T(8,128)(2,1)S(1)} %fusion.12), channel_id=1, source_target_pairs={{0,2},{1,3},{2,0},{3,1},{4,6},{5,7},{6,4},{7,5},{8,10},{9,11},{10,... | collective-permute-start | bytes 221192 | tf_op jit(solution)/shard_map/ppermute | solution.py:514
  33.5 3.2 %collective-permute-start.11 = (f32[24,128]{1,0:T(8,128)S(1)}, f32[24,128]{1,0:T(8,128)S(1)}, u32[]{:S(2)}, u32[]{:S(2)}) collective-permute-start(f32[24,128]{1,0:T(8,128)S(1)} %get-tuple-element.316.t0), channel_id=1, source_target_pairs={{0,3},{1,2},{2,1},{3,0},{4,7},{5,6},{6,5},{7,4},{8,11},{9,10},{10,... | collective-permute-start | bytes 36872 | tf_op jit(solution)/shard_map/ppermute | solution.py:514
  33.5 3.7 %collective-permute-start.10 = (f32[24,128]{1,0:T(8,128)S(1)}, f32[24,128]{1,0:T(8,128)S(1)}, u32[]{:S(2)}, u32[]{:S(2)}) collective-permute-start(f32[24,128]{1,0:T(8,128)S(1)} %get-tuple-element.316.t0), channel_id=1, source_target_pairs={{0,2},{1,3},{2,0},{3,1},{4,6},{5,7},{6,4},{7,5},{8,10},{9,11},{10,... | collective-permute-start | bytes 36872 | tf_op jit(solution)/shard_map/ppermute | solution.py:514
  42.3 2.8 %collective-permute-start.14 = (bf16[6,81,512]{2,1,0:T(8,128)(2,1)S(1)}, bf16[6,81,512]{2,1,0:T(8,128)(2,1)S(1)}, u32[]{:S(2)}, u32[]{:S(2)}) collective-permute-start(bf16[6,81,512]{2,1,0:T(8,128)(2,1)S(1)} %get-tuple-element.337), channel_id=1, source_target_pairs={{0,1},{1,0},{2,3},{3,2},{4,5},{5,4},{6,7},{7,6},{8,9},{9,8},{10,11... | collective-permute-start | bytes 1493000 | tf_op jit(solution)/shard_map/ppermute | solution.py:514
  42.4 2.7 %collective-permute-start.15 = (bf16[6,81,512]{2,1,0:T(8,128)(2,1)S(1)}, bf16[6,81,512]{2,1,0:T(8,128)(2,1)S(1)}, u32[]{:S(2)}, u32[]{:S(2)}) collective-permute-start(bf16[6,81,512]{2,1,0:T(8,128)(2,1)S(1)} %get-tuple-element.338), channel_id=1, source_target_pairs={{0,1},{1,0},{2,3},{3,2},{4,5},{5,4},{6,7},{7,6},{8,9},{9,8},{10,11... | collective-permute-start | bytes 1493000 | tf_op jit(solution)/shard_map/ppermute | solution.py:514
  42.9 7.9 %collective-permute-start.19 = (bf16[2,160,384]{2,1,0:T(8,128)(2,1)S(1)}, bf16[2,160,384]{2,1,0:T(8,128)(2,1)S(1)}, u32[]{:S(2)}, u32[]{:S(2)}) collective-permute-start(bf16[2,160,384]{2,1,0:T(8,128)(2,1)S(1)} %get-tuple-element.349), channel_id=1, source_target_pairs={{0,4},{4,0},{8,12},{12,8},{16,20},{20,16},{24,28},{28,24},{1,5},{5... | collective-permute-start | bytes 737288 | tf_op jit(solution)/shard_map/ppermute | solution.py:517
  43.5 9.0 %collective-permute-start.18 = (bf16[256,384]{1,0:T(8,128)(2,1)S(1)}, bf16[256,384]{1,0:T(8,128)(2,1)S(1)}, u32[]{:S(2)}, u32[]{:S(2)}) collective-permute-start(bf16[256,384]{1,0:T(8,128)(2,1)S(1)} %fusion.2), channel_id=1, source_target_pairs={{0,8},{4,12},{8,0},{12,4},{16,24},{20,28},{24,16},{28,20},{1,9},{5... | collective-permute-start | bytes 589832 | tf_op jit(solution)/shard_map/ppermute | solution.py:517
  45.3 22.3 %collective-permute-start.17 = (bf16[6,81,512]{2,1,0:T(8,128)(2,1)S(1)}, bf16[6,81,512]{2,1,0:T(8,128)(2,1)S(1)}, u32[]{:S(2)}, u32[]{:S(2)}) collective-permute-start(bf16[6,81,512]{2,1,0:T(8,128)(2,1)S(1)} %add_convert_fusion), channel_id=1, source_target_pairs={{0,2},{1,3},{2,0},{3,1},{4,6},{5,7},{6,4},{7,5},{8,10},{9,11},{10,... | collective-permute-start | bytes 1493000 | tf_op jit(solution)/shard_map/ppermute | solution.py:514
  50.9 6.1 %collective-permute-start.21 = (bf16[160,384]{1,0:T(8,128)(2,1)S(1)}, bf16[160,384]{1,0:T(8,128)(2,1)S(1)}, u32[]{:S(2)}, u32[]{:S(2)}) collective-permute-start(bf16[160,384]{1,0:T(8,128)(2,1)S(1)} %fusion.5), channel_id=1, source_target_pairs={{0,8},{4,12},{8,0},{12,4},{16,24},{20,28},{24,16},{28,20},{1,9},{5... | collective-permute-start | bytes 368648 | tf_op jit(solution)/shard_map/ppermute | solution.py:517
  52.6 14.9 %collective-permute-start.20 = (bf16[256,384]{1,0:T(8,128)(2,1)S(1)}, bf16[256,384]{1,0:T(8,128)(2,1)S(1)}, u32[]{:S(2)}, u32[]{:S(2)}) collective-permute-start(bf16[256,384]{1,0:T(8,128)(2,1)S(1)} %fusion.1), channel_id=1, source_target_pairs={{0,16},{4,20},{8,24},{12,28},{16,0},{20,4},{24,8},{28,12},{1,17},{... | collective-permute-start | bytes 589832 | tf_op jit(solution)/shard_map/ppermute | solution.py:517
  57.0 12.4 %collective-permute-start.22 = (bf16[160,384]{1,0:T(8,128)(2,1)S(1)}, bf16[160,384]{1,0:T(8,128)(2,1)S(1)}, u32[]{:S(2)}, u32[]{:S(2)}) collective-permute-start(bf16[160,384]{1,0:T(8,128)(2,1)S(1)} %fusion.4), channel_id=1, source_target_pairs={{0,16},{4,20},{8,24},{12,28},{16,0},{20,4},{24,8},{28,12},{1,17},{... | collective-permute-start | bytes 368648 | tf_op jit(solution)/shard_map/ppermute | solution.py:517
  67.5 5.7 %collective-permute-start.24 = (bf16[256,384]{1,0:T(8,128)(2,1)S(1)}, bf16[256,384]{1,0:T(8,128)(2,1)S(1)}, u32[]{:S(2)}, u32[]{:S(2)}) collective-permute-start(bf16[256,384]{1,0:T(8,128)(2,1)S(1)} %add_convert_fusion.1), channel_id=1, source_target_pairs={{0,8},{4,12},{8,0},{12,4},{16,24},{20,28},{24,16},{28,20},{1,9},{5... | collective-permute-start | bytes 589832 | tf_op jit(solution)/shard_map/ppermute | solution.py:517
  73.3 7.2 %collective-permute-start.25 = (bf16[2,256,384]{2,1,0:T(8,128)(2,1)S(1)}, bf16[2,256,384]{2,1,0:T(8,128)(2,1)S(1)}, u32[]{:S(2)}, u32[]{:S(2)}) collective-permute-start(bf16[2,256,384]{2,1,0:T(8,128)(2,1)S(1)} %pad_maximum_fusion.refs_0_), channel_id=1, source_target_pairs={{0,1},{1,0},{2,3},{3,2},{4,5},{5,4},{6,7},{7,6},{8,9},{9,8},{10,11... | collective-permute-start | bytes 1179656 | tf_op jit(solution)/shard_map/ppermute | solution.py:514
  73.4 11.8 %collective-permute-start.29 = (bf16[2,256,384]{2,1,0:T(8,128)(2,1)S(1)}, bf16[2,256,384]{2,1,0:T(8,128)(2,1)S(1)}, u32[]{:S(2)}, u32[]{:S(2)}) collective-permute-start(bf16[2,256,384]{2,1,0:T(8,128)(2,1)S(1)} %pad_maximum_fusion.refs_0_), channel_id=1, source_target_pairs={{0,2},{1,5},{2,0},{3,7},{4,6},{5,1},{6,4},{7,3},{8,10},{9,13},{10,... | collective-permute-start | bytes 1179656 | tf_op jit(solution)/shard_map/ppermute | solution.py:525
  74.9 10.3 %collective-permute-start.28 = (bf16[2,256,384]{2,1,0:T(8,128)(2,1)S(1)}, bf16[2,256,384]{2,1,0:T(8,128)(2,1)S(1)}, u32[]{:S(2)}, u32[]{:S(2)}) collective-permute-start(bf16[2,256,384]{2,1,0:T(8,128)(2,1)S(1)} %pad_maximum_fusion.refs_0_), channel_id=1, source_target_pairs={{0,4},{1,3},{2,6},{3,1},{4,0},{5,7},{6,2},{7,5},{8,12},{9,11},{10,... | collective-permute-start | bytes 1179656 | tf_op jit(solution)/shard_map/ppermute | solution.py:525
  75.4 5.1 %collective-permute-start.23 = (bf16[160,384]{1,0:T(8,128)(2,1)S(1)}, bf16[160,384]{1,0:T(8,128)(2,1)S(1)}, u32[]{:S(2)}, u32[]{:S(2)}) collective-permute-start(bf16[160,384]{1,0:T(8,128)(2,1)S(1)} %add_convert_fusion.2), channel_id=1, source_target_pairs={{0,8},{4,12},{8,0},{12,4},{16,24},{20,28},{24,16},{28,20},{1,9},{5... | collective-permute-start | bytes 368648 | tf_op jit(solution)/shard_map/ppermute | solution.py:517
  85.2 10.8 %collective-permute-start.31 = (bf16[2,256,384]{2,1,0:T(8,128)(2,1)S(1)}, bf16[2,256,384]{2,1,0:T(8,128)(2,1)S(1)}, u32[]{:S(2)}, u32[]{:S(2)}) collective-permute-start(bf16[2,256,384]{2,1,0:T(8,128)(2,1)S(1)} %collective-permute-done.29.refs_2_), channel_id=1, source_target_pairs={{0,1},{1,0},{2,3},{3,2},{4,5},{5,4},{6,7},{7,6},{8,9},{9,8},{10,11... | collective-permute-start | bytes 1179656 | tf_op jit(solution)/shard_map/ppermute | solution.py:514
  85.2 10.8 %collective-permute-start.30 = (bf16[2,256,384]{2,1,0:T(8,128)(2,1)S(1)}, bf16[2,256,384]{2,1,0:T(8,128)(2,1)S(1)}, u32[]{:S(2)}, u32[]{:S(2)}) collective-permute-start(bf16[2,256,384]{2,1,0:T(8,128)(2,1)S(1)} %collective-permute-done.28.refs_1_), channel_id=1, source_target_pairs={{0,1},{1,0},{2,3},{3,2},{4,5},{5,4},{6,7},{7,6},{8,9},{9,8},{10,11... | collective-permute-start | bytes 1179656 | tf_op jit(solution)/shard_map/ppermute | solution.py:514
  85.7 8.2 %collective-permute-start.27 = (bf16[2,160,384]{2,1,0:T(8,128)(2,1)S(1)}, bf16[2,160,384]{2,1,0:T(8,128)(2,1)S(1)}, u32[]{:S(2)}, u32[]{:S(2)}) collective-permute-start(bf16[2,160,384]{2,1,0:T(8,128)(2,1)S(1)} %pad_maximum_fusion.2.refs_0_), channel_id=1, source_target_pairs={{0,2},{1,5},{2,0},{3,7},{4,6},{5,1},{6,4},{7,3},{8,10},{9,13},{10,... | collective-permute-start | bytes 737288 | tf_op jit(solution)/shard_map/ppermute | solution.py:525
  87.1 8.9 %collective-permute-start.26 = (bf16[2,160,384]{2,1,0:T(8,128)(2,1)S(1)}, bf16[2,160,384]{2,1,0:T(8,128)(2,1)S(1)}, u32[]{:S(2)}, u32[]{:S(2)}) collective-permute-start(bf16[2,160,384]{2,1,0:T(8,128)(2,1)S(1)} %pad_maximum_fusion.2.refs_0_), channel_id=1, source_target_pairs={{0,4},{1,3},{2,6},{3,1},{4,0},{5,7},{6,2},{7,5},{8,12},{9,11},{10,... | collective-permute-start | bytes 737288 | tf_op jit(solution)/shard_map/ppermute | solution.py:525
  87.4 10.8 %collective-permute-start.33 = (bf16[2,256,384]{2,1,0:T(8,128)(2,1)S(1)}, bf16[2,256,384]{2,1,0:T(8,128)(2,1)S(1)}, u32[]{:S(2)}, u32[]{:S(2)}) collective-permute-start(bf16[2,256,384]{2,1,0:T(8,128)(2,1)S(1)} %collective-permute-done.28.refs_1_), channel_id=1, source_target_pairs={{0,2},{1,5},{2,0},{3,7},{4,6},{5,1},{6,4},{7,3},{8,10},{9,13},{10,... | collective-permute-start | bytes 1179656 | tf_op jit(solution)/shard_map/ppermute | solution.py:525
  98.1 6.2 %collective-permute-start.32 = (bf16[2,160,384]{2,1,0:T(8,128)(2,1)S(1)}, bf16[2,160,384]{2,1,0:T(8,128)(2,1)S(1)}, u32[]{:S(2)}, u32[]{:S(2)}) collective-permute-start(bf16[2,160,384]{2,1,0:T(8,128)(2,1)S(1)} %collective-permute-done.26.refs_1_), channel_id=1, source_target_pairs={{0,2},{1,5},{2,0},{3,7},{4,6},{5,1},{6,4},{7,3},{8,10},{9,13},{10,... | collective-permute-start | bytes 737288 | tf_op jit(solution)/shard_map/ppermute | solution.py:525
  99.5 4.8 %collective-permute-start.37 = (bf16[2,160,384]{2,1,0:T(8,128)(2,1)S(1)}, bf16[2,160,384]{2,1,0:T(8,128)(2,1)S(1)}, u32[]{:S(2)}, u32[]{:S(2)}) collective-permute-start(bf16[2,160,384]{2,1,0:T(8,128)(2,1)S(1)} %collective-permute-done.27.refs_2_), channel_id=1, source_target_pairs={{0,1},{1,0},{2,3},{3,2},{4,5},{5,4},{6,7},{7,6},{8,9},{9,8},{10,11... | collective-permute-start | bytes 737288 | tf_op jit(solution)/shard_map/ppermute | solution.py:514
  (15 other events, 78.9 us)

commit v3 on v2

v3 whole, which is shorter than its diff:
```python
import functools

import jax
import jax.numpy as jnp
from jax import lax
from jax.experimental import pallas as pl
from jax.experimental.pallas import tpu as pltpu
from jax.sharding import PartitionSpec as P

PATCHES = 324
SMALL_P = 100
MID_P = 196

EPSILON = 1e-05
SURVIVAL = 0.9

BF = jnp.bfloat16
F32 = jnp.float32
CHUNK = 16
VM = pl.BlockSpec(memory_space=pltpu.VMEM)
SM = pl.BlockSpec(memory_space=pltpu.SMEM)
HB = pl.BlockSpec(memory_space=pltpu.HBM)


ORDER = (
    "weights", "stats", "a_send", "sums", "back", "rows", "a_rs", "tick", "v_send", "rows_core", "v_rs", "a_z2",
    "v_z2", "a_pair", "finish", "v_pair", "a_mark", "v_mark", "a_twin0", "a_twin1", "a_third", "a_twin2", "a_twin3",
    "v_twin0", "v_twin1", "place_first", "v_third", "v_twin2", "v_twin3", "place_most", "place_last",
)


def round_up(size, multiple):
    return -(-size // multiple) * multiple


def dot(a, b, ca, cb):
    return lax.dot_general(a, b, (((ca,), (cb,)), ((), ())), preferred_element_type=F32)


def iota(shape, axis):
    return lax.broadcasted_iota(jnp.int32, shape, axis)


def rows_at(start, size, multiple):
    return pl.ds(pl.multiple_of(start, multiple), size)


def call(body, outs, ins, scratch=(), specs=None, out_specs=None, flops=1, **more):
    return pl.pallas_call(
        body,
        out_shape=outs,
        in_specs=specs if specs is not None else [VM] * len(ins),
        out_specs=out_specs if out_specs is not None else [VM] * len(outs),
        scratch_shapes=list(scratch),
        compiler_params=pltpu.CompilerParams(vmem_limit_bytes=20 * 2**20),
        cost_estimate=pl.CostEstimate(flops=flops, bytes_accessed=1, transcendentals=0),
        **more,
    )(*ins)


def shape_of(shape, dtype):
    return jax.ShapeDtypeStruct(shape, dtype)


def add_body(*refs):
    total = refs[0][...].astype(F32)
    for ref in refs[1:-1]:
        total = total + ref[...].astype(F32)
    refs[-1][...] = total.astype(BF)


def tick_body(clock, out):
    out[...] = clock[...] + 1.0


def pair_body(a, b, out):
    out[0] = a[...]
    out[1] = b[...]


def project_body(pad, first_block, *refs):
    refs = list(refs)
    n_tok = len(refs) - 13 - (1 if first_block else 0)
    toks, refs = refs[:n_tok], refs[n_tok:]
    g1, s1, wu, wv = refs[:4]
    refs = refs[4:]
    if first_block:
        st_in, refs = refs[0], refs[1:]
    normed, gu, dgu, v, dgv, st, xs, hid, tile = refs
    samples, rows, width = toks[0].shape
    half = wu.shape[1]
    size = samples * pad
    found = [jnp.zeros((CHUNK, 128), F32)] * (128 // CHUNK)
    low = rows // 8 * 8
    gain, shift = g1[...], s1[...]
    for b, tok in enumerate(toks):
        for i in range(samples):
            base = (b * samples + i) * pad
            xs[base + low : base + pad, :] = jnp.zeros((pad - low, width), F32)
            xs[base : base + rows, :] = tok[i].astype(F32)
            for c in range(base, base + pad, CHUNK):
                x = xs[c : c + CHUNK, :]
                center = x - jnp.mean(x, axis=-1, keepdims=True)
                inverse = lax.rsqrt(jnp.mean(center * center, axis=-1, keepdims=True) + EPSILON)
                normed[c : c + CHUNK, :] = (center * inverse * gain + shift).astype(BF)
        at = slice(b * size, (b + 1) * size)
        hid[at, 0:half] = dot(normed[at, :], wu[...], 1, 0)
        hid[at, half:] = dot(normed[at, :], wv[...], 1, 0)
    c0 = 0.7978845608028654
    c1 = 0.7978845608028654 * 0.044715

    def gelu_pair(h):
        a = (c1 * h) * h
        s = 0.5 + 0.5 * jnp.tanh(h * (c0 + a))
        g = h * s
        return g, s + (2.0 * g) * (1.0 - s) * (c0 + 3.0 * a)

    lane = iota((CHUNK, 128), 1)
    for b in range(len(toks)):
        for i in range(samples):
            base = (b * samples + i) * pad
            blk = 2 * (i * 4 + first_block + b)
            for c in range(pad // CHUNK):
                at = slice(base + c * CHUNK, base + (c + 1) * CHUNK)
                g, d = gelu_pair(hid[at, 0:half])
                gu[at, :] = g.astype(BF)
                dgu[at, :] = d.astype(BF)
                g, d = gelu_pair(hid[at, half:])
                v[at, :] = g
                dgv[at, :] = d.astype(BF)
                mean = jnp.mean(g, axis=-1, keepdims=True)
                center = g - mean
                square = jnp.sum(center * center, axis=-1, keepdims=True)
                found[c] = jnp.where(
                    lane == blk, mean, jnp.where(lane == blk + 1, square, found[c])
                )
    for c, part_found in enumerate(found):
        tile[c * CHUNK : (c + 1) * CHUNK, :] = part_found
    flipped = jnp.transpose(tile[...])[0 : st.shape[0], :]
    st[...] = flipped + st_in[...] if first_block else flipped


def project(pad, first_block, toks, g1, s1, wu, wv, st_in=None):
    samples, rows, width = toks[0].shape
    half = wu.shape[1]
    n_rows = len(toks) * samples * pad
    outs = [
        shape_of((n_rows, width), BF),
        shape_of((n_rows, half), BF),
        shape_of((n_rows, half), BF),
        shape_of((n_rows, half), F32),
        shape_of((n_rows, half), BF),
        shape_of((round_up(samples * 8, 8), 128), F32),
    ]
    scratch = [
        pltpu.VMEM((n_rows, width), F32),
        pltpu.VMEM((n_rows, 2 * half), F32),
        pltpu.VMEM((128, 128), F32),
    ]
    ins = [*toks, g1, s1, wu, wv] + ([st_in] if first_block else [])
    return call(
        functools.partial(project_body, pad, first_block),
        outs,
        ins,
        scratch,
        name="project",
    )


GROUPS = ((0, 1), (2,), (3,))


def part(r, i, samples, pad):
    for k, blocks in enumerate(GROUPS):
        if r in blocks:
            return k, ((r - blocks[0]) * samples + i) * pad


def group_rows(size):
    return [slice(blocks[0] * size, (blocks[-1] + 1) * size) for blocks in GROUPS]


def position_map(seq, rows, pad, n, columns):
    a = iota((columns, n * pad), 0)
    j = iota((columns, n * pad), 1)
    r = jnp.zeros_like(j)
    for k in range(1, n):
        r = r + (j >= k * pad).astype(jnp.int32)
    q = j - r * pad
    hit = (a == (r ^ seq) * rows + q) & (q < rows)
    hit = hit | ((a == n * rows) & (j == pad - 1)) | ((a == n * rows + 1) & (j == pad - 2))
    return jnp.where(hit, 1.0, 0.0).astype(BF)


def patch_count(meta, i):
    kind = meta[2 + i]
    return jnp.where(kind == 0, SMALL_P, jnp.where(kind == 1, MID_P, PATCHES))


def branch_scale(meta, i, samples, where):
    keep = jnp.where(where < patch_count(meta, i), meta[2 + samples + i], 0)
    return keep.astype(F32) / SURVIVAL


def valid_rows(meta, i, r, c, rows):
    p = c * CHUNK + iota((CHUNK, 1), 0)
    return (p < rows) & ((meta[0] ^ r) * rows + p < patch_count(meta, i))


def front_rows(pad, first_block, meta, cots, wo, gu, gb, gp, put):
    rows, width = cots[0].shape[1], cots[0].shape[2]
    samples = cots[0].shape[0] - 1
    low = rows // 16 * 16
    size = samples * pad
    for b, cot in enumerate(cots):
        where = (meta[0] ^ (first_block + b)) * rows + iota((rows, 1), 0)
        for i in range(samples):
            base = b * size + i * pad
            scale = branch_scale(meta, i, samples, where)
            gb[base + low : base + pad, :] = jnp.zeros((pad - low, width), BF)
            gb[base : base + rows, :] = (cot[i].astype(F32) * scale).astype(BF)
        at = slice(b * size, (b + 1) * size)
        gp[at, :] = dot(gb[at, :], wo[...], 1, 1)
        for i in range(samples):
            for c in range(0, pad, CHUNK):
                at = slice(b * size + i * pad + c, b * size + i * pad + c + CHUNK)
                put(b, i, c, (gp[at, :] * gu[at, :].astype(F32)).astype(BF))


def matrix_rows(pad, block, cot, pm, sp):
    samples, rows = cot.shape[0] - 1, cot.shape[1]
    low = rows // 16 * 16
    sp[block * pad + low : (block + 1) * pad, :] = jnp.zeros((pad - low, sp.shape[1]), BF)
    out = dot(cot[samples, :, 0 : pm.shape[0]], pm[...], 1, 0)
    sp[block * pad : block * pad + rows, :] = out.astype(BF)


def front_body(n, pad, first_block, count, meta, *refs):
    cots, refs = refs[:count], refs[count:]
    if first_block:
        wo, gu, pm, gb, gp, gs, sp = refs
    else:
        wo, gu, gb, gp, gs, sp, pm = refs
        pm[...] = position_map(meta[0], cots[0].shape[1], pad, n, pm.shape[0])
    samples = cots[0].shape[0] - 1

    def put(b, i, c, out):
        base = (b * samples + i) * pad + c
        gs[base : base + CHUNK, :] = out

    front_rows(pad, first_block, meta, cots, wo, gu, gb, gp, put)
    for b, cot in enumerate(cots):
        matrix_rows(pad, b, cot, pm, sp)


def prepare_body(n, pad, meta, c3, wo, gu2, pm, gs0, gs1, sp0, sp1, gb, gp, gs, gmix, sp, spt):
    samples, rows = c3.shape[0] - 1, c3.shape[1]
    most = (n - 1) * pad
    sp[0 : sp0.shape[0], :] = sp0[...]
    sp[sp0.shape[0] : most, :] = sp1[...]
    matrix_rows(pad, n - 1, c3, pm, sp)
    spt[...] = jnp.transpose(sp[...].astype(F32)).astype(BF)

    half = gp.shape[1]

    def put(b, i, c, out):
        gs[most + c : most + c + CHUNK, i * half : (i + 1) * half] = out

    front_rows(pad, n - 1, meta, (c3,), wo, gu2, gb, gp, put)
    for i in range(samples):
        for r in range(n - 1):
            k, base = part(r, i, samples, pad)
            here = slice(i * half, (i + 1) * half)
            gs[r * pad : (r + 1) * pad, here] = (gs0, gs1)[k][base : base + pad, :]
    full = dot(spt[...], gs[...], 1, 0)
    for i in range(samples):
        for r in range(n):
            base = (r * samples + i) * pad
            for c in range(pad // CHUNK):
                at = slice(r * pad + c * CHUNK, r * pad + (c + 1) * CHUNK)
                out = full[at, i * half : (i + 1) * half]
                out = jnp.where(valid_rows(meta, i, r, c, rows), out, 0.0)
                gmix[base + c * CHUNK : base + (c + 1) * CHUNK, :] = out


def own_lanes(rows, seq, half):
    count = half // 128
    return jnp.concatenate([rows[pl.ds(seq * count + k, 1), :] for k in range(count)], axis=1)


def lane_sum(x):
    total = x[:, 0:128]
    for k in range(1, x.shape[1] // 128):
        total = total + x[:, k * 128 : (k + 1) * 128]
    return total


def row_sum(x):
    ones = jnp.ones((8, x.shape[1]), BF)
    high = x.astype(BF)
    low = (x - high.astype(F32)).astype(BF)
    return dot(ones, high, 1, 1) + dot(ones, low, 1, 1)


def row_sums(parts, st, pad):
    blocks = parts.shape[0] // 2
    for b in range(blocks):
        for j in range(2):
            st[2 * b + j : 2 * b + j + 1, 0:pad] = row_sum(parts[j * blocks + b])[0:1, :]


def pack_sums(st):
    x = jnp.concatenate([st[8 * k : 8 * (k + 1), :] for k in range(3)], axis=1)
    terms = []
    for _ in range(3):
        terms.append(x.astype(BF).astype(F32))
        x = x - terms[-1]
    return jnp.concatenate(terms + [jnp.zeros_like(x)], axis=0).astype(BF)


def unpack_sums(packed):
    x = packed.astype(F32)
    x = (x[16:24] + x[8:16]) + x[0:8]
    return jnp.concatenate([x[:, 128 * k : 128 * (k + 1)] for k in range(3)], axis=0)


def spatial_body(
    n, pad, meta, v0, v1, v2, gu0, gu1, gu2, dgu0, dgu1, dgu2, sp, gp0, gp1, gp2, gs, pm, gmix, g2, s2, t0, t1, t2, t3,
    prod, ghu, cols, st, edge, m1, m2, m3,
    mixed, so, tile, parts,
):
    half, rows = gp0.shape[1], PATCHES // n
    samples = gs.shape[1] // half
    gps = (gp0, gp1, gp2)
    whole = half * n
    stats, vs, gus, dgus = (t0, t1, t2, t3), (v0, v1, v2), (gu0, gu1, gu2), (dgu0, dgu1, dgu2)
    tile[...] = jnp.zeros_like(tile)
    for i in range(samples):
        for r in range(n):
            at = [2 * (i * n + (r ^ k)) for k in range(n)]
            means = [stats[k][at[k] : at[k] + 1, :] for k in range(n)]
            squares = [stats[k][at[k] + 1 : at[k] + 2, :] for k in range(n)]
            mean = ((means[0] + means[1]) + (means[2] + means[3])) / n
            spread = (squares[0] + squares[1]) + (squares[2] + squares[3])
            for k in range(n):
                spread = spread + half * (means[k] - mean) * (means[k] - mean)
            blk = 2 * (i * n + r)
            tile[blk : blk + 1, :] = mean
            tile[blk + 1 : blk + 2, :] = lax.rsqrt(spread / whole + EPSILON)
    cols[...] = jnp.transpose(tile[...])
    gain, shift = own_lanes(g2, meta[0], half), own_lanes(s2, meta[0], half)
    for i in range(samples):
        for r in range(n):
            k, base = part(r, i, samples, pad)
            first = (r * samples + i) * pad
            blk = 2 * (i * n + r)
            for c in range(pad // CHUNK):
                here = slice(c * CHUNK, (c + 1) * CHUNK)
                mean, inverse = cols[here, blk : blk + 1], cols[here, blk + 1 : blk + 2]
                standard = (vs[k][base + c * CHUNK : base + (c + 1) * CHUNK, :] - mean) * inverse
                out = jnp.where(valid_rows(meta, i, r, c, rows), standard * gain + shift, 0.0)
                if r == 0 and (c + 1) * CHUNK == pad:
                    p = c * CHUNK + iota((CHUNK, 1), 0)
                    out = jnp.where(p >= pad - 2, 1.0, out)
                at = slice(r * pad + c * CHUNK, r * pad + (c + 1) * CHUNK)
                mixed[at, i * half : (i + 1) * half] = out.astype(BF)
                t = gmix[first + c * CHUNK : first + (c + 1) * CHUNK, :] * gain
                parts[i * n + r, here, :] = lane_sum(t)
                parts[samples * n + i * n + r, here, :] = lane_sum(t * standard)
    so[...] = dot(sp[...], mixed[...], 1, 0)
    row_sums(parts, st, pad)
    total = dot(gs[...], mixed[...], 1, 1)
    placed = dot(total.astype(BF), pm[...], 1, 1).astype(BF)
    packed = pack_sums(st)
    edge[...] = placed[0:pad, :]
    for r, message in enumerate((m1, m2, m3), 1):
        message[0:pad, :] = placed[r * pad : (r + 1) * pad, :]
        message[pad:, :] = packed
    for i in range(samples):
        for r in range(n):
            k, base = part(r, i, samples, pad)
            first = (r * samples + i) * pad
            for c in range(0, pad, CHUNK):
                src = slice(base + c, base + c + CHUNK)
                at = slice(first + c, first + c + CHUNK)
                s = so[r * pad + c : r * pad + c + CHUNK, i * half : (i + 1) * half]
                prod[at, :] = (gus[k][src, :].astype(F32) * s).astype(BF)
                ghu[at, :] = (gps[k][src, :] * s * dgus[k][src, :].astype(F32)).astype(BF)


def weight_sum(lefts, rights):
    total = None
    for left, right in zip(lefts, rights):
        term = dot(left, right, 0, 0)
        total = term if total is None else total + term
    return total


def store_shards(dp, whole, outs, base):
    shard = whole.shape[0] // 4
    for rho, out in enumerate(outs):
        here = whole[rows_at(((dp ^ rho) & 3) * shard, shard, 16), :]
        out[base : base + shard, :] = here.astype(BF)


def norm_sums(w, grad_w, grads):
    columns = None
    for c in range(0, grads.shape[0], CHUNK):
        g = grads[c : c + CHUNK, :].astype(F32)
        columns = g if columns is None else columns + g
    columns = jnp.sum(columns, axis=0, keepdims=True)
    first, second = [], []
    for c in range(w.shape[0] // CHUNK):
        at = slice(c * CHUNK, (c + 1) * CHUNK)
        x = w[at, :].astype(F32)
        first.append(lane_sum(x * grad_w[at, :]))
        second.append(lane_sum(x * columns))
    first = row_sum(jnp.concatenate(first, axis=0))
    second = row_sum(jnp.concatenate(second, axis=0))
    return jnp.where(iota(first.shape, 0) == 0, first, second)


def flip_body(n0, n1, n2, out, whole):
    base = 0
    for ref in (n0, n1, n2):
        whole[base : base + ref.shape[0], :] = ref[...]
        base += ref.shape[0]
    out[...] = jnp.transpose(whole[...])


def weights_body(meta, prod, gb0, gb1, gb2, ghu, flipped, s0, s1, s2, s3, uw, ow):
    groups = group_rows(prod.shape[0] // 4)
    outs = (s0, s1, s2, s3)
    ow[...] = weight_sum([g[...] for g in (gb0, gb1, gb2)], [prod[at, :] for at in groups])
    uw[...] = dot(flipped[...], ghu[...], 1, 0)
    store_shards(meta[1], ow, outs, 0)
    store_shards(meta[1], uw, outs, ow.shape[0] // 4)


def sums_body(w, grad_w, grads, out):
    out[...] = norm_sums(w, grad_w, grads)


EXTRA = 32


def back_body(
    n, pad, meta, gmix, v0, v1, v2, dgv0, dgv1, dgv2, cols, st, edge0, m1, m2, m3, g1, s1, g2, flipped,
    wv, first_sums,
    ghv, w0, w1, w2, w3,
    tile, col, vw, acc, extra,
):
    samples, half = gmix.shape[0] // (n * pad), gmix.shape[1]
    width = wv.shape[0]
    messages, vs, dgvs = (m1, m2, m3), (v0, v1, v2), (dgv0, dgv1, dgv2)
    stats = [st[...]] + [unpack_sums(m[pad:, :]) for m in messages]
    tile[...] = jnp.zeros_like(tile)
    for i in range(samples):
        for r in range(n):
            blk = 2 * (i * n + r)
            terms = [
                stats[k][2 * (i * n + (r ^ k)) : 2 * (i * n + (r ^ k)) + 2, :] for k in range(n)
            ]
            tile[blk : blk + 2, :] = ((terms[0] + terms[1]) + (terms[2] + terms[3])) / (half * n)
    col[...] = jnp.transpose(tile[...])
    gain = own_lanes(g2, meta[0], half)
    acc[...] = jnp.zeros_like(acc)
    for i in range(samples):
        for r in range(n):
            k, base = part(r, i, samples, pad)
            row = (r * samples + i) * pad
            blk = 2 * (i * n + r)
            for c in range(pad // CHUNK):
                here = slice(c * CHUNK, (c + 1) * CHUNK)
                at = slice(row + c * CHUNK, row + (c + 1) * CHUNK)
                src = slice(base + c * CHUNK, base + (c + 1) * CHUNK)
                mean, inverse = cols[here, blk : blk + 1], cols[here, blk + 1 : blk + 2]
                first, second = col[here, blk : blk + 1], col[here, blk + 1 : blk + 2]
                standard = (vs[k][src, :] - mean) * inverse
                g = gmix[at, :]
                out = inverse * (g * gain - first - standard * second)
                ghv[at, :] = (out * dgvs[k][src, :].astype(F32)).astype(BF)
                acc[0] += g * standard
                acc[1] += g
    vw[...] = dot(flipped[...], ghv[...], 1, 0)
    sums = first_sums[...] + norm_sums(wv, vw, ghv)
    shift_one = sums[1:2, :]
    gain_one = (sums[0:1, :] - s1[...] * shift_one) / g1[...]
    edge = edge0[...].astype(F32)
    for m in messages:
        edge = edge + m[0:pad, :].astype(F32)
    size = pad // 4
    extra[...] = jnp.zeros_like(extra)
    for k in range(4):
        extra[k, 0:size, :] = edge[k * size : (k + 1) * size, :]
    extra[0, size : size + 1, :] = jnp.sum(acc[0], axis=0, keepdims=True)
    extra[1, size : size + 1, :] = jnp.sum(acc[1], axis=0, keepdims=True)
    for k, row in ((2, gain_one), (3, shift_one)):
        extra[k, size : size + 1, :] = row[:, 0:half]
        extra[k, size + 1 : size + 2, 0 : width - half] = row[:, half:]
    outs = (w0, w1, w2, w3)
    store_shards(meta[1], vw, outs, 0)
    shard = vw.shape[0] // 4
    for rho, out in enumerate(outs):
        out[shard:, :] = extra[(meta[1] ^ rho) & 3].astype(BF)


def rows_body(n, pad, prod, wo, ghu, ghv, wu, wv, keep_a, send_a, keep_b, send_b):
    samples, rows = keep_a.shape[0] // 2, keep_a.shape[1]
    for r, out in enumerate((keep_a, send_a, keep_b, send_b)):
        at = slice(r * samples * pad, (r + 1) * samples * pad)
        branch = dot(prod[at, :], wo[...], 1, 0)
        grad = dot(ghu[at, :], wu[...], 1, 1) + dot(ghv[at, :], wv[...], 1, 1)
        for i in range(samples):
            out[i] = branch[i * pad : i * pad + rows, :].astype(BF)
            out[samples + i] = grad[i * pad : i * pad + rows, :].astype(BF)


def finish_rows_body(meta, tok, cot, keep, got_a, got_b, g1, output, grad_tokens):
    samples, rows = tok.shape[0], tok.shape[1]
    gain = g1[...]
    p = meta[0] * rows + iota((rows, 1), 0)
    for i in range(samples):
        x = tok[i].astype(F32)
        total = keep[i].astype(F32) + got_a[i].astype(F32) + got_b[i].astype(F32)
        output[i] = (x + branch_scale(meta, i, samples, p) * total).astype(BF)
        center = x - jnp.mean(x, axis=-1, keepdims=True)
        inverse = lax.rsqrt(jnp.mean(center * center, axis=-1, keepdims=True) + EPSILON)
        standard = center * inverse
        k = samples + i
        t = (keep[k].astype(F32) + got_a[k].astype(F32) + got_b[k].astype(F32)) * gain
        first = jnp.mean(t, axis=-1, keepdims=True)
        second = jnp.mean(t * standard, axis=-1, keepdims=True)
        grad = cot[i].astype(F32) + inverse * (t - first - standard * second)
        grad_tokens[i] = grad.astype(BF)


def sources(meta):
    seq, shard = meta[0], meta[1] & 3
    out = []
    for flip in (0, 1):
        s = seq ^ flip
        core = s & 1
        out += [
            (shard, s),
            (shard ^ (1 - core), s ^ (2 * core)),
            (shard ^ core, s ^ (2 * (1 - core))),
            (shard ^ 1, s ^ 2),
        ]
    return out


def place_first_body(half, meta, *refs):
    pieces = refs[:8]
    w_in, w_out, wide, tall, sems = refs[8:]
    shard = wide.shape[1]
    copies = []
    for k, (group, seq) in enumerate(sources(meta)):
        for e in range(2):
            slot = 2 * k + e
            row = (group ^ (2 * e)) * shard
            columns = rows_at(seq * half, half, 128)
            tall[slot] = jnp.transpose(pieces[k][e, 0:shard, :].astype(F32))
            target = w_out.at[columns, rows_at(row, shard, 128)]
            copies.append(pltpu.make_async_copy(tall.at[slot], target, sems.at[2 * slot]))
            copies[-1].start()
            wide[slot] = pieces[k][e, shard:, :].astype(F32)
            target = w_in.at[rows_at(row, shard, 16), columns]
            copies.append(pltpu.make_async_copy(wide.at[slot], target, sems.at[2 * slot + 1]))
            copies[-1].start()
    for copy in copies:
        copy.wait()


def place_v(half, gate, meta, pieces, which, w_in, wide, sems):
    shard = wide.shape[1]
    copies = []
    origins = sources(meta)
    for piece, k in zip(pieces, which):
        group, seq = origins[k]
        for e in range(2):
            slot = len(copies)
            wide[slot] = piece[e, 0:shard, :].astype(F32)
            columns = rows_at(gate + seq * half, half, 128)
            target = w_in.at[rows_at((group ^ (2 * e)) * shard, shard, 16), columns]
            copies.append(pltpu.make_async_copy(wide.at[slot], target, sems.at[slot]))
            copies[-1].start()
    return copies


def place_most_body(half, gate, which, meta, *refs):
    *pieces, _, w_in, wide, sems = refs
    for copy in place_v(half, gate, meta, pieces, which, w_in, wide, sems):
        copy.wait()


def place_last_body(half, gate, which, meta, *refs):
    pieces = refs[:8]
    w_in, spatial, bias, gain_one, shift_one, gain_two, shift_two, wide, edge, norms, sems = refs[10:]
    shard = wide.shape[1]
    rows, patches = spatial.shape
    size = edge.shape[0] // 4
    core = meta[0] & 1
    copies = place_v(half, gate, meta, [pieces[k] for k in which], which, w_in, wide, sems)
    small = []
    for k, (group, seq) in enumerate(sources(meta)):
        for e in range(2):
            at = group ^ (2 * e)
            rest = pieces[k][e, shard:, :].astype(F32)
            small.append((at, rest[0:size]))
            norms[at, seq] = rest[size:]
    for e in range(2):
        at, own = small[e]
        edge[rows_at(at * size, size, 8), :] = own
        at = (meta[1] & 3) ^ 1 ^ (2 * e)
        edge[rows_at(at * size, size, 8), :] = jnp.where(core == 0, small[2 + e][1], small[4 + e][1])
    spatial[...] = edge[0:rows, 0:patches]
    first = patches // 128 * 128
    tail = edge[0:rows, first:]
    column = jnp.sum(
        jnp.where(iota(tail.shape, 1) == patches - first, tail, 0.0), axis=1, keepdims=True
    )
    diagonal = iota((rows, rows), 0) == iota((rows, rows), 1)
    bias[...] = jnp.sum(jnp.where(diagonal, column, 0.0), axis=0)
    for at, out in ((2, gain_one), (3, shift_one)):
        total = (norms[at, 0] + norms[at, 1]) + (norms[at, 2] + norms[at, 3])
        out[0:half] = total[0, :]
        out[half:] = total[1, 0 : out.shape[0] - half]
    for at, out in ((0, gain_two), (1, shift_two)):
        for j in range(4):
            out[j * half : (j + 1) * half] = norms[at, j, 0, :]
    for copy in copies:
        copy.wait()


def solution(mesh):
    n, m = mesh.shape["seq"], mesh.shape["dp"]

    def over_seq(x, flip):
        return lax.ppermute(x, "seq", [(i, i ^ flip) for i in range(n)])

    def over_dp(x, flip):
        return lax.ppermute(x, "dp", [(i, i ^ flip) for i in range(m)])

    def mixed_axes(x, core_of_x):
        pairs = []
        for d in range(m):
            for s in range(n):
                other = (d ^ 1, s) if s & 1 == core_of_x else (d, s ^ 2)
                pairs.append((d * n + s, other[0] * n + other[1]))
        return lax.ppermute(x, ("dp", "seq"), pairs)

    def add(*terms):
        total = terms[0].astype(F32)
        for t in terms[1:]:
            total = total + t.astype(F32)
        return total.astype(BF)

    def pair_up(*terms):
        return jnp.stack(terms)

    def ordered():
        last = []

        def step(body, *ins):
            if last:
                ins, _ = lax.optimization_barrier((ins, last[0]))
            out = body(*ins) if body else ins[0]
            last[:] = [jax.tree.leaves(out)[0]]
            return out

        return step

    def shards(
        tokens,
        res_class,
        skip_mask,
        w_in,
        w_out,
        spatial,
        spatial_bias,
        gain_one,
        shift_one,
        gain_two,
        shift_two,
        cotangent,
    ):
        samples, rows, width = tokens.shape
        gate = w_out.shape[0]
        half = gate // n
        pad = round_up(rows + 2, 16)
        full = n * pad
        columns = round_up(n * rows + 2, 128)
        seq, dp = lax.axis_index("seq"), lax.axis_index("dp")
        meta = jnp.concatenate([seq[None], dp[None], res_class, skip_mask]).astype(jnp.int32)
        step = ordered()

        def tick(clock):
            return call(tick_body, [shape_of(clock.shape, F32)], [clock], flops=4 * 10**9, name="tick")[0]

        big_bf, big_f32 = (shape_of((samples * full, half), d) for d in (BF, F32))
        images = shape_of((full, samples * half), BF)
        shard = width // 4
        square = shape_of((round_up(samples * 2 * n, 8), 128), F32)

        t0 = tokens
        t2 = over_seq(t0, 2)
        t1 = over_seq(t0, 1)
        high = lax.reduce_precision(spatial_bias, 8, 7)
        side = jnp.stack([high, spatial_bias - high], axis=1).astype(BF)
        packed = jnp.concatenate([spatial, side], axis=1)
        packed = jnp.pad(packed, ((0, 0), (0, width - packed.shape[1])))
        c0 = jnp.concatenate([cotangent, packed[None]])
        c2 = over_seq(c0, 2)
        wu = lax.dynamic_slice(w_in, (0, seq * half), (width, half))
        wv = lax.dynamic_slice(w_in, (0, gate + seq * half), (width, half))
        wo = lax.dynamic_slice(w_out, (seq * half, 0), (half, width))
        g1, s1 = gain_one[None], shift_one[None]
        g2, s2 = gain_two.reshape(-1, 128), shift_two.reshape(-1, 128)
        meta, wu, wv, wo, c0, t1 = lax.optimization_barrier((meta, wu, wv, wo, c0, t1))
        c1 = over_seq(c0, 1)

        n0, gu0, dgu0, v0, dgv0, st = step(
            lambda *a: project(pad, 0, a[:2], *a[2:]), t0, t1, g1, s1, wu, wv
        )
        t2 = step(None, t2)
        t3 = over_seq(t2, 1)
        n1, gu1, dgu1, v1, dgv1, st = step(
            lambda *a: project(pad, 2, a[:1], *a[1:]), t2, g1, s1, wu, wv, st
        )
        n2, gu2, dgu2, v2, dgv2, st = step(
            lambda *a: project(pad, 3, a[:1], *a[1:]), t3, g1, s1, wu, wv, st
        )
        normed = [n0, n1, n2]
        stats = [st] + [over_seq(st, k) for k in range(1, n)]

        def front(first_block, count, *ins):
            def shape(columns, dtype):
                return shape_of((count * samples * pad, columns), dtype)

            outs = [shape(width, BF), shape(half, F32), shape(half, BF)]
            outs.append(shape_of((count * pad, full), BF))
            return call(
                functools.partial(front_body, n, pad, first_block, count),
                outs + ([] if first_block else [shape_of((columns, full), BF)]),
                ins,
                specs=[SM] + [VM] * (len(ins) - 1),
                name="front",
            )

        gb0, gp0, gs0, sp0, pm = step(functools.partial(front, 0, 2), meta, c0, c1, wo, gu0)

        def flip(*ins):
            return call(
                flip_body,
                [shape_of((width, samples * full), BF)],
                ins,
                [pltpu.VMEM((samples * full, width), BF)],
                name="flip",
            )

        (flipped,) = step(flip, *normed)
        stats = step(None, stats)
        c2 = step(None, c2)
        c3 = over_seq(c2, 1)
        gb1, gp1, gs1, sp1 = step(functools.partial(front, 2, 1), meta, c2, wo, gu1, pm)

        def prepare(*ins):
            square_bf = shape_of((full, full), BF)
            last = [shape_of((samples * pad, c), d) for c, d in ((width, BF), (half, F32))]
            return call(
                functools.partial(prepare_body, n, pad),
                [*last, images, big_f32, square_bf],
                ins,
                [pltpu.VMEM((full, full), BF)],
                specs=[SM] + [VM] * (len(ins) - 1),
                name="prepare",
            )

        gb2, gp2, gs, gmix, sp = step(prepare, meta, c3, wo, gu2, pm, gs0, gs1, sp0, sp1)

        def spatial_unit(*ins):
            message = shape_of((pad + 32, columns), BF)
            return call(
                functools.partial(spatial_body, n, pad),
                [big_bf, big_bf, shape_of((128, 128), F32), square, shape_of((pad, columns), BF)]
                + [message] * (n - 1),
                ins,
                [
                    pltpu.VMEM((full, samples * half), BF),
                    pltpu.VMEM((full, samples * half), F32),
                    pltpu.VMEM((128, 128), F32),
                    pltpu.VMEM((2 * samples * n, pad, 128), F32),
                ],
                specs=[SM] + [VM] * (len(ins) - 1),
                name="spatial",
            )

        clock = jnp.zeros((8, 128), F32)
        prod, ghu, cols, st2, edge, *messages = step(
            spatial_unit, meta, v0, v1, v2, gu0, gu1, gu2, dgu0, dgu1, dgu2, sp, gp0, gp1, gp2, gs, pm,
            gmix, g2, s2, *stats,
        )
        messages = [over_seq(x, k) for k, x in enumerate(messages, 1)]

        def weights(*ins):
            return call(
                weights_body,
                [shape_of((2 * shard, half), BF)] * 4 + [shape_of((width, half), F32)],
                ins,
                [pltpu.VMEM((width, half), F32)],
                specs=[SM] + [VM] * (len(ins) - 1),
                name="weights",
            )

        def norm_shares(*ins):
            return call(sums_body, [shape_of((8, width), F32)], ins, name="norm_shares")

        def back(*ins):
            return call(
                functools.partial(back_body, n, pad),
                [big_bf] + [shape_of((shard + EXTRA, half), BF)] * 4,
                ins,
                [
                    pltpu.VMEM((128, 128), F32),
                    pltpu.VMEM((128, 128), F32),
                    pltpu.VMEM((width, half), F32),
                    pltpu.VMEM((2, CHUNK, half), F32),
                    pltpu.VMEM((4, EXTRA, half), F32),
                ],
                specs=[SM] + [VM] * (len(ins) - 1),
                name="back",
            )

        def rows_out(*ins):
            shape = shape_of((2 * samples, rows, width), BF)
            return call(functools.partial(rows_body, n, pad), [shape] * 4, ins, name="rows_out")

        def finish_rows(*ins):
            shape = shape_of(tokens.shape, BF)
            return call(
                finish_rows_body, [shape, shape], ins, specs=[SM] + [VM] * 6, name="finish_rows"
            )

        def place_first(*ins):
            return call(
                functools.partial(place_first_body, half),
                [shape_of((width, 2 * gate), F32), shape_of((gate, width), F32)],
                ins,
                [
                    pltpu.VMEM((16, shard, half), F32),
                    pltpu.VMEM((16, half, shard), F32),
                    pltpu.SemaphoreType.DMA((32,)),
                ],
                specs=[SM] + [VM] * 8,
                out_specs=[HB] * 2,
                name="place_first",
            )

        def place_most(which, *ins):
            return call(
                functools.partial(place_most_body, half, gate, which),
                [shape_of((width, 2 * gate), F32)],
                ins,
                [
                    pltpu.VMEM((2 * len(which), shard, half), F32),
                    pltpu.SemaphoreType.DMA((2 * len(which),)),
                ],
                specs=[SM] + [VM] * len(which) + [HB],
                out_specs=[HB],
                input_output_aliases={1 + len(which): 0},
                name="place_most",
            )

        def place_last(which, *ins):
            one, two = shape_of((width,), F32), shape_of((gate,), F32)
            small = [shape_of((rows, n * rows), F32), shape_of((rows,), F32), one, one, two, two]
            return call(
                functools.partial(place_last_body, half, gate, which),
                [shape_of((width, 2 * gate), F32)] + small,
                ins,
                [
                    pltpu.VMEM((2 * len(which), shard, half), F32),
                    pltpu.VMEM((pad, columns), F32),
                    pltpu.VMEM((4, n, EXTRA - pad // 4, half), F32),
                    pltpu.SemaphoreType.DMA((2 * len(which),)),
                ],
                specs=[SM] + [VM] * 8 + [HB, VM],
                out_specs=[HB] + [VM] * 6,
                input_output_aliases={9: 0},
                name="place_last",
            )

        def twin(x):
            return over_seq(x, 1)

        x = dict(messages=messages, clock=clock)

        def ev_tick():
            x["clock"] = step(tick, x["clock"])

        def reduce_start(key, shards):
            x[key] = shards[0]
            for rho in range(1, 4):
                x[f"{key}{rho}"] = over_dp(shards[rho], rho)

        def ev_weights():
            *x["a_shards"], x["uw"] = step(weights, meta, prod, gb0, gb1, gb2, ghu, flipped)

        def ev_a_send():
            reduce_start("a", step(None, x["a_shards"]))

        def ev_sums():
            (x["sums"],) = step(norm_shares, wu, x["uw"], ghu)

        def ev_stats():
            x["messages"] = step(None, x["messages"])

        def ev_back():
            x["ghv"], *x["v_shards"] = step(
                back, meta, gmix, v0, v1, v2, dgv0, dgv1, dgv2, cols, st2, edge, *x["messages"], g1, s1,
                g2, flipped, wv, x["sums"],
            )

        def ev_v_send():
            reduce_start("v", step(None, x["v_shards"]))

        def ev_rows():
            x["r_a"], send_a, x["r_b"], send_b = step(rows_out, prod, wo, ghu, x["ghv"], wu, wv)
            x["r_got"], x["r_got_b"] = twin(send_a), twin(send_b)

        def ev_rows_core():
            x["r_got"], x["r_got_b"] = step(None, (x["r_got"], x["r_got_b"]))
            x["r_last"] = over_seq(step(add, x["r_b"], x["r_got_b"]), 2)

        def ev_finish():
            x["output"], x["grad_tokens"] = step(
                finish_rows, meta, t0, c0, x["r_a"], x["r_got"], x["r_last"], g1
            )

        def ev_rs(k):
            x[k] = step(add, x[k], x[k + "1"], x[k + "2"], x[k + "3"])
            x[k + "z"] = over_dp(x[k], 4) if m > 4 else None

        def ev_z2(k):
            flip = 8
            while flip <= m:
                x[k] = step(add, x[k], x[k + "z"])
                if flip < m:
                    x[k + "z"] = over_dp(x[k], flip)
                flip *= 2
            x[k + "z"] = over_dp(x[k], 2)

        def ev_pair(k):
            x[k + "p0"] = step(pair_up, x[k], x[k + "z"])
            x[k + "p1"], x[k + "p2"] = mixed_axes(x[k + "p0"], 0), mixed_axes(x[k + "p0"], 1)

        def ev_mark(k):
            x[k + "p1"], x[k + "p2"] = step(None, (x[k + "p1"], x[k + "p2"]))
            x[k + "p3"] = mixed_axes(x[k + "p1"], 1)

        def ev_third(k):
            x[k + "p3"] = step(None, x[k + "p3"])

        def ev_twin(k, j):
            x[f"{k}q{j}"] = twin(x[f"{k}p{j}"])

        def ev_got(k, j):
            x[f"{k}q{j}"] = step(None, x[f"{k}q{j}"])

        def ev_place_first():
            ins = [x[f"ap{j}"] for j in range(4)] + [x[f"aq{j}"] for j in range(4)]
            x["w_in"], x["w_out"] = step(place_first, meta, *ins)

        def ev_place_most():
            which = (0, 1, 2, 4, 5, 6)
            ins = [x[f"v{'pq'[k // 4]}{k % 4}"] for k in which]
            (x["w_in"],) = step(functools.partial(place_most, which), meta, *ins, x["w_in"])

        def ev_place_last():
            ins = [x[f"vp{j}"] for j in range(4)] + [x[f"vq{j}"] for j in range(4)]
            x["w_in"], x["spatial"], *x["small"] = step(
                functools.partial(place_last, (3, 7)), meta, *ins, x["w_in"], x["clock"]
            )

        events = dict(
            weights=ev_weights, sums=ev_sums, stats=ev_stats, back=ev_back,
            rows=ev_rows, rows_core=ev_rows_core, finish=ev_finish,
            place_first=ev_place_first, place_last=ev_place_last, place_most=ev_place_most,
            a_send=ev_a_send, v_send=ev_v_send, tick=ev_tick,
        )
        for k in ("a", "v"):
            for name, f in (("rs", ev_rs), ("z2", ev_z2), ("pair", ev_pair), ("mark", ev_mark), ("third", ev_third)):
                events[f"{k}_{name}"] = functools.partial(f, k)
            for j in range(4):
                events[f"{k}_twin{j}"] = functools.partial(ev_twin, k, j)
                events[f"{k}_got{j}"] = functools.partial(ev_got, k, j)
        for name in ORDER:
            events[name]()
        output, grad_tokens, grad_w_in, grad_w_out = (
            x[k] for k in ("output", "grad_tokens", "w_in", "w_out")
        )
        grad_spatial, sums = x["spatial"], x["small"]
        return (output, grad_tokens, grad_w_in, grad_w_out, grad_spatial, *sums)

    placed = (
        P("dp", "seq", None),
        P("dp"),
        P("dp"),
        P(),
        P(),
        P("seq", None),
        P("seq"),
        P(),
        P(),
        P(),
        P(),
        P("dp", "seq", None),
    )
    return jax.shard_map(
        shards,
        mesh=mesh,
        in_specs=placed,
        out_specs=(
            P("dp", "seq", None),
            P("dp", "seq", None),
            P(),
            P(),
            P("seq", None),
            P("seq"),
            P(),
            P(),
            P(),
            P(),
        ),
        check_vma=False,
    )
```

time: 110 us -> 100 us (0.909)
  waiting for transfers between devices: 47.7 us -> 33.9 us
  starting transfers between devices: 29 us -> 31.7 us
  Pallas kernels: 26.5 us -> 28.8 us
  other arithmetic: 4.48 us -> 3.18 us
    ppermute x6, waiting for transfers between devices: 15.6 us -> 10 us  [mixed_axes(): return lax.ppermute(x, ('dp', 'seq'), pairs)]
    ppermute x8 -> x10, waiting for transfers between devices: 22.3 us -> 17.6 us  [over_dp(): return lax.ppermute(x, 'dp', [(i, i ^ flip) for i in range(m)])]
    ppermute x25 -> x23, waiting for transfers between devices: 9.75 us -> 6.21 us  [over_seq(): return lax.ppermute(x, 'seq', [(i, i ^ flip) for i in range(n)])]
    pallas_call x11 -> x17, Pallas kernels: 26.5 us -> 28.8 us  [call(): pl.pallas_call(body, out_shape=outs, in_specs=specs if specs is not None...]
    ppermute x8 -> x10, starting transfers between devices: 11.1 us -> 13 us  [over_dp(): return lax.ppermute(x, 'dp', [(i, i ^ flip) for i in range(m)])]
    ppermute x6, starting transfers between devices: 5.71 us -> 7.02 us  [mixed_axes(): return lax.ppermute(x, ('dp', 'seq'), pairs)]
    pallas_call x2 -> x0, other arithmetic: 1.24 us -> none  [call(): pl.pallas_call(body, out_shape=outs, in_specs=specs if specs is not None...]
    ppermute x25 -> x23, starting transfers between devices: 12.2 us -> 11.7 us  [over_seq(): return lax.ppermute(x, 'seq', [(i, i ^ flip) for i in range(n)])]
  transfers between devices with their start and end apart: 39 -> 39, of which waited for: 19 -> 17; matrix products, arithmetic and copies ran while one was open for 4% -> 5% of each run, Pallas kernels for 16% -> 22%
where the time goes in v3:
time: 100 us
  waiting for transfers between devices  33.9 us (34%)
  starting transfers between devices  31.7 us (32%)
  Pallas kernels  28.8 us (29%)
  other arithmetic  3.18 us (3%)
  local copies, waits for them, and re-layouts  1.54 us (2%)
  between operations  1.11 us (1%)
    pallas_call x17, Pallas kernels, call(): pl.pallas_call(body, out_shape=outs, in_specs=specs if specs is not None...  28.8 us
    ppermute x10, waiting for transfers between devices, over_dp(): return lax.ppermute(x, 'dp', [(i, i ^ flip) for i in range(m)])  17.6 us
    ppermute x10, starting transfers between devices, over_dp(): return lax.ppermute(x, 'dp', [(i, i ^ flip) for i in range(m)])  13 us
    ppermute x23, starting transfers between devices, over_seq(): return lax.ppermute(x, 'seq', [(i, i ^ flip) for i in range(n)])  11.7 us
    ppermute x6, waiting for transfers between devices, mixed_axes(): return lax.ppermute(x, ('dp', 'seq'), pairs)  10 us
    ppermute x6, starting transfers between devices, mixed_axes(): return lax.ppermute(x, ('dp', 'seq'), pairs)  7.02 us
    ppermute x23, waiting for transfers between devices, over_seq(): return lax.ppermute(x, 'seq', [(i, i ^ flip) for i in range(n)])  6.21 us
  transfers between devices with their start and end apart: 39, of which 17 were waited for; matrix products, arithmetic and copies ran while one was open for 5% of the time, Pallas kernels for 22%

profile of v3, /device:TPU:0, one launch (start us, length us, event | category | flops | bytes accessed | tf_op | source)
XLA Modules:
  0.0 100.2 jit_solution(7491072420072487086)
XLA Ops:
  1.2 2.6 %collective-permute-start.1 = (bf16[3,81,512]{2,1,0:T(8,128)(2,1)}, bf16[3,81,512]{2,1,0:T(8,128)(2,1)S(1)}, u32[]{:S(2)}, u32[]{:S(2)}) collective-permute-start(bf16[3,81,512]{2,1,0:T(8,128)(2,1)} %tok), channel_id=1, source_target_pairs={{0,2},{1,3},{2,0},{3,1},{4,6},{5,7},{6,4},{7,5},{8,10},{9,11},{10,... | collective-permute-start | bytes 746504 | tf_op jit(solution)/shard_map/ppermute | solution.py:640
  8.6 1.8 %project.3 = (bf16[576,512]{1,0:T(8,128)(2,1)S(1)}, bf16[576,384]{1,0:T(8,128)(2,1)S(1)}, bf16[576,384]{1,0:T(8,128)(2,1)S(1)}, f32[576,384]{1,0:T(8,128)S(1)}, ...) custom-call(bf16[3,81,512]{2,1,0:T(8,128)(2,1)S(1)} %copy-done.1, ...), custom_call_target="tpu_custom_call" | custom-call | flops 1 | bytes 1 | tf_op jit(solution)/shard_map/project/pallas_call | solution.py:49
  13.8 2.0 %collective-permute-start.6 = (f32[24,128]{1,0:T(8,128)S(1)}, f32[24,128]{1,0:T(8,128)S(1)}, u32[]{:S(2)}, u32[]{:S(2)}) collective-permute-start(f32[24,128]{1,0:T(8,128)S(1)} %get-tuple-element.347.t0), channel_id=1, source_target_pairs={{0,3},{1,2},{2,1},{3,0},{4,7},{5,6},{6,5},{7,4},{8,11},{9,10},{10,... | collective-permute-start | bytes 36872 | tf_op jit(solution)/shard_map/ppermute | solution.py:640
  21.2 1.5 %prepare.1 = (bf16[288,512]{1,0:T(8,128)(2,1)S(1)}, f32[288,384]{1,0:T(8,128)S(1)}, bf16[384,1152]{1,0:T(8,128)(2,1)S(1)}, f32[1152,384]{1,0:T(8,128)S(1)}, bf16[384,384]{1,0:T(8,128)(2,1)S(1)}) custom-call(s32[8]{0:T(128)S(1)} %pad_add_fusion.meta, bf16[4,81,512]{2,1,0:T(8,128)(2,1)S(1)} %collective-permute-done.8.c3, ...), custom_call_target="tpu_custom_call" | custom-call | flops 1 | bytes 1 | tf_op jit(solution)/shard_map/prepare/pallas_call | solution.py:49
  22.7 3.4 %spatial.1 = (bf16[1152,384]{1,0:T(8,128)(2,1)S(1)}, bf16[1152,384]{1,0:T(8,128)(2,1)S(1)}, f32[128,128]{1,0:T(8,128)S(1)}, f32[24,128]{1,0:T(8,128)S(1)}, bf16[...) custom-call(s32[8]{0:T(128)S(1)} %pad_add_fusion.meta, ...), custom_call_target="tpu_custom_call" | custom-call | flops 1 | bytes 1 | tf_op jit(solution)/shard_map/spatial/pallas_call | solution.py:49
  26.3 1.6 %collective-permute-start.10 = (bf16[128,384]{1,0:T(8,128)(2,1)S(1)}, bf16[128,384]{1,0:T(8,128)(2,1)S(1)}, u32[]{:S(2)}, u32[]{:S(2)}) collective-permute-start(bf16[128,384]{1,0:T(8,128)(2,1)S(1)} %get-tuple-element.360), channel_id=1, source_target_pairs={{0,2},{1,3},{2,0},{3,1},{4,6},{5,7},{6,4},{7,5},{8,10},{9,11},{10,... | collective-permute-start | bytes 294920 | tf_op jit(solution)/shard_map/ppermute | solution.py:640
  28.0 2.4 %weights.1 = (bf16[256,384]{1,0:T(8,128)(2,1)S(1)}, bf16[256,384]{1,0:T(8,128)(2,1)S(1)}, bf16[256,384]{1,0:T(8,128)(2,1)S(1)}, bf16[256,384]{1,0:T(8,128)(2,1)S(1)}, f32[512,384]{1,0:T(8,128)S(1)}) custom-call(s32[8]{0:T(128)S(1)} %pad_add_fusion.meta, bf16[1152,384]{1,0:T(8,128)(2,1)S(1)} %get-tuple-element.402.prod, ...), custom_call_target="tpu_custom_call" | custom-call | flops 1 | bytes 1 | tf_op jit(solution)/shard_map/weights/pallas_call | solution.py:49
  30.5 1.4 %collective-permute-done.10.m2 = bf16[128,384]{1,0:T(8,128)(2,1)S(1)} collective-permute-done((bf16[128,384]{1,0:T(8,128)(2,1)S(1)}, bf16[128,384]{1,0:T(8,128)(2,1)S(1)}, u32[]{:S(2)}, u32[]{:S(2)}) %collective-permute-start.10) | collective-permute-done | bytes 98336 | tf_op jit(solution)/shard_map/ppermute | solution.py:640
  31.8 1.2 %collective-permute-done.11.m3 = bf16[128,384]{1,0:T(8,128)(2,1)S(1)} collective-permute-done((bf16[128,384]{1,0:T(8,128)(2,1)S(1)}, bf16[128,384]{1,0:T(8,128)(2,1)S(1)}, u32[]{:S(2)}, u32[]{:S(2)}) %collective-permute-start.11) | collective-permute-done | bytes 98336 | tf_op jit(solution)/shard_map/ppermute | solution.py:640
  33.1 1.5 %collective-permute-start.14 = (bf16[256,384]{1,0:T(8,128)(2,1)S(1)}, bf16[256,384]{1,0:T(8,128)(2,1)S(1)}, u32[]{:S(2)}, u32[]{:S(2)}) collective-permute-start(bf16[256,384]{1,0:T(8,128)(2,1)S(1)} %get-tuple-element.415), channel_id=1, source_target_pairs={{0,4},{4,0},{8,12},{12,8},{16,20},{20,16},{24,28},{28,24},{1,5},{5... | collective-permute-start | bytes 589832 | tf_op jit(solution)/shard_map/ppermute | solution.py:643
  34.5 1.6 %collective-permute-start.15 = (bf16[256,384]{1,0:T(8,128)(2,1)S(1)}, bf16[256,384]{1,0:T(8,128)(2,1)S(1)}, u32[]{:S(2)}, u32[]{:S(2)}) collective-permute-start(bf16[256,384]{1,0:T(8,128)(2,1)S(1)} %get-tuple-element.416), channel_id=1, source_target_pairs={{0,8},{4,12},{8,0},{12,4},{16,24},{20,28},{24,16},{28,20},{1,9},{5... | collective-permute-start | bytes 589832 | tf_op jit(solution)/shard_map/ppermute | solution.py:643
  37.0 2.9 %back.1 = (bf16[1152,384]{1,0:T(8,128)(2,1)S(1)}, bf16[160,384]{1,0:T(8,128)(2,1)S(1)}, bf16[160,384]{1,0:T(8,128)(2,1)S(1)}, bf16[160,384]{1,0:T(8,128)(2,1)S(1)}, bf16[160,384]{1,0:T(8,128)(2,1)S(1)}) custom-call(s32[8]{0:T(128)S(1)} %pad_add_fusion.meta, f32[1152,384]{1,0:T(8,128)S(1)} %get-tuple-element.382.gmix, f32[576,384]{1,0:T(8,128)S(1)} %get-tuple-element.383.v0, ...), custom_call_target="tpu_custom_call" | custom-call | flops 1 | bytes 1 | tf_op jit(solution)/shard_map/back/pallas_call | solution.py:49
  39.8 2.0 %rows_out.1 = (bf16[6,81,512]{2,1,0:T(8,128)(2,1)S(1)}, bf16[6,81,512]{2,1,0:T(8,128)(2,1)S(1)}, bf16[6,81,512]{2,1,0:T(8,128)(2,1)S(1)}, bf16[6,81,512]{2,1,0:T(8,128)(2,1)S(1)}) custom-call(bf16[1152,384]{1,0:T(8,128)(2,1)S(1)} %get-tuple-element.402.prod, bf16[384,512]{1,0:T(8,128)(2,1)S(1)} %constant_dynamic-slice_fusion.refs_2_.refs_1_.wo, ...), custom_call_target="tpu_custom_call" | custom-call | flops 1 | bytes 1 | tf_op jit(solution)/shard_map/rows_out/pallas_call | solution.py:49
  42.4 3.1 %collective-permute-done.16 = bf16[256,384]{1,0:T(8,128)(2,1)S(1)} collective-permute-done((bf16[256,384]{1,0:T(8,128)(2,1)S(1)}, bf16[256,384]{1,0:T(8,128)(2,1)S(1)}, u32[]{:S(2)}, u32[]{:S(2)}) %collective-permute-start.16) | collective-permute-done | bytes 196640 | tf_op jit(solution)/shard_map/ppermute | solution.py:643
  45.6 2.8 %collective-permute-start.18 = (bf16[256,384]{1,0:T(8,128)(2,1)S(1)}, bf16[256,384]{1,0:T(8,128)(2,1)S(1)}, u32[]{:S(2)}, u32[]{:S(2)}) collective-permute-start(bf16[256,384]{1,0:T(8,128)(2,1)S(1)} %add_convert_fusion.2), channel_id=1, source_target_pairs={{0,16},{4,20},{8,24},{12,28},{16,0},{20,4},{24,8},{28,12},{1,17},{... | collective-permute-start | bytes 589832 | tf_op jit(solution)/shard_map/ppermute | solution.py:643
  48.4 1.5 %collective-permute-start.19 = (bf16[160,384]{1,0:T(8,128)(2,1)S(1)}, bf16[160,384]{1,0:T(8,128)(2,1)S(1)}, u32[]{:S(2)}, u32[]{:S(2)}) collective-permute-start(bf16[160,384]{1,0:T(8,128)(2,1)S(1)} %get-tuple-element.429), channel_id=1, source_target_pairs={{0,4},{4,0},{8,12},{12,8},{16,20},{20,16},{24,28},{28,24},{1,5},{5... | collective-permute-start | bytes 368648 | tf_op jit(solution)/shard_map/ppermute | solution.py:643
  49.9 1.6 %collective-permute-start.20 = (bf16[160,384]{1,0:T(8,128)(2,1)S(1)}, bf16[160,384]{1,0:T(8,128)(2,1)S(1)}, u32[]{:S(2)}, u32[]{:S(2)}) collective-permute-start(bf16[160,384]{1,0:T(8,128)(2,1)S(1)} %get-tuple-element.430), channel_id=1, source_target_pairs={{0,8},{4,12},{8,0},{12,4},{16,24},{20,28},{24,16},{28,20},{1,9},{5... | collective-permute-start | bytes 368648 | tf_op jit(solution)/shard_map/ppermute | solution.py:643
  52.0 1.6 %collective-permute-start.17 = (bf16[6,81,512]{2,1,0:T(8,128)(2,1)S(1)}, bf16[6,81,512]{2,1,0:T(8,128)(2,1)S(1)}, u32[]{:S(2)}, u32[]{:S(2)}) collective-permute-start(bf16[6,81,512]{2,1,0:T(8,128)(2,1)S(1)} %add_convert_fusion), channel_id=1, source_target_pairs={{0,2},{1,3},{2,0},{3,1},{4,6},{5,7},{6,4},{7,5},{8,10},{9,11},{10,... | collective-permute-start | bytes 1493000 | tf_op jit(solution)/shard_map/ppermute | solution.py:640
  53.6 4.5 %collective-permute-done.20 = bf16[160,384]{1,0:T(8,128)(2,1)S(1)} collective-permute-done((bf16[160,384]{1,0:T(8,128)(2,1)S(1)}, bf16[160,384]{1,0:T(8,128)(2,1)S(1)}, u32[]{:S(2)}, u32[]{:S(2)}) %collective-permute-start.20) | collective-permute-done | bytes 122912 | tf_op jit(solution)/shard_map/ppermute | solution.py:643
  58.2 2.1 %collective-permute-done.21 = bf16[160,384]{1,0:T(8,128)(2,1)S(1)} collective-permute-done((bf16[160,384]{1,0:T(8,128)(2,1)S(1)}, bf16[160,384]{1,0:T(8,128)(2,1)S(1)}, u32[]{:S(2)}, u32[]{:S(2)}) %collective-permute-start.21) | collective-permute-done | bytes 122912 | tf_op jit(solution)/shard_map/ppermute | solution.py:643
  60.8 2.1 %collective-permute-start.22 = (bf16[256,384]{1,0:T(8,128)(2,1)S(1)}, bf16[256,384]{1,0:T(8,128)(2,1)S(1)}, u32[]{:S(2)}, u32[]{:S(2)}) collective-permute-start(bf16[256,384]{1,0:T(8,128)(2,1)S(1)} %add_convert_fusion.1), channel_id=1, source_target_pairs={{0,8},{4,12},{8,0},{12,4},{16,24},{20,28},{24,16},{28,20},{1,9},{5... | collective-permute-start | bytes 589832 | tf_op jit(solution)/shard_map/ppermute | solution.py:643
  62.8 4.6 %collective-permute-done.23 = bf16[160,384]{1,0:T(8,128)(2,1)S(1)} collective-permute-done((bf16[160,384]{1,0:T(8,128)(2,1)S(1)}, bf16[160,384]{1,0:T(8,128)(2,1)S(1)}, u32[]{:S(2)}, u32[]{:S(2)}) %collective-permute-start.23) | collective-permute-done | bytes 122912 | tf_op jit(solution)/shard_map/ppermute | solution.py:643
  68.5 1.6 %collective-permute-start.28 = (bf16[2,256,384]{2,1,0:T(8,128)(2,1)S(1)}, bf16[2,256,384]{2,1,0:T(8,128)(2,1)S(1)}, u32[]{:S(2)}, u32[]{:S(2)}) collective-permute-start(bf16[2,256,384]{2,1,0:T(8,128)(2,1)S(1)} %pad_maximum_fusion.refs_0_), channel_id=1, source_target_pairs={{0,2},{1,5},{2,0},{3,7},{4,6},{5,1},{6,4},{7,3},{8,10},{9,13},{10,... | collective-permute-start | bytes 1179656 | tf_op jit(solution)/shard_map/ppermute | solution.py:651
  71.6 1.8 %finish_rows.1 = (bf16[3,81,512]{2,1,0:T(8,128)(2,1)}, bf16[3,81,512]{2,1,0:T(8,128)(2,1)}) custom-call(s32[8]{0:T(128)S(1)} %pad_add_fusion.meta, bf16[3,81,512]{2,1,0:T(8,128)(2,1)S(1)} %copy-done.1, bf16[4,81,512]{2,1,0:T(8,128)(2,1)S(1)} %pad_maximum_fusion.1.refs_0_.cot, bf16[6,81,512]{2,1,0:T(8,128)(2,1)S(1)} %get-tuple-element.445.keep, ...), custom_call_target="tpu_custom_call" | custom-call | flops 1 | bytes 1 | tf_op jit(solution)/shard_map/finish_rows/pallas_call | solution.py:49
  73.4 2.2 %collective-permute-done.24 = bf16[160,384]{1,0:T(8,128)(2,1)S(1)} collective-permute-done((bf16[160,384]{1,0:T(8,128)(2,1)S(1)}, bf16[160,384]{1,0:T(8,128)(2,1)S(1)}, u32[]{:S(2)}, u32[]{:S(2)}) %collective-permute-start.24) | collective-permute-done | bytes 122912 | tf_op jit(solution)/shard_map/ppermute | solution.py:643
  75.7 1.8 %collective-permute-done.28.refs_2_ = bf16[2,256,384]{2,1,0:T(8,128)(2,1)S(1)} collective-permute-done((bf16[2,256,384]{2,1,0:T(8,128)(2,1)S(1)}, bf16[2,256,384]{2,1,0:T(8,128)(2,1)S(1)}, u32[]{:S(2)}, u32[]{:S(2)}) %collective-permute-start.28) | collective-permute-done | bytes 393248 | tf_op jit(solution)/shard_map/ppermute | solution.py:651
  79.9 1.3 %collective-permute-start.25 = (bf16[2,160,384]{2,1,0:T(8,128)(2,1)S(1)}, bf16[2,160,384]{2,1,0:T(8,128)(2,1)S(1)}, u32[]{:S(2)}, u32[]{:S(2)}) collective-permute-start(bf16[2,160,384]{2,1,0:T(8,128)(2,1)S(1)} %pad_maximum_fusion.2.refs_0_), channel_id=1, source_target_pairs={{0,4},{1,3},{2,6},{3,1},{4,0},{5,7},{6,2},{7,5},{8,12},{9,11},{10,... | collective-permute-start | bytes 737288 | tf_op jit(solution)/shard_map/ppermute | solution.py:651
  81.7 7.3 %collective-permute-done.26.refs_2_ = bf16[2,160,384]{2,1,0:T(8,128)(2,1)S(1)} collective-permute-done((bf16[2,160,384]{2,1,0:T(8,128)(2,1)S(1)}, bf16[2,160,384]{2,1,0:T(8,128)(2,1)S(1)}, u32[]{:S(2)}, u32[]{:S(2)}) %collective-permute-start.26) | collective-permute-done | bytes 245792 | tf_op jit(solution)/shard_map/ppermute | solution.py:651
  89.5 1.5 %collective-permute-start.29 = (bf16[2,160,384]{2,1,0:T(8,128)(2,1)S(1)}, bf16[2,160,384]{2,1,0:T(8,128)(2,1)S(1)}, u32[]{:S(2)}, u32[]{:S(2)}) collective-permute-start(bf16[2,160,384]{2,1,0:T(8,128)(2,1)S(1)} %collective-permute-done.25.refs_1_), channel_id=1, source_target_pairs={{0,2},{1,5},{2,0},{3,7},{4,6},{5,1},{6,4},{7,3},{8,10},{9,13},{10,... | collective-permute-start | bytes 737288 | tf_op jit(solution)/shard_map/ppermute | solution.py:651
  91.6 3.6 %place_first.1 = (f32[512,3072]{1,0:T(8,128)}, f32[1536,512]{1,0:T(8,128)}) custom-call(s32[8]{0:T(128)S(1)} %pad_add_fusion.meta, bf16[2,256,384]{2,1,0:T(8,128)(2,1)S(1)} %pad_maximum_fusion.refs_0_, bf16[2,256,384]{2,1,0:T(8,128)(2,1)S(1)} %collective-permute-done.27.refs_1_, bf16[2,256,384]{2,1,0:T(8,128)(2,1)S(1)} %collective-permute-done.28.refs_2_, ...), custom_call_target="tpu_custom_call" | custom-call | flops 1 | bytes 1 | tf_op jit(solution)/shard_map/place_first/pallas_call | solution.py:49
  95.7 2.0 %place_most.1.refs_8_ = f32[512,3072]{1,0:T(8,128)} custom-call(s32[8]{0:T(128)S(1)} %pad_add_fusion.meta, bf16[2,160,384]{2,1,0:T(8,128)(2,1)S(1)} %pad_maximum_fusion.2.refs_0_, bf16[2,160,384]{2,1,0:T(8,128)(2,1)S(1)} %collective-permute-done.25.refs_1_, bf16[2,160,384]{2,1,0:T(8,128)(2,1)S(1)} %collective-permute-done.26.refs_2_, ...), custom_call_target="tpu_custom_call", output_to_operand_aliasing={{}: (7, {})} | custom-call | flops 1 | bytes 1 | tf_op jit(solution)/shard_map/place_most/pallas_call | solution.py:49
  97.8 2.2 %place_last.1 = (f32[512,3072]{1,0:T(8,128)}, f32[81,324]{1,0:T(8,128)}, f32[81]{0:T(128)}, f32[512]{0:T(512)}, f32[512]{0:T(512)}, /*index=5*/f32[1536]{0:T(1024)}, f32[1536]{0:T(1024)}) custom-call(s32[8]{0:T(128)S(1)} %pad_add_fusion.meta, bf16[2,160,384]{2,1,0:T(8,128)(2,1)S(1)} %pad_maximum_fusion.2.refs_0_, ...), custom_call_target="tpu_custom_call", output_to_operand_aliasing={{0}: (9, {})} | custom-call | flops 1 | bytes 1 | tf_op jit(solution)/shard_map/place_last/pallas_call | solution.py:49
  (95 shorter events, 24.0 us)
Async XLA Ops:
  0.7 7.4 %collective-permute-start = (bf16[3,81,512]{2,1,0:T(8,128)(2,1)}, bf16[3,81,512]{2,1,0:T(8,128)(2,1)S(1)}, u32[]{:S(2)}, u32[]{:S(2)}) collective-permute-start(bf16[3,81,512]{2,1,0:T(8,128)(2,1)} %tok), channel_id=1, source_target_pairs={{0,1},{1,0},{2,3},{3,2},{4,5},{5,4},{6,7},{7,6},{8,9},{9,8},{10,11... | collective-permute-start | bytes 746504 | tf_op jit(solution)/shard_map/ppermute | solution.py:640
  1.2 9.9 %collective-permute-start.1 = (bf16[3,81,512]{2,1,0:T(8,128)(2,1)}, bf16[3,81,512]{2,1,0:T(8,128)(2,1)S(1)}, u32[]{:S(2)}, u32[]{:S(2)}) collective-permute-start(bf16[3,81,512]{2,1,0:T(8,128)(2,1)} %tok), channel_id=1, source_target_pairs={{0,2},{1,3},{2,0},{3,1},{4,6},{5,7},{6,4},{7,5},{8,10},{9,11},{10,... | collective-permute-start | bytes 746504 | tf_op jit(solution)/shard_map/ppermute | solution.py:640
  8.1 8.1 %collective-permute-start.7 = (bf16[4,81,512]{2,1,0:T(8,128)(2,1)S(1)}, bf16[4,81,512]{2,1,0:T(8,128)(2,1)S(1)}, u32[]{:S(2)}, u32[]{:S(2)}) collective-permute-start(bf16[4,81,512]{2,1,0:T(8,128)(2,1)S(1)} %pad_maximum_fusion.1.refs_0_.cot), channel_id=1, source_target_pairs={{0,1},{1,0},{2,3},{3,2},{4,5},{5,4},{6,7},{7,6},{8,9},{9,8},{10,11... | collective-permute-start | bytes 995336 | tf_op jit(solution)/shard_map/ppermute | solution.py:640
  8.3 11.2 %collective-permute-start.3 = (bf16[4,81,512]{2,1,0:T(8,128)(2,1)S(1)}, bf16[4,81,512]{2,1,0:T(8,128)(2,1)S(1)}, u32[]{:S(2)}, u32[]{:S(2)}) collective-permute-start(bf16[4,81,512]{2,1,0:T(8,128)(2,1)S(1)} %pad_maximum_fusion.1.refs_0_.cot), channel_id=1, source_target_pairs={{0,2},{1,3},{2,0},{3,1},{4,6},{5,7},{6,4},{7,5},{8,10},{9,11},{10,... | collective-permute-start | bytes 995336 | tf_op jit(solution)/shard_map/ppermute | solution.py:640
  13.8 4.9 %collective-permute-start.6 = (f32[24,128]{1,0:T(8,128)S(1)}, f32[24,128]{1,0:T(8,128)S(1)}, u32[]{:S(2)}, u32[]{:S(2)}) collective-permute-start(f32[24,128]{1,0:T(8,128)S(1)} %get-tuple-element.347.t0), channel_id=1, source_target_pairs={{0,3},{1,2},{2,1},{3,0},{4,7},{5,6},{6,5},{7,4},{8,11},{9,10},{10,... | collective-permute-start | bytes 36872 | tf_op jit(solution)/shard_map/ppermute | solution.py:640
  26.1 4.3 %collective-permute-start.9 = (bf16[128,384]{1,0:T(8,128)(2,1)S(1)}, bf16[128,384]{1,0:T(8,128)(2,1)S(1)}, u32[]{:S(2)}, u32[]{:S(2)}) collective-permute-start(bf16[128,384]{1,0:T(8,128)(2,1)S(1)} %get-tuple-element.359), channel_id=1, source_target_pairs={{0,1},{1,0},{2,3},{3,2},{4,5},{5,4},{6,7},{7,6},{8,9},{9,8},{10,11... | collective-permute-start | bytes 294920 | tf_op jit(solution)/shard_map/ppermute | solution.py:640
  26.3 5.5 %collective-permute-start.10 = (bf16[128,384]{1,0:T(8,128)(2,1)S(1)}, bf16[128,384]{1,0:T(8,128)(2,1)S(1)}, u32[]{:S(2)}, u32[]{:S(2)}) collective-permute-start(bf16[128,384]{1,0:T(8,128)(2,1)S(1)} %get-tuple-element.360), channel_id=1, source_target_pairs={{0,2},{1,3},{2,0},{3,1},{4,6},{5,7},{6,4},{7,5},{8,10},{9,11},{10,... | collective-permute-start | bytes 294920 | tf_op jit(solution)/shard_map/ppermute | solution.py:640
  28.0 5.1 %collective-permute-start.11 = (bf16[128,384]{1,0:T(8,128)(2,1)S(1)}, bf16[128,384]{1,0:T(8,128)(2,1)S(1)}, u32[]{:S(2)}, u32[]{:S(2)}) collective-permute-start(bf16[128,384]{1,0:T(8,128)(2,1)S(1)} %get-tuple-element.361), channel_id=1, source_target_pairs={{0,3},{1,2},{2,1},{3,0},{4,7},{5,6},{6,5},{7,4},{8,11},{9,10},{10,... | collective-permute-start | bytes 294920 | tf_op jit(solution)/shard_map/ppermute | solution.py:640
  33.1 9.4 %collective-permute-start.14 = (bf16[256,384]{1,0:T(8,128)(2,1)S(1)}, bf16[256,384]{1,0:T(8,128)(2,1)S(1)}, u32[]{:S(2)}, u32[]{:S(2)}) collective-permute-start(bf16[256,384]{1,0:T(8,128)(2,1)S(1)} %get-tuple-element.415), channel_id=1, source_target_pairs={{0,4},{4,0},{8,12},{12,8},{16,20},{20,16},{24,28},{28,24},{1,5},{5... | collective-permute-start | bytes 589832 | tf_op jit(solution)/shard_map/ppermute | solution.py:643
  34.5 7.9 %collective-permute-start.15 = (bf16[256,384]{1,0:T(8,128)(2,1)S(1)}, bf16[256,384]{1,0:T(8,128)(2,1)S(1)}, u32[]{:S(2)}, u32[]{:S(2)}) collective-permute-start(bf16[256,384]{1,0:T(8,128)(2,1)S(1)} %get-tuple-element.416), channel_id=1, source_target_pairs={{0,8},{4,12},{8,0},{12,4},{16,24},{20,28},{24,16},{28,20},{1,9},{5... | collective-permute-start | bytes 589832 | tf_op jit(solution)/shard_map/ppermute | solution.py:643
  36.1 9.4 %collective-permute-start.16 = (bf16[256,384]{1,0:T(8,128)(2,1)S(1)}, bf16[256,384]{1,0:T(8,128)(2,1)S(1)}, u32[]{:S(2)}, u32[]{:S(2)}) collective-permute-start(bf16[256,384]{1,0:T(8,128)(2,1)S(1)} %get-tuple-element.417), channel_id=1, source_target_pairs={{0,12},{4,8},{8,4},{12,0},{16,28},{20,24},{24,20},{28,16},{1,13},{... | collective-permute-start | bytes 589832 | tf_op jit(solution)/shard_map/ppermute | solution.py:643
  41.9 9.6 %collective-permute-start.12 = (bf16[6,81,512]{2,1,0:T(8,128)(2,1)S(1)}, bf16[6,81,512]{2,1,0:T(8,128)(2,1)S(1)}, u32[]{:S(2)}, u32[]{:S(2)}) collective-permute-start(bf16[6,81,512]{2,1,0:T(8,128)(2,1)S(1)} %get-tuple-element.409), channel_id=1, source_target_pairs={{0,1},{1,0},{2,3},{3,2},{4,5},{5,4},{6,7},{7,6},{8,9},{9,8},{10,11... | collective-permute-start | bytes 1493000 | tf_op jit(solution)/shard_map/ppermute | solution.py:640
  41.9 10.0 %collective-permute-start.13 = (bf16[6,81,512]{2,1,0:T(8,128)(2,1)S(1)}, bf16[6,81,512]{2,1,0:T(8,128)(2,1)S(1)}, u32[]{:S(2)}, u32[]{:S(2)}) collective-permute-start(bf16[6,81,512]{2,1,0:T(8,128)(2,1)S(1)} %get-tuple-element.410), channel_id=1, source_target_pairs={{0,1},{1,0},{2,3},{3,2},{4,5},{5,4},{6,7},{7,6},{8,9},{9,8},{10,11... | collective-permute-start | bytes 1493000 | tf_op jit(solution)/shard_map/ppermute | solution.py:640
  45.6 15.1 %collective-permute-start.18 = (bf16[256,384]{1,0:T(8,128)(2,1)S(1)}, bf16[256,384]{1,0:T(8,128)(2,1)S(1)}, u32[]{:S(2)}, u32[]{:S(2)}) collective-permute-start(bf16[256,384]{1,0:T(8,128)(2,1)S(1)} %add_convert_fusion.2), channel_id=1, source_target_pairs={{0,16},{4,20},{8,24},{12,28},{16,0},{20,4},{24,8},{28,12},{1,17},{... | collective-permute-start | bytes 589832 | tf_op jit(solution)/shard_map/ppermute | solution.py:643
  48.4 5.2 %collective-permute-start.19 = (bf16[160,384]{1,0:T(8,128)(2,1)S(1)}, bf16[160,384]{1,0:T(8,128)(2,1)S(1)}, u32[]{:S(2)}, u32[]{:S(2)}) collective-permute-start(bf16[160,384]{1,0:T(8,128)(2,1)S(1)} %get-tuple-element.429), channel_id=1, source_target_pairs={{0,4},{4,0},{8,12},{12,8},{16,20},{20,16},{24,28},{28,24},{1,5},{5... | collective-permute-start | bytes 368648 | tf_op jit(solution)/shard_map/ppermute | solution.py:643
  49.9 8.3 %collective-permute-start.20 = (bf16[160,384]{1,0:T(8,128)(2,1)S(1)}, bf16[160,384]{1,0:T(8,128)(2,1)S(1)}, u32[]{:S(2)}, u32[]{:S(2)}) collective-permute-start(bf16[160,384]{1,0:T(8,128)(2,1)S(1)} %get-tuple-element.430), channel_id=1, source_target_pairs={{0,8},{4,12},{8,0},{12,4},{16,24},{20,28},{24,16},{28,20},{1,9},{5... | collective-permute-start | bytes 368648 | tf_op jit(solution)/shard_map/ppermute | solution.py:643
  51.5 8.8 %collective-permute-start.21 = (bf16[160,384]{1,0:T(8,128)(2,1)S(1)}, bf16[160,384]{1,0:T(8,128)(2,1)S(1)}, u32[]{:S(2)}, u32[]{:S(2)}) collective-permute-start(bf16[160,384]{1,0:T(8,128)(2,1)S(1)} %get-tuple-element.431), channel_id=1, source_target_pairs={{0,12},{4,8},{8,4},{12,0},{16,28},{20,24},{24,20},{28,16},{1,13},{... | collective-permute-start | bytes 368648 | tf_op jit(solution)/shard_map/ppermute | solution.py:643
  52.0 19.5 %collective-permute-start.17 = (bf16[6,81,512]{2,1,0:T(8,128)(2,1)S(1)}, bf16[6,81,512]{2,1,0:T(8,128)(2,1)S(1)}, u32[]{:S(2)}, u32[]{:S(2)}) collective-permute-start(bf16[6,81,512]{2,1,0:T(8,128)(2,1)S(1)} %add_convert_fusion), channel_id=1, source_target_pairs={{0,2},{1,3},{2,0},{3,1},{4,6},{5,7},{6,4},{7,5},{8,10},{9,11},{10,... | collective-permute-start | bytes 1493000 | tf_op jit(solution)/shard_map/ppermute | solution.py:640
  60.3 7.1 %collective-permute-start.23 = (bf16[160,384]{1,0:T(8,128)(2,1)S(1)}, bf16[160,384]{1,0:T(8,128)(2,1)S(1)}, u32[]{:S(2)}, u32[]{:S(2)}) collective-permute-start(bf16[160,384]{1,0:T(8,128)(2,1)S(1)} %add_convert_fusion.4), channel_id=1, source_target_pairs={{0,16},{4,20},{8,24},{12,28},{16,0},{20,4},{24,8},{28,12},{1,17},{... | collective-permute-start | bytes 368648 | tf_op jit(solution)/shard_map/ppermute | solution.py:643
  60.8 7.7 %collective-permute-start.22 = (bf16[256,384]{1,0:T(8,128)(2,1)S(1)}, bf16[256,384]{1,0:T(8,128)(2,1)S(1)}, u32[]{:S(2)}, u32[]{:S(2)}) collective-permute-start(bf16[256,384]{1,0:T(8,128)(2,1)S(1)} %add_convert_fusion.1), channel_id=1, source_target_pairs={{0,8},{4,12},{8,0},{12,4},{16,24},{20,28},{24,16},{28,20},{1,9},{5... | collective-permute-start | bytes 589832 | tf_op jit(solution)/shard_map/ppermute | solution.py:643
  68.5 9.0 %collective-permute-start.28 = (bf16[2,256,384]{2,1,0:T(8,128)(2,1)S(1)}, bf16[2,256,384]{2,1,0:T(8,128)(2,1)S(1)}, u32[]{:S(2)}, u32[]{:S(2)}) collective-permute-start(bf16[2,256,384]{2,1,0:T(8,128)(2,1)S(1)} %pad_maximum_fusion.refs_0_), channel_id=1, source_target_pairs={{0,2},{1,5},{2,0},{3,7},{4,6},{5,1},{6,4},{7,3},{8,10},{9,13},{10,... | collective-permute-start | bytes 1179656 | tf_op jit(solution)/shard_map/ppermute | solution.py:651
  70.1 7.8 %collective-permute-start.27 = (bf16[2,256,384]{2,1,0:T(8,128)(2,1)S(1)}, bf16[2,256,384]{2,1,0:T(8,128)(2,1)S(1)}, u32[]{:S(2)}, u32[]{:S(2)}) collective-permute-start(bf16[2,256,384]{2,1,0:T(8,128)(2,1)S(1)} %pad_maximum_fusion.refs_0_), channel_id=1, source_target_pairs={{0,4},{1,3},{2,6},{3,1},{4,0},{5,7},{6,2},{7,5},{8,12},{9,11},{10,... | collective-permute-start | bytes 1179656 | tf_op jit(solution)/shard_map/ppermute | solution.py:651
  70.8 4.9 %collective-permute-start.24 = (bf16[160,384]{1,0:T(8,128)(2,1)S(1)}, bf16[160,384]{1,0:T(8,128)(2,1)S(1)}, u32[]{:S(2)}, u32[]{:S(2)}) collective-permute-start(bf16[160,384]{1,0:T(8,128)(2,1)S(1)} %add_convert_fusion.3), channel_id=1, source_target_pairs={{0,8},{4,12},{8,0},{12,4},{16,24},{20,28},{24,16},{28,20},{1,9},{5... | collective-permute-start | bytes 368648 | tf_op jit(solution)/shard_map/ppermute | solution.py:643
  77.9 11.1 %collective-permute-start.30 = (bf16[2,256,384]{2,1,0:T(8,128)(2,1)S(1)}, bf16[2,256,384]{2,1,0:T(8,128)(2,1)S(1)}, u32[]{:S(2)}, u32[]{:S(2)}) collective-permute-start(bf16[2,256,384]{2,1,0:T(8,128)(2,1)S(1)} %collective-permute-done.27.refs_1_), channel_id=1, source_target_pairs={{0,2},{1,5},{2,0},{3,7},{4,6},{5,1},{6,4},{7,3},{8,10},{9,13},{10,... | collective-permute-start | bytes 1179656 | tf_op jit(solution)/shard_map/ppermute | solution.py:651
  79.0 10.0 %collective-permute-start.26 = (bf16[2,160,384]{2,1,0:T(8,128)(2,1)S(1)}, bf16[2,160,384]{2,1,0:T(8,128)(2,1)S(1)}, u32[]{:S(2)}, u32[]{:S(2)}) collective-permute-start(bf16[2,160,384]{2,1,0:T(8,128)(2,1)S(1)} %pad_maximum_fusion.2.refs_0_), channel_id=1, source_target_pairs={{0,2},{1,5},{2,0},{3,7},{4,6},{5,1},{6,4},{7,3},{8,10},{9,13},{10,... | collective-permute-start | bytes 737288 | tf_op jit(solution)/shard_map/ppermute | solution.py:651
  79.9 9.1 %collective-permute-start.25 = (bf16[2,160,384]{2,1,0:T(8,128)(2,1)S(1)}, bf16[2,160,384]{2,1,0:T(8,128)(2,1)S(1)}, u32[]{:S(2)}, u32[]{:S(2)}) collective-permute-start(bf16[2,160,384]{2,1,0:T(8,128)(2,1)S(1)} %pad_maximum_fusion.2.refs_0_), channel_id=1, source_target_pairs={{0,4},{1,3},{2,6},{3,1},{4,0},{5,7},{6,2},{7,5},{8,12},{9,11},{10,... | collective-permute-start | bytes 737288 | tf_op jit(solution)/shard_map/ppermute | solution.py:651
  81.2 9.8 %collective-permute-start.31 = (bf16[2,256,384]{2,1,0:T(8,128)(2,1)S(1)}, bf16[2,256,384]{2,1,0:T(8,128)(2,1)S(1)}, u32[]{:S(2)}, u32[]{:S(2)}) collective-permute-start(bf16[2,256,384]{2,1,0:T(8,128)(2,1)S(1)} %pad_maximum_fusion.refs_0_), channel_id=1, source_target_pairs={{0,1},{1,0},{2,3},{3,2},{4,5},{5,4},{6,7},{7,6},{8,9},{9,8},{10,11... | collective-permute-start | bytes 1179656 | tf_op jit(solution)/shard_map/ppermute | solution.py:640
  81.2 10.3 %collective-permute-start.32 = (bf16[2,256,384]{2,1,0:T(8,128)(2,1)S(1)}, bf16[2,256,384]{2,1,0:T(8,128)(2,1)S(1)}, u32[]{:S(2)}, u32[]{:S(2)}) collective-permute-start(bf16[2,256,384]{2,1,0:T(8,128)(2,1)S(1)} %collective-permute-done.27.refs_1_), channel_id=1, source_target_pairs={{0,1},{1,0},{2,3},{3,2},{4,5},{5,4},{6,7},{7,6},{8,9},{9,8},{10,11... | collective-permute-start | bytes 1179656 | tf_op jit(solution)/shard_map/ppermute | solution.py:640
  89.5 6.2 %collective-permute-start.29 = (bf16[2,160,384]{2,1,0:T(8,128)(2,1)S(1)}, bf16[2,160,384]{2,1,0:T(8,128)(2,1)S(1)}, u32[]{:S(2)}, u32[]{:S(2)}) collective-permute-start(bf16[2,160,384]{2,1,0:T(8,128)(2,1)S(1)} %collective-permute-done.25.refs_1_), channel_id=1, source_target_pairs={{0,2},{1,5},{2,0},{3,7},{4,6},{5,1},{6,4},{7,3},{8,10},{9,13},{10,... | collective-permute-start | bytes 737288 | tf_op jit(solution)/shard_map/ppermute | solution.py:651
  91.0 4.7 %collective-permute-start.35 = (bf16[2,160,384]{2,1,0:T(8,128)(2,1)S(1)}, bf16[2,160,384]{2,1,0:T(8,128)(2,1)S(1)}, u32[]{:S(2)}, u32[]{:S(2)}) collective-permute-start(bf16[2,160,384]{2,1,0:T(8,128)(2,1)S(1)} %pad_maximum_fusion.2.refs_0_), channel_id=1, source_target_pairs={{0,1},{1,0},{2,3},{3,2},{4,5},{5,4},{6,7},{7,6},{8,9},{9,8},{10,11... | collective-permute-start | bytes 737288 | tf_op jit(solution)/shard_map/ppermute | solution.py:640
  91.0 4.7 %collective-permute-start.36 = (bf16[2,160,384]{2,1,0:T(8,128)(2,1)S(1)}, bf16[2,160,384]{2,1,0:T(8,128)(2,1)S(1)}, u32[]{:S(2)}, u32[]{:S(2)}) collective-permute-start(bf16[2,160,384]{2,1,0:T(8,128)(2,1)S(1)} %collective-permute-done.25.refs_1_), channel_id=1, source_target_pairs={{0,1},{1,0},{2,3},{3,2},{4,5},{5,4},{6,7},{7,6},{8,9},{9,8},{10,11... | collective-permute-start | bytes 737288 | tf_op jit(solution)/shard_map/ppermute | solution.py:640
  91.5 4.2 %collective-permute-start.37 = (bf16[2,160,384]{2,1,0:T(8,128)(2,1)S(1)}, bf16[2,160,384]{2,1,0:T(8,128)(2,1)S(1)}, u32[]{:S(2)}, u32[]{:S(2)}) collective-permute-start(bf16[2,160,384]{2,1,0:T(8,128)(2,1)S(1)} %collective-permute-done.26.refs_2_), channel_id=1, source_target_pairs={{0,1},{1,0},{2,3},{3,2},{4,5},{5,4},{6,7},{7,6},{8,9},{9,8},{10,11... | collective-permute-start | bytes 737288 | tf_op jit(solution)/shard_map/ppermute | solution.py:640
  (15 other events, 67.0 us)

commit v4 on v3

--- a/solution.py
+++ b/solution.py
@@ -23,9 +23,10 @@
 
 
 ORDER = (
-    "weights", "stats", "a_send", "sums", "back", "rows", "a_rs", "tick", "v_send", "rows_core", "v_rs", "a_z2",
-    "v_z2", "a_pair", "finish", "v_pair", "a_mark", "v_mark", "a_twin0", "a_twin1", "a_third", "a_twin2", "a_twin3",
-    "v_twin0", "v_twin1", "place_first", "v_third", "v_twin2", "v_twin3", "place_most", "place_last",
+    "weights", "a_send", "tick", "stats", "sums", "back", "v_send", "rows", "a_rs", "tick", "rows_core", "v_rs",
+    "a_z2", "v_z2", "a_pair", "tick", "v_pair", "finish", "a_mark", "tick", "v_mark", "tick", "a_twin0", "a_twin1",
+    "a_twin2", "place_head", "a_third", "a_twin3", "v_third", "v_twin3", "v_twin0", "v_twin1", "v_twin2", "tick",
+    "place_most", "place_last",
 )
 
 
@@ -550,26 +551,25 @@
     return out
 
 
-def place_first_body(half, meta, *refs):
-    pieces = refs[:8]
-    w_in, w_out, wide, tall, sems = refs[8:]
+def place_wu(half, meta, pieces, which, w_in, w_out, wide, tall, sems):
     shard = wide.shape[1]
     copies = []
-    for k, (group, seq) in enumerate(sources(meta)):
+    origins = sources(meta)
+    for piece, k in zip(pieces, which):
+        group, seq = origins[k]
         for e in range(2):
-            slot = 2 * k + e
+            slot = len(copies) // 2
             row = (group ^ (2 * e)) * shard
             columns = rows_at(seq * half, half, 128)
-            tall[slot] = jnp.transpose(pieces[k][e, 0:shard, :].astype(F32))
+            tall[slot] = jnp.transpose(piece[e, 0:shard, :].astype(F32))
             target = w_out.at[columns, rows_at(row, shard, 128)]
             copies.append(pltpu.make_async_copy(tall.at[slot], target, sems.at[2 * slot]))
             copies[-1].start()
-            wide[slot] = pieces[k][e, shard:, :].astype(F32)
+            wide[slot] = piece[e, shard:, :].astype(F32)
             target = w_in.at[rows_at(row, shard, 16), columns]
             copies.append(pltpu.make_async_copy(wide.at[slot], target, sems.at[2 * slot + 1]))
             copies[-1].start()
-    for copy in copies:
-        copy.wait()
+    return copies
 
 
 def place_v(half, gate, meta, pieces, which, w_in, wide, sems):
@@ -588,15 +588,21 @@
     return copies
 
 
-def place_most_body(half, gate, which, meta, *refs):
-    *pieces, _, w_in, wide, sems = refs
-    for copy in place_v(half, gate, meta, pieces, which, w_in, wide, sems):
+def place_body(half, gate, fresh, which_wu, which_v, meta, *refs):
+    *pieces, w_in, w_out, wide, tall, sems, more, more_sems = refs
+    if not fresh:
+        pieces = pieces[:-2]
+    count = len(which_wu)
+    copies = place_wu(half, meta, pieces[:count], which_wu, w_in, w_out, wide, tall, sems)
+    copies += place_v(half, gate, meta, pieces[count:], which_v, w_in, more, more_sems)
+    for copy in copies:
         copy.wait()
 
 
 def place_last_body(half, gate, which, meta, *refs):
     pieces = refs[:8]
-    w_in, spatial, bias, gain_one, shift_one, gain_two, shift_two, wide, edge, norms, sems = refs[10:]
+    w_in, *targets, wide, edge, norms = refs[10:20]
+    spatial, bias, gain_one, shift_one, gain_two, shift_two, sems, small_sems = refs[20:]
     shard = wide.shape[1]
     rows, patches = spatial.shape
     size = edge.shape[0] // 4
@@ -629,6 +635,10 @@
     for at, out in ((0, gain_two), (1, shift_two)):
         for j in range(4):
             out[j * half : (j + 1) * half] = norms[at, j, 0, :]
+    smalls = (spatial, bias, gain_one, shift_one, gain_two, shift_two)
+    for k, (source, target) in enumerate(zip(smalls, targets)):
+        copies.append(pltpu.make_async_copy(source, target, small_sems.at[k]))
+        copies[-1].start()
     for copy in copies:
         copy.wait()
 
@@ -842,34 +852,25 @@
                 finish_rows_body, [shape, shape], ins, specs=[SM] + [VM] * 6, name="finish_rows"
             )
 
-        def place_first(*ins):
+        wide_shapes = shape_of((width, 2 * gate), F32), shape_of((gate, width), F32)
+
+        def place(fresh, which_wu, which_v, *ins):
+            count = len(which_wu) + len(which_v)
             return call(
-                functools.partial(place_first_body, half),
-                [shape_of((width, 2 * gate), F32), shape_of((gate, width), F32)],
+                functools.partial(place_body, half, gate, fresh, which_wu, which_v),
+                wide_shapes,
                 ins,
                 [
-                    pltpu.VMEM((16, shard, half), F32),
-                    pltpu.VMEM((16, half, shard), F32),
-                    pltpu.SemaphoreType.DMA((32,)),
+                    pltpu.VMEM((2 * len(which_wu), shard, half), F32),
+                    pltpu.VMEM((2 * len(which_wu), half, shard), F32),
+                    pltpu.SemaphoreType.DMA((4 * len(which_wu),)),
+                    pltpu.VMEM((max(2 * len(which_v), 1), shard, half), F32),
+                    pltpu.SemaphoreType.DMA((max(2 * len(which_v), 1),)),
                 ],
-                specs=[SM] + [VM] * 8,
+                specs=[SM] + [VM] * count + ([] if fresh else [HB] * 2),
                 out_specs=[HB] * 2,
-                name="place_first",
-            )
-
-        def place_most(which, *ins):
-            return call(
-                functools.partial(place_most_body, half, gate, which),
-                [shape_of((width, 2 * gate), F32)],
-                ins,
-                [
-                    pltpu.VMEM((2 * len(which), shard, half), F32),
-                    pltpu.SemaphoreType.DMA((2 * len(which),)),
-                ],
-                specs=[SM] + [VM] * len(which) + [HB],
-                out_specs=[HB],
-                input_output_aliases={1 + len(which): 0},
-                name="place_most",
+                input_output_aliases={} if fresh else {1 + count: 0, 2 + count: 1},
+                name="place",
             )
 
         def place_last(which, *ins):
@@ -883,10 +884,12 @@
                     pltpu.VMEM((2 * len(which), shard, half), F32),
                     pltpu.VMEM((pad, columns), F32),
                     pltpu.VMEM((4, n, EXTRA - pad // 4, half), F32),
+                    *(pltpu.VMEM(s.shape, F32) for s in small),
                     pltpu.SemaphoreType.DMA((2 * len(which),)),
+                    pltpu.SemaphoreType.DMA((len(small),)),
                 ],
                 specs=[SM] + [VM] * 8 + [HB, VM],
-                out_specs=[HB] + [VM] * 6,
+                out_specs=[HB] * 7,
                 input_output_aliases={9: 0},
                 name="place_last",
             )
@@ -968,14 +971,15 @@
         def ev_got(k, j):
             x[f"{k}q{j}"] = step(None, x[f"{k}q{j}"])
 
-        def ev_place_first():
-            ins = [x[f"ap{j}"] for j in range(4)] + [x[f"aq{j}"] for j in range(4)]
-            x["w_in"], x["w_out"] = step(place_first, meta, *ins)
-
-        def ev_place_most():
-            which = (0, 1, 2, 4, 5, 6)
-            ins = [x[f"v{'pq'[k // 4]}{k % 4}"] for k in which]
-            (x["w_in"],) = step(functools.partial(place_most, which), meta, *ins, x["w_in"])
+        def pieces(k, which):
+            return [x[f"{k}{'pq'[j // 4]}{j % 4}"] for j in which]
+
+        def ev_place(fresh, which_wu, which_v):
+            ins = [*pieces("a", which_wu), *pieces("v", which_v)]
+            ins += [] if fresh else [x["w_in"], x["w_out"]]
+            x["w_in"], x["w_out"] = step(
+                functools.partial(place, fresh, which_wu, which_v), meta, *ins
+            )
 
         def ev_place_last():
             ins = [x[f"vp{j}"] for j in range(4)] + [x[f"vq{j}"] for j in range(4)]
@@ -986,7 +990,12 @@
         events = dict(
             weights=ev_weights, sums=ev_sums, stats=ev_stats, back=ev_back,
             rows=ev_rows, rows_core=ev_rows_core, finish=ev_finish,
-            place_first=ev_place_first, place_last=ev_place_last, place_most=ev_place_most,
+            place_last=ev_place_last,
+            place_own=functools.partial(ev_place, True, (0, 4), (0, 4)),
+            place_near=functools.partial(ev_place, False, (1, 2, 5, 6), ()),
+            place_far=functools.partial(ev_place, False, (3, 7), (1, 2, 5, 6)),
+            place_head=functools.partial(ev_place, True, (0, 1, 2, 4, 5, 6), ()),
+            place_most=functools.partial(ev_place, False, (3, 7), (0, 1, 2, 4, 5, 6)),
             a_send=ev_a_send, v_send=ev_v_send, tick=ev_tick,
         )
         for k in ("a", "v"):

time: 100 us -> 92.2 us (0.922)
  waiting for transfers between devices: 33.9 us -> 26.5 us
  starting transfers between devices: 31.7 us -> 30.7 us
    ppermute x10, waiting for transfers between devices: 17.6 us -> 13.6 us  [over_dp(): return lax.ppermute(x, 'dp', [(i, i ^ flip) for i in range(m)])]
    ppermute x23, waiting for transfers between devices: 6.21 us -> 4.4 us  [over_seq(): return lax.ppermute(x, 'seq', [(i, i ^ flip) for i in range(n)])]
    ppermute x6, waiting for transfers between devices: 10 us -> 8.45 us  [mixed_axes(): return lax.ppermute(x, ('dp', 'seq'), pairs)]
    pallas_call x17 -> x22, Pallas kernels: 28.8 us -> 28.4 us  [call(): pl.pallas_call(body, out_shape=outs, in_specs=specs if specs is not None...]
  transfers between devices with their start and end apart: 39 -> 39, of which waited for: 17 -> 16; matrix products, arithmetic and copies ran while one was open for 5% -> 6% of each run, Pallas kernels for 22% -> 24%
where the time goes in v4:
time: 92.2 us; the launch traced here: 92 us
  starting transfers between devices  30.7 us (33%)
  Pallas kernels  28.4 us (31%)
  waiting for transfers between devices  26.5 us (29%)
  other arithmetic  3.84 us (4%)
  local copies, waits for them, and re-layouts  1.53 us (2%)
  between operations  1.09 us (1%)
    pallas_call x22, Pallas kernels, call(): pl.pallas_call(body, out_shape=outs, in_specs=specs if specs is not None...  28.4 us
    ppermute x10, waiting for transfers between devices, over_dp(): return lax.ppermute(x, 'dp', [(i, i ^ flip) for i in range(m)])  13.6 us
    ppermute x10, starting transfers between devices, over_dp(): return lax.ppermute(x, 'dp', [(i, i ^ flip) for i in range(m)])  13 us
    ppermute x23, starting transfers between devices, over_seq(): return lax.ppermute(x, 'seq', [(i, i ^ flip) for i in range(n)])  11.1 us
    ppermute x6, waiting for transfers between devices, mixed_axes(): return lax.ppermute(x, ('dp', 'seq'), pairs)  8.45 us
    ppermute x6, starting transfers between devices, mixed_axes(): return lax.ppermute(x, ('dp', 'seq'), pairs)  6.52 us
    ppermute x23, waiting for transfers between devices, over_seq(): return lax.ppermute(x, 'seq', [(i, i ^ flip) for i in range(n)])  4.4 us
  transfers between devices with their start and end apart: 39, of which 16 were waited for; matrix products, arithmetic and copies ran while one was open for 6% of the time, Pallas kernels for 24%

profile of v4, /device:TPU:0, one launch (start us, length us, event | category | flops | bytes accessed | tf_op | source)
XLA Modules:
  0.0 92.0 jit_solution(15544586815326983961)
XLA Ops:
  1.2 2.6 %collective-permute-start.1 = (bf16[3,81,512]{2,1,0:T(8,128)(2,1)}, bf16[3,81,512]{2,1,0:T(8,128)(2,1)S(1)}, u32[]{:S(2)}, u32[]{:S(2)}) collective-permute-start(bf16[3,81,512]{2,1,0:T(8,128)(2,1)} %tok), channel_id=1, source_target_pairs={{0,2},{1,3},{2,0},{3,1},{4,6},{5,7},{6,4},{7,5},{8,10},{9,11},{10,... | collective-permute-start | bytes 746504 | tf_op jit(solution)/shard_map/ppermute | solution.py:650
  7.5 1.2 %constant_dynamic-slice_fusion.1 = (bf16[512,384]{1,0:T(8,128)(2,1)S(1)}, bf16[512,384]{1,0:T(8,128)(2,1)S(1)}) fusion(bf16[512,3072]{1,0:T(8,128)(2,1)} %param.15, s32[]{:T(128)S(6)} %select_n.10, s32[]{:T(128)S(6)} %select_n.9), kind=kLoop, calls=%fused_computation.16 | loop fusion | bytes 1572872 | tf_op jit(solution)/shard_map/dynamic_slice | solution.py:726
  9.2 1.8 %project.3 = (bf16[576,512]{1,0:T(8,128)(2,1)S(1)}, bf16[576,384]{1,0:T(8,128)(2,1)S(1)}, bf16[576,384]{1,0:T(8,128)(2,1)S(1)}, f32[576,384]{1,0:T(8,128)S(1)}, ...) custom-call(bf16[3,81,512]{2,1,0:T(8,128)(2,1)S(1)} %copy-done.1, ...), custom_call_target="tpu_custom_call" | custom-call | flops 1 | bytes 1 | tf_op jit(solution)/shard_map/project/pallas_call | solution.py:50
  14.0 2.2 %collective-permute-start.5 = (f32[24,128]{1,0:T(8,128)S(1)}, f32[24,128]{1,0:T(8,128)S(1)}, u32[]{:S(2)}, u32[]{:S(2)}) collective-permute-start(f32[24,128]{1,0:T(8,128)S(1)} %get-tuple-element.355.t0), channel_id=1, source_target_pairs={{0,2},{1,3},{2,0},{3,1},{4,6},{5,7},{6,4},{7,5},{8,10},{9,11},{10,... | collective-permute-start | bytes 36872 | tf_op jit(solution)/shard_map/ppermute | solution.py:650
  17.8 2.2 %collective-permute-done.5.t2 = f32[24,128]{1,0:T(8,128)S(1)} collective-permute-done((f32[24,128]{1,0:T(8,128)S(1)}, f32[24,128]{1,0:T(8,128)S(1)}, u32[]{:S(2)}, u32[]{:S(2)}) %collective-permute-start.5) | collective-permute-done | bytes 12320 | tf_op jit(solution)/shard_map/ppermute | solution.py:650
  21.7 1.5 %prepare.1 = (bf16[288,512]{1,0:T(8,128)(2,1)S(1)}, f32[288,384]{1,0:T(8,128)S(1)}, bf16[384,1152]{1,0:T(8,128)(2,1)S(1)}, f32[1152,384]{1,0:T(8,128)S(1)}, bf16[384,384]{1,0:T(8,128)(2,1)S(1)}) custom-call(s32[8]{0:T(128)S(1)} %pad_add_fusion.meta, bf16[4,81,512]{2,1,0:T(8,128)(2,1)S(1)} %collective-permute-done.8.c3, ...), custom_call_target="tpu_custom_call" | custom-call | flops 1 | bytes 1 | tf_op jit(solution)/shard_map/prepare/pallas_call | solution.py:50
  23.2 3.4 %spatial.1 = (bf16[1152,384]{1,0:T(8,128)(2,1)S(1)}, bf16[1152,384]{1,0:T(8,128)(2,1)S(1)}, f32[128,128]{1,0:T(8,128)S(1)}, f32[24,128]{1,0:T(8,128)S(1)}, bf16[...) custom-call(s32[8]{0:T(128)S(1)} %pad_add_fusion.meta, ...), custom_call_target="tpu_custom_call" | custom-call | flops 1 | bytes 1 | tf_op jit(solution)/shard_map/spatial/pallas_call | solution.py:50
  27.7 2.4 %weights.1 = (bf16[256,384]{1,0:T(8,128)(2,1)S(1)}, bf16[256,384]{1,0:T(8,128)(2,1)S(1)}, bf16[256,384]{1,0:T(8,128)(2,1)S(1)}, bf16[256,384]{1,0:T(8,128)(2,1)S(1)}, f32[512,384]{1,0:T(8,128)S(1)}) custom-call(s32[8]{0:T(128)S(1)} %pad_add_fusion.meta, bf16[1152,384]{1,0:T(8,128)(2,1)S(1)} %get-tuple-element.416.prod, ...), custom_call_target="tpu_custom_call" | custom-call | flops 1 | bytes 1 | tf_op jit(solution)/shard_map/weights/pallas_call | solution.py:50
  31.3 1.5 %collective-permute-start.14 = (bf16[256,384]{1,0:T(8,128)(2,1)S(1)}, bf16[256,384]{1,0:T(8,128)(2,1)S(1)}, u32[]{:S(2)}, u32[]{:S(2)}) collective-permute-start(bf16[256,384]{1,0:T(8,128)(2,1)S(1)} %get-tuple-element.425), channel_id=1, source_target_pairs={{0,4},{4,0},{8,12},{12,8},{16,20},{20,16},{24,28},{28,24},{1,5},{5... | collective-permute-start | bytes 589832 | tf_op jit(solution)/shard_map/ppermute | solution.py:653
  32.8 1.6 %collective-permute-start.15 = (bf16[256,384]{1,0:T(8,128)(2,1)S(1)}, bf16[256,384]{1,0:T(8,128)(2,1)S(1)}, u32[]{:S(2)}, u32[]{:S(2)}) collective-permute-start(bf16[256,384]{1,0:T(8,128)(2,1)S(1)} %get-tuple-element.426), channel_id=1, source_target_pairs={{0,8},{4,12},{8,0},{12,4},{16,24},{20,28},{24,16},{28,20},{1,9},{5... | collective-permute-start | bytes 589832 | tf_op jit(solution)/shard_map/ppermute | solution.py:653
  35.6 2.9 %back.1 = (bf16[1152,384]{1,0:T(8,128)(2,1)S(1)}, bf16[160,384]{1,0:T(8,128)(2,1)S(1)}, bf16[160,384]{1,0:T(8,128)(2,1)S(1)}, bf16[160,384]{1,0:T(8,128)(2,1)S(1)}, bf16[160,384]{1,0:T(8,128)(2,1)S(1)}) custom-call(s32[8]{0:T(128)S(1)} %pad_add_fusion.meta, f32[1152,384]{1,0:T(8,128)S(1)} %get-tuple-element.391.gmix, f32[576,384]{1,0:T(8,128)S(1)} %get-tuple-element.392.v0, ...), custom_call_target="tpu_custom_call" | custom-call | flops 1 | bytes 1 | tf_op jit(solution)/shard_map/back/pallas_call | solution.py:50
  38.5 2.0 %rows_out.1 = (bf16[6,81,512]{2,1,0:T(8,128)(2,1)S(1)}, bf16[6,81,512]{2,1,0:T(8,128)(2,1)S(1)}, bf16[6,81,512]{2,1,0:T(8,128)(2,1)S(1)}, bf16[6,81,512]{2,1,0:T(8,128)(2,1)S(1)}) custom-call(bf16[1152,384]{1,0:T(8,128)(2,1)S(1)} %get-tuple-element.416.prod, bf16[384,512]{1,0:T(8,128)(2,1)S(1)} %constant_dynamic-slice_fusion.refs_2_.refs_1_.wo, ...), custom_call_target="tpu_custom_call" | custom-call | flops 1 | bytes 1 | tf_op jit(solution)/shard_map/rows_out/pallas_call | solution.py:50
  41.1 1.5 %collective-permute-start.18 = (bf16[160,384]{1,0:T(8,128)(2,1)S(1)}, bf16[160,384]{1,0:T(8,128)(2,1)S(1)}, u32[]{:S(2)}, u32[]{:S(2)}) collective-permute-start(bf16[160,384]{1,0:T(8,128)(2,1)S(1)} %get-tuple-element.438), channel_id=1, source_target_pairs={{0,4},{4,0},{8,12},{12,8},{16,20},{20,16},{24,28},{28,24},{1,5},{5... | collective-permute-start | bytes 368648 | tf_op jit(solution)/shard_map/ppermute | solution.py:653
  42.6 1.6 %collective-permute-start.19 = (bf16[160,384]{1,0:T(8,128)(2,1)S(1)}, bf16[160,384]{1,0:T(8,128)(2,1)S(1)}, u32[]{:S(2)}, u32[]{:S(2)}) collective-permute-start(bf16[160,384]{1,0:T(8,128)(2,1)S(1)} %get-tuple-element.439), channel_id=1, source_target_pairs={{0,8},{4,12},{8,0},{12,4},{16,24},{20,28},{24,16},{28,20},{1,9},{5... | collective-permute-start | bytes 368648 | tf_op jit(solution)/shard_map/ppermute | solution.py:653
  44.2 1.8 %collective-permute-start.20 = (bf16[160,384]{1,0:T(8,128)(2,1)S(1)}, bf16[160,384]{1,0:T(8,128)(2,1)S(1)}, u32[]{:S(2)}, u32[]{:S(2)}) collective-permute-start(bf16[160,384]{1,0:T(8,128)(2,1)S(1)} %get-tuple-element.440), channel_id=1, source_target_pairs={{0,12},{4,8},{8,4},{12,0},{16,28},{20,24},{24,20},{28,16},{1,13},{... | collective-permute-start | bytes 368648 | tf_op jit(solution)/shard_map/ppermute | solution.py:653
  46.2 2.6 %collective-permute-start.22 = (bf16[256,384]{1,0:T(8,128)(2,1)S(1)}, bf16[256,384]{1,0:T(8,128)(2,1)S(1)}, u32[]{:S(2)}, u32[]{:S(2)}) collective-permute-start(bf16[256,384]{1,0:T(8,128)(2,1)S(1)} %add_convert_fusion.2), channel_id=1, source_target_pairs={{0,16},{4,20},{8,24},{12,28},{16,0},{20,4},{24,8},{28,12},{1,17},{... | collective-permute-start | bytes 589832 | tf_op jit(solution)/shard_map/ppermute | solution.py:653
  50.0 1.7 %collective-permute-done.19 = bf16[160,384]{1,0:T(8,128)(2,1)S(1)} collective-permute-done((bf16[160,384]{1,0:T(8,128)(2,1)S(1)}, bf16[160,384]{1,0:T(8,128)(2,1)S(1)}, u32[]{:S(2)}, u32[]{:S(2)}) %collective-permute-start.19) | collective-permute-done | bytes 122912 | tf_op jit(solution)/shard_map/ppermute | solution.py:653
  51.7 2.4 %collective-permute-done.20 = bf16[160,384]{1,0:T(8,128)(2,1)S(1)} collective-permute-done((bf16[160,384]{1,0:T(8,128)(2,1)S(1)}, bf16[160,384]{1,0:T(8,128)(2,1)S(1)}, u32[]{:S(2)}, u32[]{:S(2)}) %collective-permute-start.20) | collective-permute-done | bytes 122912 | tf_op jit(solution)/shard_map/ppermute | solution.py:653
  54.8 4.7 %collective-permute-done.22 = bf16[256,384]{1,0:T(8,128)(2,1)S(1)} collective-permute-done((bf16[256,384]{1,0:T(8,128)(2,1)S(1)}, bf16[256,384]{1,0:T(8,128)(2,1)S(1)}, u32[]{:S(2)}, u32[]{:S(2)}) %collective-permute-start.22) | collective-permute-done | bytes 196640 | tf_op jit(solution)/shard_map/ppermute | solution.py:653
  59.6 1.4 %collective-permute-start.24 = (bf16[256,384]{1,0:T(8,128)(2,1)S(1)}, bf16[256,384]{1,0:T(8,128)(2,1)S(1)}, u32[]{:S(2)}, u32[]{:S(2)}) collective-permute-start(bf16[256,384]{1,0:T(8,128)(2,1)S(1)} %add_convert_fusion.1), channel_id=1, source_target_pairs={{0,8},{4,12},{8,0},{12,4},{16,24},{20,28},{24,16},{28,20},{1,9},{5... | collective-permute-start | bytes 589832 | tf_op jit(solution)/shard_map/ppermute | solution.py:653
  60.9 1.3 %collective-permute-done.21 = bf16[160,384]{1,0:T(8,128)(2,1)S(1)} collective-permute-done((bf16[160,384]{1,0:T(8,128)(2,1)S(1)}, bf16[160,384]{1,0:T(8,128)(2,1)S(1)}, u32[]{:S(2)}, u32[]{:S(2)}) %collective-permute-start.21) | collective-permute-done | bytes 122912 | tf_op jit(solution)/shard_map/ppermute | solution.py:653
  62.4 3.3 %collective-permute-done.24 = bf16[256,384]{1,0:T(8,128)(2,1)S(1)} collective-permute-done((bf16[256,384]{1,0:T(8,128)(2,1)S(1)}, bf16[256,384]{1,0:T(8,128)(2,1)S(1)}, u32[]{:S(2)}, u32[]{:S(2)}) %collective-permute-start.24) | collective-permute-done | bytes 196640 | tf_op jit(solution)/shard_map/ppermute | solution.py:653
  66.7 1.2 %collective-permute-start.28 = (bf16[2,256,384]{2,1,0:T(8,128)(2,1)S(1)}, bf16[2,256,384]{2,1,0:T(8,128)(2,1)S(1)}, u32[]{:S(2)}, u32[]{:S(2)}) collective-permute-start(bf16[2,256,384]{2,1,0:T(8,128)(2,1)S(1)} %pad_maximum_fusion.refs_0_), channel_id=1, source_target_pairs={{0,2},{1,5},{2,0},{3,7},{4,6},{5,1},{6,4},{7,3},{8,10},{9,13},{10,... | collective-permute-start | bytes 1179656 | tf_op jit(solution)/shard_map/ppermute | solution.py:661
  68.0 1.5 %collective-permute-start.25 = (bf16[2,160,384]{2,1,0:T(8,128)(2,1)S(1)}, bf16[2,160,384]{2,1,0:T(8,128)(2,1)S(1)}, u32[]{:S(2)}, u32[]{:S(2)}) collective-permute-start(bf16[2,160,384]{2,1,0:T(8,128)(2,1)S(1)} %pad_maximum_fusion.2.refs_2_.refs_0_), channel_id=1, source_target_pairs={{0,4},{1,3},{2,6},{3,1},{4,0},{5,7},{6,2},{7,5},{8,12},{9,11},{10,... | collective-permute-start | bytes 737288 | tf_op jit(solution)/shard_map/ppermute | solution.py:661
  70.0 1.8 %finish_rows.1 = (bf16[3,81,512]{2,1,0:T(8,128)(2,1)}, bf16[3,81,512]{2,1,0:T(8,128)(2,1)}) custom-call(s32[8]{0:T(128)S(1)} %pad_add_fusion.meta, bf16[3,81,512]{2,1,0:T(8,128)(2,1)S(1)} %copy-done.1, bf16[4,81,512]{2,1,0:T(8,128)(2,1)S(1)} %pad_maximum_fusion.1.refs_0_.cot, bf16[6,81,512]{2,1,0:T(8,128)(2,1)S(1)} %get-tuple-element.457.keep, ...), custom_call_target="tpu_custom_call" | custom-call | flops 1 | bytes 1 | tf_op jit(solution)/shard_map/finish_rows/pallas_call | solution.py:50
  71.8 4.7 %collective-permute-done.27.refs_1_ = bf16[2,256,384]{2,1,0:T(8,128)(2,1)S(1)} collective-permute-done((bf16[2,256,384]{2,1,0:T(8,128)(2,1)S(1)}, bf16[2,256,384]{2,1,0:T(8,128)(2,1)S(1)}, u32[]{:S(2)}, u32[]{:S(2)}) %collective-permute-start.27) | collective-permute-done | bytes 393248 | tf_op jit(solution)/shard_map/ppermute | solution.py:661
  76.9 1.3 %collective-permute-start.30 = (bf16[2,256,384]{2,1,0:T(8,128)(2,1)S(1)}, bf16[2,256,384]{2,1,0:T(8,128)(2,1)S(1)}, u32[]{:S(2)}, u32[]{:S(2)}) collective-permute-start(bf16[2,256,384]{2,1,0:T(8,128)(2,1)S(1)} %collective-permute-done.27.refs_1_), channel_id=1, source_target_pairs={{0,2},{1,5},{2,0},{3,7},{4,6},{5,1},{6,4},{7,3},{8,10},{9,13},{10,... | collective-permute-start | bytes 1179656 | tf_op jit(solution)/shard_map/ppermute | solution.py:661
  78.2 1.6 %collective-permute-done.25.refs_3_.refs_1_ = bf16[2,160,384]{2,1,0:T(8,128)(2,1)S(1)} collective-permute-done((bf16[2,160,384]{2,1,0:T(8,128)(2,1)S(1)}, bf16[2,160,384]{2,1,0:T(8,128)(2,1)S(1)}, u32[]{:S(2)}, u32[]{:S(2)}) %collective-permute-start.25) | collective-permute-done | bytes 245792 | tf_op jit(solution)/shard_map/ppermute | solution.py:661
  81.5 3.0 %place.2 = (f32[512,3072]{1,0:T(8,128)}, f32[1536,512]{1,0:T(8,128)}) custom-call(s32[8]{0:T(128)S(1)} %pad_add_fusion.meta, bf16[2,256,384]{2,1,0:T(8,128)(2,1)S(1)} %pad_maximum_fusion.refs_0_, bf16[2,256,384]{2,1,0:T(8,128)(2,1)S(1)} %collective-permute-done.27.refs_1_, bf16[2,256,384]{2,1,0:T(8,128)(2,1)S(1)} %collective-permute-done.28.refs_2_, ...), custom_call_target="tpu_custom_call" | custom-call | flops 1 | bytes 1 | tf_op jit(solution)/shard_map/place/pallas_call | solution.py:50
  85.7 1.6 %collective-permute-done.29.refs_3_ = bf16[2,160,384]{2,1,0:T(8,128)(2,1)S(1)} collective-permute-done((bf16[2,160,384]{2,1,0:T(8,128)(2,1)S(1)}, bf16[2,160,384]{2,1,0:T(8,128)(2,1)S(1)}, u32[]{:S(2)}, u32[]{:S(2)}) %collective-permute-start.29) | collective-permute-done | bytes 245792 | tf_op jit(solution)/shard_map/ppermute | solution.py:661
  87.5 2.7 %place.3 = (f32[512,3072]{1,0:T(8,128)}, f32[1536,512]{1,0:T(8,128)}) custom-call(s32[8]{0:T(128)S(1)} %pad_add_fusion.meta, bf16[2,256,384]{2,1,0:T(8,128)(2,1)S(1)} %collective-permute-done.30.refs_0_, bf16[2,256,384]{2,1,0:T(8,128)(2,1)S(1)} %collective-permute-done.38.refs_1_, ...), custom_call_target="tpu_custom_call", output_to_operand_aliasing={{0}: (9, {}), {1}: (10, {})} | custom-call | flops 1 | bytes 1 | tf_op jit(solution)/shard_map/place/pallas_call | solution.py:50
  90.2 1.6 %place_last.1 = (f32[512,3072]{1,0:T(8,128)}, f32[81,324]{1,0:T(8,128)}, f32[81]{0:T(128)}, f32[512]{0:T(512)}, f32[512]{0:T(512)}, /*index=5*/f32[1536]{0:T(1024)}, f32[1536]{0:T(1024)}) custom-call(s32[8]{0:T(128)S(1)} %pad_add_fusion.meta, bf16[2,160,384]{2,1,0:T(8,128)(2,1)S(1)} %pad_maximum_fusion.2.refs_2_.refs_0_, ...), custom_call_target="tpu_custom_call", output_to_operand_aliasing={{0}: (9, {})} | custom-call | flops 1 | bytes 1 | tf_op jit(solution)/shard_map/place_last/pallas_call | solution.py:50
  (96 shorter events, 22.1 us)
Async XLA Ops:
  0.7 8.0 %collective-permute-start = (bf16[3,81,512]{2,1,0:T(8,128)(2,1)}, bf16[3,81,512]{2,1,0:T(8,128)(2,1)S(1)}, u32[]{:S(2)}, u32[]{:S(2)}) collective-permute-start(bf16[3,81,512]{2,1,0:T(8,128)(2,1)} %tok), channel_id=1, source_target_pairs={{0,1},{1,0},{2,3},{3,2},{4,5},{5,4},{6,7},{7,6},{8,9},{9,8},{10,11... | collective-permute-start | bytes 746504 | tf_op jit(solution)/shard_map/ppermute | solution.py:650
  1.2 9.9 %collective-permute-start.1 = (bf16[3,81,512]{2,1,0:T(8,128)(2,1)}, bf16[3,81,512]{2,1,0:T(8,128)(2,1)S(1)}, u32[]{:S(2)}, u32[]{:S(2)}) collective-permute-start(bf16[3,81,512]{2,1,0:T(8,128)(2,1)} %tok), channel_id=1, source_target_pairs={{0,2},{1,3},{2,0},{3,1},{4,6},{5,7},{6,4},{7,5},{8,10},{9,11},{10,... | collective-permute-start | bytes 746504 | tf_op jit(solution)/shard_map/ppermute | solution.py:650
  8.7 7.5 %collective-permute-start.7 = (bf16[4,81,512]{2,1,0:T(8,128)(2,1)S(1)}, bf16[4,81,512]{2,1,0:T(8,128)(2,1)S(1)}, u32[]{:S(2)}, u32[]{:S(2)}) collective-permute-start(bf16[4,81,512]{2,1,0:T(8,128)(2,1)S(1)} %pad_maximum_fusion.1.refs_0_.cot), channel_id=1, source_target_pairs={{0,1},{1,0},{2,3},{3,2},{4,5},{5,4},{6,7},{7,6},{8,9},{9,8},{10,11... | collective-permute-start | bytes 995336 | tf_op jit(solution)/shard_map/ppermute | solution.py:650
  8.9 11.1 %collective-permute-start.3 = (bf16[4,81,512]{2,1,0:T(8,128)(2,1)S(1)}, bf16[4,81,512]{2,1,0:T(8,128)(2,1)S(1)}, u32[]{:S(2)}, u32[]{:S(2)}) collective-permute-start(bf16[4,81,512]{2,1,0:T(8,128)(2,1)S(1)} %pad_maximum_fusion.1.refs_0_.cot), channel_id=1, source_target_pairs={{0,2},{1,3},{2,0},{3,1},{4,6},{5,7},{6,4},{7,5},{8,10},{9,11},{10,... | collective-permute-start | bytes 995336 | tf_op jit(solution)/shard_map/ppermute | solution.py:650
  13.8 4.0 %collective-permute-start.4 = (f32[24,128]{1,0:T(8,128)S(1)}, f32[24,128]{1,0:T(8,128)S(1)}, u32[]{:S(2)}, u32[]{:S(2)}) collective-permute-start(f32[24,128]{1,0:T(8,128)S(1)} %get-tuple-element.355.t0), channel_id=1, source_target_pairs={{0,1},{1,0},{2,3},{3,2},{4,5},{5,4},{6,7},{7,6},{8,9},{9,8},{10,11... | collective-permute-start | bytes 36872 | tf_op jit(solution)/shard_map/ppermute | solution.py:650
  14.0 6.0 %collective-permute-start.5 = (f32[24,128]{1,0:T(8,128)S(1)}, f32[24,128]{1,0:T(8,128)S(1)}, u32[]{:S(2)}, u32[]{:S(2)}) collective-permute-start(f32[24,128]{1,0:T(8,128)S(1)} %get-tuple-element.355.t0), channel_id=1, source_target_pairs={{0,2},{1,3},{2,0},{3,1},{4,6},{5,7},{6,4},{7,5},{8,10},{9,11},{10,... | collective-permute-start | bytes 36872 | tf_op jit(solution)/shard_map/ppermute | solution.py:650
  16.2 3.8 %collective-permute-start.6 = (f32[24,128]{1,0:T(8,128)S(1)}, f32[24,128]{1,0:T(8,128)S(1)}, u32[]{:S(2)}, u32[]{:S(2)}) collective-permute-start(f32[24,128]{1,0:T(8,128)S(1)} %get-tuple-element.355.t0), channel_id=1, source_target_pairs={{0,3},{1,2},{2,1},{3,0},{4,7},{5,6},{6,5},{7,4},{8,11},{9,10},{10,... | collective-permute-start | bytes 36872 | tf_op jit(solution)/shard_map/ppermute | solution.py:650
  26.6 7.8 %collective-permute-start.10 = (bf16[128,384]{1,0:T(8,128)(2,1)S(1)}, bf16[128,384]{1,0:T(8,128)(2,1)S(1)}, u32[]{:S(2)}, u32[]{:S(2)}) collective-permute-start(bf16[128,384]{1,0:T(8,128)(2,1)S(1)} %get-tuple-element.368), channel_id=1, source_target_pairs={{0,2},{1,3},{2,0},{3,1},{4,6},{5,7},{6,4},{7,5},{8,10},{9,11},{10,... | collective-permute-start | bytes 294920 | tf_op jit(solution)/shard_map/ppermute | solution.py:650
  30.1 5.1 %collective-permute-start.11 = (bf16[128,384]{1,0:T(8,128)(2,1)S(1)}, bf16[128,384]{1,0:T(8,128)(2,1)S(1)}, u32[]{:S(2)}, u32[]{:S(2)}) collective-permute-start(bf16[128,384]{1,0:T(8,128)(2,1)S(1)} %get-tuple-element.369), channel_id=1, source_target_pairs={{0,3},{1,2},{2,1},{3,0},{4,7},{5,6},{6,5},{7,4},{8,11},{9,10},{10,... | collective-permute-start | bytes 294920 | tf_op jit(solution)/shard_map/ppermute | solution.py:650
  30.7 4.5 %collective-permute-start.9 = (bf16[128,384]{1,0:T(8,128)(2,1)S(1)}, bf16[128,384]{1,0:T(8,128)(2,1)S(1)}, u32[]{:S(2)}, u32[]{:S(2)}) collective-permute-start(bf16[128,384]{1,0:T(8,128)(2,1)S(1)} %get-tuple-element.367), channel_id=1, source_target_pairs={{0,1},{1,0},{2,3},{3,2},{4,5},{5,4},{6,7},{7,6},{8,9},{9,8},{10,11... | collective-permute-start | bytes 294920 | tf_op jit(solution)/shard_map/ppermute | solution.py:650
  31.3 9.8 %collective-permute-start.14 = (bf16[256,384]{1,0:T(8,128)(2,1)S(1)}, bf16[256,384]{1,0:T(8,128)(2,1)S(1)}, u32[]{:S(2)}, u32[]{:S(2)}) collective-permute-start(bf16[256,384]{1,0:T(8,128)(2,1)S(1)} %get-tuple-element.425), channel_id=1, source_target_pairs={{0,4},{4,0},{8,12},{12,8},{16,20},{20,16},{24,28},{28,24},{1,5},{5... | collective-permute-start | bytes 589832 | tf_op jit(solution)/shard_map/ppermute | solution.py:653
  32.8 9.8 %collective-permute-start.15 = (bf16[256,384]{1,0:T(8,128)(2,1)S(1)}, bf16[256,384]{1,0:T(8,128)(2,1)S(1)}, u32[]{:S(2)}, u32[]{:S(2)}) collective-permute-start(bf16[256,384]{1,0:T(8,128)(2,1)S(1)} %get-tuple-element.426), channel_id=1, source_target_pairs={{0,8},{4,12},{8,0},{12,4},{16,24},{20,28},{24,16},{28,20},{1,9},{5... | collective-permute-start | bytes 589832 | tf_op jit(solution)/shard_map/ppermute | solution.py:653
  34.4 9.8 %collective-permute-start.16 = (bf16[256,384]{1,0:T(8,128)(2,1)S(1)}, bf16[256,384]{1,0:T(8,128)(2,1)S(1)}, u32[]{:S(2)}, u32[]{:S(2)}) collective-permute-start(bf16[256,384]{1,0:T(8,128)(2,1)S(1)} %get-tuple-element.427), channel_id=1, source_target_pairs={{0,12},{4,8},{8,4},{12,0},{16,28},{20,24},{24,20},{28,16},{1,13},{... | collective-permute-start | bytes 589832 | tf_op jit(solution)/shard_map/ppermute | solution.py:653
  40.5 5.6 %collective-permute-start.12 = (bf16[6,81,512]{2,1,0:T(8,128)(2,1)S(1)}, bf16[6,81,512]{2,1,0:T(8,128)(2,1)S(1)}, u32[]{:S(2)}, u32[]{:S(2)}) collective-permute-start(bf16[6,81,512]{2,1,0:T(8,128)(2,1)S(1)} %get-tuple-element.423), channel_id=1, source_target_pairs={{0,1},{1,0},{2,3},{3,2},{4,5},{5,4},{6,7},{7,6},{8,9},{9,8},{10,11... | collective-permute-start | bytes 1493000 | tf_op jit(solution)/shard_map/ppermute | solution.py:650
  40.8 8.1 %collective-permute-start.13 = (bf16[6,81,512]{2,1,0:T(8,128)(2,1)S(1)}, bf16[6,81,512]{2,1,0:T(8,128)(2,1)S(1)}, u32[]{:S(2)}, u32[]{:S(2)}) collective-permute-start(bf16[6,81,512]{2,1,0:T(8,128)(2,1)S(1)} %get-tuple-element.424), channel_id=1, source_target_pairs={{0,1},{1,0},{2,3},{3,2},{4,5},{5,4},{6,7},{7,6},{8,9},{9,8},{10,11... | collective-permute-start | bytes 1493000 | tf_op jit(solution)/shard_map/ppermute | solution.py:650
  41.1 8.9 %collective-permute-start.18 = (bf16[160,384]{1,0:T(8,128)(2,1)S(1)}, bf16[160,384]{1,0:T(8,128)(2,1)S(1)}, u32[]{:S(2)}, u32[]{:S(2)}) collective-permute-start(bf16[160,384]{1,0:T(8,128)(2,1)S(1)} %get-tuple-element.438), channel_id=1, source_target_pairs={{0,4},{4,0},{8,12},{12,8},{16,20},{20,16},{24,28},{28,24},{1,5},{5... | collective-permute-start | bytes 368648 | tf_op jit(solution)/shard_map/ppermute | solution.py:653
  42.6 9.1 %collective-permute-start.19 = (bf16[160,384]{1,0:T(8,128)(2,1)S(1)}, bf16[160,384]{1,0:T(8,128)(2,1)S(1)}, u32[]{:S(2)}, u32[]{:S(2)}) collective-permute-start(bf16[160,384]{1,0:T(8,128)(2,1)S(1)} %get-tuple-element.439), channel_id=1, source_target_pairs={{0,8},{4,12},{8,0},{12,4},{16,24},{20,28},{24,16},{28,20},{1,9},{5... | collective-permute-start | bytes 368648 | tf_op jit(solution)/shard_map/ppermute | solution.py:653
  44.2 10.0 %collective-permute-start.20 = (bf16[160,384]{1,0:T(8,128)(2,1)S(1)}, bf16[160,384]{1,0:T(8,128)(2,1)S(1)}, u32[]{:S(2)}, u32[]{:S(2)}) collective-permute-start(bf16[160,384]{1,0:T(8,128)(2,1)S(1)} %get-tuple-element.440), channel_id=1, source_target_pairs={{0,12},{4,8},{8,4},{12,0},{16,28},{20,24},{24,20},{28,16},{1,13},{... | collective-permute-start | bytes 368648 | tf_op jit(solution)/shard_map/ppermute | solution.py:653
  46.2 13.3 %collective-permute-start.22 = (bf16[256,384]{1,0:T(8,128)(2,1)S(1)}, bf16[256,384]{1,0:T(8,128)(2,1)S(1)}, u32[]{:S(2)}, u32[]{:S(2)}) collective-permute-start(bf16[256,384]{1,0:T(8,128)(2,1)S(1)} %add_convert_fusion.2), channel_id=1, source_target_pairs={{0,16},{4,20},{8,24},{12,28},{16,0},{20,4},{24,8},{28,12},{1,17},{... | collective-permute-start | bytes 589832 | tf_op jit(solution)/shard_map/ppermute | solution.py:653
  49.0 20.5 %collective-permute-start.17 = (bf16[6,81,512]{2,1,0:T(8,128)(2,1)S(1)}, bf16[6,81,512]{2,1,0:T(8,128)(2,1)S(1)}, u32[]{:S(2)}, u32[]{:S(2)}) collective-permute-start(bf16[6,81,512]{2,1,0:T(8,128)(2,1)S(1)} %add_convert_fusion), channel_id=1, source_target_pairs={{0,2},{1,3},{2,0},{3,1},{4,6},{5,7},{6,4},{7,5},{8,10},{9,11},{10,... | collective-permute-start | bytes 1493000 | tf_op jit(solution)/shard_map/ppermute | solution.py:650
  54.2 8.0 %collective-permute-start.21 = (bf16[160,384]{1,0:T(8,128)(2,1)S(1)}, bf16[160,384]{1,0:T(8,128)(2,1)S(1)}, u32[]{:S(2)}, u32[]{:S(2)}) collective-permute-start(bf16[160,384]{1,0:T(8,128)(2,1)S(1)} %add_convert_fusion.4), channel_id=1, source_target_pairs={{0,16},{4,20},{8,24},{12,28},{16,0},{20,4},{24,8},{28,12},{1,17},{... | collective-permute-start | bytes 368648 | tf_op jit(solution)/shard_map/ppermute | solution.py:653
  59.6 6.1 %collective-permute-start.24 = (bf16[256,384]{1,0:T(8,128)(2,1)S(1)}, bf16[256,384]{1,0:T(8,128)(2,1)S(1)}, u32[]{:S(2)}, u32[]{:S(2)}) collective-permute-start(bf16[256,384]{1,0:T(8,128)(2,1)S(1)} %add_convert_fusion.1), channel_id=1, source_target_pairs={{0,8},{4,12},{8,0},{12,4},{16,24},{20,28},{24,16},{28,20},{1,9},{5... | collective-permute-start | bytes 589832 | tf_op jit(solution)/shard_map/ppermute | solution.py:653
  62.3 5.6 %collective-permute-start.23 = (bf16[160,384]{1,0:T(8,128)(2,1)S(1)}, bf16[160,384]{1,0:T(8,128)(2,1)S(1)}, u32[]{:S(2)}, u32[]{:S(2)}) collective-permute-start(bf16[160,384]{1,0:T(8,128)(2,1)S(1)} %add_convert_fusion.3), channel_id=1, source_target_pairs={{0,8},{4,12},{8,0},{12,4},{16,24},{20,28},{24,16},{28,20},{1,9},{5... | collective-permute-start | bytes 368648 | tf_op jit(solution)/shard_map/ppermute | solution.py:653
  65.7 10.7 %collective-permute-start.27 = (bf16[2,256,384]{2,1,0:T(8,128)(2,1)S(1)}, bf16[2,256,384]{2,1,0:T(8,128)(2,1)S(1)}, u32[]{:S(2)}, u32[]{:S(2)}) collective-permute-start(bf16[2,256,384]{2,1,0:T(8,128)(2,1)S(1)} %pad_maximum_fusion.refs_0_), channel_id=1, source_target_pairs={{0,4},{1,3},{2,6},{3,1},{4,0},{5,7},{6,2},{7,5},{8,12},{9,11},{10,... | collective-permute-start | bytes 1179656 | tf_op jit(solution)/shard_map/ppermute | solution.py:661
  66.7 10.2 %collective-permute-start.28 = (bf16[2,256,384]{2,1,0:T(8,128)(2,1)S(1)}, bf16[2,256,384]{2,1,0:T(8,128)(2,1)S(1)}, u32[]{:S(2)}, u32[]{:S(2)}) collective-permute-start(bf16[2,256,384]{2,1,0:T(8,128)(2,1)S(1)} %pad_maximum_fusion.refs_0_), channel_id=1, source_target_pairs={{0,2},{1,5},{2,0},{3,7},{4,6},{5,1},{6,4},{7,3},{8,10},{9,13},{10,... | collective-permute-start | bytes 1179656 | tf_op jit(solution)/shard_map/ppermute | solution.py:661
  68.0 11.8 %collective-permute-start.25 = (bf16[2,160,384]{2,1,0:T(8,128)(2,1)S(1)}, bf16[2,160,384]{2,1,0:T(8,128)(2,1)S(1)}, u32[]{:S(2)}, u32[]{:S(2)}) collective-permute-start(bf16[2,160,384]{2,1,0:T(8,128)(2,1)S(1)} %pad_maximum_fusion.2.refs_2_.refs_0_), channel_id=1, source_target_pairs={{0,4},{1,3},{2,6},{3,1},{4,0},{5,7},{6,2},{7,5},{8,12},{9,11},{10,... | collective-permute-start | bytes 737288 | tf_op jit(solution)/shard_map/ppermute | solution.py:661
  69.4 11.5 %collective-permute-start.31 = (bf16[2,256,384]{2,1,0:T(8,128)(2,1)S(1)}, bf16[2,256,384]{2,1,0:T(8,128)(2,1)S(1)}, u32[]{:S(2)}, u32[]{:S(2)}) collective-permute-start(bf16[2,256,384]{2,1,0:T(8,128)(2,1)S(1)} %pad_maximum_fusion.refs_0_), channel_id=1, source_target_pairs={{0,1},{1,0},{2,3},{3,2},{4,5},{5,4},{6,7},{7,6},{8,9},{9,8},{10,11... | collective-permute-start | bytes 1179656 | tf_op jit(solution)/shard_map/ppermute | solution.py:650
  69.4 10.4 %collective-permute-start.26 = (bf16[2,160,384]{2,1,0:T(8,128)(2,1)S(1)}, bf16[2,160,384]{2,1,0:T(8,128)(2,1)S(1)}, u32[]{:S(2)}, u32[]{:S(2)}) collective-permute-start(bf16[2,160,384]{2,1,0:T(8,128)(2,1)S(1)} %pad_maximum_fusion.2.refs_2_.refs_0_), channel_id=1, source_target_pairs={{0,2},{1,5},{2,0},{3,7},{4,6},{5,1},{6,4},{7,3},{8,10},{9,13},{10,... | collective-permute-start | bytes 737288 | tf_op jit(solution)/shard_map/ppermute | solution.py:661
  76.9 4.0 %collective-permute-start.32 = (bf16[2,256,384]{2,1,0:T(8,128)(2,1)S(1)}, bf16[2,256,384]{2,1,0:T(8,128)(2,1)S(1)}, u32[]{:S(2)}, u32[]{:S(2)}) collective-permute-start(bf16[2,256,384]{2,1,0:T(8,128)(2,1)S(1)} %collective-permute-done.27.refs_1_), channel_id=1, source_target_pairs={{0,1},{1,0},{2,3},{3,2},{4,5},{5,4},{6,7},{7,6},{8,9},{9,8},{10,11... | collective-permute-start | bytes 1179656 | tf_op jit(solution)/shard_map/ppermute | solution.py:650
  76.9 7.8 %collective-permute-start.30 = (bf16[2,256,384]{2,1,0:T(8,128)(2,1)S(1)}, bf16[2,256,384]{2,1,0:T(8,128)(2,1)S(1)}, u32[]{:S(2)}, u32[]{:S(2)}) collective-permute-start(bf16[2,256,384]{2,1,0:T(8,128)(2,1)S(1)} %collective-permute-done.27.refs_1_), channel_id=1, source_target_pairs={{0,2},{1,5},{2,0},{3,7},{4,6},{5,1},{6,4},{7,3},{8,10},{9,13},{10,... | collective-permute-start | bytes 1179656 | tf_op jit(solution)/shard_map/ppermute | solution.py:661
  79.8 7.5 %collective-permute-start.29 = (bf16[2,160,384]{2,1,0:T(8,128)(2,1)S(1)}, bf16[2,160,384]{2,1,0:T(8,128)(2,1)S(1)}, u32[]{:S(2)}, u32[]{:S(2)}) collective-permute-start(bf16[2,160,384]{2,1,0:T(8,128)(2,1)S(1)} %collective-permute-done.25.refs_3_.refs_1_), channel_id=1, source_target_pairs={{0,2},{1,5},{2,0},{3,7},{4,6},{5,1},{6,4},{7,3},{8,10},{9,13},{10,... | collective-permute-start | bytes 737288 | tf_op jit(solution)/shard_map/ppermute | solution.py:661
  87.3 2.9 %collective-permute-start.37 = (bf16[2,160,384]{2,1,0:T(8,128)(2,1)S(1)}, bf16[2,160,384]{2,1,0:T(8,128)(2,1)S(1)}, u32[]{:S(2)}, u32[]{:S(2)}) collective-permute-start(bf16[2,160,384]{2,1,0:T(8,128)(2,1)S(1)} %collective-permute-done.29.refs_3_), channel_id=1, source_target_pairs={{0,1},{1,0},{2,3},{3,2},{4,5},{5,4},{6,7},{7,6},{8,9},{9,8},{10,11... | collective-permute-start | bytes 737288 | tf_op jit(solution)/shard_map/ppermute | solution.py:650
  (13 other events, 55.7 us)

commit v5 on v4

--- a/solution.py
+++ b/solution.py
@@ -23,10 +23,10 @@
 
 
 ORDER = (
-    "weights", "a_send", "tick", "stats", "sums", "back", "v_send", "rows", "a_rs", "tick", "rows_core", "v_rs",
-    "a_z2", "v_z2", "a_pair", "tick", "v_pair", "finish", "a_mark", "tick", "v_mark", "tick", "a_twin0", "a_twin1",
-    "a_twin2", "place_head", "a_third", "a_twin3", "v_third", "v_twin3", "v_twin0", "v_twin1", "v_twin2", "tick",
-    "place_most", "place_last",
+    "weights", "a_send", "tick", "stats", "sums", "back", "v_send", "rows", "a_rs", "tick", "tick", "tick",
+    "rows_core", "v_rs", "a_z2", "v_z2", "a_pair", "tick", "v_pair", "finish", "a_mark", "tick", "v_mark", "tick",
+    "a_twin0", "a_twin1", "a_twin2", "place_head", "a_third", "a_twin3", "v_third", "v_twin3", "v_twin0", "v_twin1",
+    "v_twin2", "tick", "place_most", "place_last",
 )
 
 
@@ -506,15 +506,16 @@
         out[shard:, :] = extra[(meta[1] ^ rho) & 3].astype(BF)
 
 
-def rows_body(n, pad, prod, wo, ghu, ghv, wu, wv, keep_a, send_a, keep_b, send_b):
+def rows_body(n, pad, prod, wo, ghu, ghv, wu, wv, keep_a, keep_b, send):
     samples, rows = keep_a.shape[0] // 2, keep_a.shape[1]
-    for r, out in enumerate((keep_a, send_a, keep_b, send_b)):
+    places = ((keep_a, 0), (send, 0), (keep_b, 0), (send, 2 * samples))
+    for r, (out, first) in enumerate(places):
         at = slice(r * samples * pad, (r + 1) * samples * pad)
         branch = dot(prod[at, :], wo[...], 1, 0)
         grad = dot(ghu[at, :], wu[...], 1, 1) + dot(ghv[at, :], wv[...], 1, 1)
         for i in range(samples):
-            out[i] = branch[i * pad : i * pad + rows, :].astype(BF)
-            out[samples + i] = grad[i * pad : i * pad + rows, :].astype(BF)
+            out[first + i] = branch[i * pad : i * pad + rows, :].astype(BF)
+            out[first + samples + i] = grad[i * pad : i * pad + rows, :].astype(BF)
 
 
 def finish_rows_body(meta, tok, cot, keep, got_a, got_b, g1, output, grad_tokens):
@@ -704,6 +705,7 @@
         seq, dp = lax.axis_index("seq"), lax.axis_index("dp")
         meta = jnp.concatenate([seq[None], dp[None], res_class, skip_mask]).astype(jnp.int32)
         step = ordered()
+        clock = jnp.zeros((8, 128), F32)
 
         def tick(clock):
             return call(tick_body, [shape_of(clock.shape, F32)], [clock], flops=4 * 10**9, name="tick")[0]
@@ -770,7 +772,6 @@
             )
 
         (flipped,) = step(flip, *normed)
-        stats = step(None, stats)
         c2 = step(None, c2)
         c3 = over_seq(c2, 1)
         gb1, gp1, gs1, sp1 = step(functools.partial(front, 2, 1), meta, c2, wo, gu1, pm)
@@ -787,6 +788,7 @@
                 name="prepare",
             )
 
+        clock = step(tick, clock)
         gb2, gp2, gs, gmix, sp = step(prepare, meta, c3, wo, gu2, pm, gs0, gs1, sp0, sp1)
 
         def spatial_unit(*ins):
@@ -806,7 +808,6 @@
                 name="spatial",
             )
 
-        clock = jnp.zeros((8, 128), F32)
         prod, ghu, cols, st2, edge, *messages = step(
             spatial_unit, meta, v0, v1, v2, gu0, gu1, gu2, dgu0, dgu1, dgu2, sp, gp0, gp1, gp2, gs, pm,
             gmix, g2, s2, *stats,
@@ -843,8 +844,9 @@
             )
 
         def rows_out(*ins):
-            shape = shape_of((2 * samples, rows, width), BF)
-            return call(functools.partial(rows_body, n, pad), [shape] * 4, ins, name="rows_out")
+            shape = (2 * samples, rows, width)
+            outs = [shape_of(s, BF) for s in (shape, shape, (4 * samples, rows, width))]
+            return call(functools.partial(rows_body, n, pad), outs, ins, name="rows_out")
 
         def finish_rows(*ins):
             shape = shape_of(tokens.shape, BF)
@@ -929,12 +931,11 @@
             reduce_start("v", step(None, x["v_shards"]))
 
         def ev_rows():
-            x["r_a"], send_a, x["r_b"], send_b = step(rows_out, prod, wo, ghu, x["ghv"], wu, wv)
-            x["r_got"], x["r_got_b"] = twin(send_a), twin(send_b)
+            x["r_a"], x["r_b"], send = step(rows_out, prod, wo, ghu, x["ghv"], wu, wv)
+            x["r_got"] = twin(send)
 
         def ev_rows_core():
-            x["r_got"], x["r_got_b"] = step(None, (x["r_got"], x["r_got_b"]))
-            x["r_last"] = over_seq(step(add, x["r_b"], x["r_got_b"]), 2)
+            x["r_last"] = over_seq(step(lambda a, b: add(a, b[2 * samples :]), x["r_b"], x["r_got"]), 2)
 
         def ev_finish():
             x["output"], x["grad_tokens"] = step(

time: 92.2 us -> 90.9 us (0.986)
  waiting for transfers between devices: 26.5 us -> 23.4 us
  starting transfers between devices: 30.7 us -> 32.9 us
    ppermute x10, starting transfers between devices: 13 us -> 16.5 us  [over_dp(): return lax.ppermute(x, 'dp', [(i, i ^ flip) for i in range(m)])]
    ppermute x10, waiting for transfers between devices: 13.6 us -> 11.1 us  [over_dp(): return lax.ppermute(x, 'dp', [(i, i ^ flip) for i in range(m)])]
    ppermute x23 -> x22, starting transfers between devices: 11.1 us -> 10.1 us  [over_seq(): return lax.ppermute(x, 'seq', [(i, i ^ flip) for i in range(n)])]
    ppermute x23 -> x22, waiting for transfers between devices: 4.4 us -> 4.55 us  [over_seq(): return lax.ppermute(x, 'seq', [(i, i ^ flip) for i in range(n)])]
    pallas_call x22 -> x25, Pallas kernels: 28.4 us -> 28.5 us  [call(): pl.pallas_call(body, out_shape=outs, in_specs=specs if specs is not None...]
  transfers between devices with their start and end apart: 39 -> 38, of which waited for: 16 -> 17; matrix products, arithmetic and copies ran while one was open for 6% -> 5% of each run, Pallas kernels for 24% -> 26%
where the time goes in v5:
time: 90.9 us; the launch traced here: 90.6 us
  starting transfers between devices  32.9 us (36%)
  Pallas kernels  28.5 us (31%)
  waiting for transfers between devices  23.4 us (26%)
  other arithmetic  3.23 us (4%)
  local copies, waits for them, and re-layouts  1.55 us (2%)
  between operations  1.13 us (1%)
    pallas_call x25, Pallas kernels, call(): pl.pallas_call(body, out_shape=outs, in_specs=specs if specs is not None...  28.5 us
    ppermute x10, starting transfers between devices, over_dp(): return lax.ppermute(x, 'dp', [(i, i ^ flip) for i in range(m)])  16.5 us
    ppermute x10, waiting for transfers between devices, over_dp(): return lax.ppermute(x, 'dp', [(i, i ^ flip) for i in range(m)])  11.1 us
    ppermute x22, starting transfers between devices, over_seq(): return lax.ppermute(x, 'seq', [(i, i ^ flip) for i in range(n)])  10.1 us
    ppermute x6, waiting for transfers between devices, mixed_axes(): return lax.ppermute(x, ('dp', 'seq'), pairs)  7.75 us
    ppermute x6, starting transfers between devices, mixed_axes(): return lax.ppermute(x, ('dp', 'seq'), pairs)  6.31 us
    ppermute x22, waiting for transfers between devices, over_seq(): return lax.ppermute(x, 'seq', [(i, i ^ flip) for i in range(n)])  4.55 us
  transfers between devices with their start and end apart: 38, of which 17 were waited for; matrix products, arithmetic and copies ran while one was open for 5% of the time, Pallas kernels for 26%

profile of v5, /device:TPU:0, one launch (start us, length us, event | category | flops | bytes accessed | tf_op | source)
XLA Modules:
  0.0 90.6 jit_solution(15787542524965295408)
XLA Ops:
  1.2 2.6 %collective-permute-start.1 = (bf16[3,81,512]{2,1,0:T(8,128)(2,1)}, bf16[3,81,512]{2,1,0:T(8,128)(2,1)S(1)}, u32[]{:S(2)}, u32[]{:S(2)}) collective-permute-start(bf16[3,81,512]{2,1,0:T(8,128)(2,1)} %tok), channel_id=1, source_target_pairs={{0,2},{1,3},{2,0},{3,1},{4,6},{5,7},{6,4},{7,5},{8,10},{9,11},{10,... | collective-permute-start | bytes 746504 | tf_op jit(solution)/shard_map/ppermute | solution.py:651
  6.9 1.2 %constant_dynamic-slice_fusion.1 = (bf16[512,384]{1,0:T(8,128)(2,1)S(1)}, bf16[512,384]{1,0:T(8,128)(2,1)S(1)}) fusion(bf16[512,3072]{1,0:T(8,128)(2,1)} %param.15, s32[]{:T(128)S(6)} %select_n.10, s32[]{:T(128)S(6)} %select_n.9), kind=kLoop, calls=%fused_computation.16 | loop fusion | bytes 1572872 | tf_op jit(solution)/shard_map/dynamic_slice | solution.py:728
  8.6 1.8 %project.3 = (bf16[576,512]{1,0:T(8,128)(2,1)S(1)}, bf16[576,384]{1,0:T(8,128)(2,1)S(1)}, bf16[576,384]{1,0:T(8,128)(2,1)S(1)}, f32[576,384]{1,0:T(8,128)S(1)}, ...) custom-call(bf16[3,81,512]{2,1,0:T(8,128)(2,1)S(1)} %copy-done.1, ...), custom_call_target="tpu_custom_call" | custom-call | flops 1 | bytes 1 | tf_op jit(solution)/shard_map/project/pallas_call | solution.py:50
  12.6 1.1 %project.5 = (bf16[288,512]{1,0:T(8,128)(2,1)S(1)}, bf16[288,384]{1,0:T(8,128)(2,1)S(1)}, bf16[288,384]{1,0:T(8,128)(2,1)S(1)}, f32[288,384]{1,0:T(8,128)S(1)}, ...) custom-call(bf16[3,81,512]{2,1,0:T(8,128)(2,1)S(1)} %collective-permute-done.2.refs_0_, f32[1,512]{1,0:T(1,128)S(1)} %bitcast.18, ...), custom_call_target="tpu_custom_call" | custom-call | flops 1 | bytes 1 | tf_op jit(solution)/shard_map/project/pallas_call | solution.py:50
  13.9 2.2 %collective-permute-start.7 = (f32[24,128]{1,0:T(8,128)S(1)}, f32[24,128]{1,0:T(8,128)S(1)}, u32[]{:S(2)}, u32[]{:S(2)}) collective-permute-start(f32[24,128]{1,0:T(8,128)S(1)} %get-tuple-element.346.t0), channel_id=1, source_target_pairs={{0,2},{1,3},{2,0},{3,1},{4,6},{5,7},{6,4},{7,5},{8,10},{9,11},{10,... | collective-permute-start | bytes 36872 | tf_op jit(solution)/shard_map/ppermute | solution.py:651
  16.2 1.2 %front.2 = (bf16[576,512]{1,0:T(8,128)(2,1)S(1)}, f32[576,384]{1,0:T(8,128)S(1)}, bf16[576,384]{1,0:T(8,128)(2,1)S(1)}, bf16[192,384]{1,0:T(8,128)(2,1)S(1)}, bf16[384,384]{1,0:T(8,128)(2,1)S(1)}) custom-call(s32[8]{0:T(128)S(1)} %pad_add_fusion.meta, bf16[4,81,512]{2,1,0:T(8,128)(2,1)S(1)} %pad_maximum_fusion.1.refs_0_.cot, ...), custom_call_target="tpu_custom_call" | custom-call | flops 1 | bytes 1 | tf_op jit(solution)/shard_map/front/pallas_call | solution.py:50
  17.7 1.4 %collective-permute-done.3.refs_0_ = bf16[4,81,512]{2,1,0:T(8,128)(2,1)S(1)} collective-permute-done((bf16[4,81,512]{2,1,0:T(8,128)(2,1)S(1)}, bf16[4,81,512]{2,1,0:T(8,128)(2,1)S(1)}, u32[]{:S(2)}, u32[]{:S(2)}) %collective-permute-start.3) | collective-permute-done | bytes 331808 | tf_op jit(solution)/shard_map/ppermute | solution.py:651
  20.8 1.5 %prepare.1 = (bf16[288,512]{1,0:T(8,128)(2,1)S(1)}, f32[288,384]{1,0:T(8,128)S(1)}, bf16[384,1152]{1,0:T(8,128)(2,1)S(1)}, f32[1152,384]{1,0:T(8,128)S(1)}, bf16[384,384]{1,0:T(8,128)(2,1)S(1)}) custom-call(s32[8]{0:T(128)S(1)} %pad_add_fusion.meta, bf16[4,81,512]{2,1,0:T(8,128)(2,1)S(1)} %collective-permute-done.5.c3, ...), custom_call_target="tpu_custom_call" | custom-call | flops 1 | bytes 1 | tf_op jit(solution)/shard_map/prepare/pallas_call | solution.py:50
  22.3 3.4 %spatial.1 = (bf16[1152,384]{1,0:T(8,128)(2,1)S(1)}, bf16[1152,384]{1,0:T(8,128)(2,1)S(1)}, f32[128,128]{1,0:T(8,128)S(1)}, f32[24,128]{1,0:T(8,128)S(1)}, bf16[...) custom-call(s32[8]{0:T(128)S(1)} %pad_add_fusion.meta, ...), custom_call_target="tpu_custom_call" | custom-call | flops 1 | bytes 1 | tf_op jit(solution)/shard_map/spatial/pallas_call | solution.py:50
  25.8 1.7 %collective-permute-start.10 = (bf16[128,384]{1,0:T(8,128)(2,1)S(1)}, bf16[128,384]{1,0:T(8,128)(2,1)S(1)}, u32[]{:S(2)}, u32[]{:S(2)}) collective-permute-start(bf16[128,384]{1,0:T(8,128)(2,1)S(1)} %get-tuple-element.359), channel_id=1, source_target_pairs={{0,2},{1,3},{2,0},{3,1},{4,6},{5,7},{6,4},{7,5},{8,10},{9,11},{10,... | collective-permute-start | bytes 294920 | tf_op jit(solution)/shard_map/ppermute | solution.py:651
  27.5 2.4 %weights.1 = (bf16[256,384]{1,0:T(8,128)(2,1)S(1)}, bf16[256,384]{1,0:T(8,128)(2,1)S(1)}, bf16[256,384]{1,0:T(8,128)(2,1)S(1)}, bf16[256,384]{1,0:T(8,128)(2,1)S(1)}, f32[512,384]{1,0:T(8,128)S(1)}) custom-call(s32[8]{0:T(128)S(1)} %pad_add_fusion.meta, bf16[1152,384]{1,0:T(8,128)(2,1)S(1)} %get-tuple-element.407.prod, ...), custom_call_target="tpu_custom_call" | custom-call | flops 1 | bytes 1 | tf_op jit(solution)/shard_map/weights/pallas_call | solution.py:50
  30.5 1.5 %collective-permute-start.13 = (bf16[256,384]{1,0:T(8,128)(2,1)S(1)}, bf16[256,384]{1,0:T(8,128)(2,1)S(1)}, u32[]{:S(2)}, u32[]{:S(2)}) collective-permute-start(bf16[256,384]{1,0:T(8,128)(2,1)S(1)} %get-tuple-element.416), channel_id=1, source_target_pairs={{0,4},{4,0},{8,12},{12,8},{16,20},{20,16},{24,28},{28,24},{1,5},{5... | collective-permute-start | bytes 589832 | tf_op jit(solution)/shard_map/ppermute | solution.py:654
  32.0 1.6 %collective-permute-start.14 = (bf16[256,384]{1,0:T(8,128)(2,1)S(1)}, bf16[256,384]{1,0:T(8,128)(2,1)S(1)}, u32[]{:S(2)}, u32[]{:S(2)}) collective-permute-start(bf16[256,384]{1,0:T(8,128)(2,1)S(1)} %get-tuple-element.417), channel_id=1, source_target_pairs={{0,8},{4,12},{8,0},{12,4},{16,24},{20,28},{24,16},{28,20},{1,9},{5... | collective-permute-start | bytes 589832 | tf_op jit(solution)/shard_map/ppermute | solution.py:654
  35.5 2.9 %back.1 = (bf16[1152,384]{1,0:T(8,128)(2,1)S(1)}, bf16[160,384]{1,0:T(8,128)(2,1)S(1)}, bf16[160,384]{1,0:T(8,128)(2,1)S(1)}, bf16[160,384]{1,0:T(8,128)(2,1)S(1)}, bf16[160,384]{1,0:T(8,128)(2,1)S(1)}) custom-call(s32[8]{0:T(128)S(1)} %pad_add_fusion.meta, f32[1152,384]{1,0:T(8,128)S(1)} %get-tuple-element.382.gmix, f32[576,384]{1,0:T(8,128)S(1)} %get-tuple-element.383.v0, ...), custom_call_target="tpu_custom_call" | custom-call | flops 1 | bytes 1 | tf_op jit(solution)/shard_map/back/pallas_call | solution.py:50
  38.4 2.0 %rows_out.1 = (bf16[6,81,512]{2,1,0:T(8,128)(2,1)S(1)}, bf16[6,81,512]{2,1,0:T(8,128)(2,1)S(1)}, bf16[12,81,512]{2,1,0:T(8,128)(2,1)S(1)}) custom-call(bf16[1152,384]{1,0:T(8,128)(2,1)S(1)} %get-tuple-element.407.prod, bf16[384,512]{1,0:T(8,128)(2,1)S(1)} %constant_dynamic-slice_fusion.refs_2_.refs_1_.wo, ...), custom_call_target="tpu_custom_call" | custom-call | flops 1 | bytes 1 | tf_op jit(solution)/shard_map/rows_out/pallas_call | solution.py:50
  40.7 1.5 %collective-permute-start.17 = (bf16[160,384]{1,0:T(8,128)(2,1)S(1)}, bf16[160,384]{1,0:T(8,128)(2,1)S(1)}, u32[]{:S(2)}, u32[]{:S(2)}) collective-permute-start(bf16[160,384]{1,0:T(8,128)(2,1)S(1)} %get-tuple-element.426), channel_id=1, source_target_pairs={{0,4},{4,0},{8,12},{12,8},{16,20},{20,16},{24,28},{28,24},{1,5},{5... | collective-permute-start | bytes 368648 | tf_op jit(solution)/shard_map/ppermute | solution.py:654
  42.2 1.6 %collective-permute-start.18 = (bf16[160,384]{1,0:T(8,128)(2,1)S(1)}, bf16[160,384]{1,0:T(8,128)(2,1)S(1)}, u32[]{:S(2)}, u32[]{:S(2)}) collective-permute-start(bf16[160,384]{1,0:T(8,128)(2,1)S(1)} %get-tuple-element.427), channel_id=1, source_target_pairs={{0,8},{4,12},{8,0},{12,4},{16,24},{20,28},{24,16},{28,20},{1,9},{5... | collective-permute-start | bytes 368648 | tf_op jit(solution)/shard_map/ppermute | solution.py:654
  44.3 2.7 %collective-permute-start.21 = (bf16[256,384]{1,0:T(8,128)(2,1)S(1)}, bf16[256,384]{1,0:T(8,128)(2,1)S(1)}, u32[]{:S(2)}, u32[]{:S(2)}) collective-permute-start(bf16[256,384]{1,0:T(8,128)(2,1)S(1)} %add_convert_fusion.2), channel_id=1, source_target_pairs={{0,16},{4,20},{8,24},{12,28},{16,0},{20,4},{24,8},{28,12},{1,17},{... | collective-permute-start | bytes 589832 | tf_op jit(solution)/shard_map/ppermute | solution.py:654
  47.7 4.9 %collective-permute-done.18 = bf16[160,384]{1,0:T(8,128)(2,1)S(1)} collective-permute-done((bf16[160,384]{1,0:T(8,128)(2,1)S(1)}, bf16[160,384]{1,0:T(8,128)(2,1)S(1)}, u32[]{:S(2)}, u32[]{:S(2)}) %collective-permute-start.18) | collective-permute-done | bytes 122912 | tf_op jit(solution)/shard_map/ppermute | solution.py:654
  52.5 1.4 %collective-permute-done.19 = bf16[160,384]{1,0:T(8,128)(2,1)S(1)} collective-permute-done((bf16[160,384]{1,0:T(8,128)(2,1)S(1)}, bf16[160,384]{1,0:T(8,128)(2,1)S(1)}, u32[]{:S(2)}, u32[]{:S(2)}) %collective-permute-start.19) | collective-permute-done | bytes 122912 | tf_op jit(solution)/shard_map/ppermute | solution.py:654
  54.5 6.1 %collective-permute-start.23 = (bf16[256,384]{1,0:T(8,128)(2,1)S(1)}, bf16[256,384]{1,0:T(8,128)(2,1)S(1)}, u32[]{:S(2)}, u32[]{:S(2)}) collective-permute-start(bf16[256,384]{1,0:T(8,128)(2,1)S(1)} %add_convert_fusion.1), channel_id=1, source_target_pairs={{0,8},{4,12},{8,0},{12,4},{16,24},{20,28},{24,16},{28,20},{1,9},{5... | collective-permute-start | bytes 589832 | tf_op jit(solution)/shard_map/ppermute | solution.py:654
  62.0 3.1 %collective-permute-done.23 = bf16[256,384]{1,0:T(8,128)(2,1)S(1)} collective-permute-done((bf16[256,384]{1,0:T(8,128)(2,1)S(1)}, bf16[256,384]{1,0:T(8,128)(2,1)S(1)}, u32[]{:S(2)}, u32[]{:S(2)}) %collective-permute-start.23) | collective-permute-done | bytes 196640 | tf_op jit(solution)/shard_map/ppermute | solution.py:654
  67.0 1.6 %collective-permute-start.24 = (bf16[2,160,384]{2,1,0:T(8,128)(2,1)S(1)}, bf16[2,160,384]{2,1,0:T(8,128)(2,1)S(1)}, u32[]{:S(2)}, u32[]{:S(2)}) collective-permute-start(bf16[2,160,384]{2,1,0:T(8,128)(2,1)S(1)} %pad_maximum_fusion.2.refs_2_.refs_0_), channel_id=1, source_target_pairs={{0,4},{1,3},{2,6},{3,1},{4,0},{5,7},{6,2},{7,5},{8,12},{9,11},{10,... | collective-permute-start | bytes 737288 | tf_op jit(solution)/shard_map/ppermute | solution.py:662
  69.4 1.8 %finish_rows.1 = (bf16[3,81,512]{2,1,0:T(8,128)(2,1)}, bf16[3,81,512]{2,1,0:T(8,128)(2,1)}) custom-call(s32[8]{0:T(128)S(1)} %pad_add_fusion.meta, bf16[3,81,512]{2,1,0:T(8,128)(2,1)S(1)} %copy-done.1, bf16[4,81,512]{2,1,0:T(8,128)(2,1)S(1)} %pad_maximum_fusion.1.refs_0_.cot, bf16[6,81,512]{2,1,0:T(8,128)(2,1)S(1)} %get-tuple-element.445.keep, ...), custom_call_target="tpu_custom_call" | custom-call | flops 1 | bytes 1 | tf_op jit(solution)/shard_map/finish_rows/pallas_call | solution.py:50
  71.3 3.8 %collective-permute-done.26.refs_1_ = bf16[2,256,384]{2,1,0:T(8,128)(2,1)S(1)} collective-permute-done((bf16[2,256,384]{2,1,0:T(8,128)(2,1)S(1)}, bf16[2,256,384]{2,1,0:T(8,128)(2,1)S(1)}, u32[]{:S(2)}, u32[]{:S(2)}) %collective-permute-start.26) | collective-permute-done | bytes 393248 | tf_op jit(solution)/shard_map/ppermute | solution.py:662
  75.5 1.2 %collective-permute-start.29 = (bf16[2,256,384]{2,1,0:T(8,128)(2,1)S(1)}, bf16[2,256,384]{2,1,0:T(8,128)(2,1)S(1)}, u32[]{:S(2)}, u32[]{:S(2)}) collective-permute-start(bf16[2,256,384]{2,1,0:T(8,128)(2,1)S(1)} %collective-permute-done.26.refs_1_), channel_id=1, source_target_pairs={{0,2},{1,5},{2,0},{3,7},{4,6},{5,1},{6,4},{7,3},{8,10},{9,13},{10,... | collective-permute-start | bytes 1179656 | tf_op jit(solution)/shard_map/ppermute | solution.py:662
  76.7 1.8 %collective-permute-done.24.refs_3_.refs_1_ = bf16[2,160,384]{2,1,0:T(8,128)(2,1)S(1)} collective-permute-done((bf16[2,160,384]{2,1,0:T(8,128)(2,1)S(1)}, bf16[2,160,384]{2,1,0:T(8,128)(2,1)S(1)}, u32[]{:S(2)}, u32[]{:S(2)}) %collective-permute-start.24) | collective-permute-done | bytes 245792 | tf_op jit(solution)/shard_map/ppermute | solution.py:662
  78.5 1.5 %collective-permute-start.28 = (bf16[2,160,384]{2,1,0:T(8,128)(2,1)S(1)}, bf16[2,160,384]{2,1,0:T(8,128)(2,1)S(1)}, u32[]{:S(2)}, u32[]{:S(2)}) collective-permute-start(bf16[2,160,384]{2,1,0:T(8,128)(2,1)S(1)} %collective-permute-done.24.refs_3_.refs_1_), channel_id=1, source_target_pairs={{0,2},{1,5},{2,0},{3,7},{4,6},{5,1},{6,4},{7,3},{8,10},{9,13},{10,... | collective-permute-start | bytes 737288 | tf_op jit(solution)/shard_map/ppermute | solution.py:662
  80.2 3.0 %place.2 = (f32[512,3072]{1,0:T(8,128)}, f32[1536,512]{1,0:T(8,128)}) custom-call(s32[8]{0:T(128)S(1)} %pad_add_fusion.meta, bf16[2,256,384]{2,1,0:T(8,128)(2,1)S(1)} %pad_maximum_fusion.refs_0_, bf16[2,256,384]{2,1,0:T(8,128)(2,1)S(1)} %collective-permute-done.26.refs_1_, bf16[2,256,384]{2,1,0:T(8,128)(2,1)S(1)} %collective-permute-done.27.refs_2_, ...), custom_call_target="tpu_custom_call" | custom-call | flops 1 | bytes 1 | tf_op jit(solution)/shard_map/place/pallas_call | solution.py:50
  84.3 1.6 %collective-permute-done.28.refs_3_ = bf16[2,160,384]{2,1,0:T(8,128)(2,1)S(1)} collective-permute-done((bf16[2,160,384]{2,1,0:T(8,128)(2,1)S(1)}, bf16[2,160,384]{2,1,0:T(8,128)(2,1)S(1)}, u32[]{:S(2)}, u32[]{:S(2)}) %collective-permute-start.28) | collective-permute-done | bytes 245792 | tf_op jit(solution)/shard_map/ppermute | solution.py:662
  86.1 2.7 %place.3 = (f32[512,3072]{1,0:T(8,128)}, f32[1536,512]{1,0:T(8,128)}) custom-call(s32[8]{0:T(128)S(1)} %pad_add_fusion.meta, bf16[2,256,384]{2,1,0:T(8,128)(2,1)S(1)} %collective-permute-done.29.refs_0_, bf16[2,256,384]{2,1,0:T(8,128)(2,1)S(1)} %collective-permute-done.37.refs_1_, ...), custom_call_target="tpu_custom_call", output_to_operand_aliasing={{0}: (9, {}), {1}: (10, {})} | custom-call | flops 1 | bytes 1 | tf_op jit(solution)/shard_map/place/pallas_call | solution.py:50
  88.8 1.6 %place_last.1 = (f32[512,3072]{1,0:T(8,128)}, f32[81,324]{1,0:T(8,128)}, f32[81]{0:T(128)}, f32[512]{0:T(512)}, f32[512]{0:T(512)}, /*index=5*/f32[1536]{0:T(1024)}, f32[1536]{0:T(1024)}) custom-call(s32[8]{0:T(128)S(1)} %pad_add_fusion.meta, bf16[2,160,384]{2,1,0:T(8,128)(2,1)S(1)} %pad_maximum_fusion.2.refs_2_.refs_0_, ...), custom_call_target="tpu_custom_call", output_to_operand_aliasing={{0}: (9, {})} | custom-call | flops 1 | bytes 1 | tf_op jit(solution)/shard_map/place_last/pallas_call | solution.py:50
  (101 shorter events, 18.8 us)
Async XLA Ops:
  0.7 7.4 %collective-permute-start = (bf16[3,81,512]{2,1,0:T(8,128)(2,1)}, bf16[3,81,512]{2,1,0:T(8,128)(2,1)S(1)}, u32[]{:S(2)}, u32[]{:S(2)}) collective-permute-start(bf16[3,81,512]{2,1,0:T(8,128)(2,1)} %tok), channel_id=1, source_target_pairs={{0,1},{1,0},{2,3},{3,2},{4,5},{5,4},{6,7},{7,6},{8,9},{9,8},{10,11... | collective-permute-start | bytes 746504 | tf_op jit(solution)/shard_map/ppermute | solution.py:651
  1.2 9.9 %collective-permute-start.1 = (bf16[3,81,512]{2,1,0:T(8,128)(2,1)}, bf16[3,81,512]{2,1,0:T(8,128)(2,1)S(1)}, u32[]{:S(2)}, u32[]{:S(2)}) collective-permute-start(bf16[3,81,512]{2,1,0:T(8,128)(2,1)} %tok), channel_id=1, source_target_pairs={{0,2},{1,3},{2,0},{3,1},{4,6},{5,7},{6,4},{7,5},{8,10},{9,11},{10,... | collective-permute-start | bytes 746504 | tf_op jit(solution)/shard_map/ppermute | solution.py:651
  8.1 8.1 %collective-permute-start.4 = (bf16[4,81,512]{2,1,0:T(8,128)(2,1)S(1)}, bf16[4,81,512]{2,1,0:T(8,128)(2,1)S(1)}, u32[]{:S(2)}, u32[]{:S(2)}) collective-permute-start(bf16[4,81,512]{2,1,0:T(8,128)(2,1)S(1)} %pad_maximum_fusion.1.refs_0_.cot), channel_id=1, source_target_pairs={{0,1},{1,0},{2,3},{3,2},{4,5},{5,4},{6,7},{7,6},{8,9},{9,8},{10,11... | collective-permute-start | bytes 995336 | tf_op jit(solution)/shard_map/ppermute | solution.py:651
  8.3 10.8 %collective-permute-start.3 = (bf16[4,81,512]{2,1,0:T(8,128)(2,1)S(1)}, bf16[4,81,512]{2,1,0:T(8,128)(2,1)S(1)}, u32[]{:S(2)}, u32[]{:S(2)}) collective-permute-start(bf16[4,81,512]{2,1,0:T(8,128)(2,1)S(1)} %pad_maximum_fusion.1.refs_0_.cot), channel_id=1, source_target_pairs={{0,2},{1,3},{2,0},{3,1},{4,6},{5,7},{6,4},{7,5},{8,10},{9,11},{10,... | collective-permute-start | bytes 995336 | tf_op jit(solution)/shard_map/ppermute | solution.py:651
  13.8 8.5 %collective-permute-start.6 = (f32[24,128]{1,0:T(8,128)S(1)}, f32[24,128]{1,0:T(8,128)S(1)}, u32[]{:S(2)}, u32[]{:S(2)}) collective-permute-start(f32[24,128]{1,0:T(8,128)S(1)} %get-tuple-element.346.t0), channel_id=1, source_target_pairs={{0,1},{1,0},{2,3},{3,2},{4,5},{5,4},{6,7},{7,6},{8,9},{9,8},{10,11... | collective-permute-start | bytes 36872 | tf_op jit(solution)/shard_map/ppermute | solution.py:651
  13.9 8.4 %collective-permute-start.7 = (f32[24,128]{1,0:T(8,128)S(1)}, f32[24,128]{1,0:T(8,128)S(1)}, u32[]{:S(2)}, u32[]{:S(2)}) collective-permute-start(f32[24,128]{1,0:T(8,128)S(1)} %get-tuple-element.346.t0), channel_id=1, source_target_pairs={{0,2},{1,3},{2,0},{3,1},{4,6},{5,7},{6,4},{7,5},{8,10},{9,11},{10,... | collective-permute-start | bytes 36872 | tf_op jit(solution)/shard_map/ppermute | solution.py:651
  16.2 6.1 %collective-permute-start.8 = (f32[24,128]{1,0:T(8,128)S(1)}, f32[24,128]{1,0:T(8,128)S(1)}, u32[]{:S(2)}, u32[]{:S(2)}) collective-permute-start(f32[24,128]{1,0:T(8,128)S(1)} %get-tuple-element.346.t0), channel_id=1, source_target_pairs={{0,3},{1,2},{2,1},{3,0},{4,7},{5,6},{6,5},{7,4},{8,11},{9,10},{10,... | collective-permute-start | bytes 36872 | tf_op jit(solution)/shard_map/ppermute | solution.py:651
  25.8 7.8 %collective-permute-start.10 = (bf16[128,384]{1,0:T(8,128)(2,1)S(1)}, bf16[128,384]{1,0:T(8,128)(2,1)S(1)}, u32[]{:S(2)}, u32[]{:S(2)}) collective-permute-start(bf16[128,384]{1,0:T(8,128)(2,1)S(1)} %get-tuple-element.359), channel_id=1, source_target_pairs={{0,2},{1,3},{2,0},{3,1},{4,6},{5,7},{6,4},{7,5},{8,10},{9,11},{10,... | collective-permute-start | bytes 294920 | tf_op jit(solution)/shard_map/ppermute | solution.py:651
  29.9 5.1 %collective-permute-start.11 = (bf16[128,384]{1,0:T(8,128)(2,1)S(1)}, bf16[128,384]{1,0:T(8,128)(2,1)S(1)}, u32[]{:S(2)}, u32[]{:S(2)}) collective-permute-start(bf16[128,384]{1,0:T(8,128)(2,1)S(1)} %get-tuple-element.360), channel_id=1, source_target_pairs={{0,3},{1,2},{2,1},{3,0},{4,7},{5,6},{6,5},{7,4},{8,11},{9,10},{10,... | collective-permute-start | bytes 294920 | tf_op jit(solution)/shard_map/ppermute | solution.py:651
  30.0 5.1 %collective-permute-start.9 = (bf16[128,384]{1,0:T(8,128)(2,1)S(1)}, bf16[128,384]{1,0:T(8,128)(2,1)S(1)}, u32[]{:S(2)}, u32[]{:S(2)}) collective-permute-start(bf16[128,384]{1,0:T(8,128)(2,1)S(1)} %get-tuple-element.358), channel_id=1, source_target_pairs={{0,1},{1,0},{2,3},{3,2},{4,5},{5,4},{6,7},{7,6},{8,9},{9,8},{10,11... | collective-permute-start | bytes 294920 | tf_op jit(solution)/shard_map/ppermute | solution.py:651
  30.5 11.7 %collective-permute-start.13 = (bf16[256,384]{1,0:T(8,128)(2,1)S(1)}, bf16[256,384]{1,0:T(8,128)(2,1)S(1)}, u32[]{:S(2)}, u32[]{:S(2)}) collective-permute-start(bf16[256,384]{1,0:T(8,128)(2,1)S(1)} %get-tuple-element.416), channel_id=1, source_target_pairs={{0,4},{4,0},{8,12},{12,8},{16,20},{20,16},{24,28},{28,24},{1,5},{5... | collective-permute-start | bytes 589832 | tf_op jit(solution)/shard_map/ppermute | solution.py:654
  32.0 11.8 %collective-permute-start.14 = (bf16[256,384]{1,0:T(8,128)(2,1)S(1)}, bf16[256,384]{1,0:T(8,128)(2,1)S(1)}, u32[]{:S(2)}, u32[]{:S(2)}) collective-permute-start(bf16[256,384]{1,0:T(8,128)(2,1)S(1)} %get-tuple-element.417), channel_id=1, source_target_pairs={{0,8},{4,12},{8,0},{12,4},{16,24},{20,28},{24,16},{28,20},{1,9},{5... | collective-permute-start | bytes 589832 | tf_op jit(solution)/shard_map/ppermute | solution.py:654
  33.6 10.6 %collective-permute-start.15 = (bf16[256,384]{1,0:T(8,128)(2,1)S(1)}, bf16[256,384]{1,0:T(8,128)(2,1)S(1)}, u32[]{:S(2)}, u32[]{:S(2)}) collective-permute-start(bf16[256,384]{1,0:T(8,128)(2,1)S(1)} %get-tuple-element.418), channel_id=1, source_target_pairs={{0,12},{4,8},{8,4},{12,0},{16,28},{20,24},{24,20},{28,16},{1,13},{... | collective-permute-start | bytes 589832 | tf_op jit(solution)/shard_map/ppermute | solution.py:654
  40.4 6.5 %collective-permute-start.12 = (bf16[12,81,512]{2,1,0:T(8,128)(2,1)S(1)}, bf16[12,81,512]{2,1,0:T(8,128)(2,1)S(1)}, u32[]{:S(2)}, u32[]{:S(2)}) collective-permute-start(bf16[12,81,512]{2,1,0:T(8,128)(2,1)S(1)} %get-tuple-element.414), channel_id=1, source_target_pairs={{0,1},{1,0},{2,3},{3,2},{4,5},{5,4},{6,7},{7,6},{8,9},{9,8},{10,11... | collective-permute-start | bytes 2985992 | tf_op jit(solution)/shard_map/ppermute | solution.py:651
  40.7 7.0 %collective-permute-start.17 = (bf16[160,384]{1,0:T(8,128)(2,1)S(1)}, bf16[160,384]{1,0:T(8,128)(2,1)S(1)}, u32[]{:S(2)}, u32[]{:S(2)}) collective-permute-start(bf16[160,384]{1,0:T(8,128)(2,1)S(1)} %get-tuple-element.426), channel_id=1, source_target_pairs={{0,4},{4,0},{8,12},{12,8},{16,20},{20,16},{24,28},{28,24},{1,5},{5... | collective-permute-start | bytes 368648 | tf_op jit(solution)/shard_map/ppermute | solution.py:654
  42.2 10.4 %collective-permute-start.18 = (bf16[160,384]{1,0:T(8,128)(2,1)S(1)}, bf16[160,384]{1,0:T(8,128)(2,1)S(1)}, u32[]{:S(2)}, u32[]{:S(2)}) collective-permute-start(bf16[160,384]{1,0:T(8,128)(2,1)S(1)} %get-tuple-element.427), channel_id=1, source_target_pairs={{0,8},{4,12},{8,0},{12,4},{16,24},{20,28},{24,16},{28,20},{1,9},{5... | collective-permute-start | bytes 368648 | tf_op jit(solution)/shard_map/ppermute | solution.py:654
  43.7 10.2 %collective-permute-start.19 = (bf16[160,384]{1,0:T(8,128)(2,1)S(1)}, bf16[160,384]{1,0:T(8,128)(2,1)S(1)}, u32[]{:S(2)}, u32[]{:S(2)}) collective-permute-start(bf16[160,384]{1,0:T(8,128)(2,1)S(1)} %get-tuple-element.428), channel_id=1, source_target_pairs={{0,12},{4,8},{8,4},{12,0},{16,28},{20,24},{24,20},{28,16},{1,13},{... | collective-permute-start | bytes 368648 | tf_op jit(solution)/shard_map/ppermute | solution.py:654
  44.3 10.2 %collective-permute-start.21 = (bf16[256,384]{1,0:T(8,128)(2,1)S(1)}, bf16[256,384]{1,0:T(8,128)(2,1)S(1)}, u32[]{:S(2)}, u32[]{:S(2)}) collective-permute-start(bf16[256,384]{1,0:T(8,128)(2,1)S(1)} %add_convert_fusion.2), channel_id=1, source_target_pairs={{0,16},{4,20},{8,24},{12,28},{16,0},{20,4},{24,8},{28,12},{1,17},{... | collective-permute-start | bytes 589832 | tf_op jit(solution)/shard_map/ppermute | solution.py:654
  47.1 21.5 %collective-permute-start.16 = (bf16[6,81,512]{2,1,0:T(8,128)(2,1)S(1)}, bf16[6,81,512]{2,1,0:T(8,128)(2,1)S(1)}, u32[]{:S(2)}, u32[]{:S(2)}) collective-permute-start(bf16[6,81,512]{2,1,0:T(8,128)(2,1)S(1)} %add_convert_fusion), channel_id=1, source_target_pairs={{0,2},{1,3},{2,0},{3,1},{4,6},{5,7},{6,4},{7,5},{8,10},{9,11},{10,... | collective-permute-start | bytes 1493000 | tf_op jit(solution)/shard_map/ppermute | solution.py:651
  54.0 7.7 %collective-permute-start.20 = (bf16[160,384]{1,0:T(8,128)(2,1)S(1)}, bf16[160,384]{1,0:T(8,128)(2,1)S(1)}, u32[]{:S(2)}, u32[]{:S(2)}) collective-permute-start(bf16[160,384]{1,0:T(8,128)(2,1)S(1)} %add_convert_fusion.4), channel_id=1, source_target_pairs={{0,16},{4,20},{8,24},{12,28},{16,0},{20,4},{24,8},{28,12},{1,17},{... | collective-permute-start | bytes 368648 | tf_op jit(solution)/shard_map/ppermute | solution.py:654
  54.5 10.6 %collective-permute-start.23 = (bf16[256,384]{1,0:T(8,128)(2,1)S(1)}, bf16[256,384]{1,0:T(8,128)(2,1)S(1)}, u32[]{:S(2)}, u32[]{:S(2)}) collective-permute-start(bf16[256,384]{1,0:T(8,128)(2,1)S(1)} %add_convert_fusion.1), channel_id=1, source_target_pairs={{0,8},{4,12},{8,0},{12,4},{16,24},{20,28},{24,16},{28,20},{1,9},{5... | collective-permute-start | bytes 589832 | tf_op jit(solution)/shard_map/ppermute | solution.py:654
  61.7 5.2 %collective-permute-start.22 = (bf16[160,384]{1,0:T(8,128)(2,1)S(1)}, bf16[160,384]{1,0:T(8,128)(2,1)S(1)}, u32[]{:S(2)}, u32[]{:S(2)}) collective-permute-start(bf16[160,384]{1,0:T(8,128)(2,1)S(1)} %add_convert_fusion.3), channel_id=1, source_target_pairs={{0,8},{4,12},{8,0},{12,4},{16,24},{20,28},{24,16},{28,20},{1,9},{5... | collective-permute-start | bytes 368648 | tf_op jit(solution)/shard_map/ppermute | solution.py:654
  65.2 9.9 %collective-permute-start.26 = (bf16[2,256,384]{2,1,0:T(8,128)(2,1)S(1)}, bf16[2,256,384]{2,1,0:T(8,128)(2,1)S(1)}, u32[]{:S(2)}, u32[]{:S(2)}) collective-permute-start(bf16[2,256,384]{2,1,0:T(8,128)(2,1)S(1)} %pad_maximum_fusion.refs_0_), channel_id=1, source_target_pairs={{0,4},{1,3},{2,6},{3,1},{4,0},{5,7},{6,2},{7,5},{8,12},{9,11},{10,... | collective-permute-start | bytes 1179656 | tf_op jit(solution)/shard_map/ppermute | solution.py:662
  66.3 9.2 %collective-permute-start.27 = (bf16[2,256,384]{2,1,0:T(8,128)(2,1)S(1)}, bf16[2,256,384]{2,1,0:T(8,128)(2,1)S(1)}, u32[]{:S(2)}, u32[]{:S(2)}) collective-permute-start(bf16[2,256,384]{2,1,0:T(8,128)(2,1)S(1)} %pad_maximum_fusion.refs_0_), channel_id=1, source_target_pairs={{0,2},{1,5},{2,0},{3,7},{4,6},{5,1},{6,4},{7,3},{8,10},{9,13},{10,... | collective-permute-start | bytes 1179656 | tf_op jit(solution)/shard_map/ppermute | solution.py:662
  67.0 11.5 %collective-permute-start.24 = (bf16[2,160,384]{2,1,0:T(8,128)(2,1)S(1)}, bf16[2,160,384]{2,1,0:T(8,128)(2,1)S(1)}, u32[]{:S(2)}, u32[]{:S(2)}) collective-permute-start(bf16[2,160,384]{2,1,0:T(8,128)(2,1)S(1)} %pad_maximum_fusion.2.refs_2_.refs_0_), channel_id=1, source_target_pairs={{0,4},{1,3},{2,6},{3,1},{4,0},{5,7},{6,2},{7,5},{8,12},{9,11},{10,... | collective-permute-start | bytes 737288 | tf_op jit(solution)/shard_map/ppermute | solution.py:662
  68.6 11.4 %collective-permute-start.30 = (bf16[2,256,384]{2,1,0:T(8,128)(2,1)S(1)}, bf16[2,256,384]{2,1,0:T(8,128)(2,1)S(1)}, u32[]{:S(2)}, u32[]{:S(2)}) collective-permute-start(bf16[2,256,384]{2,1,0:T(8,128)(2,1)S(1)} %pad_maximum_fusion.refs_0_), channel_id=1, source_target_pairs={{0,1},{1,0},{2,3},{3,2},{4,5},{5,4},{6,7},{7,6},{8,9},{9,8},{10,11... | collective-permute-start | bytes 1179656 | tf_op jit(solution)/shard_map/ppermute | solution.py:651
  68.6 9.9 %collective-permute-start.25 = (bf16[2,160,384]{2,1,0:T(8,128)(2,1)S(1)}, bf16[2,160,384]{2,1,0:T(8,128)(2,1)S(1)}, u32[]{:S(2)}, u32[]{:S(2)}) collective-permute-start(bf16[2,160,384]{2,1,0:T(8,128)(2,1)S(1)} %pad_maximum_fusion.2.refs_2_.refs_0_), channel_id=1, source_target_pairs={{0,2},{1,5},{2,0},{3,7},{4,6},{5,1},{6,4},{7,3},{8,10},{9,13},{10,... | collective-permute-start | bytes 737288 | tf_op jit(solution)/shard_map/ppermute | solution.py:662
  75.5 4.5 %collective-permute-start.31 = (bf16[2,256,384]{2,1,0:T(8,128)(2,1)S(1)}, bf16[2,256,384]{2,1,0:T(8,128)(2,1)S(1)}, u32[]{:S(2)}, u32[]{:S(2)}) collective-permute-start(bf16[2,256,384]{2,1,0:T(8,128)(2,1)S(1)} %collective-permute-done.26.refs_1_), channel_id=1, source_target_pairs={{0,1},{1,0},{2,3},{3,2},{4,5},{5,4},{6,7},{7,6},{8,9},{9,8},{10,11... | collective-permute-start | bytes 1179656 | tf_op jit(solution)/shard_map/ppermute | solution.py:651
  75.5 7.8 %collective-permute-start.29 = (bf16[2,256,384]{2,1,0:T(8,128)(2,1)S(1)}, bf16[2,256,384]{2,1,0:T(8,128)(2,1)S(1)}, u32[]{:S(2)}, u32[]{:S(2)}) collective-permute-start(bf16[2,256,384]{2,1,0:T(8,128)(2,1)S(1)} %collective-permute-done.26.refs_1_), channel_id=1, source_target_pairs={{0,2},{1,5},{2,0},{3,7},{4,6},{5,1},{6,4},{7,3},{8,10},{9,13},{10,... | collective-permute-start | bytes 1179656 | tf_op jit(solution)/shard_map/ppermute | solution.py:662
  78.5 7.4 %collective-permute-start.28 = (bf16[2,160,384]{2,1,0:T(8,128)(2,1)S(1)}, bf16[2,160,384]{2,1,0:T(8,128)(2,1)S(1)}, u32[]{:S(2)}, u32[]{:S(2)}) collective-permute-start(bf16[2,160,384]{2,1,0:T(8,128)(2,1)S(1)} %collective-permute-done.24.refs_3_.refs_1_), channel_id=1, source_target_pairs={{0,2},{1,5},{2,0},{3,7},{4,6},{5,1},{6,4},{7,3},{8,10},{9,13},{10,... | collective-permute-start | bytes 737288 | tf_op jit(solution)/shard_map/ppermute | solution.py:662
  83.3 2.8 %collective-permute-start.37 = (bf16[2,256,384]{2,1,0:T(8,128)(2,1)S(1)}, bf16[2,256,384]{2,1,0:T(8,128)(2,1)S(1)}, u32[]{:S(2)}, u32[]{:S(2)}) collective-permute-start(bf16[2,256,384]{2,1,0:T(8,128)(2,1)S(1)} %collective-permute-done.29.refs_0_), channel_id=1, source_target_pairs={{0,1},{1,0},{2,3},{3,2},{4,5},{5,4},{6,7},{7,6},{8,9},{9,8},{10,11... | collective-permute-start | bytes 1179656 | tf_op jit(solution)/shard_map/ppermute | solution.py:651
  85.9 2.9 %collective-permute-start.36 = (bf16[2,160,384]{2,1,0:T(8,128)(2,1)S(1)}, bf16[2,160,384]{2,1,0:T(8,128)(2,1)S(1)}, u32[]{:S(2)}, u32[]{:S(2)}) collective-permute-start(bf16[2,160,384]{2,1,0:T(8,128)(2,1)S(1)} %collective-permute-done.28.refs_3_), channel_id=1, source_target_pairs={{0,1},{1,0},{2,3},{3,2},{4,5},{5,4},{6,7},{7,6},{8,9},{9,8},{10,11... | collective-permute-start | bytes 737288 | tf_op jit(solution)/shard_map/ppermute | solution.py:651
  (14 other events, 44.0 us)

commit v6 on v5

--- a/solution.py
+++ b/solution.py
@@ -23,7 +23,7 @@
 
 
 ORDER = (
-    "weights", "a_send", "tick", "stats", "sums", "back", "v_send", "rows", "a_rs", "tick", "tick", "tick",
+    "weights", "a_send", "sums", "tick", "stats", "back", "v_send", "rows", "a_rs", "tick", "tick", "tick",
     "rows_core", "v_rs", "a_z2", "v_z2", "a_pair", "tick", "v_pair", "finish", "a_mark", "tick", "v_mark", "tick",
     "a_twin0", "a_twin1", "a_twin2", "place_head", "a_third", "a_twin3", "v_third", "v_twin3", "v_twin0", "v_twin1",
     "v_twin2", "tick", "place_most", "place_last",
@@ -209,8 +209,9 @@
 
 
 def front_rows(pad, first_block, meta, cots, wo, gu, gb, gp, put):
-    rows, width = cots[0].shape[1], cots[0].shape[2]
-    samples = cots[0].shape[0] - 1
+    width = cots[0].shape[1]
+    rows = PATCHES // 4
+    samples = cots[0].shape[0] // rows - 1
     low = rows // 16 * 16
     size = samples * pad
     for b, cot in enumerate(cots):
@@ -219,7 +220,7 @@
             base = b * size + i * pad
             scale = branch_scale(meta, i, samples, where)
             gb[base + low : base + pad, :] = jnp.zeros((pad - low, width), BF)
-            gb[base : base + rows, :] = (cot[i].astype(F32) * scale).astype(BF)
+            gb[base : base + rows, :] = (cot[i * rows : (i + 1) * rows, :].astype(F32) * scale).astype(BF)
         at = slice(b * size, (b + 1) * size)
         gp[at, :] = dot(gb[at, :], wo[...], 1, 1)
         for i in range(samples):
@@ -229,10 +230,10 @@
 
 
 def matrix_rows(pad, block, cot, pm, sp):
-    samples, rows = cot.shape[0] - 1, cot.shape[1]
+    rows = PATCHES // 4
     low = rows // 16 * 16
     sp[block * pad + low : (block + 1) * pad, :] = jnp.zeros((pad - low, sp.shape[1]), BF)
-    out = dot(cot[samples, :, 0 : pm.shape[0]], pm[...], 1, 0)
+    out = dot(cot[cot.shape[0] - rows :, 0 : pm.shape[0]], pm[...], 1, 0)
     sp[block * pad : block * pad + rows, :] = out.astype(BF)
 
 
@@ -242,8 +243,8 @@
         wo, gu, pm, gb, gp, gs, sp = refs
     else:
         wo, gu, gb, gp, gs, sp, pm = refs
-        pm[...] = position_map(meta[0], cots[0].shape[1], pad, n, pm.shape[0])
-    samples = cots[0].shape[0] - 1
+        pm[...] = position_map(meta[0], PATCHES // n, pad, n, pm.shape[0])
+    samples = cots[0].shape[0] // (PATCHES // n) - 1
 
     def put(b, i, c, out):
         base = (b * samples + i) * pad + c
@@ -255,7 +256,8 @@
 
 
 def prepare_body(n, pad, meta, c3, wo, gu2, pm, gs0, gs1, sp0, sp1, gb, gp, gs, gmix, sp, spt):
-    samples, rows = c3.shape[0] - 1, c3.shape[1]
+    rows = PATCHES // n
+    samples = c3.shape[0] // rows - 1
     most = (n - 1) * pad
     sp[0 : sp0.shape[0], :] = sp0[...]
     sp[sp0.shape[0] : most, :] = sp1[...]
@@ -533,7 +535,7 @@
         t = (keep[k].astype(F32) + got_a[k].astype(F32) + got_b[k].astype(F32)) * gain
         first = jnp.mean(t, axis=-1, keepdims=True)
         second = jnp.mean(t * standard, axis=-1, keepdims=True)
-        grad = cot[i].astype(F32) + inverse * (t - first - standard * second)
+        grad = cot[i * rows : (i + 1) * rows, :].astype(F32) + inverse * (t - first - standard * second)
         grad_tokens[i] = grad.astype(BF)
 
 
@@ -722,7 +724,7 @@
         side = jnp.stack([high, spatial_bias - high], axis=1).astype(BF)
         packed = jnp.concatenate([spatial, side], axis=1)
         packed = jnp.pad(packed, ((0, 0), (0, width - packed.shape[1])))
-        c0 = jnp.concatenate([cotangent, packed[None]])
+        c0 = jnp.concatenate([cotangent.reshape(-1, width), packed])
         c2 = over_seq(c0, 2)
         wu = lax.dynamic_slice(w_in, (0, seq * half), (width, half))
         wv = lax.dynamic_slice(w_in, (0, gate + seq * half), (width, half))

time: 90.9 us -> 90.3 us (level)
  local copies, waits for them, and re-layouts: 1.55 us -> 2.57 us
  waiting for transfers between devices: 23.4 us -> 22.4 us
  other arithmetic: 3.23 us -> 2.26 us
    reshape x0 -> x1, local copies, waits for them, and re-layouts: none -> 1.02 us  [shards(): c0 = jnp.concatenate([cotangent.reshape(-1, width), packed])]
    broadcast_in_dim x1 -> x0, other arithmetic: 1.01 us -> none  [shards(): c0 = jnp.concatenate([cotangent, packed[None]])]
where the time goes in v6:
time: 90.3 us; the launch traced here: 90 us
  starting transfers between devices  33.1 us (37%)
  Pallas kernels  28.5 us (32%)
  waiting for transfers between devices  22.4 us (25%)
  local copies, waits for them, and re-layouts  2.57 us (3%)
  other arithmetic  2.26 us (3%)
  between operations  1.15 us (1%)
    pallas_call x25, Pallas kernels, call(): pl.pallas_call(body, out_shape=outs, in_specs=specs if specs is not None...  28.5 us
    ppermute x10, starting transfers between devices, over_dp(): return lax.ppermute(x, 'dp', [(i, i ^ flip) for i in range(m)])  16.5 us
    ppermute x10, waiting for transfers between devices, over_dp(): return lax.ppermute(x, 'dp', [(i, i ^ flip) for i in range(m)])  10.7 us
    ppermute x22, starting transfers between devices, over_seq(): return lax.ppermute(x, 'seq', [(i, i ^ flip) for i in range(n)])  10.3 us
    ppermute x6, waiting for transfers between devices, mixed_axes(): return lax.ppermute(x, ('dp', 'seq'), pairs)  7.69 us
    ppermute x6, starting transfers between devices, mixed_axes(): return lax.ppermute(x, ('dp', 'seq'), pairs)  6.38 us
    ppermute x22, waiting for transfers between devices, over_seq(): return lax.ppermute(x, 'seq', [(i, i ^ flip) for i in range(n)])  3.95 us
  transfers between devices with their start and end apart: 38, of which 17 were waited for; matrix products, arithmetic and copies ran while one was open for 5% of the time, Pallas kernels for 26%

profile of v6, /device:TPU:0, one launch (start us, length us, event | category | flops | bytes accessed | tf_op | source)
XLA Modules:
  0.0 90.0 jit_solution(3785806247627512481)
XLA Ops:
  1.2 2.6 %collective-permute-start.1 = (bf16[3,81,512]{2,1,0:T(8,128)(2,1)}, bf16[3,81,512]{2,1,0:T(8,128)(2,1)S(1)}, u32[]{:S(2)}, u32[]{:S(2)}) collective-permute-start(bf16[3,81,512]{2,1,0:T(8,128)(2,1)} %tok), channel_id=1, source_target_pairs={{0,2},{1,3},{2,0},{3,1},{4,6},{5,7},{6,4},{7,5},{8,10},{9,11},{10,... | collective-permute-start | bytes 746504 | tf_op jit(solution)/shard_map/ppermute | solution.py:653
  7.0 1.2 %constant_dynamic-slice_fusion.1 = (bf16[512,384]{1,0:T(8,128)(2,1)S(1)}, bf16[512,384]{1,0:T(8,128)(2,1)S(1)}) fusion(bf16[512,3072]{1,0:T(8,128)(2,1)} %param.15, s32[]{:T(128)S(6)} %select_n.10, s32[]{:T(128)S(6)} %select_n.9), kind=kLoop, calls=%fused_computation.15 | loop fusion | bytes 1572872 | tf_op jit(solution)/shard_map/dynamic_slice | solution.py:730
  8.7 1.8 %project.3 = (bf16[576,512]{1,0:T(8,128)(2,1)S(1)}, bf16[576,384]{1,0:T(8,128)(2,1)S(1)}, bf16[576,384]{1,0:T(8,128)(2,1)S(1)}, f32[576,384]{1,0:T(8,128)S(1)}, ...) custom-call(bf16[3,81,512]{2,1,0:T(8,128)(2,1)S(1)} %copy-done.1, ...), custom_call_target="tpu_custom_call" | custom-call | flops 1 | bytes 1 | tf_op jit(solution)/shard_map/project/pallas_call | solution.py:50
  11.1 1.1 %project.4 = (bf16[288,512]{1,0:T(8,128)(2,1)S(1)}, bf16[288,384]{1,0:T(8,128)(2,1)S(1)}, bf16[288,384]{1,0:T(8,128)(2,1)S(1)}, f32[288,384]{1,0:T(8,128)S(1)}, ...) custom-call(bf16[3,81,512]{2,1,0:T(8,128)(2,1)S(1)} %collective-permute-done.1.refs_0_, f32[1,512]{1,0:T(1,128)S(1)} %bitcast.15, ...), custom_call_target="tpu_custom_call" | custom-call | flops 1 | bytes 1 | tf_op jit(solution)/shard_map/project/pallas_call | solution.py:50
  12.6 1.1 %project.5 = (bf16[288,512]{1,0:T(8,128)(2,1)S(1)}, bf16[288,384]{1,0:T(8,128)(2,1)S(1)}, bf16[288,384]{1,0:T(8,128)(2,1)S(1)}, f32[288,384]{1,0:T(8,128)S(1)}, ...) custom-call(bf16[3,81,512]{2,1,0:T(8,128)(2,1)S(1)} %collective-permute-done.2.refs_0_, f32[1,512]{1,0:T(1,128)S(1)} %bitcast.16, ...), custom_call_target="tpu_custom_call" | custom-call | flops 1 | bytes 1 | tf_op jit(solution)/shard_map/project/pallas_call | solution.py:50
  13.9 2.2 %collective-permute-start.7 = (f32[24,128]{1,0:T(8,128)S(1)}, f32[24,128]{1,0:T(8,128)S(1)}, u32[]{:S(2)}, u32[]{:S(2)}) collective-permute-start(f32[24,128]{1,0:T(8,128)S(1)} %get-tuple-element.346.t0), channel_id=1, source_target_pairs={{0,2},{1,3},{2,0},{3,1},{4,6},{5,7},{6,4},{7,5},{8,10},{9,11},{10,... | collective-permute-start | bytes 36872 | tf_op jit(solution)/shard_map/ppermute | solution.py:653
  16.2 1.2 %front.2 = (bf16[576,512]{1,0:T(8,128)(2,1)S(1)}, f32[576,384]{1,0:T(8,128)S(1)}, bf16[576,384]{1,0:T(8,128)(2,1)S(1)}, bf16[192,384]{1,0:T(8,128)(2,1)S(1)}, bf16[384,384]{1,0:T(8,128)(2,1)S(1)}) custom-call(s32[8]{0:T(128)S(1)} %pad_add_fusion.meta, bf16[324,512]{1,0:T(8,128)(2,1)S(1)} %pad_maximum_fusion.1.refs_0_.cot, ...), custom_call_target="tpu_custom_call" | custom-call | flops 1 | bytes 1 | tf_op jit(solution)/shard_map/front/pallas_call | solution.py:50
  20.3 1.5 %prepare.1 = (bf16[288,512]{1,0:T(8,128)(2,1)S(1)}, f32[288,384]{1,0:T(8,128)S(1)}, bf16[384,1152]{1,0:T(8,128)(2,1)S(1)}, f32[1152,384]{1,0:T(8,128)S(1)}, bf16[384,384]{1,0:T(8,128)(2,1)S(1)}) custom-call(s32[8]{0:T(128)S(1)} %pad_add_fusion.meta, bf16[324,512]{1,0:T(8,128)(2,1)S(1)} %collective-permute-done.5.c3, ...), custom_call_target="tpu_custom_call" | custom-call | flops 1 | bytes 1 | tf_op jit(solution)/shard_map/prepare/pallas_call | solution.py:50
  21.9 3.4 %spatial.1 = (bf16[1152,384]{1,0:T(8,128)(2,1)S(1)}, bf16[1152,384]{1,0:T(8,128)(2,1)S(1)}, f32[128,128]{1,0:T(8,128)S(1)}, f32[24,128]{1,0:T(8,128)S(1)}, bf16[...) custom-call(s32[8]{0:T(128)S(1)} %pad_add_fusion.meta, ...), custom_call_target="tpu_custom_call" | custom-call | flops 1 | bytes 1 | tf_op jit(solution)/shard_map/spatial/pallas_call | solution.py:50
  25.3 1.7 %collective-permute-start.10 = (bf16[128,384]{1,0:T(8,128)(2,1)S(1)}, bf16[128,384]{1,0:T(8,128)(2,1)S(1)}, u32[]{:S(2)}, u32[]{:S(2)}) collective-permute-start(bf16[128,384]{1,0:T(8,128)(2,1)S(1)} %get-tuple-element.359), channel_id=1, source_target_pairs={{0,2},{1,3},{2,0},{3,1},{4,6},{5,7},{6,4},{7,5},{8,10},{9,11},{10,... | collective-permute-start | bytes 294920 | tf_op jit(solution)/shard_map/ppermute | solution.py:653
  27.0 2.4 %weights.1 = (bf16[256,384]{1,0:T(8,128)(2,1)S(1)}, bf16[256,384]{1,0:T(8,128)(2,1)S(1)}, bf16[256,384]{1,0:T(8,128)(2,1)S(1)}, bf16[256,384]{1,0:T(8,128)(2,1)S(1)}, f32[512,384]{1,0:T(8,128)S(1)}) custom-call(s32[8]{0:T(128)S(1)} %pad_add_fusion.meta, bf16[1152,384]{1,0:T(8,128)(2,1)S(1)} %get-tuple-element.407.prod, ...), custom_call_target="tpu_custom_call" | custom-call | flops 1 | bytes 1 | tf_op jit(solution)/shard_map/weights/pallas_call | solution.py:50
  30.4 1.5 %collective-permute-start.13 = (bf16[256,384]{1,0:T(8,128)(2,1)S(1)}, bf16[256,384]{1,0:T(8,128)(2,1)S(1)}, u32[]{:S(2)}, u32[]{:S(2)}) collective-permute-start(bf16[256,384]{1,0:T(8,128)(2,1)S(1)} %get-tuple-element.416), channel_id=1, source_target_pairs={{0,4},{4,0},{8,12},{12,8},{16,20},{20,16},{24,28},{28,24},{1,5},{5... | collective-permute-start | bytes 589832 | tf_op jit(solution)/shard_map/ppermute | solution.py:656
  31.9 1.6 %collective-permute-start.14 = (bf16[256,384]{1,0:T(8,128)(2,1)S(1)}, bf16[256,384]{1,0:T(8,128)(2,1)S(1)}, u32[]{:S(2)}, u32[]{:S(2)}) collective-permute-start(bf16[256,384]{1,0:T(8,128)(2,1)S(1)} %get-tuple-element.417), channel_id=1, source_target_pairs={{0,8},{4,12},{8,0},{12,4},{16,24},{20,28},{24,16},{28,20},{1,9},{5... | collective-permute-start | bytes 589832 | tf_op jit(solution)/shard_map/ppermute | solution.py:656
  34.9 2.9 %back.1 = (bf16[1152,384]{1,0:T(8,128)(2,1)S(1)}, bf16[160,384]{1,0:T(8,128)(2,1)S(1)}, bf16[160,384]{1,0:T(8,128)(2,1)S(1)}, bf16[160,384]{1,0:T(8,128)(2,1)S(1)}, bf16[160,384]{1,0:T(8,128)(2,1)S(1)}) custom-call(s32[8]{0:T(128)S(1)} %pad_add_fusion.meta, f32[1152,384]{1,0:T(8,128)S(1)} %get-tuple-element.382.gmix, f32[576,384]{1,0:T(8,128)S(1)} %get-tuple-element.383.v0, ...), custom_call_target="tpu_custom_call" | custom-call | flops 1 | bytes 1 | tf_op jit(solution)/shard_map/back/pallas_call | solution.py:50
  37.8 2.0 %rows_out.1 = (bf16[6,81,512]{2,1,0:T(8,128)(2,1)S(1)}, bf16[6,81,512]{2,1,0:T(8,128)(2,1)S(1)}, bf16[12,81,512]{2,1,0:T(8,128)(2,1)S(1)}) custom-call(bf16[1152,384]{1,0:T(8,128)(2,1)S(1)} %get-tuple-element.407.prod, bf16[384,512]{1,0:T(8,128)(2,1)S(1)} %constant_dynamic-slice_fusion.refs_2_.refs_1_.wo, ...), custom_call_target="tpu_custom_call" | custom-call | flops 1 | bytes 1 | tf_op jit(solution)/shard_map/rows_out/pallas_call | solution.py:50
  40.1 1.5 %collective-permute-start.17 = (bf16[160,384]{1,0:T(8,128)(2,1)S(1)}, bf16[160,384]{1,0:T(8,128)(2,1)S(1)}, u32[]{:S(2)}, u32[]{:S(2)}) collective-permute-start(bf16[160,384]{1,0:T(8,128)(2,1)S(1)} %get-tuple-element.426), channel_id=1, source_target_pairs={{0,4},{4,0},{8,12},{12,8},{16,20},{20,16},{24,28},{28,24},{1,5},{5... | collective-permute-start | bytes 368648 | tf_op jit(solution)/shard_map/ppermute | solution.py:656
  41.5 1.6 %collective-permute-start.18 = (bf16[160,384]{1,0:T(8,128)(2,1)S(1)}, bf16[160,384]{1,0:T(8,128)(2,1)S(1)}, u32[]{:S(2)}, u32[]{:S(2)}) collective-permute-start(bf16[160,384]{1,0:T(8,128)(2,1)S(1)} %get-tuple-element.427), channel_id=1, source_target_pairs={{0,8},{4,12},{8,0},{12,4},{16,24},{20,28},{24,16},{28,20},{1,9},{5... | collective-permute-start | bytes 368648 | tf_op jit(solution)/shard_map/ppermute | solution.py:656
  43.7 2.7 %collective-permute-start.21 = (bf16[256,384]{1,0:T(8,128)(2,1)S(1)}, bf16[256,384]{1,0:T(8,128)(2,1)S(1)}, u32[]{:S(2)}, u32[]{:S(2)}) collective-permute-start(bf16[256,384]{1,0:T(8,128)(2,1)S(1)} %add_convert_fusion.2), channel_id=1, source_target_pairs={{0,16},{4,20},{8,24},{12,28},{16,0},{20,4},{24,8},{28,12},{1,17},{... | collective-permute-start | bytes 589832 | tf_op jit(solution)/shard_map/ppermute | solution.py:656
  47.3 4.7 %collective-permute-done.18 = bf16[160,384]{1,0:T(8,128)(2,1)S(1)} collective-permute-done((bf16[160,384]{1,0:T(8,128)(2,1)S(1)}, bf16[160,384]{1,0:T(8,128)(2,1)S(1)}, u32[]{:S(2)}, u32[]{:S(2)}) %collective-permute-start.18) | collective-permute-done | bytes 122912 | tf_op jit(solution)/shard_map/ppermute | solution.py:656
  51.9 1.4 %collective-permute-done.19 = bf16[160,384]{1,0:T(8,128)(2,1)S(1)} collective-permute-done((bf16[160,384]{1,0:T(8,128)(2,1)S(1)}, bf16[160,384]{1,0:T(8,128)(2,1)S(1)}, u32[]{:S(2)}, u32[]{:S(2)}) %collective-permute-start.19) | collective-permute-done | bytes 122912 | tf_op jit(solution)/shard_map/ppermute | solution.py:656
  53.9 6.1 %collective-permute-start.23 = (bf16[256,384]{1,0:T(8,128)(2,1)S(1)}, bf16[256,384]{1,0:T(8,128)(2,1)S(1)}, u32[]{:S(2)}, u32[]{:S(2)}) collective-permute-start(bf16[256,384]{1,0:T(8,128)(2,1)S(1)} %add_convert_fusion.1), channel_id=1, source_target_pairs={{0,8},{4,12},{8,0},{12,4},{16,24},{20,28},{24,16},{28,20},{1,9},{5... | collective-permute-start | bytes 589832 | tf_op jit(solution)/shard_map/ppermute | solution.py:656
  61.4 3.1 %collective-permute-done.23 = bf16[256,384]{1,0:T(8,128)(2,1)S(1)} collective-permute-done((bf16[256,384]{1,0:T(8,128)(2,1)S(1)}, bf16[256,384]{1,0:T(8,128)(2,1)S(1)}, u32[]{:S(2)}, u32[]{:S(2)}) %collective-permute-start.23) | collective-permute-done | bytes 196640 | tf_op jit(solution)/shard_map/ppermute | solution.py:656
  64.6 1.1 %collective-permute-start.26 = (bf16[2,256,384]{2,1,0:T(8,128)(2,1)S(1)}, bf16[2,256,384]{2,1,0:T(8,128)(2,1)S(1)}, u32[]{:S(2)}, u32[]{:S(2)}) collective-permute-start(bf16[2,256,384]{2,1,0:T(8,128)(2,1)S(1)} %pad_maximum_fusion.refs_0_), channel_id=1, source_target_pairs={{0,4},{1,3},{2,6},{3,1},{4,0},{5,7},{6,2},{7,5},{8,12},{9,11},{10,... | collective-permute-start | bytes 1179656 | tf_op jit(solution)/shard_map/ppermute | solution.py:664
  66.4 1.6 %collective-permute-start.24 = (bf16[2,160,384]{2,1,0:T(8,128)(2,1)S(1)}, bf16[2,160,384]{2,1,0:T(8,128)(2,1)S(1)}, u32[]{:S(2)}, u32[]{:S(2)}) collective-permute-start(bf16[2,160,384]{2,1,0:T(8,128)(2,1)S(1)} %pad_maximum_fusion.2.refs_2_.refs_0_), channel_id=1, source_target_pairs={{0,4},{1,3},{2,6},{3,1},{4,0},{5,7},{6,2},{7,5},{8,12},{9,11},{10,... | collective-permute-start | bytes 737288 | tf_op jit(solution)/shard_map/ppermute | solution.py:664
  68.8 1.9 %finish_rows.1 = (bf16[3,81,512]{2,1,0:T(8,128)(2,1)}, bf16[3,81,512]{2,1,0:T(8,128)(2,1)}) custom-call(s32[8]{0:T(128)S(1)} %pad_add_fusion.meta, bf16[3,81,512]{2,1,0:T(8,128)(2,1)S(1)} %copy-done.1, bf16[324,512]{1,0:T(8,128)(2,1)S(1)} %pad_maximum_fusion.1.refs_0_.cot, bf16[6,81,512]{2,1,0:T(8,128)(2,1)S(1)} %get-tuple-element.445.keep, ...), custom_call_target="tpu_custom_call" | custom-call | flops 1 | bytes 1 | tf_op jit(solution)/shard_map/finish_rows/pallas_call | solution.py:50
  70.7 3.7 %collective-permute-done.26.refs_1_ = bf16[2,256,384]{2,1,0:T(8,128)(2,1)S(1)} collective-permute-done((bf16[2,256,384]{2,1,0:T(8,128)(2,1)S(1)}, bf16[2,256,384]{2,1,0:T(8,128)(2,1)S(1)}, u32[]{:S(2)}, u32[]{:S(2)}) %collective-permute-start.26) | collective-permute-done | bytes 393248 | tf_op jit(solution)/shard_map/ppermute | solution.py:664
  76.1 1.8 %collective-permute-done.24.refs_3_.refs_1_ = bf16[2,160,384]{2,1,0:T(8,128)(2,1)S(1)} collective-permute-done((bf16[2,160,384]{2,1,0:T(8,128)(2,1)S(1)}, bf16[2,160,384]{2,1,0:T(8,128)(2,1)S(1)}, u32[]{:S(2)}, u32[]{:S(2)}) %collective-permute-start.24) | collective-permute-done | bytes 245792 | tf_op jit(solution)/shard_map/ppermute | solution.py:664
  77.9 1.5 %collective-permute-start.28 = (bf16[2,160,384]{2,1,0:T(8,128)(2,1)S(1)}, bf16[2,160,384]{2,1,0:T(8,128)(2,1)S(1)}, u32[]{:S(2)}, u32[]{:S(2)}) collective-permute-start(bf16[2,160,384]{2,1,0:T(8,128)(2,1)S(1)} %collective-permute-done.24.refs_3_.refs_1_), channel_id=1, source_target_pairs={{0,2},{1,5},{2,0},{3,7},{4,6},{5,1},{6,4},{7,3},{8,10},{9,13},{10,... | collective-permute-start | bytes 737288 | tf_op jit(solution)/shard_map/ppermute | solution.py:664
  79.6 3.0 %place.2 = (f32[512,3072]{1,0:T(8,128)}, f32[1536,512]{1,0:T(8,128)}) custom-call(s32[8]{0:T(128)S(1)} %pad_add_fusion.meta, bf16[2,256,384]{2,1,0:T(8,128)(2,1)S(1)} %pad_maximum_fusion.refs_0_, bf16[2,256,384]{2,1,0:T(8,128)(2,1)S(1)} %collective-permute-done.26.refs_1_, bf16[2,256,384]{2,1,0:T(8,128)(2,1)S(1)} %collective-permute-done.27.refs_2_, ...), custom_call_target="tpu_custom_call" | custom-call | flops 1 | bytes 1 | tf_op jit(solution)/shard_map/place/pallas_call | solution.py:50
  83.7 1.6 %collective-permute-done.28.refs_3_ = bf16[2,160,384]{2,1,0:T(8,128)(2,1)S(1)} collective-permute-done((bf16[2,160,384]{2,1,0:T(8,128)(2,1)S(1)}, bf16[2,160,384]{2,1,0:T(8,128)(2,1)S(1)}, u32[]{:S(2)}, u32[]{:S(2)}) %collective-permute-start.28) | collective-permute-done | bytes 245792 | tf_op jit(solution)/shard_map/ppermute | solution.py:664
  85.5 2.7 %place.3 = (f32[512,3072]{1,0:T(8,128)}, f32[1536,512]{1,0:T(8,128)}) custom-call(s32[8]{0:T(128)S(1)} %pad_add_fusion.meta, bf16[2,256,384]{2,1,0:T(8,128)(2,1)S(1)} %collective-permute-done.29.refs_0_, bf16[2,256,384]{2,1,0:T(8,128)(2,1)S(1)} %collective-permute-done.37.refs_1_, ...), custom_call_target="tpu_custom_call", output_to_operand_aliasing={{0}: (9, {}), {1}: (10, {})} | custom-call | flops 1 | bytes 1 | tf_op jit(solution)/shard_map/place/pallas_call | solution.py:50
  88.2 1.6 %place_last.1 = (f32[512,3072]{1,0:T(8,128)}, f32[81,324]{1,0:T(8,128)}, f32[81]{0:T(128)}, f32[512]{0:T(512)}, f32[512]{0:T(512)}, /*index=5*/f32[1536]{0:T(1024)}, f32[1536]{0:T(1024)}) custom-call(s32[8]{0:T(128)S(1)} %pad_add_fusion.meta, bf16[2,160,384]{2,1,0:T(8,128)(2,1)S(1)} %pad_maximum_fusion.2.refs_2_.refs_0_, ...), custom_call_target="tpu_custom_call", output_to_operand_aliasing={{0}: (9, {})} | custom-call | flops 1 | bytes 1 | tf_op jit(solution)/shard_map/place_last/pallas_call | solution.py:50
  (102 shorter events, 18.8 us)
Async XLA Ops:
  0.7 7.5 %collective-permute-start = (bf16[3,81,512]{2,1,0:T(8,128)(2,1)}, bf16[3,81,512]{2,1,0:T(8,128)(2,1)S(1)}, u32[]{:S(2)}, u32[]{:S(2)}) collective-permute-start(bf16[3,81,512]{2,1,0:T(8,128)(2,1)} %tok), channel_id=1, source_target_pairs={{0,1},{1,0},{2,3},{3,2},{4,5},{5,4},{6,7},{7,6},{8,9},{9,8},{10,11... | collective-permute-start | bytes 746504 | tf_op jit(solution)/shard_map/ppermute | solution.py:653
  1.2 9.9 %collective-permute-start.1 = (bf16[3,81,512]{2,1,0:T(8,128)(2,1)}, bf16[3,81,512]{2,1,0:T(8,128)(2,1)S(1)}, u32[]{:S(2)}, u32[]{:S(2)}) collective-permute-start(bf16[3,81,512]{2,1,0:T(8,128)(2,1)} %tok), channel_id=1, source_target_pairs={{0,2},{1,3},{2,0},{3,1},{4,6},{5,7},{6,4},{7,5},{8,10},{9,11},{10,... | collective-permute-start | bytes 746504 | tf_op jit(solution)/shard_map/ppermute | solution.py:653
  8.2 8.0 %collective-permute-start.4 = (bf16[324,512]{1,0:T(8,128)(2,1)S(1)}, bf16[324,512]{1,0:T(8,128)(2,1)S(1)}, u32[]{:S(2)}, u32[]{:S(2)}) collective-permute-start(bf16[324,512]{1,0:T(8,128)(2,1)S(1)} %pad_maximum_fusion.1.refs_0_.cot), channel_id=1, source_target_pairs={{0,1},{1,0},{2,3},{3,2},{4,5},{5,4},{6,7},{7,6},{8,9},{9,8},{10,11... | collective-permute-start | bytes 995336 | tf_op jit(solution)/shard_map/ppermute | solution.py:653
  8.4 10.3 %collective-permute-start.3 = (bf16[324,512]{1,0:T(8,128)(2,1)S(1)}, bf16[324,512]{1,0:T(8,128)(2,1)S(1)}, u32[]{:S(2)}, u32[]{:S(2)}) collective-permute-start(bf16[324,512]{1,0:T(8,128)(2,1)S(1)} %pad_maximum_fusion.1.refs_0_.cot), channel_id=1, source_target_pairs={{0,2},{1,3},{2,0},{3,1},{4,6},{5,7},{6,4},{7,5},{8,10},{9,11},{10,... | collective-permute-start | bytes 995336 | tf_op jit(solution)/shard_map/ppermute | solution.py:653
  13.8 8.0 %collective-permute-start.6 = (f32[24,128]{1,0:T(8,128)S(1)}, f32[24,128]{1,0:T(8,128)S(1)}, u32[]{:S(2)}, u32[]{:S(2)}) collective-permute-start(f32[24,128]{1,0:T(8,128)S(1)} %get-tuple-element.346.t0), channel_id=1, source_target_pairs={{0,1},{1,0},{2,3},{3,2},{4,5},{5,4},{6,7},{7,6},{8,9},{9,8},{10,11... | collective-permute-start | bytes 36872 | tf_op jit(solution)/shard_map/ppermute | solution.py:653
  13.9 7.9 %collective-permute-start.7 = (f32[24,128]{1,0:T(8,128)S(1)}, f32[24,128]{1,0:T(8,128)S(1)}, u32[]{:S(2)}, u32[]{:S(2)}) collective-permute-start(f32[24,128]{1,0:T(8,128)S(1)} %get-tuple-element.346.t0), channel_id=1, source_target_pairs={{0,2},{1,3},{2,0},{3,1},{4,6},{5,7},{6,4},{7,5},{8,10},{9,11},{10,... | collective-permute-start | bytes 36872 | tf_op jit(solution)/shard_map/ppermute | solution.py:653
  16.2 5.7 %collective-permute-start.8 = (f32[24,128]{1,0:T(8,128)S(1)}, f32[24,128]{1,0:T(8,128)S(1)}, u32[]{:S(2)}, u32[]{:S(2)}) collective-permute-start(f32[24,128]{1,0:T(8,128)S(1)} %get-tuple-element.346.t0), channel_id=1, source_target_pairs={{0,3},{1,2},{2,1},{3,0},{4,7},{5,6},{6,5},{7,4},{8,11},{9,10},{10,... | collective-permute-start | bytes 36872 | tf_op jit(solution)/shard_map/ppermute | solution.py:653
  25.3 8.2 %collective-permute-start.10 = (bf16[128,384]{1,0:T(8,128)(2,1)S(1)}, bf16[128,384]{1,0:T(8,128)(2,1)S(1)}, u32[]{:S(2)}, u32[]{:S(2)}) collective-permute-start(bf16[128,384]{1,0:T(8,128)(2,1)S(1)} %get-tuple-element.359), channel_id=1, source_target_pairs={{0,2},{1,3},{2,0},{3,1},{4,6},{5,7},{6,4},{7,5},{8,10},{9,11},{10,... | collective-permute-start | bytes 294920 | tf_op jit(solution)/shard_map/ppermute | solution.py:653
  29.8 5.1 %collective-permute-start.11 = (bf16[128,384]{1,0:T(8,128)(2,1)S(1)}, bf16[128,384]{1,0:T(8,128)(2,1)S(1)}, u32[]{:S(2)}, u32[]{:S(2)}) collective-permute-start(bf16[128,384]{1,0:T(8,128)(2,1)S(1)} %get-tuple-element.360), channel_id=1, source_target_pairs={{0,3},{1,2},{2,1},{3,0},{4,7},{5,6},{6,5},{7,4},{8,11},{9,10},{10,... | collective-permute-start | bytes 294920 | tf_op jit(solution)/shard_map/ppermute | solution.py:653
  29.8 5.1 %collective-permute-start.9 = (bf16[128,384]{1,0:T(8,128)(2,1)S(1)}, bf16[128,384]{1,0:T(8,128)(2,1)S(1)}, u32[]{:S(2)}, u32[]{:S(2)}) collective-permute-start(bf16[128,384]{1,0:T(8,128)(2,1)S(1)} %get-tuple-element.358), channel_id=1, source_target_pairs={{0,1},{1,0},{2,3},{3,2},{4,5},{5,4},{6,7},{7,6},{8,9},{9,8},{10,11... | collective-permute-start | bytes 294920 | tf_op jit(solution)/shard_map/ppermute | solution.py:653
  30.4 11.1 %collective-permute-start.13 = (bf16[256,384]{1,0:T(8,128)(2,1)S(1)}, bf16[256,384]{1,0:T(8,128)(2,1)S(1)}, u32[]{:S(2)}, u32[]{:S(2)}) collective-permute-start(bf16[256,384]{1,0:T(8,128)(2,1)S(1)} %get-tuple-element.416), channel_id=1, source_target_pairs={{0,4},{4,0},{8,12},{12,8},{16,20},{20,16},{24,28},{28,24},{1,5},{5... | collective-permute-start | bytes 589832 | tf_op jit(solution)/shard_map/ppermute | solution.py:656
  31.9 11.2 %collective-permute-start.14 = (bf16[256,384]{1,0:T(8,128)(2,1)S(1)}, bf16[256,384]{1,0:T(8,128)(2,1)S(1)}, u32[]{:S(2)}, u32[]{:S(2)}) collective-permute-start(bf16[256,384]{1,0:T(8,128)(2,1)S(1)} %get-tuple-element.417), channel_id=1, source_target_pairs={{0,8},{4,12},{8,0},{12,4},{16,24},{20,28},{24,16},{28,20},{1,9},{5... | collective-permute-start | bytes 589832 | tf_op jit(solution)/shard_map/ppermute | solution.py:656
  33.5 10.1 %collective-permute-start.15 = (bf16[256,384]{1,0:T(8,128)(2,1)S(1)}, bf16[256,384]{1,0:T(8,128)(2,1)S(1)}, u32[]{:S(2)}, u32[]{:S(2)}) collective-permute-start(bf16[256,384]{1,0:T(8,128)(2,1)S(1)} %get-tuple-element.418), channel_id=1, source_target_pairs={{0,12},{4,8},{8,4},{12,0},{16,28},{20,24},{24,20},{28,16},{1,13},{... | collective-permute-start | bytes 589832 | tf_op jit(solution)/shard_map/ppermute | solution.py:656
  39.8 6.5 %collective-permute-start.12 = (bf16[12,81,512]{2,1,0:T(8,128)(2,1)S(1)}, bf16[12,81,512]{2,1,0:T(8,128)(2,1)S(1)}, u32[]{:S(2)}, u32[]{:S(2)}) collective-permute-start(bf16[12,81,512]{2,1,0:T(8,128)(2,1)S(1)} %get-tuple-element.414), channel_id=1, source_target_pairs={{0,1},{1,0},{2,3},{3,2},{4,5},{5,4},{6,7},{7,6},{8,9},{9,8},{10,11... | collective-permute-start | bytes 2985992 | tf_op jit(solution)/shard_map/ppermute | solution.py:653
  40.1 7.2 %collective-permute-start.17 = (bf16[160,384]{1,0:T(8,128)(2,1)S(1)}, bf16[160,384]{1,0:T(8,128)(2,1)S(1)}, u32[]{:S(2)}, u32[]{:S(2)}) collective-permute-start(bf16[160,384]{1,0:T(8,128)(2,1)S(1)} %get-tuple-element.426), channel_id=1, source_target_pairs={{0,4},{4,0},{8,12},{12,8},{16,20},{20,16},{24,28},{28,24},{1,5},{5... | collective-permute-start | bytes 368648 | tf_op jit(solution)/shard_map/ppermute | solution.py:656
  41.5 10.4 %collective-permute-start.18 = (bf16[160,384]{1,0:T(8,128)(2,1)S(1)}, bf16[160,384]{1,0:T(8,128)(2,1)S(1)}, u32[]{:S(2)}, u32[]{:S(2)}) collective-permute-start(bf16[160,384]{1,0:T(8,128)(2,1)S(1)} %get-tuple-element.427), channel_id=1, source_target_pairs={{0,8},{4,12},{8,0},{12,4},{16,24},{20,28},{24,16},{28,20},{1,9},{5... | collective-permute-start | bytes 368648 | tf_op jit(solution)/shard_map/ppermute | solution.py:656
  43.1 10.2 %collective-permute-start.19 = (bf16[160,384]{1,0:T(8,128)(2,1)S(1)}, bf16[160,384]{1,0:T(8,128)(2,1)S(1)}, u32[]{:S(2)}, u32[]{:S(2)}) collective-permute-start(bf16[160,384]{1,0:T(8,128)(2,1)S(1)} %get-tuple-element.428), channel_id=1, source_target_pairs={{0,12},{4,8},{8,4},{12,0},{16,28},{20,24},{24,20},{28,16},{1,13},{... | collective-permute-start | bytes 368648 | tf_op jit(solution)/shard_map/ppermute | solution.py:656
  43.7 10.2 %collective-permute-start.21 = (bf16[256,384]{1,0:T(8,128)(2,1)S(1)}, bf16[256,384]{1,0:T(8,128)(2,1)S(1)}, u32[]{:S(2)}, u32[]{:S(2)}) collective-permute-start(bf16[256,384]{1,0:T(8,128)(2,1)S(1)} %add_convert_fusion.2), channel_id=1, source_target_pairs={{0,16},{4,20},{8,24},{12,28},{16,0},{20,4},{24,8},{28,12},{1,17},{... | collective-permute-start | bytes 589832 | tf_op jit(solution)/shard_map/ppermute | solution.py:656
  46.5 21.5 %collective-permute-start.16 = (bf16[6,81,512]{2,1,0:T(8,128)(2,1)S(1)}, bf16[6,81,512]{2,1,0:T(8,128)(2,1)S(1)}, u32[]{:S(2)}, u32[]{:S(2)}) collective-permute-start(bf16[6,81,512]{2,1,0:T(8,128)(2,1)S(1)} %add_convert_fusion), channel_id=1, source_target_pairs={{0,2},{1,3},{2,0},{3,1},{4,6},{5,7},{6,4},{7,5},{8,10},{9,11},{10,... | collective-permute-start | bytes 1493000 | tf_op jit(solution)/shard_map/ppermute | solution.py:653
  53.4 7.7 %collective-permute-start.20 = (bf16[160,384]{1,0:T(8,128)(2,1)S(1)}, bf16[160,384]{1,0:T(8,128)(2,1)S(1)}, u32[]{:S(2)}, u32[]{:S(2)}) collective-permute-start(bf16[160,384]{1,0:T(8,128)(2,1)S(1)} %add_convert_fusion.4), channel_id=1, source_target_pairs={{0,16},{4,20},{8,24},{12,28},{16,0},{20,4},{24,8},{28,12},{1,17},{... | collective-permute-start | bytes 368648 | tf_op jit(solution)/shard_map/ppermute | solution.py:656
  53.9 10.6 %collective-permute-start.23 = (bf16[256,384]{1,0:T(8,128)(2,1)S(1)}, bf16[256,384]{1,0:T(8,128)(2,1)S(1)}, u32[]{:S(2)}, u32[]{:S(2)}) collective-permute-start(bf16[256,384]{1,0:T(8,128)(2,1)S(1)} %add_convert_fusion.1), channel_id=1, source_target_pairs={{0,8},{4,12},{8,0},{12,4},{16,24},{20,28},{24,16},{28,20},{1,9},{5... | collective-permute-start | bytes 589832 | tf_op jit(solution)/shard_map/ppermute | solution.py:656
  61.1 5.2 %collective-permute-start.22 = (bf16[160,384]{1,0:T(8,128)(2,1)S(1)}, bf16[160,384]{1,0:T(8,128)(2,1)S(1)}, u32[]{:S(2)}, u32[]{:S(2)}) collective-permute-start(bf16[160,384]{1,0:T(8,128)(2,1)S(1)} %add_convert_fusion.3), channel_id=1, source_target_pairs={{0,8},{4,12},{8,0},{12,4},{16,24},{20,28},{24,16},{28,20},{1,9},{5... | collective-permute-start | bytes 368648 | tf_op jit(solution)/shard_map/ppermute | solution.py:656
  64.6 9.9 %collective-permute-start.26 = (bf16[2,256,384]{2,1,0:T(8,128)(2,1)S(1)}, bf16[2,256,384]{2,1,0:T(8,128)(2,1)S(1)}, u32[]{:S(2)}, u32[]{:S(2)}) collective-permute-start(bf16[2,256,384]{2,1,0:T(8,128)(2,1)S(1)} %pad_maximum_fusion.refs_0_), channel_id=1, source_target_pairs={{0,4},{1,3},{2,6},{3,1},{4,0},{5,7},{6,2},{7,5},{8,12},{9,11},{10,... | collective-permute-start | bytes 1179656 | tf_op jit(solution)/shard_map/ppermute | solution.py:664
  65.7 9.2 %collective-permute-start.27 = (bf16[2,256,384]{2,1,0:T(8,128)(2,1)S(1)}, bf16[2,256,384]{2,1,0:T(8,128)(2,1)S(1)}, u32[]{:S(2)}, u32[]{:S(2)}) collective-permute-start(bf16[2,256,384]{2,1,0:T(8,128)(2,1)S(1)} %pad_maximum_fusion.refs_0_), channel_id=1, source_target_pairs={{0,2},{1,5},{2,0},{3,7},{4,6},{5,1},{6,4},{7,3},{8,10},{9,13},{10,... | collective-permute-start | bytes 1179656 | tf_op jit(solution)/shard_map/ppermute | solution.py:664
  66.4 11.5 %collective-permute-start.24 = (bf16[2,160,384]{2,1,0:T(8,128)(2,1)S(1)}, bf16[2,160,384]{2,1,0:T(8,128)(2,1)S(1)}, u32[]{:S(2)}, u32[]{:S(2)}) collective-permute-start(bf16[2,160,384]{2,1,0:T(8,128)(2,1)S(1)} %pad_maximum_fusion.2.refs_2_.refs_0_), channel_id=1, source_target_pairs={{0,4},{1,3},{2,6},{3,1},{4,0},{5,7},{6,2},{7,5},{8,12},{9,11},{10,... | collective-permute-start | bytes 737288 | tf_op jit(solution)/shard_map/ppermute | solution.py:664
  68.0 11.4 %collective-permute-start.30 = (bf16[2,256,384]{2,1,0:T(8,128)(2,1)S(1)}, bf16[2,256,384]{2,1,0:T(8,128)(2,1)S(1)}, u32[]{:S(2)}, u32[]{:S(2)}) collective-permute-start(bf16[2,256,384]{2,1,0:T(8,128)(2,1)S(1)} %pad_maximum_fusion.refs_0_), channel_id=1, source_target_pairs={{0,1},{1,0},{2,3},{3,2},{4,5},{5,4},{6,7},{7,6},{8,9},{9,8},{10,11... | collective-permute-start | bytes 1179656 | tf_op jit(solution)/shard_map/ppermute | solution.py:653
  68.0 9.9 %collective-permute-start.25 = (bf16[2,160,384]{2,1,0:T(8,128)(2,1)S(1)}, bf16[2,160,384]{2,1,0:T(8,128)(2,1)S(1)}, u32[]{:S(2)}, u32[]{:S(2)}) collective-permute-start(bf16[2,160,384]{2,1,0:T(8,128)(2,1)S(1)} %pad_maximum_fusion.2.refs_2_.refs_0_), channel_id=1, source_target_pairs={{0,2},{1,5},{2,0},{3,7},{4,6},{5,1},{6,4},{7,3},{8,10},{9,13},{10,... | collective-permute-start | bytes 737288 | tf_op jit(solution)/shard_map/ppermute | solution.py:664
  74.9 4.5 %collective-permute-start.31 = (bf16[2,256,384]{2,1,0:T(8,128)(2,1)S(1)}, bf16[2,256,384]{2,1,0:T(8,128)(2,1)S(1)}, u32[]{:S(2)}, u32[]{:S(2)}) collective-permute-start(bf16[2,256,384]{2,1,0:T(8,128)(2,1)S(1)} %collective-permute-done.26.refs_1_), channel_id=1, source_target_pairs={{0,1},{1,0},{2,3},{3,2},{4,5},{5,4},{6,7},{7,6},{8,9},{9,8},{10,11... | collective-permute-start | bytes 1179656 | tf_op jit(solution)/shard_map/ppermute | solution.py:653
  74.9 7.8 %collective-permute-start.29 = (bf16[2,256,384]{2,1,0:T(8,128)(2,1)S(1)}, bf16[2,256,384]{2,1,0:T(8,128)(2,1)S(1)}, u32[]{:S(2)}, u32[]{:S(2)}) collective-permute-start(bf16[2,256,384]{2,1,0:T(8,128)(2,1)S(1)} %collective-permute-done.26.refs_1_), channel_id=1, source_target_pairs={{0,2},{1,5},{2,0},{3,7},{4,6},{5,1},{6,4},{7,3},{8,10},{9,13},{10,... | collective-permute-start | bytes 1179656 | tf_op jit(solution)/shard_map/ppermute | solution.py:664
  77.9 7.4 %collective-permute-start.28 = (bf16[2,160,384]{2,1,0:T(8,128)(2,1)S(1)}, bf16[2,160,384]{2,1,0:T(8,128)(2,1)S(1)}, u32[]{:S(2)}, u32[]{:S(2)}) collective-permute-start(bf16[2,160,384]{2,1,0:T(8,128)(2,1)S(1)} %collective-permute-done.24.refs_3_.refs_1_), channel_id=1, source_target_pairs={{0,2},{1,5},{2,0},{3,7},{4,6},{5,1},{6,4},{7,3},{8,10},{9,13},{10,... | collective-permute-start | bytes 737288 | tf_op jit(solution)/shard_map/ppermute | solution.py:664
  82.7 2.8 %collective-permute-start.37 = (bf16[2,256,384]{2,1,0:T(8,128)(2,1)S(1)}, bf16[2,256,384]{2,1,0:T(8,128)(2,1)S(1)}, u32[]{:S(2)}, u32[]{:S(2)}) collective-permute-start(bf16[2,256,384]{2,1,0:T(8,128)(2,1)S(1)} %collective-permute-done.29.refs_0_), channel_id=1, source_target_pairs={{0,1},{1,0},{2,3},{3,2},{4,5},{5,4},{6,7},{7,6},{8,9},{9,8},{10,11... | collective-permute-start | bytes 1179656 | tf_op jit(solution)/shard_map/ppermute | solution.py:653
  85.3 2.9 %collective-permute-start.36 = (bf16[2,160,384]{2,1,0:T(8,128)(2,1)S(1)}, bf16[2,160,384]{2,1,0:T(8,128)(2,1)S(1)}, u32[]{:S(2)}, u32[]{:S(2)}) collective-permute-start(bf16[2,160,384]{2,1,0:T(8,128)(2,1)S(1)} %collective-permute-done.28.refs_3_), channel_id=1, source_target_pairs={{0,1},{1,0},{2,3},{3,2},{4,5},{5,4},{6,7},{7,6},{8,9},{9,8},{10,11... | collective-permute-start | bytes 737288 | tf_op jit(solution)/shard_map/ppermute | solution.py:653
  (14 other events, 42.2 us)

commit v7 on v6

--- a/solution.py
+++ b/solution.py
@@ -24,8 +24,8 @@
 
 ORDER = (
     "weights", "a_send", "sums", "tick", "stats", "back", "v_send", "rows", "a_rs", "tick", "tick", "tick",
-    "rows_core", "v_rs", "a_z2", "v_z2", "a_pair", "tick", "v_pair", "finish", "a_mark", "tick", "v_mark", "tick",
-    "a_twin0", "a_twin1", "a_twin2", "place_head", "a_third", "a_twin3", "v_third", "v_twin3", "v_twin0", "v_twin1",
+    "rows_core", "v_rs", "a_z2", "v_z2", "a_pair", "tick", "v_pair", "finish", "a_twin0", "a_mark", "tick", "v_mark",
+    "tick", "a_twin1", "a_twin2", "place_head", "a_third", "v_third", "a_twin3", "v_twin3", "v_twin0", "v_twin1",
     "v_twin2", "tick", "place_most", "place_last",
 )
 

time: 90.3 us -> 90.3 us (level)
  no operation moved by 1% of the time
where the time goes in v7:
time: 90.3 us; the launch traced here: 90 us
  starting transfers between devices  33.1 us (37%)
  Pallas kernels  28.5 us (32%)
  waiting for transfers between devices  22.4 us (25%)
  local copies, waits for them, and re-layouts  2.57 us (3%)
  other arithmetic  2.26 us (3%)
  between operations  1.15 us (1%)
    pallas_call x25, Pallas kernels, call(): pl.pallas_call(body, out_shape=outs, in_specs=specs if specs is not None...  28.5 us
    ppermute x10, starting transfers between devices, over_dp(): return lax.ppermute(x, 'dp', [(i, i ^ flip) for i in range(m)])  16.5 us
    ppermute x10, waiting for transfers between devices, over_dp(): return lax.ppermute(x, 'dp', [(i, i ^ flip) for i in range(m)])  10.7 us
    ppermute x22, starting transfers between devices, over_seq(): return lax.ppermute(x, 'seq', [(i, i ^ flip) for i in range(n)])  10.3 us
    ppermute x6, waiting for transfers between devices, mixed_axes(): return lax.ppermute(x, ('dp', 'seq'), pairs)  7.69 us
    ppermute x6, starting transfers between devices, mixed_axes(): return lax.ppermute(x, ('dp', 'seq'), pairs)  6.38 us
    ppermute x22, waiting for transfers between devices, over_seq(): return lax.ppermute(x, 'seq', [(i, i ^ flip) for i in range(n)])  3.95 us
  transfers between devices with their start and end apart: 38, of which 17 were waited for; matrix products, arithmetic and copies ran while one was open for 5% of the time, Pallas kernels for 26%

profile of v7, /device:TPU:0, one launch (start us, length us, event | category | flops | bytes accessed | tf_op | source)
XLA Modules:
  0.0 90.0 jit_solution(3785806247627512481)
XLA Ops:
  1.2 2.6 %collective-permute-start.1 = (bf16[3,81,512]{2,1,0:T(8,128)(2,1)}, bf16[3,81,512]{2,1,0:T(8,128)(2,1)S(1)}, u32[]{:S(2)}, u32[]{:S(2)}) collective-permute-start(bf16[3,81,512]{2,1,0:T(8,128)(2,1)} %tok), channel_id=1, source_target_pairs={{0,2},{1,3},{2,0},{3,1},{4,6},{5,7},{6,4},{7,5},{8,10},{9,11},{10,... | collective-permute-start | bytes 746504 | tf_op jit(solution)/shard_map/ppermute | solution.py:653
  7.0 1.2 %constant_dynamic-slice_fusion.1 = (bf16[512,384]{1,0:T(8,128)(2,1)S(1)}, bf16[512,384]{1,0:T(8,128)(2,1)S(1)}) fusion(bf16[512,3072]{1,0:T(8,128)(2,1)} %param.15, s32[]{:T(128)S(6)} %select_n.10, s32[]{:T(128)S(6)} %select_n.9), kind=kLoop, calls=%fused_computation.15 | loop fusion | bytes 1572872 | tf_op jit(solution)/shard_map/dynamic_slice | solution.py:730
  8.7 1.8 %project.3 = (bf16[576,512]{1,0:T(8,128)(2,1)S(1)}, bf16[576,384]{1,0:T(8,128)(2,1)S(1)}, bf16[576,384]{1,0:T(8,128)(2,1)S(1)}, f32[576,384]{1,0:T(8,128)S(1)}, ...) custom-call(bf16[3,81,512]{2,1,0:T(8,128)(2,1)S(1)} %copy-done.1, ...), custom_call_target="tpu_custom_call" | custom-call | flops 1 | bytes 1 | tf_op jit(solution)/shard_map/project/pallas_call | solution.py:50
  11.1 1.1 %project.4 = (bf16[288,512]{1,0:T(8,128)(2,1)S(1)}, bf16[288,384]{1,0:T(8,128)(2,1)S(1)}, bf16[288,384]{1,0:T(8,128)(2,1)S(1)}, f32[288,384]{1,0:T(8,128)S(1)}, ...) custom-call(bf16[3,81,512]{2,1,0:T(8,128)(2,1)S(1)} %collective-permute-done.1.refs_0_, f32[1,512]{1,0:T(1,128)S(1)} %bitcast.15, ...), custom_call_target="tpu_custom_call" | custom-call | flops 1 | bytes 1 | tf_op jit(solution)/shard_map/project/pallas_call | solution.py:50
  12.6 1.1 %project.5 = (bf16[288,512]{1,0:T(8,128)(2,1)S(1)}, bf16[288,384]{1,0:T(8,128)(2,1)S(1)}, bf16[288,384]{1,0:T(8,128)(2,1)S(1)}, f32[288,384]{1,0:T(8,128)S(1)}, ...) custom-call(bf16[3,81,512]{2,1,0:T(8,128)(2,1)S(1)} %collective-permute-done.2.refs_0_, f32[1,512]{1,0:T(1,128)S(1)} %bitcast.16, ...), custom_call_target="tpu_custom_call" | custom-call | flops 1 | bytes 1 | tf_op jit(solution)/shard_map/project/pallas_call | solution.py:50
  13.9 2.2 %collective-permute-start.7 = (f32[24,128]{1,0:T(8,128)S(1)}, f32[24,128]{1,0:T(8,128)S(1)}, u32[]{:S(2)}, u32[]{:S(2)}) collective-permute-start(f32[24,128]{1,0:T(8,128)S(1)} %get-tuple-element.346.t0), channel_id=1, source_target_pairs={{0,2},{1,3},{2,0},{3,1},{4,6},{5,7},{6,4},{7,5},{8,10},{9,11},{10,... | collective-permute-start | bytes 36872 | tf_op jit(solution)/shard_map/ppermute | solution.py:653
  16.2 1.2 %front.2 = (bf16[576,512]{1,0:T(8,128)(2,1)S(1)}, f32[576,384]{1,0:T(8,128)S(1)}, bf16[576,384]{1,0:T(8,128)(2,1)S(1)}, bf16[192,384]{1,0:T(8,128)(2,1)S(1)}, bf16[384,384]{1,0:T(8,128)(2,1)S(1)}) custom-call(s32[8]{0:T(128)S(1)} %pad_add_fusion.meta, bf16[324,512]{1,0:T(8,128)(2,1)S(1)} %pad_maximum_fusion.1.refs_0_.cot, ...), custom_call_target="tpu_custom_call" | custom-call | flops 1 | bytes 1 | tf_op jit(solution)/shard_map/front/pallas_call | solution.py:50
  20.3 1.5 %prepare.1 = (bf16[288,512]{1,0:T(8,128)(2,1)S(1)}, f32[288,384]{1,0:T(8,128)S(1)}, bf16[384,1152]{1,0:T(8,128)(2,1)S(1)}, f32[1152,384]{1,0:T(8,128)S(1)}, bf16[384,384]{1,0:T(8,128)(2,1)S(1)}) custom-call(s32[8]{0:T(128)S(1)} %pad_add_fusion.meta, bf16[324,512]{1,0:T(8,128)(2,1)S(1)} %collective-permute-done.5.c3, ...), custom_call_target="tpu_custom_call" | custom-call | flops 1 | bytes 1 | tf_op jit(solution)/shard_map/prepare/pallas_call | solution.py:50
  21.9 3.4 %spatial.1 = (bf16[1152,384]{1,0:T(8,128)(2,1)S(1)}, bf16[1152,384]{1,0:T(8,128)(2,1)S(1)}, f32[128,128]{1,0:T(8,128)S(1)}, f32[24,128]{1,0:T(8,128)S(1)}, bf16[...) custom-call(s32[8]{0:T(128)S(1)} %pad_add_fusion.meta, ...), custom_call_target="tpu_custom_call" | custom-call | flops 1 | bytes 1 | tf_op jit(solution)/shard_map/spatial/pallas_call | solution.py:50
  25.3 1.7 %collective-permute-start.10 = (bf16[128,384]{1,0:T(8,128)(2,1)S(1)}, bf16[128,384]{1,0:T(8,128)(2,1)S(1)}, u32[]{:S(2)}, u32[]{:S(2)}) collective-permute-start(bf16[128,384]{1,0:T(8,128)(2,1)S(1)} %get-tuple-element.359), channel_id=1, source_target_pairs={{0,2},{1,3},{2,0},{3,1},{4,6},{5,7},{6,4},{7,5},{8,10},{9,11},{10,... | collective-permute-start | bytes 294920 | tf_op jit(solution)/shard_map/ppermute | solution.py:653
  27.0 2.4 %weights.1 = (bf16[256,384]{1,0:T(8,128)(2,1)S(1)}, bf16[256,384]{1,0:T(8,128)(2,1)S(1)}, bf16[256,384]{1,0:T(8,128)(2,1)S(1)}, bf16[256,384]{1,0:T(8,128)(2,1)S(1)}, f32[512,384]{1,0:T(8,128)S(1)}) custom-call(s32[8]{0:T(128)S(1)} %pad_add_fusion.meta, bf16[1152,384]{1,0:T(8,128)(2,1)S(1)} %get-tuple-element.407.prod, ...), custom_call_target="tpu_custom_call" | custom-call | flops 1 | bytes 1 | tf_op jit(solution)/shard_map/weights/pallas_call | solution.py:50
  30.4 1.5 %collective-permute-start.13 = (bf16[256,384]{1,0:T(8,128)(2,1)S(1)}, bf16[256,384]{1,0:T(8,128)(2,1)S(1)}, u32[]{:S(2)}, u32[]{:S(2)}) collective-permute-start(bf16[256,384]{1,0:T(8,128)(2,1)S(1)} %get-tuple-element.416), channel_id=1, source_target_pairs={{0,4},{4,0},{8,12},{12,8},{16,20},{20,16},{24,28},{28,24},{1,5},{5... | collective-permute-start | bytes 589832 | tf_op jit(solution)/shard_map/ppermute | solution.py:656
  31.9 1.6 %collective-permute-start.14 = (bf16[256,384]{1,0:T(8,128)(2,1)S(1)}, bf16[256,384]{1,0:T(8,128)(2,1)S(1)}, u32[]{:S(2)}, u32[]{:S(2)}) collective-permute-start(bf16[256,384]{1,0:T(8,128)(2,1)S(1)} %get-tuple-element.417), channel_id=1, source_target_pairs={{0,8},{4,12},{8,0},{12,4},{16,24},{20,28},{24,16},{28,20},{1,9},{5... | collective-permute-start | bytes 589832 | tf_op jit(solution)/shard_map/ppermute | solution.py:656
  34.9 2.9 %back.1 = (bf16[1152,384]{1,0:T(8,128)(2,1)S(1)}, bf16[160,384]{1,0:T(8,128)(2,1)S(1)}, bf16[160,384]{1,0:T(8,128)(2,1)S(1)}, bf16[160,384]{1,0:T(8,128)(2,1)S(1)}, bf16[160,384]{1,0:T(8,128)(2,1)S(1)}) custom-call(s32[8]{0:T(128)S(1)} %pad_add_fusion.meta, f32[1152,384]{1,0:T(8,128)S(1)} %get-tuple-element.382.gmix, f32[576,384]{1,0:T(8,128)S(1)} %get-tuple-element.383.v0, ...), custom_call_target="tpu_custom_call" | custom-call | flops 1 | bytes 1 | tf_op jit(solution)/shard_map/back/pallas_call | solution.py:50
  37.8 2.0 %rows_out.1 = (bf16[6,81,512]{2,1,0:T(8,128)(2,1)S(1)}, bf16[6,81,512]{2,1,0:T(8,128)(2,1)S(1)}, bf16[12,81,512]{2,1,0:T(8,128)(2,1)S(1)}) custom-call(bf16[1152,384]{1,0:T(8,128)(2,1)S(1)} %get-tuple-element.407.prod, bf16[384,512]{1,0:T(8,128)(2,1)S(1)} %constant_dynamic-slice_fusion.refs_2_.refs_1_.wo, ...), custom_call_target="tpu_custom_call" | custom-call | flops 1 | bytes 1 | tf_op jit(solution)/shard_map/rows_out/pallas_call | solution.py:50
  40.1 1.5 %collective-permute-start.17 = (bf16[160,384]{1,0:T(8,128)(2,1)S(1)}, bf16[160,384]{1,0:T(8,128)(2,1)S(1)}, u32[]{:S(2)}, u32[]{:S(2)}) collective-permute-start(bf16[160,384]{1,0:T(8,128)(2,1)S(1)} %get-tuple-element.426), channel_id=1, source_target_pairs={{0,4},{4,0},{8,12},{12,8},{16,20},{20,16},{24,28},{28,24},{1,5},{5... | collective-permute-start | bytes 368648 | tf_op jit(solution)/shard_map/ppermute | solution.py:656
  41.5 1.6 %collective-permute-start.18 = (bf16[160,384]{1,0:T(8,128)(2,1)S(1)}, bf16[160,384]{1,0:T(8,128)(2,1)S(1)}, u32[]{:S(2)}, u32[]{:S(2)}) collective-permute-start(bf16[160,384]{1,0:T(8,128)(2,1)S(1)} %get-tuple-element.427), channel_id=1, source_target_pairs={{0,8},{4,12},{8,0},{12,4},{16,24},{20,28},{24,16},{28,20},{1,9},{5... | collective-permute-start | bytes 368648 | tf_op jit(solution)/shard_map/ppermute | solution.py:656
  43.7 2.7 %collective-permute-start.21 = (bf16[256,384]{1,0:T(8,128)(2,1)S(1)}, bf16[256,384]{1,0:T(8,128)(2,1)S(1)}, u32[]{:S(2)}, u32[]{:S(2)}) collective-permute-start(bf16[256,384]{1,0:T(8,128)(2,1)S(1)} %add_convert_fusion.2), channel_id=1, source_target_pairs={{0,16},{4,20},{8,24},{12,28},{16,0},{20,4},{24,8},{28,12},{1,17},{... | collective-permute-start | bytes 589832 | tf_op jit(solution)/shard_map/ppermute | solution.py:656
  47.3 4.7 %collective-permute-done.18 = bf16[160,384]{1,0:T(8,128)(2,1)S(1)} collective-permute-done((bf16[160,384]{1,0:T(8,128)(2,1)S(1)}, bf16[160,384]{1,0:T(8,128)(2,1)S(1)}, u32[]{:S(2)}, u32[]{:S(2)}) %collective-permute-start.18) | collective-permute-done | bytes 122912 | tf_op jit(solution)/shard_map/ppermute | solution.py:656
  51.9 1.4 %collective-permute-done.19 = bf16[160,384]{1,0:T(8,128)(2,1)S(1)} collective-permute-done((bf16[160,384]{1,0:T(8,128)(2,1)S(1)}, bf16[160,384]{1,0:T(8,128)(2,1)S(1)}, u32[]{:S(2)}, u32[]{:S(2)}) %collective-permute-start.19) | collective-permute-done | bytes 122912 | tf_op jit(solution)/shard_map/ppermute | solution.py:656
  53.9 6.1 %collective-permute-start.23 = (bf16[256,384]{1,0:T(8,128)(2,1)S(1)}, bf16[256,384]{1,0:T(8,128)(2,1)S(1)}, u32[]{:S(2)}, u32[]{:S(2)}) collective-permute-start(bf16[256,384]{1,0:T(8,128)(2,1)S(1)} %add_convert_fusion.1), channel_id=1, source_target_pairs={{0,8},{4,12},{8,0},{12,4},{16,24},{20,28},{24,16},{28,20},{1,9},{5... | collective-permute-start | bytes 589832 | tf_op jit(solution)/shard_map/ppermute | solution.py:656
  61.4 3.1 %collective-permute-done.23 = bf16[256,384]{1,0:T(8,128)(2,1)S(1)} collective-permute-done((bf16[256,384]{1,0:T(8,128)(2,1)S(1)}, bf16[256,384]{1,0:T(8,128)(2,1)S(1)}, u32[]{:S(2)}, u32[]{:S(2)}) %collective-permute-start.23) | collective-permute-done | bytes 196640 | tf_op jit(solution)/shard_map/ppermute | solution.py:656
  64.6 1.1 %collective-permute-start.26 = (bf16[2,256,384]{2,1,0:T(8,128)(2,1)S(1)}, bf16[2,256,384]{2,1,0:T(8,128)(2,1)S(1)}, u32[]{:S(2)}, u32[]{:S(2)}) collective-permute-start(bf16[2,256,384]{2,1,0:T(8,128)(2,1)S(1)} %pad_maximum_fusion.refs_0_), channel_id=1, source_target_pairs={{0,4},{1,3},{2,6},{3,1},{4,0},{5,7},{6,2},{7,5},{8,12},{9,11},{10,... | collective-permute-start | bytes 1179656 | tf_op jit(solution)/shard_map/ppermute | solution.py:664
  66.4 1.6 %collective-permute-start.24 = (bf16[2,160,384]{2,1,0:T(8,128)(2,1)S(1)}, bf16[2,160,384]{2,1,0:T(8,128)(2,1)S(1)}, u32[]{:S(2)}, u32[]{:S(2)}) collective-permute-start(bf16[2,160,384]{2,1,0:T(8,128)(2,1)S(1)} %pad_maximum_fusion.2.refs_2_.refs_0_), channel_id=1, source_target_pairs={{0,4},{1,3},{2,6},{3,1},{4,0},{5,7},{6,2},{7,5},{8,12},{9,11},{10,... | collective-permute-start | bytes 737288 | tf_op jit(solution)/shard_map/ppermute | solution.py:664
  68.8 1.9 %finish_rows.1 = (bf16[3,81,512]{2,1,0:T(8,128)(2,1)}, bf16[3,81,512]{2,1,0:T(8,128)(2,1)}) custom-call(s32[8]{0:T(128)S(1)} %pad_add_fusion.meta, bf16[3,81,512]{2,1,0:T(8,128)(2,1)S(1)} %copy-done.1, bf16[324,512]{1,0:T(8,128)(2,1)S(1)} %pad_maximum_fusion.1.refs_0_.cot, bf16[6,81,512]{2,1,0:T(8,128)(2,1)S(1)} %get-tuple-element.445.keep, ...), custom_call_target="tpu_custom_call" | custom-call | flops 1 | bytes 1 | tf_op jit(solution)/shard_map/finish_rows/pallas_call | solution.py:50
  70.7 3.7 %collective-permute-done.26.refs_1_ = bf16[2,256,384]{2,1,0:T(8,128)(2,1)S(1)} collective-permute-done((bf16[2,256,384]{2,1,0:T(8,128)(2,1)S(1)}, bf16[2,256,384]{2,1,0:T(8,128)(2,1)S(1)}, u32[]{:S(2)}, u32[]{:S(2)}) %collective-permute-start.26) | collective-permute-done | bytes 393248 | tf_op jit(solution)/shard_map/ppermute | solution.py:664
  76.1 1.8 %collective-permute-done.24.refs_3_.refs_1_ = bf16[2,160,384]{2,1,0:T(8,128)(2,1)S(1)} collective-permute-done((bf16[2,160,384]{2,1,0:T(8,128)(2,1)S(1)}, bf16[2,160,384]{2,1,0:T(8,128)(2,1)S(1)}, u32[]{:S(2)}, u32[]{:S(2)}) %collective-permute-start.24) | collective-permute-done | bytes 245792 | tf_op jit(solution)/shard_map/ppermute | solution.py:664
  77.9 1.5 %collective-permute-start.28 = (bf16[2,160,384]{2,1,0:T(8,128)(2,1)S(1)}, bf16[2,160,384]{2,1,0:T(8,128)(2,1)S(1)}, u32[]{:S(2)}, u32[]{:S(2)}) collective-permute-start(bf16[2,160,384]{2,1,0:T(8,128)(2,1)S(1)} %collective-permute-done.24.refs_3_.refs_1_), channel_id=1, source_target_pairs={{0,2},{1,5},{2,0},{3,7},{4,6},{5,1},{6,4},{7,3},{8,10},{9,13},{10,... | collective-permute-start | bytes 737288 | tf_op jit(solution)/shard_map/ppermute | solution.py:664
  79.6 3.0 %place.2 = (f32[512,3072]{1,0:T(8,128)}, f32[1536,512]{1,0:T(8,128)}) custom-call(s32[8]{0:T(128)S(1)} %pad_add_fusion.meta, bf16[2,256,384]{2,1,0:T(8,128)(2,1)S(1)} %pad_maximum_fusion.refs_0_, bf16[2,256,384]{2,1,0:T(8,128)(2,1)S(1)} %collective-permute-done.26.refs_1_, bf16[2,256,384]{2,1,0:T(8,128)(2,1)S(1)} %collective-permute-done.27.refs_2_, ...), custom_call_target="tpu_custom_call" | custom-call | flops 1 | bytes 1 | tf_op jit(solution)/shard_map/place/pallas_call | solution.py:50
  83.7 1.6 %collective-permute-done.28.refs_3_ = bf16[2,160,384]{2,1,0:T(8,128)(2,1)S(1)} collective-permute-done((bf16[2,160,384]{2,1,0:T(8,128)(2,1)S(1)}, bf16[2,160,384]{2,1,0:T(8,128)(2,1)S(1)}, u32[]{:S(2)}, u32[]{:S(2)}) %collective-permute-start.28) | collective-permute-done | bytes 245792 | tf_op jit(solution)/shard_map/ppermute | solution.py:664
  85.5 2.7 %place.3 = (f32[512,3072]{1,0:T(8,128)}, f32[1536,512]{1,0:T(8,128)}) custom-call(s32[8]{0:T(128)S(1)} %pad_add_fusion.meta, bf16[2,256,384]{2,1,0:T(8,128)(2,1)S(1)} %collective-permute-done.29.refs_0_, bf16[2,256,384]{2,1,0:T(8,128)(2,1)S(1)} %collective-permute-done.37.refs_1_, ...), custom_call_target="tpu_custom_call", output_to_operand_aliasing={{0}: (9, {}), {1}: (10, {})} | custom-call | flops 1 | bytes 1 | tf_op jit(solution)/shard_map/place/pallas_call | solution.py:50
  88.2 1.6 %place_last.1 = (f32[512,3072]{1,0:T(8,128)}, f32[81,324]{1,0:T(8,128)}, f32[81]{0:T(128)}, f32[512]{0:T(512)}, f32[512]{0:T(512)}, /*index=5*/f32[1536]{0:T(1024)}, f32[1536]{0:T(1024)}) custom-call(s32[8]{0:T(128)S(1)} %pad_add_fusion.meta, bf16[2,160,384]{2,1,0:T(8,128)(2,1)S(1)} %pad_maximum_fusion.2.refs_2_.refs_0_, ...), custom_call_target="tpu_custom_call", output_to_operand_aliasing={{0}: (9, {})} | custom-call | flops 1 | bytes 1 | tf_op jit(solution)/shard_map/place_last/pallas_call | solution.py:50
  (102 shorter events, 18.8 us)
Async XLA Ops:
  0.7 7.5 %collective-permute-start = (bf16[3,81,512]{2,1,0:T(8,128)(2,1)}, bf16[3,81,512]{2,1,0:T(8,128)(2,1)S(1)}, u32[]{:S(2)}, u32[]{:S(2)}) collective-permute-start(bf16[3,81,512]{2,1,0:T(8,128)(2,1)} %tok), channel_id=1, source_target_pairs={{0,1},{1,0},{2,3},{3,2},{4,5},{5,4},{6,7},{7,6},{8,9},{9,8},{10,11... | collective-permute-start | bytes 746504 | tf_op jit(solution)/shard_map/ppermute | solution.py:653
  1.2 9.9 %collective-permute-start.1 = (bf16[3,81,512]{2,1,0:T(8,128)(2,1)}, bf16[3,81,512]{2,1,0:T(8,128)(2,1)S(1)}, u32[]{:S(2)}, u32[]{:S(2)}) collective-permute-start(bf16[3,81,512]{2,1,0:T(8,128)(2,1)} %tok), channel_id=1, source_target_pairs={{0,2},{1,3},{2,0},{3,1},{4,6},{5,7},{6,4},{7,5},{8,10},{9,11},{10,... | collective-permute-start | bytes 746504 | tf_op jit(solution)/shard_map/ppermute | solution.py:653
  8.2 8.0 %collective-permute-start.4 = (bf16[324,512]{1,0:T(8,128)(2,1)S(1)}, bf16[324,512]{1,0:T(8,128)(2,1)S(1)}, u32[]{:S(2)}, u32[]{:S(2)}) collective-permute-start(bf16[324,512]{1,0:T(8,128)(2,1)S(1)} %pad_maximum_fusion.1.refs_0_.cot), channel_id=1, source_target_pairs={{0,1},{1,0},{2,3},{3,2},{4,5},{5,4},{6,7},{7,6},{8,9},{9,8},{10,11... | collective-permute-start | bytes 995336 | tf_op jit(solution)/shard_map/ppermute | solution.py:653
  8.4 10.3 %collective-permute-start.3 = (bf16[324,512]{1,0:T(8,128)(2,1)S(1)}, bf16[324,512]{1,0:T(8,128)(2,1)S(1)}, u32[]{:S(2)}, u32[]{:S(2)}) collective-permute-start(bf16[324,512]{1,0:T(8,128)(2,1)S(1)} %pad_maximum_fusion.1.refs_0_.cot), channel_id=1, source_target_pairs={{0,2},{1,3},{2,0},{3,1},{4,6},{5,7},{6,4},{7,5},{8,10},{9,11},{10,... | collective-permute-start | bytes 995336 | tf_op jit(solution)/shard_map/ppermute | solution.py:653
  13.8 8.0 %collective-permute-start.6 = (f32[24,128]{1,0:T(8,128)S(1)}, f32[24,128]{1,0:T(8,128)S(1)}, u32[]{:S(2)}, u32[]{:S(2)}) collective-permute-start(f32[24,128]{1,0:T(8,128)S(1)} %get-tuple-element.346.t0), channel_id=1, source_target_pairs={{0,1},{1,0},{2,3},{3,2},{4,5},{5,4},{6,7},{7,6},{8,9},{9,8},{10,11... | collective-permute-start | bytes 36872 | tf_op jit(solution)/shard_map/ppermute | solution.py:653
  13.9 7.9 %collective-permute-start.7 = (f32[24,128]{1,0:T(8,128)S(1)}, f32[24,128]{1,0:T(8,128)S(1)}, u32[]{:S(2)}, u32[]{:S(2)}) collective-permute-start(f32[24,128]{1,0:T(8,128)S(1)} %get-tuple-element.346.t0), channel_id=1, source_target_pairs={{0,2},{1,3},{2,0},{3,1},{4,6},{5,7},{6,4},{7,5},{8,10},{9,11},{10,... | collective-permute-start | bytes 36872 | tf_op jit(solution)/shard_map/ppermute | solution.py:653
  16.2 5.7 %collective-permute-start.8 = (f32[24,128]{1,0:T(8,128)S(1)}, f32[24,128]{1,0:T(8,128)S(1)}, u32[]{:S(2)}, u32[]{:S(2)}) collective-permute-start(f32[24,128]{1,0:T(8,128)S(1)} %get-tuple-element.346.t0), channel_id=1, source_target_pairs={{0,3},{1,2},{2,1},{3,0},{4,7},{5,6},{6,5},{7,4},{8,11},{9,10},{10,... | collective-permute-start | bytes 36872 | tf_op jit(solution)/shard_map/ppermute | solution.py:653
  25.3 8.2 %collective-permute-start.10 = (bf16[128,384]{1,0:T(8,128)(2,1)S(1)}, bf16[128,384]{1,0:T(8,128)(2,1)S(1)}, u32[]{:S(2)}, u32[]{:S(2)}) collective-permute-start(bf16[128,384]{1,0:T(8,128)(2,1)S(1)} %get-tuple-element.359), channel_id=1, source_target_pairs={{0,2},{1,3},{2,0},{3,1},{4,6},{5,7},{6,4},{7,5},{8,10},{9,11},{10,... | collective-permute-start | bytes 294920 | tf_op jit(solution)/shard_map/ppermute | solution.py:653
  29.8 5.1 %collective-permute-start.11 = (bf16[128,384]{1,0:T(8,128)(2,1)S(1)}, bf16[128,384]{1,0:T(8,128)(2,1)S(1)}, u32[]{:S(2)}, u32[]{:S(2)}) collective-permute-start(bf16[128,384]{1,0:T(8,128)(2,1)S(1)} %get-tuple-element.360), channel_id=1, source_target_pairs={{0,3},{1,2},{2,1},{3,0},{4,7},{5,6},{6,5},{7,4},{8,11},{9,10},{10,... | collective-permute-start | bytes 294920 | tf_op jit(solution)/shard_map/ppermute | solution.py:653
  29.8 5.1 %collective-permute-start.9 = (bf16[128,384]{1,0:T(8,128)(2,1)S(1)}, bf16[128,384]{1,0:T(8,128)(2,1)S(1)}, u32[]{:S(2)}, u32[]{:S(2)}) collective-permute-start(bf16[128,384]{1,0:T(8,128)(2,1)S(1)} %get-tuple-element.358), channel_id=1, source_target_pairs={{0,1},{1,0},{2,3},{3,2},{4,5},{5,4},{6,7},{7,6},{8,9},{9,8},{10,11... | collective-permute-start | bytes 294920 | tf_op jit(solution)/shard_map/ppermute | solution.py:653
  30.4 11.1 %collective-permute-start.13 = (bf16[256,384]{1,0:T(8,128)(2,1)S(1)}, bf16[256,384]{1,0:T(8,128)(2,1)S(1)}, u32[]{:S(2)}, u32[]{:S(2)}) collective-permute-start(bf16[256,384]{1,0:T(8,128)(2,1)S(1)} %get-tuple-element.416), channel_id=1, source_target_pairs={{0,4},{4,0},{8,12},{12,8},{16,20},{20,16},{24,28},{28,24},{1,5},{5... | collective-permute-start | bytes 589832 | tf_op jit(solution)/shard_map/ppermute | solution.py:656
  31.9 11.2 %collective-permute-start.14 = (bf16[256,384]{1,0:T(8,128)(2,1)S(1)}, bf16[256,384]{1,0:T(8,128)(2,1)S(1)}, u32[]{:S(2)}, u32[]{:S(2)}) collective-permute-start(bf16[256,384]{1,0:T(8,128)(2,1)S(1)} %get-tuple-element.417), channel_id=1, source_target_pairs={{0,8},{4,12},{8,0},{12,4},{16,24},{20,28},{24,16},{28,20},{1,9},{5... | collective-permute-start | bytes 589832 | tf_op jit(solution)/shard_map/ppermute | solution.py:656
  33.5 10.1 %collective-permute-start.15 = (bf16[256,384]{1,0:T(8,128)(2,1)S(1)}, bf16[256,384]{1,0:T(8,128)(2,1)S(1)}, u32[]{:S(2)}, u32[]{:S(2)}) collective-permute-start(bf16[256,384]{1,0:T(8,128)(2,1)S(1)} %get-tuple-element.418), channel_id=1, source_target_pairs={{0,12},{4,8},{8,4},{12,0},{16,28},{20,24},{24,20},{28,16},{1,13},{... | collective-permute-start | bytes 589832 | tf_op jit(solution)/shard_map/ppermute | solution.py:656
  39.8 6.5 %collective-permute-start.12 = (bf16[12,81,512]{2,1,0:T(8,128)(2,1)S(1)}, bf16[12,81,512]{2,1,0:T(8,128)(2,1)S(1)}, u32[]{:S(2)}, u32[]{:S(2)}) collective-permute-start(bf16[12,81,512]{2,1,0:T(8,128)(2,1)S(1)} %get-tuple-element.414), channel_id=1, source_target_pairs={{0,1},{1,0},{2,3},{3,2},{4,5},{5,4},{6,7},{7,6},{8,9},{9,8},{10,11... | collective-permute-start | bytes 2985992 | tf_op jit(solution)/shard_map/ppermute | solution.py:653
  40.1 7.2 %collective-permute-start.17 = (bf16[160,384]{1,0:T(8,128)(2,1)S(1)}, bf16[160,384]{1,0:T(8,128)(2,1)S(1)}, u32[]{:S(2)}, u32[]{:S(2)}) collective-permute-start(bf16[160,384]{1,0:T(8,128)(2,1)S(1)} %get-tuple-element.426), channel_id=1, source_target_pairs={{0,4},{4,0},{8,12},{12,8},{16,20},{20,16},{24,28},{28,24},{1,5},{5... | collective-permute-start | bytes 368648 | tf_op jit(solution)/shard_map/ppermute | solution.py:656
  41.5 10.4 %collective-permute-start.18 = (bf16[160,384]{1,0:T(8,128)(2,1)S(1)}, bf16[160,384]{1,0:T(8,128)(2,1)S(1)}, u32[]{:S(2)}, u32[]{:S(2)}) collective-permute-start(bf16[160,384]{1,0:T(8,128)(2,1)S(1)} %get-tuple-element.427), channel_id=1, source_target_pairs={{0,8},{4,12},{8,0},{12,4},{16,24},{20,28},{24,16},{28,20},{1,9},{5... | collective-permute-start | bytes 368648 | tf_op jit(solution)/shard_map/ppermute | solution.py:656
  43.1 10.2 %collective-permute-start.19 = (bf16[160,384]{1,0:T(8,128)(2,1)S(1)}, bf16[160,384]{1,0:T(8,128)(2,1)S(1)}, u32[]{:S(2)}, u32[]{:S(2)}) collective-permute-start(bf16[160,384]{1,0:T(8,128)(2,1)S(1)} %get-tuple-element.428), channel_id=1, source_target_pairs={{0,12},{4,8},{8,4},{12,0},{16,28},{20,24},{24,20},{28,16},{1,13},{... | collective-permute-start | bytes 368648 | tf_op jit(solution)/shard_map/ppermute | solution.py:656
  43.7 10.2 %collective-permute-start.21 = (bf16[256,384]{1,0:T(8,128)(2,1)S(1)}, bf16[256,384]{1,0:T(8,128)(2,1)S(1)}, u32[]{:S(2)}, u32[]{:S(2)}) collective-permute-start(bf16[256,384]{1,0:T(8,128)(2,1)S(1)} %add_convert_fusion.2), channel_id=1, source_target_pairs={{0,16},{4,20},{8,24},{12,28},{16,0},{20,4},{24,8},{28,12},{1,17},{... | collective-permute-start | bytes 589832 | tf_op jit(solution)/shard_map/ppermute | solution.py:656
  46.5 21.5 %collective-permute-start.16 = (bf16[6,81,512]{2,1,0:T(8,128)(2,1)S(1)}, bf16[6,81,512]{2,1,0:T(8,128)(2,1)S(1)}, u32[]{:S(2)}, u32[]{:S(2)}) collective-permute-start(bf16[6,81,512]{2,1,0:T(8,128)(2,1)S(1)} %add_convert_fusion), channel_id=1, source_target_pairs={{0,2},{1,3},{2,0},{3,1},{4,6},{5,7},{6,4},{7,5},{8,10},{9,11},{10,... | collective-permute-start | bytes 1493000 | tf_op jit(solution)/shard_map/ppermute | solution.py:653
  53.4 7.7 %collective-permute-start.20 = (bf16[160,384]{1,0:T(8,128)(2,1)S(1)}, bf16[160,384]{1,0:T(8,128)(2,1)S(1)}, u32[]{:S(2)}, u32[]{:S(2)}) collective-permute-start(bf16[160,384]{1,0:T(8,128)(2,1)S(1)} %add_convert_fusion.4), channel_id=1, source_target_pairs={{0,16},{4,20},{8,24},{12,28},{16,0},{20,4},{24,8},{28,12},{1,17},{... | collective-permute-start | bytes 368648 | tf_op jit(solution)/shard_map/ppermute | solution.py:656
  53.9 10.6 %collective-permute-start.23 = (bf16[256,384]{1,0:T(8,128)(2,1)S(1)}, bf16[256,384]{1,0:T(8,128)(2,1)S(1)}, u32[]{:S(2)}, u32[]{:S(2)}) collective-permute-start(bf16[256,384]{1,0:T(8,128)(2,1)S(1)} %add_convert_fusion.1), channel_id=1, source_target_pairs={{0,8},{4,12},{8,0},{12,4},{16,24},{20,28},{24,16},{28,20},{1,9},{5... | collective-permute-start | bytes 589832 | tf_op jit(solution)/shard_map/ppermute | solution.py:656
  61.1 5.2 %collective-permute-start.22 = (bf16[160,384]{1,0:T(8,128)(2,1)S(1)}, bf16[160,384]{1,0:T(8,128)(2,1)S(1)}, u32[]{:S(2)}, u32[]{:S(2)}) collective-permute-start(bf16[160,384]{1,0:T(8,128)(2,1)S(1)} %add_convert_fusion.3), channel_id=1, source_target_pairs={{0,8},{4,12},{8,0},{12,4},{16,24},{20,28},{24,16},{28,20},{1,9},{5... | collective-permute-start | bytes 368648 | tf_op jit(solution)/shard_map/ppermute | solution.py:656
  64.6 9.9 %collective-permute-start.26 = (bf16[2,256,384]{2,1,0:T(8,128)(2,1)S(1)}, bf16[2,256,384]{2,1,0:T(8,128)(2,1)S(1)}, u32[]{:S(2)}, u32[]{:S(2)}) collective-permute-start(bf16[2,256,384]{2,1,0:T(8,128)(2,1)S(1)} %pad_maximum_fusion.refs_0_), channel_id=1, source_target_pairs={{0,4},{1,3},{2,6},{3,1},{4,0},{5,7},{6,2},{7,5},{8,12},{9,11},{10,... | collective-permute-start | bytes 1179656 | tf_op jit(solution)/shard_map/ppermute | solution.py:664
  65.7 9.2 %collective-permute-start.27 = (bf16[2,256,384]{2,1,0:T(8,128)(2,1)S(1)}, bf16[2,256,384]{2,1,0:T(8,128)(2,1)S(1)}, u32[]{:S(2)}, u32[]{:S(2)}) collective-permute-start(bf16[2,256,384]{2,1,0:T(8,128)(2,1)S(1)} %pad_maximum_fusion.refs_0_), channel_id=1, source_target_pairs={{0,2},{1,5},{2,0},{3,7},{4,6},{5,1},{6,4},{7,3},{8,10},{9,13},{10,... | collective-permute-start | bytes 1179656 | tf_op jit(solution)/shard_map/ppermute | solution.py:664
  66.4 11.5 %collective-permute-start.24 = (bf16[2,160,384]{2,1,0:T(8,128)(2,1)S(1)}, bf16[2,160,384]{2,1,0:T(8,128)(2,1)S(1)}, u32[]{:S(2)}, u32[]{:S(2)}) collective-permute-start(bf16[2,160,384]{2,1,0:T(8,128)(2,1)S(1)} %pad_maximum_fusion.2.refs_2_.refs_0_), channel_id=1, source_target_pairs={{0,4},{1,3},{2,6},{3,1},{4,0},{5,7},{6,2},{7,5},{8,12},{9,11},{10,... | collective-permute-start | bytes 737288 | tf_op jit(solution)/shard_map/ppermute | solution.py:664
  68.0 11.4 %collective-permute-start.30 = (bf16[2,256,384]{2,1,0:T(8,128)(2,1)S(1)}, bf16[2,256,384]{2,1,0:T(8,128)(2,1)S(1)}, u32[]{:S(2)}, u32[]{:S(2)}) collective-permute-start(bf16[2,256,384]{2,1,0:T(8,128)(2,1)S(1)} %pad_maximum_fusion.refs_0_), channel_id=1, source_target_pairs={{0,1},{1,0},{2,3},{3,2},{4,5},{5,4},{6,7},{7,6},{8,9},{9,8},{10,11... | collective-permute-start | bytes 1179656 | tf_op jit(solution)/shard_map/ppermute | solution.py:653
  68.0 9.9 %collective-permute-start.25 = (bf16[2,160,384]{2,1,0:T(8,128)(2,1)S(1)}, bf16[2,160,384]{2,1,0:T(8,128)(2,1)S(1)}, u32[]{:S(2)}, u32[]{:S(2)}) collective-permute-start(bf16[2,160,384]{2,1,0:T(8,128)(2,1)S(1)} %pad_maximum_fusion.2.refs_2_.refs_0_), channel_id=1, source_target_pairs={{0,2},{1,5},{2,0},{3,7},{4,6},{5,1},{6,4},{7,3},{8,10},{9,13},{10,... | collective-permute-start | bytes 737288 | tf_op jit(solution)/shard_map/ppermute | solution.py:664
  74.9 4.5 %collective-permute-start.31 = (bf16[2,256,384]{2,1,0:T(8,128)(2,1)S(1)}, bf16[2,256,384]{2,1,0:T(8,128)(2,1)S(1)}, u32[]{:S(2)}, u32[]{:S(2)}) collective-permute-start(bf16[2,256,384]{2,1,0:T(8,128)(2,1)S(1)} %collective-permute-done.26.refs_1_), channel_id=1, source_target_pairs={{0,1},{1,0},{2,3},{3,2},{4,5},{5,4},{6,7},{7,6},{8,9},{9,8},{10,11... | collective-permute-start | bytes 1179656 | tf_op jit(solution)/shard_map/ppermute | solution.py:653
  74.9 7.8 %collective-permute-start.29 = (bf16[2,256,384]{2,1,0:T(8,128)(2,1)S(1)}, bf16[2,256,384]{2,1,0:T(8,128)(2,1)S(1)}, u32[]{:S(2)}, u32[]{:S(2)}) collective-permute-start(bf16[2,256,384]{2,1,0:T(8,128)(2,1)S(1)} %collective-permute-done.26.refs_1_), channel_id=1, source_target_pairs={{0,2},{1,5},{2,0},{3,7},{4,6},{5,1},{6,4},{7,3},{8,10},{9,13},{10,... | collective-permute-start | bytes 1179656 | tf_op jit(solution)/shard_map/ppermute | solution.py:664
  77.9 7.4 %collective-permute-start.28 = (bf16[2,160,384]{2,1,0:T(8,128)(2,1)S(1)}, bf16[2,160,384]{2,1,0:T(8,128)(2,1)S(1)}, u32[]{:S(2)}, u32[]{:S(2)}) collective-permute-start(bf16[2,160,384]{2,1,0:T(8,128)(2,1)S(1)} %collective-permute-done.24.refs_3_.refs_1_), channel_id=1, source_target_pairs={{0,2},{1,5},{2,0},{3,7},{4,6},{5,1},{6,4},{7,3},{8,10},{9,13},{10,... | collective-permute-start | bytes 737288 | tf_op jit(solution)/shard_map/ppermute | solution.py:664
  82.7 2.8 %collective-permute-start.37 = (bf16[2,256,384]{2,1,0:T(8,128)(2,1)S(1)}, bf16[2,256,384]{2,1,0:T(8,128)(2,1)S(1)}, u32[]{:S(2)}, u32[]{:S(2)}) collective-permute-start(bf16[2,256,384]{2,1,0:T(8,128)(2,1)S(1)} %collective-permute-done.29.refs_0_), channel_id=1, source_target_pairs={{0,1},{1,0},{2,3},{3,2},{4,5},{5,4},{6,7},{7,6},{8,9},{9,8},{10,11... | collective-permute-start | bytes 1179656 | tf_op jit(solution)/shard_map/ppermute | solution.py:653
  85.3 2.9 %collective-permute-start.36 = (bf16[2,160,384]{2,1,0:T(8,128)(2,1)S(1)}, bf16[2,160,384]{2,1,0:T(8,128)(2,1)S(1)}, u32[]{:S(2)}, u32[]{:S(2)}) collective-permute-start(bf16[2,160,384]{2,1,0:T(8,128)(2,1)S(1)} %collective-permute-done.28.refs_3_), channel_id=1, source_target_pairs={{0,1},{1,0},{2,3},{3,2},{4,5},{5,4},{6,7},{7,6},{8,9},{9,8},{10,11... | collective-permute-start | bytes 737288 | tf_op jit(solution)/shard_map/ppermute | solution.py:653
  (14 other events, 42.2 us)
